TPU v7x, 256 devices: a whole 4x4x8 slice. The times are simulated.
256 devices in a mesh: dp: 128 (over z, y, x_hi, core), seq: 2 (over x_lo).
Axes of the slice: x: 4 (x_hi: 2, x_lo: 2; x = x_hi * 2 + x_lo), y: 4, z: 8, core: 2. Of those that a mesh axis runs over, the one named last changes fastest.
Arguments:
- hidden: bfloat16 [49152, 4096], P('dp'), may hold values from -6 to 6
- queries: bfloat16 [49152, 4096], P('dp', 'seq')
- keys: bfloat16 [49152, 1024], P('dp', 'seq')
- value_codes: bfloat16 [4096, 1024], P('dp', 'seq'), may hold values from -127 to 127, as said below
- value_scale: float32 [1024], P('seq'), may hold values from 0.0001 to 0.0004
- upstream: bfloat16 [49152, 4096], P('dp', 'seq'), may hold values from -6 to 6
- lengths: int32 [128, 4], P('dp'), may hold values from 1 to 288, 384 in all within a row
Outputs:
- grad_queries: bfloat16 [49152, 4096], P('dp', 'seq')
- grad_keys: bfloat16 [49152, 1024], P('dp', 'seq')
- grad_hidden: bfloat16 [49152, 4096], P('dp', 'seq')
- grad_log_scale: float32 [1024], P('seq')
Inputs may be any that keep to these rules, and one draw needn't show every extreme that they name: Each row holds the lengths of a pack's documents; the longest document of every pack has exactly 288 tokens. `value_codes`: whole numbers.
All inputs are finite; a program needn't handle non-finite values.
Results may differ from a plain program's by a relative error of at most 0.0076.
Values may be sent and summed in bfloat16 or wider, within the bound.
No kernel may reach another device: no remote copies, remote signals or barrier semaphores. Data moves between devices by JAX's collectives and lax.ppermute only.
A program may use at most 128 MiB of HBM per device.

v0:
```python
import jax
import jax.numpy as jnp
from jax import lax
from jax.sharding import PartitionSpec as P

D = 4096
HEADS = 32
KV_HEADS = 8


def attend(query_rows, cotangent, key_rows, value_rows, positions, doc):
    count = query_rows.shape[0]
    head_dim = D // HEADS
    group = HEADS // KV_HEADS
    kv_count = key_rows.shape[1] // head_dim
    factor = 1.0 / head_dim**0.5
    qs = query_rows.reshape(count, kv_count, group, head_dim)
    dos = cotangent.reshape(count, kv_count, group, head_dim)
    ks = key_rows.reshape(count, kv_count, head_dim)
    vs = value_rows.reshape(count, kv_count, head_dim)
    scores = jnp.einsum("qgmd,kgd->gmqk", qs, ks, preferred_element_type=jnp.float32) * factor
    keep = (positions[None, :] <= positions[:, None]) & (doc[None, :] == doc[:, None])
    scores = jnp.where(keep[None, None], scores, -1e30)
    top = jnp.max(scores, axis=-1, keepdims=True)
    expo = jnp.exp(scores - top)
    probs = expo / jnp.sum(expo, axis=-1, keepdims=True)
    probs_low = probs.astype(jnp.bfloat16)
    out = jnp.einsum("gmqk,kgd->qgmd", probs_low, vs, preferred_element_type=jnp.float32)
    dprobs = jnp.einsum("qgmd,kgd->gmqk", dos, vs, preferred_element_type=jnp.float32)
    delta = jnp.transpose(jnp.sum(dos.astype(jnp.float32) * out, axis=-1), (1, 2, 0))
    dscores = (probs * (dprobs - delta[..., None])).astype(jnp.bfloat16)
    dquery = jnp.einsum("gmqk,kgd->qgmd", dscores, ks, preferred_element_type=jnp.float32) * factor
    dkey = jnp.einsum("gmqk,qgmd->kgd", dscores, qs, preferred_element_type=jnp.float32) * factor
    dvalue = jnp.einsum("gmqk,qgmd->kgd", probs_low, dos, preferred_element_type=jnp.float32)
    return (
        dquery.reshape(count, -1),
        dkey.reshape(count, kv_count * head_dim),
        dvalue.reshape(count, kv_count * head_dim),
    )


def shards(hidden, queries, keys, value_codes, value_scale, upstream, lengths):
    count = hidden.shape[0]
    ends = jnp.cumsum(lengths[0])
    positions = jnp.arange(count)
    doc = jnp.sum((positions[:, None] >= ends[None, :]).astype(jnp.int32), axis=1)
    codes_cols = lax.all_gather(value_codes, "dp", axis=0, tiled=True)
    raw = jnp.dot(hidden, codes_cols, preferred_element_type=jnp.float32)
    values = (raw * value_scale[None, :]).astype(jnp.bfloat16)
    dquery, dkey, dvalue = attend(queries, upstream, keys, values, positions, doc)
    grad_queries = dquery.astype(jnp.bfloat16)
    grad_keys = dkey.astype(jnp.bfloat16)
    totals = lax.psum(jnp.sum(dvalue * raw, axis=0), "dp")
    grad_log_scale = value_scale * totals
    scaled = (dvalue * value_scale[None, :]).astype(jnp.bfloat16)
    partial_grad = lax.dot_general(
        scaled, codes_cols, (((1,), (1,)), ((), ())), preferred_element_type=jnp.float32
    )
    grad_hidden = lax.psum_scatter(partial_grad, "seq", scatter_dimension=1, tiled=True)
    return (grad_queries, grad_keys, grad_hidden.astype(jnp.bfloat16), grad_log_scale)


def solution(mesh):
    placed = (
        P("dp", None),
        P("dp", "seq"),
        P("dp", "seq"),
        P("dp", "seq"),
        P("seq"),
        P("dp", "seq"),
        P("dp", None),
    )
    return jax.shard_map(
        shards,
        mesh=mesh,
        in_specs=placed,
        out_specs=(P("dp", "seq"), P("dp", "seq"), P("dp", "seq"), P("seq")),
        check_vma=False,
    )
```

profile of v0, /device:TPU:1, one launch (start us, length us, event | category | flops | bytes accessed | tf_op | source)
XLA Modules:
  0.0 508.2 jit_solution(8103630339299596449)
XLA Ops:
  7.2 0.0 copy-start
  7.2 0.0 copy-start.8
  7.2 0.0 all-gather.2.cloned.1.call-start
  7.2 0.7 all-gather.2.cloned.1.call-update
  7.9 0.0 reduce-scatter.2.cloned.1.call-start
  8.0 2.0 reshape.97
  10.0 1.2 copy.47
  11.2 2.6 copy.61
  13.8 2.6 copy.28
  16.4 0.0 copy-done.8
  16.4 0.2 reduce-window.8
  16.6 0.1 convert_reduce_fusion
  16.7 0.8 fusion.13
  17.5 8.8 %fusion.18 = (f32[4,4,384]{2,1,0:T(4,128)}, f32[4,4,384,384]{2,3,1,0:T(8,128)}) fusion(pred[384,384]{0,1:T(8,128)(4,1)} %fusion.13, bf16[384,4,128,1]{0,2,3,1:T(8,128)(2,1)S(1)} %copy.47, bf16[384,4,4,128]{0,3,2,1:T(8,128)(2,1)} %bitcast.71), kind=kOutput, calls=%fused_computation.30 | convolution fusion | flops 613417344 | bytes 11575296 | tf_op jit(solution)/shard_map/sub | solution.py:25
  26.3 0.0 copy-start.2
  26.3 4.9 fusion.7
  31.2 0.0 copy-start.1
  31.2 2.1 copy-done.1
  33.3 0.0 copy-done.2
  33.3 0.0 copy-start.6
  33.3 2.4 fusion.19
  35.7 2.3 copy.60
  38.0 98.0 %all-gather.2.cloned.1.call-done = bf16[4096,512]{1,0:T(8,128)(2,1)} async-done(((bf16[32,512]{1,0:T(8,128)(2,1)}), bf16[4096,512]{1,0:T(8,128)(2,1)}) %all-gather.2.cloned.1.call-update) | async-done | bytes 4194320 | tf_op jit(solution)/shard_map/all_gather | solution.py:47
  136.0 0.0 copy-done.6
  136.0 7.0 %fusion.14 = f32[384,4096]{1,0:T(8,128)} fusion(bf16[4096,512]{1,0:T(8,128)(2,1)} %all-gather.2.cloned.1.call-done, f32[384,512]{1,0:T(8,128)} %copy.60, f32[512]{0:T(512)S(1)} %copy-done.6), kind=kOutput, calls=%fused_computation.24 | convolution fusion | flops 1611005952 | bytes 11274240 | tf_op jit(solution)/shard_map/dot_general | solution.py:56
  142.9 0.0 reduce-scatter.2.cloned.1.call-update
  143.0 0.0 copy-done
  143.0 4.9 multiply_reduce_fusion
  147.9 324.8 %psum.7 = f32[512]{0:T(512)S(1)} all-reduce(f32[512]{0:T(512)S(1)} %get-tuple-element.12), channel_id=1, replica_groups=mesh['dp'=128,'seq'=2] {'dp'}, use_global_device_ids=true, to_apply=%region_7.8 | all-reduce | flops 512 | bytes 4096 | tf_op jit(solution)/shard_map/psum | solution.py:53
  472.7 0.6 mul.62
  473.3 1.8 reshape.99
  475.1 2.0 copy.44
  477.1 0.0 copy-start.3
  477.1 0.0 copy-start.5
  477.1 0.0 copy-start.7
  477.1 4.1 fusion.8
  481.2 0.0 copy-done.3
  481.2 0.0 copy-done.5
  481.2 0.0 copy-done.7
  481.2 4.7 fusion.2
  486.0 0.0 copy-start.4
  486.0 2.1 copy-done.4
  488.1 2.2 multiply_convert_fusion
  490.2 2.6 copy.39
  492.8 4.3 fusion.10
  497.2 0.9 copy.40
  498.1 0.0 reduce-scatter.2.cloned.1.call-done
  498.1 3.3 convert_element_type.51
Async XLA Ops:
  7.2 135.8 %copy-start = (bf16[384,4096]{1,0:T(8,128)(2,1)S(1)}, bf16[384,4096]{1,0:T(8,128)(2,1)}, u32[]{:S(2)}) copy-start(bf16[384,4096]{1,0:T(8,128)(2,1)} %param.7) | copy-start | bytes 9437188
  7.2 9.2 %copy-start.8 = (s32[1,4]{1,0:T(1,128)S(1)}, s32[1,4]{1,0:T(1,128)}, u32[]{:S(2)}) copy-start(s32[1,4]{1,0:T(1,128)} %param.13) | copy-start | bytes 52
  7.2 128.8 %all-gather.2.cloned.1.call-start = ((), (), s32[]{:S(2)}) async-start(), calls=%async_computation.1 | async-start | bytes 4227072 | tf_op jit(solution)/shard_map/all_gather | solution.py:47
  7.9 490.2 %reduce-scatter.2.cloned.1.call-start = ((), (), s32[]{:S(2)}) async-start(), calls=%async_computation.2 | async-start | bytes 9437184 | tf_op jit(solution)/shard_map/reduce_scatter | solution.py:59
  26.3 7.0 %copy-start.2 = (bf16[384,2048]{0,1:T(8,128)(2,1)S(1)}, bf16[384,2048]{0,1:T(8,128)(2,1)}, u32[]{:S(2)}) copy-start(bf16[384,2048]{0,1:T(8,128)(2,1)} %copy.28) | copy-start | bytes 4718596
  31.2 2.1 copy-start.1
  33.3 102.7 %copy-start.6 = (f32[512]{0:T(512)S(1)}, f32[512]{0:T(512)}, u32[]{:S(2)}) copy-start(f32[512]{0:T(512)} %param.11) | copy-start | bytes 6148
  477.1 4.1 copy-start.3
  477.1 4.1 copy-start.5
  477.1 4.1 copy-start.7
  486.0 2.1 copy-start.4
Sparse Core Ops, SparseCore 0:
  11.9 124.0 all-gather.1
  143.1 79.6 reduce-scatter.1
where the time goes:
time: 511 us; the launch traced here: 508 us
  blocking collectives  325 us (64%)
  waiting for transfers between devices  98.7 us (19%)
  matrix products  38.4 us (8%)
  local copies, waits for them, and re-layouts  22.3 us (4%)
  between operations  14.2 us (3%)
  other arithmetic  9.78 us (2%)
    psum x1, blocking collectives, shards(): totals = lax.psum(jnp.sum(dvalue * raw, axis=0), 'dp')  325 us
    all_gather x1, waiting for transfers between devices, shards(): codes_cols = lax.all_gather(value_codes, 'dp', axis=0, tiled=True)  98 us
    unnamed x21, local copies, waits for them, and re-layouts  10.3 us
  transfers between devices with their start and end apart: 2, of which 1 were waited for; matrix products, arithmetic and copies ran while one was open for 11% of the time, Pallas kernels for 0%

commit v1 on v0

v1 whole, which is shorter than its diff:
```python
import functools
import math

import jax
import jax.numpy as jnp
from jax import lax
from jax.experimental import pallas as pl
from jax.experimental.pallas import tpu as pltpu
from jax.sharding import PartitionSpec as P

COUNT = 384
HEAD = 128
GROUP = 4
BLOCK = 128
BLOCKS = COUNT // BLOCK
FACTOR = 1.0 / math.sqrt(HEAD)
LOG2E = math.log2(math.e)
BF16 = jnp.bfloat16
F32 = jnp.float32
VMEM_LIMIT = 40 * 1024 * 1024


def dot(a, b, dims):
    return lax.dot_general(a, b, ((dims[:1], dims[1:]), ((), ())), preferred_element_type=F32)


def probs_kernel(lengths_ref, q_ref, k_ref, up_ref, scale_ref, p_ref, dv_ref, scaled_ref, bias_ref, dv_acc):
    @pl.when(pl.program_id(0) == 0)
    def _():
        rows = lax.broadcasted_iota(jnp.int32, (COUNT, COUNT), 0)
        cols = lax.broadcasted_iota(jnp.int32, (COUNT, COUNT), 1)
        start = jnp.zeros((COUNT, COUNT), jnp.int32)
        end = jnp.int32(0)
        for doc in range(3):
            end = end + lengths_ref[0, doc]
            start = jnp.where(rows >= end, end, start)
        bias_ref[...] = jnp.where((cols <= rows) & (cols >= start), 0.0, -1e30).astype(F32)

    dv_acc[...] = jnp.zeros_like(dv_acc)
    for i in range(BLOCKS):
        width = BLOCK * (i + 1)
        at = pl.ds(BLOCK * i, BLOCK)
        keys = k_ref[:width, :]
        for h in range(GROUP):
            head = pl.ds(HEAD * h, HEAD)
            scores = dot(q_ref[at, head], keys, (1, 1)) * (FACTOR * LOG2E) + bias_ref[at, :width]
            expo = jnp.exp2(scores - jnp.max(scores, axis=1, keepdims=True))
            probs = expo * (1.0 / jnp.sum(expo, axis=1, keepdims=True))
            p_ref[h, at, :width] = probs.astype(BF16)
        low = jnp.concatenate([p_ref[h, at, :width] for h in range(GROUP)], axis=0)
        ups = jnp.concatenate([up_ref[at, pl.ds(HEAD * h, HEAD)] for h in range(GROUP)], axis=0)
        dv_acc[:width, :] += dot(low, ups, (0, 0))
    dv_ref[...] = dv_acc[...]
    scaled_ref[...] = (dv_acc[...] * scale_ref[...]).astype(BF16)


def probs_part(lengths, queries, keys, upstream, scale):
    wide = pl.BlockSpec((COUNT, GROUP * HEAD), lambda g: (0, g))
    narrow = pl.BlockSpec((COUNT, HEAD), lambda g: (0, g))
    kv = keys.shape[1] // HEAD
    return pl.pallas_call(
        probs_kernel,
        grid=(kv,),
        in_specs=[pl.BlockSpec(memory_space=pltpu.SMEM), wide, narrow, wide, pl.BlockSpec((1, HEAD), lambda g: (0, g))],
        out_specs=[pl.BlockSpec((GROUP, COUNT, COUNT), lambda g: (g, 0, 0)), narrow, narrow],
        out_shape=[
            jax.ShapeDtypeStruct((kv * GROUP, COUNT, COUNT), BF16),
            jax.ShapeDtypeStruct(keys.shape, F32),
            jax.ShapeDtypeStruct(keys.shape, BF16),
        ],
        scratch_shapes=[pltpu.VMEM((COUNT, COUNT), F32), pltpu.VMEM((COUNT, HEAD), F32)],
        compiler_params=pltpu.CompilerParams(vmem_limit_bytes=VMEM_LIMIT),
        cost_estimate=pl.CostEstimate(flops=2_400_000_000, bytes_accessed=9_000_000, transcendentals=1_600_000),
        name="probs_part",
    )(lengths, queries, keys, upstream, scale)


def grads_kernel(q_ref, k_ref, up_ref, v_ref, p_ref, gq_ref, gk_ref, ds_ref, dk_acc):
    dk_acc[...] = jnp.zeros_like(dk_acc)
    for i in range(BLOCKS):
        width = BLOCK * (i + 1)
        at = pl.ds(BLOCK * i, BLOCK)
        keys = k_ref[:width, :]
        values = v_ref[:width, :]
        for h in range(GROUP):
            head = pl.ds(HEAD * h, HEAD)
            dprobs = dot(up_ref[at, head], values, (1, 1))
            probs = p_ref[h, at, :width].astype(F32)
            delta = jnp.sum(probs * dprobs, axis=1, keepdims=True)
            dscores = (probs * (dprobs - delta)).astype(BF16)
            ds_ref[pl.ds(BLOCK * h, BLOCK), :width] = dscores
            gq_ref[at, head] = (dot(dscores, keys, (1, 0)) * FACTOR).astype(BF16)
        qs = jnp.concatenate([q_ref[at, pl.ds(HEAD * h, HEAD)] for h in range(GROUP)], axis=0)
        dk_acc[:width, :] += dot(ds_ref[:, :width], qs, (0, 0))
    gk_ref[...] = (dk_acc[...] * FACTOR).astype(BF16)


def grads_part(queries, keys, upstream, values, probs):
    wide = pl.BlockSpec((COUNT, GROUP * HEAD), lambda g: (0, g))
    narrow = pl.BlockSpec((COUNT, HEAD), lambda g: (0, g))
    kv = keys.shape[1] // HEAD
    return pl.pallas_call(
        grads_kernel,
        grid=(kv,),
        in_specs=[wide, narrow, wide, narrow, pl.BlockSpec((GROUP, COUNT, COUNT), lambda g: (g, 0, 0))],
        out_specs=[wide, narrow],
        out_shape=[jax.ShapeDtypeStruct(queries.shape, BF16), jax.ShapeDtypeStruct(keys.shape, BF16)],
        scratch_shapes=[pltpu.VMEM((GROUP * BLOCK, COUNT), BF16), pltpu.VMEM((COUNT, HEAD), F32)],
        compiler_params=pltpu.CompilerParams(vmem_limit_bytes=VMEM_LIMIT),
        cost_estimate=pl.CostEstimate(flops=2_400_000_000, bytes_accessed=9_000_000, transcendentals=0),
        name="grads_part",
    )(queries, keys, upstream, values, probs)


Z_ORDER = (0, 4, 2, 6, 1, 5, 3, 7)
SHARD = 32
HALF = 256


def raw_kernel(at_ref, hidden_ref, dv_ref, scale_ref, *refs):
    pieces, (codes_ref, values_ref, sums_ref, raw_ref) = refs[:-4], refs[-4:]
    z, y, x, c = at_ref[0], at_ref[1], at_ref[2], at_ref[3]

    def place(piece, row, zi, k, xi, ci, col):
        to = (((z ^ Z_ORDER[zi]) * 4 + ((y + 4 - k) & 3)) * 2 + (x ^ xi)) * 2 + (c ^ ci)
        rows = pl.ds(pl.multiple_of(to * SHARD, SHARD), SHARD)
        codes_ref[rows, pl.ds(col, HALF)] = piece[pl.ds(row, SHARD), :]

    for ci in range(2):
        for k in range(4):
            piece = pieces[6 * ci + k]
            for xi in range(2):
                for zi in range(8):
                    place(piece, (xi * 8 + zi) * SHARD, zi, k, xi, ci, 0)
        for xi in range(2):
            piece = pieces[6 * ci + 4 + xi]
            for k in range(4):
                for zi in range(8):
                    place(piece, (k * 8 + zi) * SHARD, zi, k, xi, ci, HALF)
    raw_ref[...] = jnp.zeros_like(raw_ref)
    step = 512

    @pl.loop(0, hidden_ref.shape[1] // step)
    def _(i):
        depth = pl.ds(pl.multiple_of(i * step, step), step)
        raw_ref[...] += dot(hidden_ref[:, depth], codes_ref[depth, :], (1, 0))

    values_ref[...] = (raw_ref[...] * scale_ref[...]).astype(BF16)
    sums_ref[...] = jnp.sum(raw_ref[...] * dv_ref[...], axis=0, keepdims=True)


def raw_part(at, hidden, dv, scale, pieces):
    depth, width = hidden.shape[1], dv.shape[1]
    vmem = pl.BlockSpec(memory_space=pltpu.VMEM)
    return pl.pallas_call(
        raw_kernel,
        in_specs=[pl.BlockSpec(memory_space=pltpu.SMEM)] + [vmem] * (3 + len(pieces)),
        out_specs=[vmem] * 3,
        out_shape=[
            jax.ShapeDtypeStruct((depth, width), BF16),
            jax.ShapeDtypeStruct(dv.shape, BF16),
            jax.ShapeDtypeStruct((1, width), F32),
        ],
        scratch_shapes=[pltpu.VMEM(dv.shape, F32)],
        compiler_params=pltpu.CompilerParams(vmem_limit_bytes=VMEM_LIMIT),
        cost_estimate=pl.CostEstimate(flops=1_700_000_000, bytes_accessed=13_000_000, transcendentals=0),
        name="raw_part",
    )(at, hidden, dv, scale, *pieces)


QUARTER = 512


def hidden_kernel(at_ref, own_ref, other_ref, codes_ref, near0, near1, far0, far1, out_ref):
    c = at_ref[3]
    for other, quarters in enumerate(((near0, near1), (far0, far1))):
        for i, quarter in enumerate(quarters):
            rows = pl.ds(pl.multiple_of(((c ^ other) * 2 + i) * QUARTER, QUARTER), QUARTER)
            total = dot(own_ref[...], codes_ref[rows, :], (1, 1)) + dot(other_ref[...], quarter[...], (1, 1))
            out_ref[:, rows] = total.astype(BF16)


def hidden_part(at, own, other, codes, quarters):
    vmem = pl.BlockSpec(memory_space=pltpu.VMEM)
    return pl.pallas_call(
        hidden_kernel,
        in_specs=[pl.BlockSpec(memory_space=pltpu.SMEM)] + [vmem] * 7,
        out_specs=vmem,
        out_shape=jax.ShapeDtypeStruct((own.shape[0], 4 * QUARTER), BF16),
        compiler_params=pltpu.CompilerParams(vmem_limit_bytes=VMEM_LIMIT),
        cost_estimate=pl.CostEstimate(flops=1_700_000_000, bytes_accessed=8_000_000, transcendentals=0),
        name="hidden_part",
    )(at, own, other, codes, *quarters)


def pairs(move):
    out = []
    for i in range(128):
        z, y, x, c = move(i // 16, i // 4 % 4, i // 2 % 2, i % 2)
        out.append((i, ((z * 4 + y) * 2 + x) * 2 + c))
    return out


def z_swap(bit):
    return pairs(lambda z, y, x, c: (z ^ bit, y, x, c))


def y_shift(k):
    return pairs(lambda z, y, x, c: (z, (y + k) % 4, x, c))


def y_swap(bit):
    return pairs(lambda z, y, x, c: (z, y ^ bit, x, c))


X_SWAP = pairs(lambda z, y, x, c: (z, y, x ^ 1, c))
C_SWAP = pairs(lambda z, y, x, c: (z, y, x, c ^ 1))
BESIDE = [(2 * a + s, 2 * b + 1 - s) for a, b in X_SWAP for s in range(2)]


def send(x, perm):
    return lax.ppermute(x, "dp", perm)


def gather(shard):
    rows = shard
    for bit in (4, 2, 1):
        rows = jnp.concatenate([rows, send(rows, z_swap(bit))], axis=0)
    first, second = rows[:, :HALF], rows[:, HALF:]
    first_x = send(first, X_SWAP)
    second_y = [send(second, y_shift(k)) for k in (1, 2, 3)]
    first = jnp.concatenate([first, first_x], axis=0)
    second = jnp.concatenate([second] + second_y, axis=0)
    firsts = [first] + [send(first, y_shift(k)) for k in (1, 2, 3)]
    seconds = [second, send(second, X_SWAP)]
    mine = firsts + seconds
    return mine + [send(piece, C_SWAP) for piece in mine]


def shards(hidden, queries, keys, value_codes, value_scale, upstream, lengths):
    me, s = lax.axis_index("dp"), lax.axis_index("seq")
    at = jnp.stack([me // 16, me // 4 % 4, me // 2 % 2, me % 2]).astype(jnp.int32)
    scale = value_scale.reshape(1, -1)
    pieces = gather(value_codes)
    probs, dv, scaled = probs_part(lengths, queries, keys, upstream, scale)
    scaled_other = lax.ppermute(scaled, "seq", [(0, 1), (1, 0)])
    codes, values, sums = raw_part(at, hidden, dv, scale, pieces)
    base = 2048 * (1 - s) + 1024 * at[3]
    near0 = lax.ppermute(lax.dynamic_slice_in_dim(codes, base, QUARTER, 0), "seq", [(0, 1), (1, 0)])
    near1 = lax.ppermute(lax.dynamic_slice_in_dim(codes, base + QUARTER, QUARTER, 0), ("dp", "seq"), BESIDE)
    far0, far1 = send(near0, C_SWAP), send(near1, C_SWAP)
    for perm in (z_swap(4), z_swap(2), z_swap(1), y_swap(2), y_swap(1), X_SWAP, C_SWAP):
        sums = sums + send(sums, perm)
    grad_log_scale = (scale * sums).reshape(-1)
    grad_queries, grad_keys = grads_part(queries, keys, upstream, values, probs)
    own_codes = lax.dynamic_slice_in_dim(codes, 2048 * s, 2048, 0)
    grad_hidden = hidden_part(at, scaled, scaled_other, own_codes, (near0, near1, far0, far1))
    return grad_queries, grad_keys, grad_hidden, grad_log_scale


def solution(mesh):
    placed = (
        P("dp", None),
        P("dp", "seq"),
        P("dp", "seq"),
        P("dp", "seq"),
        P("seq"),
        P("dp", "seq"),
        P("dp", None),
    )
    return jax.shard_map(
        shards,
        mesh=mesh,
        in_specs=placed,
        out_specs=(P("dp", "seq"), P("dp", "seq"), P("dp", "seq"), P("seq")),
        check_vma=False,
    )
```

time: 511 us -> 134 us (0.26)
  blocking collectives: 325 us -> 0 us
  waiting for transfers between devices: 98.7 us -> 29 us
  starting transfers between devices: 0.08 us -> 59.8 us
  matrix products: 38.4 us -> 0 us
  Pallas kernels: 0 us -> 28 us
  between operations: 14.2 us -> 0.85 us
  local copies, waits for them, and re-layouts: 22.3 us -> 13.6 us
  other arithmetic: 9.78 us -> 2.27 us
    psum x1 -> x0, blocking collectives: 325 us -> none  [shards(): totals = lax.psum(jnp.sum(dvalue * raw, axis=0), 'dp')]
    all_gather x1 -> x0, waiting for transfers between devices: 98 us -> none  [shards(): codes_cols = lax.all_gather(value_codes, 'dp', axis=0, tiled=True)]
    ppermute x0 -> x29, starting transfers between devices: none -> 59.8 us  [the longest x26 56.7 us: send(): return lax.ppermute(x, 'dp', perm)]
    dot_general x7 -> x0, matrix products: 29.6 us -> none  [the longest x1 6.96 us: shards(): lax.dot_general(scaled, codes_cols, (((1,), (1,)), ((), ())), preferred_e...]
    ppermute x0 -> x29, waiting for transfers between devices: none -> 29 us  [the longest x26 29 us: send(): return lax.ppermute(x, 'dp', perm)]
    pallas_call x0 -> x4, Pallas kernels: none -> 28 us  [the longest x1 11.9 us: grads_part(): pl.pallas_call(grads_kernel, grid=(kv,), in_specs=[wide, narrow, wide, na...]
    reshape x6 -> x0, local copies, waits for them, and re-layouts: 11.9 us -> none  [the longest x2 3.79 us: attend(): vs = value_rows.reshape(count, kv_count, head_dim)]
    sub x1 -> x0, matrix products: 8.85 us -> none  [attend(): expo = jnp.exp(scores - top)]
  transfers between devices with their start and end apart: 2 -> 29, of which waited for: 1 -> 12; matrix products, arithmetic and copies ran while one was open for 11% -> 2% of each run, Pallas kernels for 0% -> 15%
where the time goes in v1:
time: 134 us
  starting transfers between devices  59.8 us (45%)
  waiting for transfers between devices  29 us (22%)
  Pallas kernels  28 us (21%)
  local copies, waits for them, and re-layouts  13.6 us (10%)
  other arithmetic  2.27 us (2%)
    ppermute x26, starting transfers between devices, send(): return lax.ppermute(x, 'dp', perm)  56.7 us
    ppermute x26, waiting for transfers between devices, send(): return lax.ppermute(x, 'dp', perm)  29 us
    pallas_call x1, Pallas kernels, grads_part(): pl.pallas_call(grads_kernel, grid=(kv,), in_specs=[wide, narrow, wide, na...  11.9 us
    unnamed x35, local copies, waits for them, and re-layouts  11.8 us
    pallas_call x1, Pallas kernels, probs_part(): pl.pallas_call(probs_kernel, grid=(kv,), in_specs=[pl.BlockSpec(memory_sp...  7.9 us
    pallas_call x1, Pallas kernels, raw_part(): pl.pallas_call(raw_kernel, in_specs=[pl.BlockSpec(memory_space=pltpu.SMEM...  4.79 us
    pallas_call x1, Pallas kernels, hidden_part(): pl.pallas_call(hidden_kernel, in_specs=[pl.BlockSpec(memory_space=pltpu.S...  3.51 us
  transfers between devices with their start and end apart: 29, of which 12 were waited for; matrix products, arithmetic and copies ran while one was open for 2% of the time, Pallas kernels for 15%

profile of v1, /device:TPU:1, one launch (start us, length us, event | category | flops | bytes accessed | tf_op | source)
XLA Modules:
  0.0 133.5 jit_solution(4015991335853970471)
XLA Ops:
  0.7 7.8 %collective-permute-start = (bf16[32,512]{1,0:T(8,128)(2,1)}, bf16[32,512]{1,0:T(8,128)(2,1)S(1)}, u32[]{:S(2)}, u32[]{:S(2)}) collective-permute-start(bf16[32,512]{1,0:T(8,128)(2,1)} %param.10), channel_id=1, source_target_pairs={{0,128},{2,130},{4,132},{6,134},{8,136},{10,138},{12,140},{14,142}... | collective-permute-start | bytes 98312 | tf_op jit(solution)/shard_map/ppermute | solution.py:222
  8.5 1.5 %collective-permute-done = bf16[32,512]{1,0:T(8,128)(2,1)S(1)} collective-permute-done((bf16[32,512]{1,0:T(8,128)(2,1)}, bf16[32,512]{1,0:T(8,128)(2,1)S(1)}, u32[]{:S(2)}, u32[]{:S(2)}) %collective-permute-start) | collective-permute-done | bytes 32800 | tf_op jit(solution)/shard_map/ppermute | solution.py:222
  10.0 0.8 pad_maximum_fusion.3
  10.8 1.4 %collective-permute-start.1 = (bf16[64,512]{1,0:T(8,128)(2,1)S(1)}, bf16[64,512]{1,0:T(8,128)(2,1)S(1)}, u32[]{:S(2)}, u32[]{:S(2)}) collective-permute-start(bf16[64,512]{1,0:T(8,128)(2,1)S(1)} %pad_maximum_fusion.3), channel_id=1, source_target_pairs={{0,64},{2,66},{4,68},{6,70},{8,72},{10,74},{12,76},{14,78},{16,80}... | collective-permute-start | bytes 196616 | tf_op jit(solution)/shard_map/ppermute | solution.py:222
  12.2 0.8 constant_dynamic-update-slice_fusion.3
  13.0 2.5 %collective-permute-done.1 = bf16[64,512]{1,0:T(8,128)(2,1)S(1)} collective-permute-done((bf16[64,512]{1,0:T(8,128)(2,1)S(1)}, bf16[64,512]{1,0:T(8,128)(2,1)S(1)}, u32[]{:S(2)}, u32[]{:S(2)}) %collective-permute-start.1) | collective-permute-done | bytes 65568 | tf_op jit(solution)/shard_map/ppermute | solution.py:222
  15.5 0.8 pad_maximum_fusion.2
  16.5 3.7 %collective-permute-done.2 = bf16[128,512]{1,0:T(8,128)(2,1)S(1)} collective-permute-done((bf16[128,512]{1,0:T(8,128)(2,1)S(1)}, bf16[128,512]{1,0:T(8,128)(2,1)S(1)}, u32[]{:S(2)}, u32[]{:S(2)}) %collective-permute-start.2) | collective-permute-done | bytes 131104 | tf_op jit(solution)/shard_map/ppermute | solution.py:222
  20.2 1.4 %collective-permute-start.7 = (bf16[256,256]{1,0:T(8,128)(2,1)S(1)}, bf16[256,256]{1,0:T(8,128)(2,1)S(1)}, u32[]{:S(2)}, u32[]{:S(2)}) collective-permute-start(bf16[256,256]{1,0:T(8,128)(2,1)S(1)} %get-tuple-element.22), channel_id=1, source_target_pairs={{0,8},{2,10},{4,12},{6,14},{8,16},{10,18},{12,20},{14,22},{16,24},... | collective-permute-start | bytes 393224 | tf_op jit(solution)/shard_map/ppermute | solution.py:222
  21.6 2.6 %collective-permute-start.8 = (bf16[256,256]{1,0:T(8,128)(2,1)S(1)}, bf16[256,256]{1,0:T(8,128)(2,1)S(1)}, u32[]{:S(2)}, u32[]{:S(2)}) collective-permute-start(bf16[256,256]{1,0:T(8,128)(2,1)S(1)} %get-tuple-element.22), channel_id=1, source_target_pairs={{0,16},{2,18},{4,20},{6,22},{8,24},{10,26},{12,28},{14,30},{16,0},... | collective-permute-start | bytes 393224 | tf_op jit(solution)/shard_map/ppermute | solution.py:222
  24.2 1.1 collective-permute-start.9
  25.4 2.6 %collective-permute-done.8 = bf16[256,256]{1,0:T(8,128)(2,1)S(1)} collective-permute-done((bf16[256,256]{1,0:T(8,128)(2,1)S(1)}, bf16[256,256]{1,0:T(8,128)(2,1)S(1)}, u32[]{:S(2)}, u32[]{:S(2)}) %collective-permute-start.8) | collective-permute-done | bytes 131104 | tf_op jit(solution)/shard_map/ppermute | solution.py:222
  28.0 2.8 %collective-permute-start.10 = (bf16[1024,256]{1,0:T(8,128)(2,1)S(1)}, bf16[1024,256]{1,0:T(8,128)(2,1)S(1)}, u32[]{:S(2)}, u32[]{:S(2)}) collective-permute-start(bf16[1024,256]{1,0:T(8,128)(2,1)S(1)} %pad_maximum_fusion.refs_4_), channel_id=1, source_target_pairs={{0,4},{2,6},{4,0},{6,2},{8,12},{10,14},{12,8},{14,10},{16,20},{18,... | collective-permute-start | bytes 1572872 | tf_op jit(solution)/shard_map/ppermute | solution.py:222
  31.1 9.2 %collective-permute-done.3 = bf16[256,256]{1,0:T(8,128)(2,1)S(1)} collective-permute-done((bf16[256,256]{1,0:T(8,128)(2,1)S(1)}, bf16[256,256]{1,0:T(8,128)(2,1)S(1)}, u32[]{:S(2)}, u32[]{:S(2)}) %collective-permute-start.3) | collective-permute-done | bytes 131104 | tf_op jit(solution)/shard_map/ppermute | solution.py:222
  40.3 1.3 collective-permute-start.4
  41.6 2.3 %collective-permute-start.5 = (bf16[512,256]{1,0:T(8,128)(2,1)S(1)}, bf16[512,256]{1,0:T(8,128)(2,1)S(1)}, u32[]{:S(2)}, u32[]{:S(2)}) collective-permute-start(bf16[512,256]{1,0:T(8,128)(2,1)S(1)} %pad_maximum_fusion.1.refs_0_), channel_id=1, source_target_pairs={{0,16},{2,18},{4,20},{6,22},{8,24},{10,26},{12,28},{14,30},{16,0},... | collective-permute-start | bytes 786440 | tf_op jit(solution)/shard_map/ppermute | solution.py:222
  43.9 1.7 %collective-permute-start.6 = (bf16[512,256]{1,0:T(8,128)(2,1)S(1)}, bf16[512,256]{1,0:T(8,128)(2,1)S(1)}, u32[]{:S(2)}, u32[]{:S(2)}) collective-permute-start(bf16[512,256]{1,0:T(8,128)(2,1)S(1)} %pad_maximum_fusion.1.refs_0_), channel_id=1, source_target_pairs={{0,24},{2,26},{4,28},{6,30},{8,0},{10,2},{12,4},{14,6},{16,8},{18,... | collective-permute-start | bytes 786440 | tf_op jit(solution)/shard_map/ppermute | solution.py:222
  45.6 6.7 %collective-permute-start.11 = (bf16[512,256]{1,0:T(8,128)(2,1)S(1)}, bf16[512,256]{1,0:T(8,128)(2,1)S(1)}, u32[]{:S(2)}, u32[]{:S(2)}) collective-permute-start(bf16[512,256]{1,0:T(8,128)(2,1)S(1)} %pad_maximum_fusion.1.refs_0_), channel_id=1, source_target_pairs={{0,2},{2,0},{4,6},{6,4},{8,10},{10,8},{12,14},{14,12},{16,18},{18,... | collective-permute-start | bytes 786440 | tf_op jit(solution)/shard_map/ppermute | solution.py:222
  52.3 2.1 %collective-permute-start.15 = (bf16[1024,256]{1,0:T(8,128)(2,1)S(1)}, bf16[1024,256]{1,0:T(8,128)(2,1)S(1)}, u32[]{:S(2)}, u32[]{:S(2)}) collective-permute-start(bf16[1024,256]{1,0:T(8,128)(2,1)S(1)} %pad_maximum_fusion.refs_4_), channel_id=1, source_target_pairs={{0,2},{2,0},{4,6},{6,4},{8,10},{10,8},{12,14},{14,12},{16,18},{18,... | collective-permute-start | bytes 1572872 | tf_op jit(solution)/shard_map/ppermute | solution.py:222
  54.5 3.6 %collective-permute-start.12 = (bf16[512,256]{1,0:T(8,128)(2,1)S(1)}, bf16[512,256]{1,0:T(8,128)(2,1)}, u32[]{:S(2)}, u32[]{:S(2)}) collective-permute-start(bf16[512,256]{1,0:T(8,128)(2,1)S(1)} %collective-permute-done.4.refs_1_), channel_id=1, source_target_pairs={{0,2},{2,0},{4,6},{6,4},{8,10},{10,8},{12,14},{14,12},{16,18},{18,... | collective-permute-start | bytes 786440 | tf_op jit(solution)/shard_map/ppermute | solution.py:222
  58.1 0.7 copy-done.2
  58.8 0.4 collective-permute-start.14
  59.4 1.4 %copy-done.5 = bf16[384,2048]{1,0:T(8,128)(2,1)S(1)} copy-done((bf16[384,2048]{1,0:T(8,128)(2,1)S(1)}, bf16[384,2048]{1,0:T(8,128)(2,1)}, u32[]{:S(2)}) %copy-start.5) | copy-done | bytes 1572888
  60.8 1.4 %copy-done.7 = bf16[384,2048]{1,0:T(8,128)(2,1)S(1)} copy-done((bf16[384,2048]{1,0:T(8,128)(2,1)S(1)}, bf16[384,2048]{1,0:T(8,128)(2,1)}, u32[]{:S(2)}) %copy-start.7) | copy-done | bytes 1572888
  62.2 1.0 copy-done.9
  63.2 7.9 %probs_part.1 = (bf16[16,384,384]{2,1,0:T(8,128)(2,1)S(1)}, f32[384,512]{1,0:T(8,128)S(1)}, bf16[384,512]{1,0:T(8,128)(2,1)S(1)}) custom-call(s32[1,4]{1,0:T(1,128)S(1)} %copy-done.13, bf16[384,2048]{1,0:T(8,128)(2,1)S(1)} %copy-done.5, bf16[384,512]{1,0:T(8,128)(2,1)S(1)} %copy-done.9, bf16[384,2048]{1,0:T(8,128)(2,1)S(1)} %copy-done.7, f32[1,512]{1,0:T(1,128)S(1)} %bitcast.6), custom_call_target="tpu_custom_call" | custom-call | flops 2400000000 | bytes 9000000 | tf_op jit(solution)/shard_map/probs_part/pallas_call | solution.py:61
  71.1 2.1 %copy-done.14 = bf16[16,384,384]{2,1,0:T(8,128)(2,1)} copy-done((bf16[16,384,384]{2,1,0:T(8,128)(2,1)}, bf16[16,384,384]{2,1,0:T(8,128)(2,1)S(1)}, u32[]{:S(2)}) %copy-start.14) | copy-done | bytes 4718616
  73.3 4.8 %raw_part.1 = (bf16[4096,512]{1,0:T(8,128)(2,1)S(1)}, bf16[384,512]{1,0:T(8,128)(2,1)S(1)}, f32[1,512]{1,0:T(1,128)S(1)}) custom-call(s32[4]{0:T(128)S(1)} %pad_add_fusion.at_ref, bf16[384,4096]{1,0:T(8,128)(2,1)S(1)} %copy-done, f32[384,512]{1,0:T(8,128)S(1)} %get-tuple-element.12.dv_ref, f32[1,512]{1,0:T(1,128)S(1)} %bitcast.7, ...), custom_call_target="tpu_custom_call" | custom-call | flops 1700000000 | bytes 13000000 | tf_op jit(solution)/shard_map/raw_part/pallas_call | solution.py:155
  78.1 2.0 %copy-done.1 = bf16[4096,512]{1,0:T(8,128)(2,1)} copy-done((bf16[4096,512]{1,0:T(8,128)(2,1)}, bf16[4096,512]{1,0:T(8,128)(2,1)S(1)}, u32[]{:S(2)}) %copy-start.1) | copy-done | bytes 4194328
  80.2 1.3 collective-permute-start.18
  81.5 1.8 %collective-permute-start.19 = (bf16[512,512]{1,0:T(8,128)(2,1)S(1)}, bf16[512,512]{1,0:T(8,128)(2,1)S(1)}, u32[]{:S(2)}, u32[]{:S(2)}) collective-permute-start(bf16[512,512]{1,0:T(8,128)(2,1)S(1)} %get-tuple-element.20), channel_id=1, source_target_pairs={{0,5},{1,4},{2,7},{3,6},{4,1},{5,0},{6,3},{7,2},{8,13},{9,12},{10,... | collective-permute-start | bytes 1572872 | tf_op jit(solution)/shard_map/ppermute | solution.py:250
  83.3 5.7 %collective-permute-start.22 = (f32[1,512]{1,0:T(1,128)S(1)}, f32[1,512]{1,0:T(1,128)S(1)}, u32[]{:S(2)}, u32[]{:S(2)}) collective-permute-start(f32[1,512]{1,0:T(1,128)S(1)} %get-tuple-element.19), channel_id=1, source_target_pairs={{0,128},{2,130},{4,132},{6,134},{8,136},{10,138},{12,140},{14,142}... | collective-permute-start | bytes 6152 | tf_op jit(solution)/shard_map/ppermute | solution.py:222
  89.0 1.0 collective-permute-done.22
  90.0 0.8 collective-permute-start.23
  90.8 2.8 %collective-permute-done.23 = f32[1,512]{1,0:T(1,128)S(1)} collective-permute-done((f32[1,512]{1,0:T(1,128)S(1)}, f32[1,512]{1,0:T(1,128)S(1)}, u32[]{:S(2)}, u32[]{:S(2)}) %collective-permute-start.23) | collective-permute-done | bytes 2080 | tf_op jit(solution)/shard_map/ppermute | solution.py:222
  93.6 2.7 %collective-permute-done.24 = f32[1,512]{1,0:T(1,128)S(1)} collective-permute-done((f32[1,512]{1,0:T(1,128)S(1)}, f32[1,512]{1,0:T(1,128)S(1)}, u32[]{:S(2)}, u32[]{:S(2)}) %collective-permute-start.24) | collective-permute-done | bytes 2080 | tf_op jit(solution)/shard_map/ppermute | solution.py:222
  96.3 2.1 %collective-permute-start.25 = (f32[1,512]{1,0:T(1,128)S(1)}, f32[1,512]{1,0:T(1,128)S(1)}, u32[]{:S(2)}, u32[]{:S(2)}) collective-permute-start(f32[1,512]{1,0:T(1,128)S(1)} %add.61), channel_id=1, source_target_pairs={{0,16},{2,18},{4,20},{6,22},{8,24},{10,26},{12,28},{14,30},{16,0},... | collective-permute-start | bytes 6152 | tf_op jit(solution)/shard_map/ppermute | solution.py:222
  98.5 1.8 %collective-permute-done.25 = f32[1,512]{1,0:T(1,128)S(1)} collective-permute-done((f32[1,512]{1,0:T(1,128)S(1)}, f32[1,512]{1,0:T(1,128)S(1)}, u32[]{:S(2)}, u32[]{:S(2)}) %collective-permute-start.25) | collective-permute-done | bytes 2080 | tf_op jit(solution)/shard_map/ppermute | solution.py:222
  100.3 1.5 %collective-permute-start.26 = (f32[1,512]{1,0:T(1,128)S(1)}, f32[1,512]{1,0:T(1,128)S(1)}, u32[]{:S(2)}, u32[]{:S(2)}) collective-permute-start(f32[1,512]{1,0:T(1,128)S(1)} %add.62), channel_id=1, source_target_pairs={{0,8},{2,10},{4,12},{6,14},{8,0},{10,2},{12,4},{14,6},{16,24},{18,... | collective-permute-start | bytes 6152 | tf_op jit(solution)/shard_map/ppermute | solution.py:222
  101.8 1.0 collective-permute-done.26
  102.8 1.2 collective-permute-start.27
  104.0 5.6 %collective-permute-start.20 = (bf16[512,512]{1,0:T(8,128)(2,1)S(1)}, bf16[512,512]{1,0:T(8,128)(2,1)S(1)}, u32[]{:S(2)}, u32[]{:S(2)}) collective-permute-start(bf16[512,512]{1,0:T(8,128)(2,1)S(1)} %collective-permute-done.18.near0), channel_id=1, source_target_pairs={{0,2},{2,0},{4,6},{6,4},{8,10},{10,8},{12,14},{14,12},{16,18},{18,... | collective-permute-start | bytes 1572872 | tf_op jit(solution)/shard_map/ppermute | solution.py:222
  109.7 1.7 %constant_dynamic-slice_fusion.2.codes_ref = bf16[2048,512]{1,0:T(8,128)(2,1)S(1)} fusion(bf16[4096,512]{1,0:T(8,128)(2,1)} %copy-done.1, s32[]{:T(128)S(6)} %select_n.40), kind=kLoop, calls=%fused_computation.11 | loop fusion | bytes 4194308 | tf_op jit(solution)/shard_map/dynamic_slice | solution.py:256
  111.5 3.8 %collective-permute-start.28 = (f32[1,512]{1,0:T(1,128)S(1)}, f32[1,512]{1,0:T(1,128)S(1)}, u32[]{:S(2)}, u32[]{:S(2)}) collective-permute-start(f32[1,512]{1,0:T(1,128)S(1)} %add.64), channel_id=1, source_target_pairs={{0,2},{2,0},{4,6},{6,4},{8,10},{10,8},{12,14},{14,12},{16,18},{18,... | collective-permute-start | bytes 6152 | tf_op jit(solution)/shard_map/ppermute | solution.py:222
  115.3 2.3 %copy-done.15 = bf16[16,384,384]{2,1,0:T(8,128)(2,1)S(1)} copy-done((bf16[16,384,384]{2,1,0:T(8,128)(2,1)S(1)}, bf16[16,384,384]{2,1,0:T(8,128)(2,1)}, u32[]{:S(2)}) %copy-start.15) | copy-done | bytes 4718616
  117.6 11.9 %grads_part.1 = (bf16[384,2048]{1,0:T(8,128)(2,1)}, bf16[384,512]{1,0:T(8,128)(2,1)}) custom-call(bf16[384,2048]{1,0:T(8,128)(2,1)S(1)} %copy-done.6, bf16[384,512]{1,0:T(8,128)(2,1)S(1)} %copy-done.10, bf16[384,2048]{1,0:T(8,128)(2,1)S(1)} %copy-done.8, bf16[384,512]{1,0:T(8,128)(2,1)S(1)} %copy-done.12, bf16[16,384,384]{2,1,0:T(8,128)(2,1)S(1)} %copy-done.15), custom_call_target="tpu_custom_call" | custom-call | flops 2400000000 | bytes 9000000 | tf_op jit(solution)/shard_map/grads_part/pallas_call | solution.py:102
  129.4 0.6 add_multiply_fusion
  130.0 3.5 %hidden_part.1 = bf16[384,2048]{1,0:T(8,128)(2,1)} custom-call(s32[4]{0:T(128)S(1)} %pad_add_fusion.at_ref, bf16[384,512]{1,0:T(8,128)(2,1)S(1)} %get-tuple-element.17.own_ref, bf16[384,512]{1,0:T(8,128)(2,1)S(1)} %collective-permute-done.17.other_ref, bf16[2048,512]{1,0:T(8,128)(2,1)S(1)} %constant_dynamic-slice_fusion.2.codes_ref, ...), custom_call_target="tpu_custom_call" | custom-call | flops 1700000000 | bytes 8000000 | tf_op jit(solution)/shard_map/hidden_part/pallas_call | solution.py:185
  (65 shorter events, 1.2 us)
Async XLA Ops:
  0.6 58.7 %copy-start.4 = (f32[512]{0:T(512)S(1)}, f32[512]{0:T(512)}, u32[]{:S(2)}) copy-start(f32[512]{0:T(512)} %param.11) | copy-start | bytes 6148
  0.6 58.7 %copy-start.13 = (s32[1,4]{1,0:T(1,128)S(1)}, s32[1,4]{1,0:T(1,128)}, u32[]{:S(2)}) copy-start(s32[1,4]{1,0:T(1,128)} %lengths_ref.1) | copy-start | bytes 52
  0.7 9.3 %collective-permute-start = (bf16[32,512]{1,0:T(8,128)(2,1)}, bf16[32,512]{1,0:T(8,128)(2,1)S(1)}, u32[]{:S(2)}, u32[]{:S(2)}) collective-permute-start(bf16[32,512]{1,0:T(8,128)(2,1)} %param.10), channel_id=1, source_target_pairs={{0,128},{2,130},{4,132},{6,134},{8,136},{10,138},{12,140},{14,142}... | collective-permute-start | bytes 98312 | tf_op jit(solution)/shard_map/ppermute | solution.py:222
  10.8 4.7 %collective-permute-start.1 = (bf16[64,512]{1,0:T(8,128)(2,1)S(1)}, bf16[64,512]{1,0:T(8,128)(2,1)S(1)}, u32[]{:S(2)}, u32[]{:S(2)}) collective-permute-start(bf16[64,512]{1,0:T(8,128)(2,1)S(1)} %pad_maximum_fusion.3), channel_id=1, source_target_pairs={{0,64},{2,66},{4,68},{6,70},{8,72},{10,74},{12,76},{14,78},{16,80}... | collective-permute-start | bytes 196616 | tf_op jit(solution)/shard_map/ppermute | solution.py:222
  16.2 3.9 %collective-permute-start.2 = (bf16[128,512]{1,0:T(8,128)(2,1)S(1)}, bf16[128,512]{1,0:T(8,128)(2,1)S(1)}, u32[]{:S(2)}, u32[]{:S(2)}) collective-permute-start(bf16[128,512]{1,0:T(8,128)(2,1)S(1)} %pad_maximum_fusion.2), channel_id=1, source_target_pairs={{0,32},{2,34},{4,36},{6,38},{8,40},{10,42},{12,44},{14,46},{16,48}... | collective-permute-start | bytes 393224 | tf_op jit(solution)/shard_map/ppermute | solution.py:222
  20.2 5.2 %collective-permute-start.7 = (bf16[256,256]{1,0:T(8,128)(2,1)S(1)}, bf16[256,256]{1,0:T(8,128)(2,1)S(1)}, u32[]{:S(2)}, u32[]{:S(2)}) collective-permute-start(bf16[256,256]{1,0:T(8,128)(2,1)S(1)} %get-tuple-element.22), channel_id=1, source_target_pairs={{0,8},{2,10},{4,12},{6,14},{8,16},{10,18},{12,20},{14,22},{16,24},... | collective-permute-start | bytes 393224 | tf_op jit(solution)/shard_map/ppermute | solution.py:222
  21.6 6.4 %collective-permute-start.8 = (bf16[256,256]{1,0:T(8,128)(2,1)S(1)}, bf16[256,256]{1,0:T(8,128)(2,1)S(1)}, u32[]{:S(2)}, u32[]{:S(2)}) collective-permute-start(bf16[256,256]{1,0:T(8,128)(2,1)S(1)} %get-tuple-element.22), channel_id=1, source_target_pairs={{0,16},{2,18},{4,20},{6,22},{8,24},{10,26},{12,28},{14,30},{16,0},... | collective-permute-start | bytes 393224 | tf_op jit(solution)/shard_map/ppermute | solution.py:222
  24.2 3.8 %collective-permute-start.9 = (bf16[256,256]{1,0:T(8,128)(2,1)S(1)}, bf16[256,256]{1,0:T(8,128)(2,1)S(1)}, u32[]{:S(2)}, u32[]{:S(2)}) collective-permute-start(bf16[256,256]{1,0:T(8,128)(2,1)S(1)} %get-tuple-element.22), channel_id=1, source_target_pairs={{0,24},{2,26},{4,28},{6,30},{8,0},{10,2},{12,4},{14,6},{16,8},{18,... | collective-permute-start | bytes 393224 | tf_op jit(solution)/shard_map/ppermute | solution.py:222
  28.0 26.4 %collective-permute-start.10 = (bf16[1024,256]{1,0:T(8,128)(2,1)S(1)}, bf16[1024,256]{1,0:T(8,128)(2,1)S(1)}, u32[]{:S(2)}, u32[]{:S(2)}) collective-permute-start(bf16[1024,256]{1,0:T(8,128)(2,1)S(1)} %pad_maximum_fusion.refs_4_), channel_id=1, source_target_pairs={{0,4},{2,6},{4,0},{6,2},{8,12},{10,14},{12,8},{14,10},{16,20},{18,... | collective-permute-start | bytes 1572872 | tf_op jit(solution)/shard_map/ppermute | solution.py:222
  30.9 9.4 %collective-permute-start.3 = (bf16[256,256]{1,0:T(8,128)(2,1)S(1)}, bf16[256,256]{1,0:T(8,128)(2,1)S(1)}, u32[]{:S(2)}, u32[]{:S(2)}) collective-permute-start(bf16[256,256]{1,0:T(8,128)(2,1)S(1)} %get-tuple-element.23), channel_id=1, source_target_pairs={{0,4},{2,6},{4,0},{6,2},{8,12},{10,14},{12,8},{14,10},{16,20},{18,... | collective-permute-start | bytes 393224 | tf_op jit(solution)/shard_map/ppermute | solution.py:222
  40.3 12.0 %collective-permute-start.4 = (bf16[512,256]{1,0:T(8,128)(2,1)S(1)}, bf16[512,256]{1,0:T(8,128)(2,1)S(1)}, u32[]{:S(2)}, u32[]{:S(2)}) collective-permute-start(bf16[512,256]{1,0:T(8,128)(2,1)S(1)} %pad_maximum_fusion.1.refs_0_), channel_id=1, source_target_pairs={{0,8},{2,10},{4,12},{6,14},{8,16},{10,18},{12,20},{14,22},{16,24},... | collective-permute-start | bytes 786440 | tf_op jit(solution)/shard_map/ppermute | solution.py:222
  41.6 12.9 %collective-permute-start.5 = (bf16[512,256]{1,0:T(8,128)(2,1)S(1)}, bf16[512,256]{1,0:T(8,128)(2,1)S(1)}, u32[]{:S(2)}, u32[]{:S(2)}) collective-permute-start(bf16[512,256]{1,0:T(8,128)(2,1)S(1)} %pad_maximum_fusion.1.refs_0_), channel_id=1, source_target_pairs={{0,16},{2,18},{4,20},{6,22},{8,24},{10,26},{12,28},{14,30},{16,0},... | collective-permute-start | bytes 786440 | tf_op jit(solution)/shard_map/ppermute | solution.py:222
  43.9 14.2 %collective-permute-start.6 = (bf16[512,256]{1,0:T(8,128)(2,1)S(1)}, bf16[512,256]{1,0:T(8,128)(2,1)S(1)}, u32[]{:S(2)}, u32[]{:S(2)}) collective-permute-start(bf16[512,256]{1,0:T(8,128)(2,1)S(1)} %pad_maximum_fusion.1.refs_0_), channel_id=1, source_target_pairs={{0,24},{2,26},{4,28},{6,30},{8,0},{10,2},{12,4},{14,6},{16,8},{18,... | collective-permute-start | bytes 786440 | tf_op jit(solution)/shard_map/ppermute | solution.py:222
  45.6 12.6 %collective-permute-start.11 = (bf16[512,256]{1,0:T(8,128)(2,1)S(1)}, bf16[512,256]{1,0:T(8,128)(2,1)S(1)}, u32[]{:S(2)}, u32[]{:S(2)}) collective-permute-start(bf16[512,256]{1,0:T(8,128)(2,1)S(1)} %pad_maximum_fusion.1.refs_0_), channel_id=1, source_target_pairs={{0,2},{2,0},{4,6},{6,4},{8,10},{10,8},{12,14},{14,12},{16,18},{18,... | collective-permute-start | bytes 786440 | tf_op jit(solution)/shard_map/ppermute | solution.py:222
  52.3 20.9 %collective-permute-start.15 = (bf16[1024,256]{1,0:T(8,128)(2,1)S(1)}, bf16[1024,256]{1,0:T(8,128)(2,1)S(1)}, u32[]{:S(2)}, u32[]{:S(2)}) collective-permute-start(bf16[1024,256]{1,0:T(8,128)(2,1)S(1)} %pad_maximum_fusion.refs_4_), channel_id=1, source_target_pairs={{0,2},{2,0},{4,6},{6,4},{8,10},{10,8},{12,14},{14,12},{16,18},{18,... | collective-permute-start | bytes 1572872 | tf_op jit(solution)/shard_map/ppermute | solution.py:222
  54.5 18.8 %collective-permute-start.16 = (bf16[1024,256]{1,0:T(8,128)(2,1)S(1)}, bf16[1024,256]{1,0:T(8,128)(2,1)S(1)}, u32[]{:S(2)}, u32[]{:S(2)}) collective-permute-start(bf16[1024,256]{1,0:T(8,128)(2,1)S(1)} %collective-permute-done.10.refs_5_), channel_id=1, source_target_pairs={{0,2},{2,0},{4,6},{6,4},{8,10},{10,8},{12,14},{14,12},{16,18},{18,... | collective-permute-start | bytes 1572872 | tf_op jit(solution)/shard_map/ppermute | solution.py:222
  54.5 18.8 %collective-permute-start.12 = (bf16[512,256]{1,0:T(8,128)(2,1)S(1)}, bf16[512,256]{1,0:T(8,128)(2,1)}, u32[]{:S(2)}, u32[]{:S(2)}) collective-permute-start(bf16[512,256]{1,0:T(8,128)(2,1)S(1)} %collective-permute-done.4.refs_1_), channel_id=1, source_target_pairs={{0,2},{2,0},{4,6},{6,4},{8,10},{10,8},{12,14},{14,12},{16,18},{18,... | collective-permute-start | bytes 786440 | tf_op jit(solution)/shard_map/ppermute | solution.py:222
  58.1 15.2 %collective-permute-start.13 = (bf16[512,256]{1,0:T(8,128)(2,1)S(1)}, bf16[512,256]{1,0:T(8,128)(2,1)}, u32[]{:S(2)}, u32[]{:S(2)}) collective-permute-start(bf16[512,256]{1,0:T(8,128)(2,1)S(1)} %collective-permute-done.5.refs_2_), channel_id=1, source_target_pairs={{0,2},{2,0},{4,6},{6,4},{8,10},{10,8},{12,14},{14,12},{16,18},{18,... | collective-permute-start | bytes 786440 | tf_op jit(solution)/shard_map/ppermute | solution.py:222
  58.1 0.7 copy-start.2
  58.8 14.4 %collective-permute-start.14 = (bf16[512,256]{1,0:T(8,128)(2,1)S(1)}, bf16[512,256]{1,0:T(8,128)(2,1)}, u32[]{:S(2)}, u32[]{:S(2)}) collective-permute-start(bf16[512,256]{1,0:T(8,128)(2,1)S(1)} %collective-permute-done.6.refs_3_), channel_id=1, source_target_pairs={{0,2},{2,0},{4,6},{6,4},{8,10},{10,8},{12,14},{14,12},{16,18},{18,... | collective-permute-start | bytes 786440 | tf_op jit(solution)/shard_map/ppermute | solution.py:222
  59.4 1.4 %copy-start.5 = (bf16[384,2048]{1,0:T(8,128)(2,1)S(1)}, bf16[384,2048]{1,0:T(8,128)(2,1)}, u32[]{:S(2)}) copy-start(bf16[384,2048]{1,0:T(8,128)(2,1)} %q_ref.3) | copy-start | bytes 4718596
  60.8 1.4 %copy-start.7 = (bf16[384,2048]{1,0:T(8,128)(2,1)S(1)}, bf16[384,2048]{1,0:T(8,128)(2,1)}, u32[]{:S(2)}) copy-start(bf16[384,2048]{1,0:T(8,128)(2,1)} %up_ref.3) | copy-start | bytes 4718596
  62.2 1.0 copy-start.9
  63.2 10.1 %copy-start = (bf16[384,4096]{1,0:T(8,128)(2,1)S(1)}, bf16[384,4096]{1,0:T(8,128)(2,1)}, u32[]{:S(2)}) copy-start(bf16[384,4096]{1,0:T(8,128)(2,1)} %hidden_ref.1) | copy-start | bytes 9437188
  63.2 10.1 %copy-start.3 = (bf16[512,256]{1,0:T(8,128)(2,1)S(1)}, bf16[512,256]{1,0:T(8,128)(2,1)}, u32[]{:S(2)}) copy-start(bf16[512,256]{1,0:T(8,128)(2,1)} %copy-done.2) | copy-start | bytes 786436
  71.1 2.1 %copy-start.14 = (bf16[16,384,384]{2,1,0:T(8,128)(2,1)}, bf16[16,384,384]{2,1,0:T(8,128)(2,1)S(1)}, u32[]{:S(2)}) copy-start(bf16[16,384,384]{2,1,0:T(8,128)(2,1)S(1)} %get-tuple-element.14.p_ref) | copy-start | bytes 14155780
  78.1 2.0 %copy-start.1 = (bf16[4096,512]{1,0:T(8,128)(2,1)}, bf16[4096,512]{1,0:T(8,128)(2,1)S(1)}, u32[]{:S(2)}) copy-start(bf16[4096,512]{1,0:T(8,128)(2,1)S(1)} %get-tuple-element.18) | copy-start | bytes 12582916
  78.1 23.7 %copy-start.11 = (bf16[384,512]{1,0:T(8,128)(2,1)}, bf16[384,512]{1,0:T(8,128)(2,1)S(1)}, u32[]{:S(2)}) copy-start(bf16[384,512]{1,0:T(8,128)(2,1)S(1)} %get-tuple-element.13.v_ref) | copy-start | bytes 1179652
  80.2 23.8 %collective-permute-start.18 = (bf16[512,512]{1,0:T(8,128)(2,1)S(1)}, bf16[512,512]{1,0:T(8,128)(2,1)S(1)}, u32[]{:S(2)}, u32[]{:S(2)}) collective-permute-start(bf16[512,512]{1,0:T(8,128)(2,1)S(1)} %get-tuple-element.21), channel_id=1, source_target_pairs={{0,1},{1,0},{2,3},{3,2},{4,5},{5,4},{6,7},{7,6},{8,9},{9,8},{10,11... | collective-permute-start | bytes 1572872 | tf_op jit(solution)/shard_map/ppermute | solution.py:249
  81.5 28.1 %collective-permute-start.19 = (bf16[512,512]{1,0:T(8,128)(2,1)S(1)}, bf16[512,512]{1,0:T(8,128)(2,1)S(1)}, u32[]{:S(2)}, u32[]{:S(2)}) collective-permute-start(bf16[512,512]{1,0:T(8,128)(2,1)S(1)} %get-tuple-element.20), channel_id=1, source_target_pairs={{0,5},{1,4},{2,7},{3,6},{4,1},{5,0},{6,3},{7,2},{8,13},{9,12},{10,... | collective-permute-start | bytes 1572872 | tf_op jit(solution)/shard_map/ppermute | solution.py:250
  83.3 6.7 %collective-permute-start.22 = (f32[1,512]{1,0:T(1,128)S(1)}, f32[1,512]{1,0:T(1,128)S(1)}, u32[]{:S(2)}, u32[]{:S(2)}) collective-permute-start(f32[1,512]{1,0:T(1,128)S(1)} %get-tuple-element.19), channel_id=1, source_target_pairs={{0,128},{2,130},{4,132},{6,134},{8,136},{10,138},{12,140},{14,142}... | collective-permute-start | bytes 6152 | tf_op jit(solution)/shard_map/ppermute | solution.py:222
  90.0 3.6 %collective-permute-start.23 = (f32[1,512]{1,0:T(1,128)S(1)}, f32[1,512]{1,0:T(1,128)S(1)}, u32[]{:S(2)}, u32[]{:S(2)}) collective-permute-start(f32[1,512]{1,0:T(1,128)S(1)} %add.59), channel_id=1, source_target_pairs={{0,64},{2,66},{4,68},{6,70},{8,72},{10,74},{12,76},{14,78},{16,80}... | collective-permute-start | bytes 6152 | tf_op jit(solution)/shard_map/ppermute | solution.py:222
  93.6 2.7 %collective-permute-start.24 = (f32[1,512]{1,0:T(1,128)S(1)}, f32[1,512]{1,0:T(1,128)S(1)}, u32[]{:S(2)}, u32[]{:S(2)}) collective-permute-start(f32[1,512]{1,0:T(1,128)S(1)} %add.60), channel_id=1, source_target_pairs={{0,32},{2,34},{4,36},{6,38},{8,40},{10,42},{12,44},{14,46},{16,48}... | collective-permute-start | bytes 6152 | tf_op jit(solution)/shard_map/ppermute | solution.py:222
  96.3 3.9 %collective-permute-start.25 = (f32[1,512]{1,0:T(1,128)S(1)}, f32[1,512]{1,0:T(1,128)S(1)}, u32[]{:S(2)}, u32[]{:S(2)}) collective-permute-start(f32[1,512]{1,0:T(1,128)S(1)} %add.61), channel_id=1, source_target_pairs={{0,16},{2,18},{4,20},{6,22},{8,24},{10,26},{12,28},{14,30},{16,0},... | collective-permute-start | bytes 6152 | tf_op jit(solution)/shard_map/ppermute | solution.py:222
  100.3 2.5 %collective-permute-start.26 = (f32[1,512]{1,0:T(1,128)S(1)}, f32[1,512]{1,0:T(1,128)S(1)}, u32[]{:S(2)}, u32[]{:S(2)}) collective-permute-start(f32[1,512]{1,0:T(1,128)S(1)} %add.62), channel_id=1, source_target_pairs={{0,8},{2,10},{4,12},{6,14},{8,0},{10,2},{12,4},{14,6},{16,24},{18,... | collective-permute-start | bytes 6152 | tf_op jit(solution)/shard_map/ppermute | solution.py:222
  101.8 28.2 %collective-permute-start.17 = (bf16[384,512]{1,0:T(8,128)(2,1)S(1)}, bf16[384,512]{1,0:T(8,128)(2,1)S(1)}, u32[]{:S(2)}, u32[]{:S(2)}) collective-permute-start(bf16[384,512]{1,0:T(8,128)(2,1)S(1)} %get-tuple-element.17.own_ref), channel_id=1, source_target_pairs={{0,1},{1,0},{2,3},{3,2},{4,5},{5,4},{6,7},{7,6},{8,9},{9,8},{10,11... | collective-permute-start | bytes 1179656 | tf_op jit(solution)/shard_map/ppermute | solution.py:246
  102.8 12.5 %copy-start.6 = (bf16[384,2048]{1,0:T(8,128)(2,1)S(1)}, bf16[384,2048]{1,0:T(8,128)(2,1)}, u32[]{:S(2)}) copy-start(bf16[384,2048]{1,0:T(8,128)(2,1)} %q_ref.3) | copy-start | bytes 4718596
  102.8 12.5 %copy-start.8 = (bf16[384,2048]{1,0:T(8,128)(2,1)S(1)}, bf16[384,2048]{1,0:T(8,128)(2,1)}, u32[]{:S(2)}) copy-start(bf16[384,2048]{1,0:T(8,128)(2,1)} %up_ref.3) | copy-start | bytes 4718596
  102.8 12.5 %copy-start.10 = (bf16[384,512]{1,0:T(8,128)(2,1)S(1)}, bf16[384,512]{1,0:T(8,128)(2,1)}, u32[]{:S(2)}) copy-start(bf16[384,512]{1,0:T(8,128)(2,1)} %k_ref.3) | copy-start | bytes 1179652
  102.8 12.5 %copy-start.12 = (bf16[384,512]{1,0:T(8,128)(2,1)S(1)}, bf16[384,512]{1,0:T(8,128)(2,1)}, u32[]{:S(2)}) copy-start(bf16[384,512]{1,0:T(8,128)(2,1)} %copy-done.11) | copy-start | bytes 1179652
  102.8 8.6 %collective-permute-start.27 = (f32[1,512]{1,0:T(1,128)S(1)}, f32[1,512]{1,0:T(1,128)S(1)}, u32[]{:S(2)}, u32[]{:S(2)}) collective-permute-start(f32[1,512]{1,0:T(1,128)S(1)} %add.63), channel_id=1, source_target_pairs={{0,4},{2,6},{4,0},{6,2},{8,12},{10,14},{12,8},{14,10},{16,20},{18,... | collective-permute-start | bytes 6152 | tf_op jit(solution)/shard_map/ppermute | solution.py:222
  104.0 26.1 %collective-permute-start.20 = (bf16[512,512]{1,0:T(8,128)(2,1)S(1)}, bf16[512,512]{1,0:T(8,128)(2,1)S(1)}, u32[]{:S(2)}, u32[]{:S(2)}) collective-permute-start(bf16[512,512]{1,0:T(8,128)(2,1)S(1)} %collective-permute-done.18.near0), channel_id=1, source_target_pairs={{0,2},{2,0},{4,6},{6,4},{8,10},{10,8},{12,14},{14,12},{16,18},{18,... | collective-permute-start | bytes 1572872 | tf_op jit(solution)/shard_map/ppermute | solution.py:222
  109.6 20.4 %collective-permute-start.21 = (bf16[512,512]{1,0:T(8,128)(2,1)S(1)}, bf16[512,512]{1,0:T(8,128)(2,1)S(1)}, u32[]{:S(2)}, u32[]{:S(2)}) collective-permute-start(bf16[512,512]{1,0:T(8,128)(2,1)S(1)} %collective-permute-done.19.near1), channel_id=1, source_target_pairs={{0,2},{2,0},{4,6},{6,4},{8,10},{10,8},{12,14},{14,12},{16,18},{18,... | collective-permute-start | bytes 1572872 | tf_op jit(solution)/shard_map/ppermute | solution.py:222
  111.5 18.0 %collective-permute-start.28 = (f32[1,512]{1,0:T(1,128)S(1)}, f32[1,512]{1,0:T(1,128)S(1)}, u32[]{:S(2)}, u32[]{:S(2)}) collective-permute-start(f32[1,512]{1,0:T(1,128)S(1)} %add.64), channel_id=1, source_target_pairs={{0,2},{2,0},{4,6},{6,4},{8,10},{10,8},{12,14},{14,12},{16,18},{18,... | collective-permute-start | bytes 6152 | tf_op jit(solution)/shard_map/ppermute | solution.py:222
  115.2 2.3 %copy-start.15 = (bf16[16,384,384]{2,1,0:T(8,128)(2,1)S(1)}, bf16[16,384,384]{2,1,0:T(8,128)(2,1)}, u32[]{:S(2)}) copy-start(bf16[16,384,384]{2,1,0:T(8,128)(2,1)} %copy-done.14) | copy-start | bytes 14155780

commit v2 on v0

v2 whole, which is shorter than its diff:
```python
import functools
import math

import jax
import jax.numpy as jnp
from jax import lax
from jax.experimental import pallas as pl
from jax.experimental.pallas import tpu as pltpu
from jax.sharding import PartitionSpec as P

COUNT = 384
HEAD = 128
GROUP = 4
BLOCK = 128
BLOCKS = COUNT // BLOCK
FACTOR = 1.0 / math.sqrt(HEAD)
LOG2E = math.log2(math.e)
BF16 = jnp.bfloat16
F32 = jnp.float32
VMEM_LIMIT = 20 * 1024 * 1024


def dot(a, b, dims):
    return lax.dot_general(a, b, ((dims[:1], dims[1:]), ((), ())), preferred_element_type=F32)

VMEM = pl.BlockSpec(memory_space=pltpu.VMEM)
SMEM = pl.BlockSpec(memory_space=pltpu.SMEM)
ANY = pl.BlockSpec(memory_space=pl.ANY)
TOKEN = jax.ShapeDtypeStruct((8, 128), F32)
WIDE = GROUP * HEAD


def call(kernel, name, out_shape, ins, after=(), through=(), **kw):
    specs, args = zip(*ins)
    n_in = len(args) + len(after)
    single = not isinstance(out_shape, (list, tuple))
    outs = [out_shape] if single else list(out_shape)
    kw.setdefault("out_specs", [VMEM] * len(outs))

    n_out = len(outs)
    if through:
        kw["input_output_aliases"] = {n_in + j: n_out + j for j in range(len(through))}
        outs += [jax.ShapeDtypeStruct(a.shape, a.dtype) for a in through]
        kw["out_specs"] = list(kw["out_specs"]) + [ANY] * len(through)
        single = False

    def run(*refs):
        first = n_in + len(through)
        kernel(*refs[: len(args)], *refs[first : first + n_out], *refs[first + n_out + len(through) :])

    got = pl.pallas_call(
        run,
        in_specs=list(specs) + [ANY] * (len(after) + len(through)),
        out_shape=outs,
        compiler_params=pltpu.CompilerParams(vmem_limit_bytes=VMEM_LIMIT),
        cost_estimate=pl.CostEstimate(flops=1000, bytes_accessed=1000, transcendentals=0),
        name=name,
        **kw,
    )(*args, *after, *through)
    return got[0] if single else got


def shape(*dims, dtype=BF16):
    return jax.ShapeDtypeStruct(dims, dtype)


def probs_kernel(lengths_ref, q_ref, k_ref, up_ref, p_ref, dv_ref, bias_ref, s_ref, dv_acc):
    rows = lax.broadcasted_iota(jnp.int32, (COUNT, COUNT), 0)
    cols = lax.broadcasted_iota(jnp.int32, (COUNT, COUNT), 1)
    start = jnp.zeros((COUNT, COUNT), jnp.int32)
    end = jnp.int32(0)
    for doc in range(3):
        end = end + lengths_ref[0, doc]
        start = jnp.where(rows >= end, end, start)
    bias_ref[...] = jnp.where((cols <= rows) & (cols >= start), 0.0, -1e30).astype(F32)
    dv_acc[...] = jnp.zeros_like(dv_acc)
    for i in range(BLOCKS):
        width = BLOCK * (i + 1)
        at = pl.ds(BLOCK * i, BLOCK)
        qs = jnp.concatenate([q_ref[at, pl.ds(HEAD * h, HEAD)] for h in range(GROUP)], axis=0)
        s_ref[:, :width] = dot(qs, k_ref[:width, :], (1, 1))
        for h in range(GROUP):
            scores = s_ref[pl.ds(BLOCK * h, BLOCK), :width] * (FACTOR * LOG2E) + bias_ref[at, :width]
            expo = jnp.exp2(scores - jnp.max(scores, axis=1, keepdims=True))
            probs = expo * (1.0 / jnp.sum(expo, axis=1, keepdims=True))
            p_ref[h, at, :width] = probs.astype(BF16)
        low = jnp.concatenate([p_ref[h, at, :width] for h in range(GROUP)], axis=0)
        ups = jnp.concatenate([up_ref[at, pl.ds(HEAD * h, HEAD)] for h in range(GROUP)], axis=0)
        dv_acc[:, :width] += dot(ups, low, (0, 0))
    dv_ref[...] = dv_acc[...].T


def probs_part(g, lengths, queries, keys, upstream, dv, after):
    wide = pl.BlockSpec((COUNT, WIDE), lambda i: (0, g))
    narrow = pl.BlockSpec((COUNT, HEAD), lambda i: (0, g))
    ins = [(SMEM, lengths), (wide, queries), (narrow, keys), (wide, upstream)]

    def kernel(*refs):
        probs_kernel(*refs[:4], *refs[len(refs) - 5 :])

    extra = {}
    if dv is not None:
        ins.append((ANY, dv))
        extra["input_output_aliases"] = {4: 1}
    return call(
        kernel, "probs_part", [shape(GROUP, COUNT, COUNT), shape(COUNT, 4 * HEAD, dtype=F32)], ins, after,
        out_specs=[VMEM, narrow], grid=(1,),
        scratch_shapes=[pltpu.VMEM((COUNT, COUNT), F32), pltpu.VMEM((GROUP * BLOCK, COUNT), F32), pltpu.VMEM((HEAD, COUNT), F32)], **extra,
    )


def grads_kernel(g, at_ref, q_ref, k_ref, up_ref, mine_ref, theirs_ref, p_ref, gq_ref, gk_ref, token_ref, dp_ref, ds_ref, dk_acc):
    token_ref[...] = jnp.zeros_like(token_ref)
    dk_acc[...] = jnp.zeros_like(dk_acc)
    col = pl.ds(HEAD * (g % 2), HEAD)
    all_values = jnp.where(at_ref[3] == g // 2, mine_ref[:, col], theirs_ref[:, col])
    for i in range(BLOCKS):
        width = BLOCK * (i + 1)
        at = pl.ds(BLOCK * i, BLOCK)
        ups = jnp.concatenate([up_ref[at, pl.ds(HEAD * h, HEAD)] for h in range(GROUP)], axis=0)
        dp_ref[:, :width] = dot(ups, all_values[:width], (1, 1))
        for h in range(GROUP):
            rows = pl.ds(BLOCK * h, BLOCK)
            dprobs = dp_ref[rows, :width]
            probs = p_ref[h, at, :width].astype(F32)
            delta = jnp.sum(probs * dprobs, axis=1, keepdims=True)
            ds_ref[rows, :width] = (probs * (dprobs - delta)).astype(BF16)
        dscores = ds_ref[:, :width]
        gq = dot(dscores, k_ref[:width, :], (1, 0)) * FACTOR
        for h in range(GROUP):
            gq_ref[at, pl.ds(HEAD * h, HEAD)] = gq[BLOCK * h : BLOCK * (h + 1)].astype(BF16)
        qs = jnp.concatenate([q_ref[at, pl.ds(HEAD * h, HEAD)] for h in range(GROUP)], axis=0)
        dk_acc[:, :width] += dot(qs, dscores, (0, 0))
    gk_ref[...] = (dk_acc[...] * FACTOR).T.astype(BF16)


def grads_part(g, at, queries, keys, upstream, mine, theirs, probs, held, after):
    wide = pl.BlockSpec((COUNT, WIDE), lambda i: (0, g))
    narrow = pl.BlockSpec((COUNT, HEAD), lambda i: (0, g))
    ins = [(SMEM, at), (wide, queries), (narrow, keys), (wide, upstream), (VMEM, mine), (VMEM, theirs), (VMEM, probs)]

    def kernel(*refs):
        grads_kernel(g, *refs[:7], *refs[len(refs) - 6 :])

    extra = {}
    if held is not None:
        ins += [(ANY, held[0]), (ANY, held[1])]
        extra["input_output_aliases"] = {7: 0, 8: 1}
    return call(
        kernel, "grads_part", [shape(*queries.shape), shape(*keys.shape), TOKEN], ins, after,
        out_specs=[wide, narrow, VMEM], grid=(1,),
        scratch_shapes=[pltpu.VMEM((GROUP * BLOCK, COUNT), F32), pltpu.VMEM((GROUP * BLOCK, COUNT), BF16), pltpu.VMEM((HEAD, COUNT), F32)], **extra,
    )


Z_ORDER = (0, 4, 2, 6, 1, 5, 3, 7)
SHARD = 32
CHIP = 2 * SHARD
HALF = 256
DEPTH = 4096


def own_columns(at_ref):
    return pl.ds(pl.multiple_of(at_ref[3] * HALF, HALF), HALF)


def first_join(at_ref, own_ref, other_ref, out_ref):
    c, cols = at_ref[3], own_columns(at_ref)
    out_ref[pl.ds(pl.multiple_of(c * SHARD, SHARD), SHARD), :] = own_ref[:, cols]
    out_ref[pl.ds(pl.multiple_of((1 - c) * SHARD, SHARD), SHARD), :] = other_ref[:, cols]


def copy_kernel(in_ref, out_ref, sem):
    copy = pltpu.make_async_copy(in_ref, out_ref, sem)
    copy.start()
    copy.wait()


def join_kernel(own_ref, other_ref, out_ref):
    n = own_ref.shape[0]
    out_ref[:n, :] = own_ref[...]
    out_ref[n:, :] = other_ref[...]


def join_split_kernel(own_ref, other_ref, first_ref, second_ref):
    n = own_ref.shape[0]
    for j, out_ref in enumerate((first_ref, second_ref)):
        out_ref[:n, :] = own_ref[:, HEAD * j : HEAD * (j + 1)]
        out_ref[n:, :] = other_ref[:, HEAD * j : HEAD * (j + 1)]


def two_joins_kernel(a0, a1, b0, b1, b2, b3, first_ref, second_ref):
    n = a0.shape[0]
    for j, part in enumerate((a0, a1)):
        first_ref[n * j : n * (j + 1), :] = part[...]
    for j, part in enumerate((b0, b1, b2, b3)):
        second_ref[n * j : n * (j + 1), :] = part[...]


def put_in_order(at_ref, pieces, codes_ref):
    z, y, x = at_ref[0], at_ref[1], at_ref[2]

    def place(piece, row, zi, k, xi, col):
        to = ((z ^ Z_ORDER[zi]) * 4 + ((y + 4 - k) & 3)) * 2 + (x ^ xi)
        rows = pl.ds(pl.multiple_of(to * CHIP, CHIP), CHIP)
        codes_ref[rows, pl.ds(col, HEAD)] = piece[pl.ds(row, CHIP), :]

    for k in range(4):
        for xi in range(2):
            for zi in range(8):
                place(pieces[k], (xi * 8 + zi) * CHIP, zi, k, xi, 0)
                place(pieces[4 + xi], (k * 8 + zi) * CHIP, zi, k, xi, HEAD)


STEP = 512


def raw_kernel(at_ref, own_ref, other_ref, dv_own, dv_other, scale_ref, *refs):
    pieces, (mine_ref, theirs_ref, sums_ref, codes_ref, raw_own, raw_other) = refs[:6], refs[6:]
    i = pl.program_id(0)

    @pl.when(i == 0)
    def _():
        put_in_order(at_ref, pieces, codes_ref)
        raw_own[...] = jnp.zeros_like(raw_own)
        raw_other[...] = jnp.zeros_like(raw_other)

    codes = codes_ref[pl.ds(pl.multiple_of(i * STEP, STEP), STEP), :]
    raw_own[...] += dot(own_ref[...], codes, (1, 0))
    raw_other[...] += dot(other_ref[...], codes, (1, 0))

    @pl.when(i == pl.num_programs(0) - 1)
    def _():
        cols = own_columns(at_ref)
        scale = scale_ref[:, cols]
        mine_ref[...] = (raw_own[...] * scale).astype(BF16)
        theirs_ref[...] = (raw_other[...] * scale).astype(BF16)
        products = raw_own[...] * dv_own[:, cols] + raw_other[...] * dv_other[:, cols]
        sums_ref[...] = jnp.sum(products, axis=0, keepdims=True)


def raw_part(at, hidden, hidden_other, dv, dv_other, scale, pieces):
    block = pl.BlockSpec((COUNT, STEP), lambda i: (0, i))
    return call(
        raw_kernel, "raw_part", [shape(COUNT, HALF), shape(COUNT, HALF), shape(1, HALF, dtype=F32)],
        [(SMEM, at), (block, hidden), (block, hidden_other), (VMEM, dv), (VMEM, dv_other), (VMEM, scale)] + [(VMEM, p) for p in pieces],
        grid=(DEPTH // STEP,),
        scratch_shapes=[pltpu.VMEM((DEPTH, HALF), BF16), pltpu.VMEM((COUNT, HALF), F32), pltpu.VMEM((COUNT, HALF), F32)],
    )


def split_kernel(at_ref, dv_ref, scale_ref, *refs):
    pieces, (kept_ref, near_ref, beside_ref, scaled_ref, codes_ref) = refs[:6], refs[6:]
    put_in_order(at_ref, pieces, codes_ref)
    s, half = at_ref[4], DEPTH // 2
    kept_ref[...] = codes_ref[pl.ds(pl.multiple_of(s * half, half), half), :]
    base = (1 - s) * half
    near_ref[...] = codes_ref[pl.ds(pl.multiple_of(base, half), half // 2), :]
    beside_ref[...] = codes_ref[pl.ds(pl.multiple_of(base + half // 2, half // 2), half // 2), :]
    scaled_ref[...] = (dv_ref[...] * scale_ref[...]).astype(BF16)


def split_part(at, dv, scale, pieces, after):
    return call(
        split_kernel, "split_part", [shape(DEPTH // 2, HALF), shape(DEPTH // 4, HALF), shape(DEPTH // 4, HALF), shape(COUNT, 2 * HALF)],
        [(SMEM, at), (VMEM, dv), (VMEM, scale)] + [(VMEM, p) for p in pieces], after,
        scratch_shapes=[pltpu.VMEM((DEPTH, HALF), BF16)],
    )


def hidden_kernel(at_ref, own_ref, other_ref, kept_ref, kept_far, near_ref, near_far, out_ref, token_ref):
    mine = own_columns(at_ref)
    rest = pl.ds(pl.multiple_of((1 - at_ref[3]) * HALF, HALF), HALF)
    total = dot(own_ref[:, mine], kept_ref[...], (1, 1)) + dot(own_ref[:, rest], kept_far[...], (1, 1))
    total += dot(other_ref[:, mine], near_ref[...], (1, 1)) + dot(other_ref[:, rest], near_far[...], (1, 1))
    out_ref[...] = total.astype(BF16)
    token_ref[...] = jnp.zeros_like(token_ref)


def hidden_part(at, own, other, kept, kept_far, near, near_far, after):
    block = pl.BlockSpec((STEP, HALF), lambda i: (i, 0))
    return call(
        hidden_kernel, "hidden_part", [shape(COUNT, DEPTH // 2), TOKEN],
        [(SMEM, at), (VMEM, own), (VMEM, other), (block, kept), (block, kept_far), (block, near), (block, near_far)], after,
        grid=(DEPTH // 2 // STEP,),
        out_specs=[pl.BlockSpec((COUNT, STEP), lambda i: (0, i)), VMEM],
    )


def add_kernel(a_ref, b_ref, out_ref):
    out_ref[...] = a_ref[...] + b_ref[...]


def last_kernel(at_ref, own_ref, other_ref, scale_ref, out_ref):
    c = at_ref[3]
    low = jnp.where(c == 0, own_ref[...], other_ref[...])
    high = jnp.where(c == 0, other_ref[...], own_ref[...])
    out_ref[:, :HALF] = low * scale_ref[:, :HALF]
    out_ref[:, HALF:] = high * scale_ref[:, HALF:]


def pairs(move):
    out = []
    for i in range(128):
        z, y, x, c = move(i // 16, i // 4 % 4, i // 2 % 2, i % 2)
        out.append((i, ((z * 4 + y) * 2 + x) * 2 + c))
    return out


def z_swap(bit):
    return pairs(lambda z, y, x, c: (z ^ bit, y, x, c))


def y_shift(k):
    return pairs(lambda z, y, x, c: (z, (y + k) % 4, x, c))


def y_swap(bit):
    return pairs(lambda z, y, x, c: (z, y ^ bit, x, c))


X_SWAP = pairs(lambda z, y, x, c: (z, y, x ^ 1, c))
C_SWAP = pairs(lambda z, y, x, c: (z, y, x, c ^ 1))
SEQ_SWAP = [(0, 1), (1, 0)]
BESIDE = [(2 * a + s, 2 * b + 1 - s) for a, b in X_SWAP for s in range(2)]


def send(x, perm):
    return lax.ppermute(x, "dp", perm)


def shards(hidden, queries, keys, value_codes, value_scale, upstream, lengths):
    me, s = lax.axis_index("dp"), lax.axis_index("seq")
    at = jnp.stack([me // 16, me // 4 % 4, me // 2 % 2, me % 2, s]).astype(jnp.int32)
    scale = value_scale.reshape(1, -1)

    rows = call(first_join, "join", shape(CHIP, HALF), [(SMEM, at), (VMEM, value_codes), (VMEM, send(value_codes, C_SWAP))])
    hidden = call(
        copy_kernel, "copy", shape(*hidden.shape), [(ANY, hidden)], (rows,),
        out_specs=[ANY], scratch_shapes=[pltpu.SemaphoreType.DMA],
    )
    probs, dv = [], None
    for bit, heads in ((4, (0,)), (2, (1,)), (1, (2, 3))):
        got = send(rows, z_swap(bit))
        for g in heads:
            p, dv = probs_part(g, lengths, queries, keys, upstream, dv, (rows,))
            probs.append(p)
        n = rows.shape[0]
        ins = [(VMEM, rows), (VMEM, got)]
        if bit == 4:
            rows, hidden = call(join_kernel, "join", shape(2 * n, HALF), ins, (p,), (hidden,))
            hidden_other = send(hidden, C_SWAP)
        elif bit == 2:
            rows = call(join_kernel, "join", shape(2 * n, HALF), ins, (p,))
        else:
            first, second, dv = call(join_split_kernel, "join", [shape(2 * n, HEAD)] * 2, ins, (p,), (dv,))
    dv_other = send(dv, C_SWAP)
    first_x = send(first, X_SWAP)
    second_y = [send(second, y_shift(k)) for k in (1, 2, 3)]
    n = first.shape[0]
    first, second = call(
        two_joins_kernel, "join", [shape(2 * n, HEAD), shape(4 * n, HEAD)],
        [(VMEM, a) for a in [first, first_x, second] + second_y], (hidden_other, dv_other),
    )
    pieces = [first] + [send(first, y_shift(k)) for k in (1, 2, 3)] + [second, send(second, X_SWAP)]

    mine, theirs, sums = raw_part(at, hidden, hidden_other, dv, dv_other, scale, pieces)

    got = send(sums, X_SWAP)
    values_far = send(theirs, C_SWAP)
    kept, near, beside, scaled = split_part(at, dv, scale, pieces, (values_far,))
    sums, kept, near, beside, scaled = call(
        add_kernel, "add", shape(1, HALF, dtype=F32), [(VMEM, sums), (VMEM, got)], (), (kept, near, beside, scaled)
    )
    kept_far = send(kept, C_SWAP)
    scaled_other = lax.ppermute(scaled, "seq", SEQ_SWAP)
    near = lax.ppermute(near, "seq", SEQ_SWAP)
    beside = lax.ppermute(beside, ("dp", "seq"), BESIDE)
    held = None
    for g, perm in enumerate((y_swap(1), y_swap(2), z_swap(1), z_swap(2))):
        got = send(sums, perm)
        *held, token = grads_part(g, at, queries, keys, upstream, mine, values_far, probs[g], held, (sums,))
        after = (token,)
        if g == 3:
            near = call(join_kernel, "join", shape(DEPTH // 2, HALF), [(VMEM, near), (VMEM, beside)], (sums,))
            near_far = send(near, C_SWAP)
            after += (near,)
        sums = call(add_kernel, "add", shape(1, HALF, dtype=F32), [(VMEM, sums), (VMEM, got)], after)
    got = send(sums, z_swap(4))
    grad_hidden, token = hidden_part(at, scaled, scaled_other, kept, kept_far, near, near_far, (sums,))
    sums = call(add_kernel, "add", shape(1, HALF, dtype=F32), [(VMEM, sums), (VMEM, got)], (token,))
    last = call(
        last_kernel, "last", shape(1, 2 * HALF, dtype=F32),
        [(SMEM, at), (VMEM, sums), (VMEM, send(sums, C_SWAP)), (VMEM, scale)],
    )
    return held[0], held[1], grad_hidden, last.reshape(-1)


def solution(mesh):
    placed = (
        P("dp", None),
        P("dp", "seq"),
        P("dp", "seq"),
        P("dp", "seq"),
        P("seq"),
        P("dp", "seq"),
        P("dp", None),
    )
    return jax.shard_map(
        shards,
        mesh=mesh,
        in_specs=placed,
        out_specs=(P("dp", "seq"), P("dp", "seq"), P("dp", "seq"), P("seq")),
        check_vma=False,
    )
```

time: 511 us -> 105 us (0.21)
  blocking collectives: 325 us -> 0 us
  waiting for transfers between devices: 98.7 us -> 31.2 us
  starting transfers between devices: 0.08 us -> 38.8 us
  matrix products: 38.4 us -> 0 us
  Pallas kernels: 0 us -> 31.2 us
  local copies, waits for them, and re-layouts: 22.3 us -> 3.15 us
  between operations: 14.2 us -> 0.83 us
  other arithmetic: 9.78 us -> 0 us
    psum x1 -> x0, blocking collectives: 325 us -> none  [shards(): totals = lax.psum(jnp.sum(dvalue * raw, axis=0), 'dp')]
    all_gather x1 -> x0, waiting for transfers between devices: 98 us -> none  [shards(): codes_cols = lax.all_gather(value_codes, 'dp', axis=0, tiled=True)]
    ppermute x0 -> x27, starting transfers between devices: none -> 38.8 us  [the longest x24 36.2 us: send(): return lax.ppermute(x, 'dp', perm)]
    ppermute x0 -> x27, waiting for transfers between devices: none -> 31.2 us  [the longest x24 27.6 us: send(): return lax.ppermute(x, 'dp', perm)]
    pallas_call x0 -> x25, Pallas kernels: none -> 31.2 us  [call(): pl.pallas_call(run, in_specs=list(specs) + [ANY] * (len(after) + len(thro...]
    dot_general x7 -> x0, matrix products: 29.6 us -> none  [the longest x1 6.96 us: shards(): lax.dot_general(scaled, codes_cols, (((1,), (1,)), ((), ())), preferred_e...]
    reshape x6 -> x0, local copies, waits for them, and re-layouts: 11.9 us -> none  [the longest x2 3.79 us: attend(): vs = value_rows.reshape(count, kv_count, head_dim)]
    sub x1 -> x0, matrix products: 8.85 us -> none  [attend(): expo = jnp.exp(scores - top)]
  transfers between devices with their start and end apart: 2 -> 27, of which waited for: 1 -> 13; matrix products, arithmetic and copies ran while one was open for 11% -> 0% of each run, Pallas kernels for 0% -> 23%
where the time goes in v2:
time: 105 us
  starting transfers between devices  38.8 us (37%)
  waiting for transfers between devices  31.2 us (30%)
  Pallas kernels  31.2 us (30%)
  local copies, waits for them, and re-layouts  3.15 us (3%)
    ppermute x24, starting transfers between devices, send(): return lax.ppermute(x, 'dp', perm)  36.2 us
    pallas_call x25, Pallas kernels, call(): pl.pallas_call(run, in_specs=list(specs) + [ANY] * (len(after) + len(thro...  31.2 us
    ppermute x24, waiting for transfers between devices, send(): return lax.ppermute(x, 'dp', perm)  27.6 us
    ppermute x1, waiting for transfers between devices, shards(): scaled_other = lax.ppermute(scaled, 'seq', SEQ_SWAP)  3.65 us
    unnamed x14, local copies, waits for them, and re-layouts  3.07 us
  transfers between devices with their start and end apart: 27, of which 13 were waited for; matrix products, arithmetic and copies ran while one was open for 0% of the time, Pallas kernels for 23%

profile of v2, /device:TPU:1, one launch (start us, length us, event | category | flops | bytes accessed | tf_op | source)
XLA Modules:
  0.0 105.2 jit_solution(7197953381495413284)
XLA Ops:
  0.6 3.3 %collective-permute-start = (bf16[32,512]{1,0:T(8,128)(2,1)}, bf16[32,512]{1,0:T(8,128)(2,1)S(1)}, u32[]{:S(2)}, u32[]{:S(2)}) collective-permute-start(bf16[32,512]{1,0:T(8,128)(2,1)} %refs_1_.9), channel_id=1, source_target_pairs={{0,2},{2,0},{4,6},{6,4},{8,10},{10,8},{12,14},{14,12},{16,18},{18,... | collective-permute-start | bytes 98312 | tf_op jit(solution)/shard_map/ppermute | solution.py:329
  4.0 1.0 collective-permute-done.refs_2_
  5.0 0.8 copy-done.4
  5.8 0.5 join.6.refs_4_.refs_1_.refs_0_
  6.4 5.3 %collective-permute-start.1 = (bf16[64,256]{1,0:T(8,128)(2,1)S(1)}, bf16[64,256]{1,0:T(8,128)(2,1)S(1)}, u32[]{:S(2)}, u32[]{:S(2)}) collective-permute-start(bf16[64,256]{1,0:T(8,128)(2,1)S(1)} %join.6.refs_4_.refs_1_.refs_0_), channel_id=1, source_target_pairs={{0,128},{2,130},{4,132},{6,134},{8,136},{10,138},{12,140},{14,142}... | collective-permute-start | bytes 98312 | tf_op jit(solution)/shard_map/ppermute | solution.py:329
  11.6 1.9 %copy-done.3 = bf16[384,4096]{1,0:T(8,128)(2,1)S(1)} copy-done((bf16[384,4096]{1,0:T(8,128)(2,1)S(1)}, bf16[384,4096]{1,0:T(8,128)(2,1)}, u32[]{:S(2)}) %copy-start.3) | copy-done | bytes 3145752
  13.8 0.4 copy-done.6
  14.2 2.2 %probs_part.4 = (bf16[4,384,384]{2,1,0:T(8,128)(2,1)S(1)}, f32[384,512]{1,0:T(8,128)S(1)}) custom-call(s32[1,4]{1,0:T(1,128)S(1)} %copy-done.6, bf16[384,2048]{1,0:T(8,128)(2,1)S(1)} %copy-done, bf16[384,512]{1,0:T(8,128)(2,1)S(1)} %copy-done.2, bf16[384,2048]{1,0:T(8,128)(2,1)S(1)} %copy-done.1, bf16[64,256]{1,0:T(8,128)(2,1)S(1)} %join.6.refs_4_.refs_1_.refs_0_), custom_call_target="tpu_custom_call" | custom-call | flops 1000 | bytes 1000 | tf_op jit(solution)/shard_map/probs_part/pallas_call | solution.py:51
  16.4 0.7 collective-permute-start.2
  17.1 1.2 %collective-permute-start.3 = (bf16[128,256]{1,0:T(8,128)(2,1)S(1)}, bf16[128,256]{1,0:T(8,128)(2,1)S(1)}, u32[]{:S(2)}, u32[]{:S(2)}) collective-permute-start(bf16[128,256]{1,0:T(8,128)(2,1)S(1)} %get-tuple-element.47.refs_5_.refs_0_), channel_id=1, source_target_pairs={{0,64},{2,66},{4,68},{6,70},{8,72},{10,74},{12,76},{14,78},{16,80}... | collective-permute-start | bytes 196616 | tf_op jit(solution)/shard_map/ppermute | solution.py:329
  18.3 2.2 %probs_part.5 = (bf16[4,384,384]{2,1,0:T(8,128)(2,1)S(1)}, f32[384,512]{1,0:T(8,128)S(1)}) custom-call(s32[1,4]{1,0:T(1,128)S(1)} %copy-done.6, bf16[384,2048]{1,0:T(8,128)(2,1)S(1)} %copy-done, bf16[384,512]{1,0:T(8,128)(2,1)S(1)} %copy-done.2, bf16[384,2048]{1,0:T(8,128)(2,1)S(1)} %copy-done.1, ...), custom_call_target="tpu_custom_call", output_to_operand_aliasing={{1}: (4, {})} | custom-call | flops 1000 | bytes 1000 | tf_op jit(solution)/shard_map/probs_part/pallas_call | solution.py:51
  20.5 2.6 %collective-permute-done.3.refs_1_ = bf16[128,256]{1,0:T(8,128)(2,1)S(1)} collective-permute-done((bf16[128,256]{1,0:T(8,128)(2,1)S(1)}, bf16[128,256]{1,0:T(8,128)(2,1)S(1)}, u32[]{:S(2)}, u32[]{:S(2)}) %collective-permute-start.3) | collective-permute-done | bytes 65568 | tf_op jit(solution)/shard_map/ppermute | solution.py:329
  23.2 2.2 %probs_part.6 = (bf16[4,384,384]{2,1,0:T(8,128)(2,1)S(1)}, f32[384,512]{1,0:T(8,128)S(1)}) custom-call(s32[1,4]{1,0:T(1,128)S(1)} %copy-done.6, bf16[384,2048]{1,0:T(8,128)(2,1)S(1)} %copy-done, bf16[384,512]{1,0:T(8,128)(2,1)S(1)} %copy-done.2, bf16[384,2048]{1,0:T(8,128)(2,1)S(1)} %copy-done.1, ...), custom_call_target="tpu_custom_call", output_to_operand_aliasing={{1}: (4, {})} | custom-call | flops 1000 | bytes 1000 | tf_op jit(solution)/shard_map/probs_part/pallas_call | solution.py:51
  25.4 2.2 %probs_part.7 = (bf16[4,384,384]{2,1,0:T(8,128)(2,1)S(1)}, f32[384,512]{1,0:T(8,128)S(1)}) custom-call(s32[1,4]{1,0:T(1,128)S(1)} %copy-done.6, bf16[384,2048]{1,0:T(8,128)(2,1)S(1)} %copy-done, bf16[384,512]{1,0:T(8,128)(2,1)S(1)} %copy-done.2, bf16[384,2048]{1,0:T(8,128)(2,1)S(1)} %copy-done.1, ...), custom_call_target="tpu_custom_call", output_to_operand_aliasing={{1}: (4, {})} | custom-call | flops 1000 | bytes 1000 | tf_op jit(solution)/shard_map/probs_part/pallas_call | solution.py:51
  27.7 1.6 %collective-permute-start.5 = (f32[384,512]{1,0:T(8,128)S(1)}, f32[384,512]{1,0:T(8,128)S(1)}, u32[]{:S(2)}, u32[]{:S(2)}) collective-permute-start(f32[384,512]{1,0:T(8,128)S(1)} %get-tuple-element.54.refs_3_.refs_1_), channel_id=1, source_target_pairs={{0,2},{2,0},{4,6},{6,4},{8,10},{10,8},{12,14},{14,12},{16,18},{18,... | collective-permute-start | bytes 2359304 | tf_op jit(solution)/shard_map/ppermute | solution.py:329
  29.2 2.8 %collective-permute-start.6 = (bf16[512,128]{1,0:T(8,128)(2,1)S(1)}, bf16[512,128]{1,0:T(8,128)(2,1)S(1)}, u32[]{:S(2)}, u32[]{:S(2)}) collective-permute-start(bf16[512,128]{1,0:T(8,128)(2,1)S(1)} %get-tuple-element.55.refs_0_), channel_id=1, source_target_pairs={{0,4},{2,6},{4,0},{6,2},{8,12},{10,14},{12,8},{14,10},{16,20},{18,... | collective-permute-start | bytes 393224 | tf_op jit(solution)/shard_map/ppermute | solution.py:329
  32.0 2.7 %collective-permute-start.9 = (bf16[512,128]{1,0:T(8,128)(2,1)S(1)}, bf16[512,128]{1,0:T(8,128)(2,1)S(1)}, u32[]{:S(2)}, u32[]{:S(2)}) collective-permute-start(bf16[512,128]{1,0:T(8,128)(2,1)S(1)} %get-tuple-element.56.refs_2_), channel_id=1, source_target_pairs={{0,24},{2,26},{4,28},{6,30},{8,0},{10,2},{12,4},{14,6},{16,8},{18,... | collective-permute-start | bytes 393224 | tf_op jit(solution)/shard_map/ppermute | solution.py:329
  34.7 0.3 collective-permute-start.8
  35.1 0.7 collective-permute-done.6.refs_1_
  35.8 1.3 %collective-permute-start.7 = (bf16[512,128]{1,0:T(8,128)(2,1)S(1)}, bf16[512,128]{1,0:T(8,128)(2,1)S(1)}, u32[]{:S(2)}, u32[]{:S(2)}) collective-permute-start(bf16[512,128]{1,0:T(8,128)(2,1)S(1)} %get-tuple-element.56.refs_2_), channel_id=1, source_target_pairs={{0,8},{2,10},{4,12},{6,14},{8,16},{10,18},{12,20},{14,22},{16,24},... | collective-permute-start | bytes 393224 | tf_op jit(solution)/shard_map/ppermute | solution.py:329
  37.1 2.8 %collective-permute-done.9.refs_5_ = bf16[512,128]{1,0:T(8,128)(2,1)S(1)} collective-permute-done((bf16[512,128]{1,0:T(8,128)(2,1)S(1)}, bf16[512,128]{1,0:T(8,128)(2,1)S(1)}, u32[]{:S(2)}, u32[]{:S(2)}) %collective-permute-start.9) | collective-permute-done | bytes 131104 | tf_op jit(solution)/shard_map/ppermute | solution.py:329
  39.9 0.7 collective-permute-done.8.refs_4_
  40.6 3.8 %collective-permute-done.7.refs_3_ = bf16[512,128]{1,0:T(8,128)(2,1)S(1)} collective-permute-done((bf16[512,128]{1,0:T(8,128)(2,1)S(1)}, bf16[512,128]{1,0:T(8,128)(2,1)S(1)}, u32[]{:S(2)}, u32[]{:S(2)}) %collective-permute-start.7) | collective-permute-done | bytes 131104 | tf_op jit(solution)/shard_map/ppermute | solution.py:329
  44.8 0.9 collective-permute-start.12
  46.1 0.7 collective-permute-start.10
  46.8 4.4 %collective-permute-done.12.refs_9_.refs_6_ = bf16[1024,128]{1,0:T(8,128)(2,1)S(1)} collective-permute-done((bf16[1024,128]{1,0:T(8,128)(2,1)S(1)}, bf16[1024,128]{1,0:T(8,128)(2,1)S(1)}, u32[]{:S(2)}, u32[]{:S(2)}) %collective-permute-start.12) | collective-permute-done | bytes 262176 | tf_op jit(solution)/shard_map/ppermute | solution.py:329
  51.2 1.6 %collective-permute-done.11.refs_8_.refs_5_ = bf16[1024,128]{1,0:T(8,128)(2,1)S(1)} collective-permute-done((bf16[1024,128]{1,0:T(8,128)(2,1)S(1)}, bf16[1024,128]{1,0:T(8,128)(2,1)S(1)}, u32[]{:S(2)}, u32[]{:S(2)}) %collective-permute-start.11) | collective-permute-done | bytes 262176 | tf_op jit(solution)/shard_map/ppermute | solution.py:329
  52.8 8.2 %collective-permute-done.10.refs_7_.refs_4_ = bf16[1024,128]{1,0:T(8,128)(2,1)S(1)} collective-permute-done((bf16[1024,128]{1,0:T(8,128)(2,1)S(1)}, bf16[1024,128]{1,0:T(8,128)(2,1)S(1)}, u32[]{:S(2)}, u32[]{:S(2)}) %collective-permute-start.10) | collective-permute-done | bytes 262176 | tf_op jit(solution)/shard_map/ppermute | solution.py:329
  61.0 4.9 %raw_part.1 = (bf16[384,256]{1,0:T(8,128)(2,1)S(1)}, bf16[384,256]{1,0:T(8,128)(2,1)S(1)}, f32[1,256]{1,0:T(1,128)S(1)}) custom-call(s32[5]{0:T(128)S(1)} %stack.23.refs_0_, bf16[384,4096]{1,0:T(8,128)(2,1)S(1)} %get-tuple-element.46.refs_1_, bf16[384,4096]{1,0:T(8,128)(2,1)S(1)} %collective-permute-done.2.refs_6_.refs_2_, ...), custom_call_target="tpu_custom_call" | custom-call | flops 1000 | bytes 1000 | tf_op jit(solution)/shard_map/raw_part/pallas_call | solution.py:51
  65.9 0.6 collective-permute-start.14
  66.5 2.0 %collective-permute-start.15 = (f32[1,256]{1,0:T(1,128)S(1)}, f32[1,256]{1,0:T(1,128)S(1)}, u32[]{:S(2)}, u32[]{:S(2)}) collective-permute-start(f32[1,256]{1,0:T(1,128)S(1)} %get-tuple-element.62.refs_0_), channel_id=1, source_target_pairs={{0,4},{2,6},{4,0},{6,2},{8,12},{10,14},{12,8},{14,10},{16,20},{18,... | collective-permute-start | bytes 3080 | tf_op jit(solution)/shard_map/ppermute | solution.py:329
  68.6 1.1 %split_part.1 = (bf16[2048,256]{1,0:T(8,128)(2,1)S(1)}, bf16[1024,256]{1,0:T(8,128)(2,1)S(1)}, bf16[1024,256]{1,0:T(8,128)(2,1)S(1)}, bf16[384,512]{1,0:T(8,128)(2,1)S(1)}) custom-call(s32[5]{0:T(128)S(1)} %stack.23.refs_0_, f32[384,512]{1,0:T(8,128)S(1)} %get-tuple-element.54.refs_3_.refs_1_, f32[1,512]{1,0:T(1,128)S(1)} %bitcast.8, ...), custom_call_target="tpu_custom_call" | custom-call | flops 1000 | bytes 1000 | tf_op jit(solution)/shard_map/split_part/pallas_call | solution.py:51
  69.7 0.8 collective-permute-done.15.refs_1_
  70.8 2.0 %collective-permute-start.22 = (bf16[1024,256]{1,0:T(8,128)(2,1)S(1)}, bf16[1024,256]{1,0:T(8,128)(2,1)S(1)}, u32[]{:S(2)}, u32[]{:S(2)}) collective-permute-start(bf16[1024,256]{1,0:T(8,128)(2,1)S(1)} %get-tuple-element.82), channel_id=1, source_target_pairs={{0,5},{1,4},{2,7},{3,6},{4,1},{5,0},{6,3},{7,2},{8,13},{9,12},{10,... | collective-permute-start | bytes 1572872 | tf_op jit(solution)/shard_map/ppermute | solution.py:378
  72.8 2.6 %grads_part.4 = (bf16[384,2048]{1,0:T(8,128)(2,1)}, bf16[384,512]{1,0:T(8,128)(2,1)}, f32[8,128]{1,0:T(8,128)S(1)}) custom-call(s32[5]{0:T(128)S(1)} %stack.23.refs_0_, bf16[384,2048]{1,0:T(8,128)(2,1)S(1)} %copy-done, bf16[384,512]{1,0:T(8,128)(2,1)S(1)} %copy-done.2, bf16[384,2048]{1,0:T(8,128)(2,1)S(1)} %copy-done.1, ...), custom_call_target="tpu_custom_call" | custom-call | flops 1000 | bytes 1000 | tf_op jit(solution)/shard_map/grads_part/pallas_call | solution.py:51
  75.5 2.1 %collective-permute-start.17 = (f32[1,256]{1,0:T(1,128)S(1)}, f32[1,256]{1,0:T(1,128)S(1)}, u32[]{:S(2)}, u32[]{:S(2)}) collective-permute-start(f32[1,256]{1,0:T(1,128)S(1)} %add.23.refs_9_.refs_0_), channel_id=1, source_target_pairs={{0,16},{2,18},{4,20},{6,22},{8,24},{10,26},{12,28},{14,30},{16,0},... | collective-permute-start | bytes 3080 | tf_op jit(solution)/shard_map/ppermute | solution.py:329
  77.6 2.6 %grads_part.5 = (bf16[384,2048]{1,0:T(8,128)(2,1)}, bf16[384,512]{1,0:T(8,128)(2,1)}, f32[8,128]{1,0:T(8,128)S(1)}) custom-call(s32[5]{0:T(128)S(1)} %stack.23.refs_0_, bf16[384,2048]{1,0:T(8,128)(2,1)S(1)} %copy-done, bf16[384,512]{1,0:T(8,128)(2,1)S(1)} %copy-done.2, ...), custom_call_target="tpu_custom_call", output_to_operand_aliasing={{0}: (7, {}), {1}: (8, {})} | custom-call | flops 1000 | bytes 1000 | tf_op jit(solution)/shard_map/grads_part/pallas_call | solution.py:51
  80.2 1.2 %collective-permute-start.18 = (f32[1,256]{1,0:T(1,128)S(1)}, f32[1,256]{1,0:T(1,128)S(1)}, u32[]{:S(2)}, u32[]{:S(2)}) collective-permute-start(f32[1,256]{1,0:T(1,128)S(1)} %add.24.refs_9_.refs_0_), channel_id=1, source_target_pairs={{0,32},{2,34},{4,36},{6,38},{8,40},{10,42},{12,44},{14,46},{16,48}... | collective-permute-start | bytes 3080 | tf_op jit(solution)/shard_map/ppermute | solution.py:329
  81.4 3.2 %collective-permute-start.20 = (bf16[2048,256]{1,0:T(8,128)(2,1)S(1)}, bf16[2048,256]{1,0:T(8,128)(2,1)S(1)}, u32[]{:S(2)}, u32[]{:S(2)}) collective-permute-start(bf16[2048,256]{1,0:T(8,128)(2,1)S(1)} %get-tuple-element.80.refs_3_), channel_id=1, source_target_pairs={{0,2},{2,0},{4,6},{6,4},{8,10},{10,8},{12,14},{14,12},{16,18},{18,... | collective-permute-start | bytes 3145736 | tf_op jit(solution)/shard_map/ppermute | solution.py:329
  84.6 2.6 %grads_part.6 = (bf16[384,2048]{1,0:T(8,128)(2,1)}, bf16[384,512]{1,0:T(8,128)(2,1)}, f32[8,128]{1,0:T(8,128)S(1)}) custom-call(s32[5]{0:T(128)S(1)} %stack.23.refs_0_, bf16[384,2048]{1,0:T(8,128)(2,1)S(1)} %copy-done, bf16[384,512]{1,0:T(8,128)(2,1)S(1)} %copy-done.2, ...), custom_call_target="tpu_custom_call", output_to_operand_aliasing={{0}: (7, {}), {1}: (8, {})} | custom-call | flops 1000 | bytes 1000 | tf_op jit(solution)/shard_map/grads_part/pallas_call | solution.py:51
  88.0 1.0 collective-permute-start.24
  89.0 2.6 %grads_part.7 = (bf16[384,2048]{1,0:T(8,128)(2,1)}, bf16[384,512]{1,0:T(8,128)(2,1)}, f32[8,128]{1,0:T(8,128)S(1)}) custom-call(s32[5]{0:T(128)S(1)} %stack.23.refs_0_, bf16[384,2048]{1,0:T(8,128)(2,1)S(1)} %copy-done, bf16[384,512]{1,0:T(8,128)(2,1)S(1)} %copy-done.2, ...), custom_call_target="tpu_custom_call", output_to_operand_aliasing={{0}: (7, {}), {1}: (8, {})} | custom-call | flops 1000 | bytes 1000 | tf_op jit(solution)/shard_map/grads_part/pallas_call | solution.py:51
  91.6 2.8 %collective-permute-start.25 = (f32[1,256]{1,0:T(1,128)S(1)}, f32[1,256]{1,0:T(1,128)S(1)}, u32[]{:S(2)}, u32[]{:S(2)}) collective-permute-start(f32[1,256]{1,0:T(1,128)S(1)} %add.26.refs_7_.refs_0_), channel_id=1, source_target_pairs={{0,128},{2,130},{4,132},{6,134},{8,136},{10,138},{12,140},{14,142}... | collective-permute-start | bytes 3080 | tf_op jit(solution)/shard_map/ppermute | solution.py:329
  94.4 3.7 %collective-permute-done.19.refs_2_ = bf16[384,512]{1,0:T(8,128)(2,1)S(1)} collective-permute-done((bf16[384,512]{1,0:T(8,128)(2,1)S(1)}, bf16[384,512]{1,0:T(8,128)(2,1)S(1)}, u32[]{:S(2)}, u32[]{:S(2)}) %collective-permute-start.19) | collective-permute-done | bytes 393248 | tf_op jit(solution)/shard_map/ppermute | solution.py:376
  98.0 3.9 %hidden_part.1 = (bf16[384,2048]{1,0:T(8,128)(2,1)}, f32[8,128]{1,0:T(8,128)S(1)}) custom-call(s32[5]{0:T(128)S(1)} %stack.23.refs_0_, bf16[384,512]{1,0:T(8,128)(2,1)S(1)} %get-tuple-element.79.refs_1_, bf16[384,512]{1,0:T(8,128)(2,1)S(1)} %collective-permute-done.19.refs_2_, bf16[2048,256]{1,0:T(8,128)(2,1)S(1)} %get-tuple-element.80.refs_3_, ...), custom_call_target="tpu_custom_call" | custom-call | flops 1000 | bytes 1000 | tf_op jit(solution)/shard_map/hidden_part/pallas_call | solution.py:51
  102.0 1.3 %collective-permute-start.26 = (f32[1,256]{1,0:T(1,128)S(1)}, f32[1,256]{1,0:T(1,128)S(1)}, u32[]{:S(2)}, u32[]{:S(2)}) collective-permute-start(f32[1,256]{1,0:T(1,128)S(1)} %add.27.refs_1_), channel_id=1, source_target_pairs={{0,2},{2,0},{4,6},{6,4},{8,10},{10,8},{12,14},{14,12},{16,18},{18,... | collective-permute-start | bytes 3080 | tf_op jit(solution)/shard_map/ppermute | solution.py:329
  103.3 0.8 collective-permute-done.26.refs_2_
  104.1 1.1 %last.1 = f32[1,512]{1,0:T(1,128)} custom-call(s32[5]{0:T(128)S(1)} %stack.23.refs_0_, f32[1,256]{1,0:T(1,128)S(1)} %add.27.refs_1_, f32[1,256]{1,0:T(1,128)S(1)} %collective-permute-done.26.refs_2_, f32[1,512]{1,0:T(1,128)S(1)} %bitcast.9), custom_call_target="tpu_custom_call" | custom-call | flops 1000 | bytes 1000 | tf_op jit(solution)/shard_map/last/pallas_call | solution.py:51
  (46 shorter events, 2.3 us)
Async XLA Ops:
  0.6 4.4 %collective-permute-start = (bf16[32,512]{1,0:T(8,128)(2,1)}, bf16[32,512]{1,0:T(8,128)(2,1)S(1)}, u32[]{:S(2)}, u32[]{:S(2)}) collective-permute-start(bf16[32,512]{1,0:T(8,128)(2,1)} %refs_1_.9), channel_id=1, source_target_pairs={{0,2},{2,0},{4,6},{6,4},{8,10},{10,8},{12,14},{14,12},{16,18},{18,... | collective-permute-start | bytes 98312 | tf_op jit(solution)/shard_map/ppermute | solution.py:329
  5.0 0.8 copy-start.4
  6.3 7.4 %copy-start = (bf16[384,2048]{1,0:T(8,128)(2,1)S(1)}, bf16[384,2048]{1,0:T(8,128)(2,1)}, u32[]{:S(2)}) copy-start(bf16[384,2048]{1,0:T(8,128)(2,1)} %refs_1_.17) | copy-start | bytes 4718596
  6.4 7.4 %copy-start.1 = (bf16[384,2048]{1,0:T(8,128)(2,1)S(1)}, bf16[384,2048]{1,0:T(8,128)(2,1)}, u32[]{:S(2)}) copy-start(bf16[384,2048]{1,0:T(8,128)(2,1)} %refs_3_.15) | copy-start | bytes 4718596
  6.4 7.4 %copy-start.2 = (bf16[384,512]{1,0:T(8,128)(2,1)S(1)}, bf16[384,512]{1,0:T(8,128)(2,1)}, u32[]{:S(2)}) copy-start(bf16[384,512]{1,0:T(8,128)(2,1)} %refs_2_.15) | copy-start | bytes 1179652
  6.4 10.0 %collective-permute-start.1 = (bf16[64,256]{1,0:T(8,128)(2,1)S(1)}, bf16[64,256]{1,0:T(8,128)(2,1)S(1)}, u32[]{:S(2)}, u32[]{:S(2)}) collective-permute-start(bf16[64,256]{1,0:T(8,128)(2,1)S(1)} %join.6.refs_4_.refs_1_.refs_0_), channel_id=1, source_target_pairs={{0,128},{2,130},{4,132},{6,134},{8,136},{10,138},{12,140},{14,142}... | collective-permute-start | bytes 98312 | tf_op jit(solution)/shard_map/ppermute | solution.py:329
  11.6 1.9 %copy-start.3 = (bf16[384,4096]{1,0:T(8,128)(2,1)S(1)}, bf16[384,4096]{1,0:T(8,128)(2,1)}, u32[]{:S(2)}) copy-start(bf16[384,4096]{1,0:T(8,128)(2,1)} %refs_0_.6) | copy-start | bytes 9437188
  13.5 0.7 copy-start.6
  16.4 28.1 %collective-permute-start.2 = (bf16[384,4096]{1,0:T(8,128)(2,1)S(1)}, bf16[384,4096]{1,0:T(8,128)(2,1)S(1)}, u32[]{:S(2)}, u32[]{:S(2)}) collective-permute-start(bf16[384,4096]{1,0:T(8,128)(2,1)S(1)} %get-tuple-element.46.refs_1_), channel_id=1, source_target_pairs={{0,2},{2,0},{4,6},{6,4},{8,10},{10,8},{12,14},{14,12},{16,18},{18,... | collective-permute-start | bytes 9437192 | tf_op jit(solution)/shard_map/ppermute | solution.py:329
  17.1 6.0 %collective-permute-start.3 = (bf16[128,256]{1,0:T(8,128)(2,1)S(1)}, bf16[128,256]{1,0:T(8,128)(2,1)S(1)}, u32[]{:S(2)}, u32[]{:S(2)}) collective-permute-start(bf16[128,256]{1,0:T(8,128)(2,1)S(1)} %get-tuple-element.47.refs_5_.refs_0_), channel_id=1, source_target_pairs={{0,64},{2,66},{4,68},{6,70},{8,72},{10,74},{12,76},{14,78},{16,80}... | collective-permute-start | bytes 196616 | tf_op jit(solution)/shard_map/ppermute | solution.py:329
  23.1 4.5 %collective-permute-start.4 = (bf16[256,256]{1,0:T(8,128)(2,1)S(1)}, bf16[256,256]{1,0:T(8,128)(2,1)S(1)}, u32[]{:S(2)}, u32[]{:S(2)}) collective-permute-start(bf16[256,256]{1,0:T(8,128)(2,1)S(1)} %join.8.refs_5_.refs_0_), channel_id=1, source_target_pairs={{0,32},{2,34},{4,36},{6,38},{8,40},{10,42},{12,44},{14,46},{16,48}... | collective-permute-start | bytes 393224 | tf_op jit(solution)/shard_map/ppermute | solution.py:329
  27.7 16.8 %collective-permute-start.5 = (f32[384,512]{1,0:T(8,128)S(1)}, f32[384,512]{1,0:T(8,128)S(1)}, u32[]{:S(2)}, u32[]{:S(2)}) collective-permute-start(f32[384,512]{1,0:T(8,128)S(1)} %get-tuple-element.54.refs_3_.refs_1_), channel_id=1, source_target_pairs={{0,2},{2,0},{4,6},{6,4},{8,10},{10,8},{12,14},{14,12},{16,18},{18,... | collective-permute-start | bytes 2359304 | tf_op jit(solution)/shard_map/ppermute | solution.py:329
  29.2 6.6 %collective-permute-start.6 = (bf16[512,128]{1,0:T(8,128)(2,1)S(1)}, bf16[512,128]{1,0:T(8,128)(2,1)S(1)}, u32[]{:S(2)}, u32[]{:S(2)}) collective-permute-start(bf16[512,128]{1,0:T(8,128)(2,1)S(1)} %get-tuple-element.55.refs_0_), channel_id=1, source_target_pairs={{0,4},{2,6},{4,0},{6,2},{8,12},{10,14},{12,8},{14,10},{16,20},{18,... | collective-permute-start | bytes 393224 | tf_op jit(solution)/shard_map/ppermute | solution.py:329
  32.0 29.0 %copy-start.5 = (f32[512]{0:T(512)S(1)}, f32[512]{0:T(512)}, u32[]{:S(2)}) copy-start(f32[512]{0:T(512)} %param.11) | copy-start | bytes 6148
  32.0 7.9 %collective-permute-start.9 = (bf16[512,128]{1,0:T(8,128)(2,1)S(1)}, bf16[512,128]{1,0:T(8,128)(2,1)S(1)}, u32[]{:S(2)}, u32[]{:S(2)}) collective-permute-start(bf16[512,128]{1,0:T(8,128)(2,1)S(1)} %get-tuple-element.56.refs_2_), channel_id=1, source_target_pairs={{0,24},{2,26},{4,28},{6,30},{8,0},{10,2},{12,4},{14,6},{16,8},{18,... | collective-permute-start | bytes 393224 | tf_op jit(solution)/shard_map/ppermute | solution.py:329
  34.7 5.9 %collective-permute-start.8 = (bf16[512,128]{1,0:T(8,128)(2,1)S(1)}, bf16[512,128]{1,0:T(8,128)(2,1)S(1)}, u32[]{:S(2)}, u32[]{:S(2)}) collective-permute-start(bf16[512,128]{1,0:T(8,128)(2,1)S(1)} %get-tuple-element.56.refs_2_), channel_id=1, source_target_pairs={{0,16},{2,18},{4,20},{6,22},{8,24},{10,26},{12,28},{14,30},{16,0},... | collective-permute-start | bytes 393224 | tf_op jit(solution)/shard_map/ppermute | solution.py:329
  35.8 8.7 %collective-permute-start.7 = (bf16[512,128]{1,0:T(8,128)(2,1)S(1)}, bf16[512,128]{1,0:T(8,128)(2,1)S(1)}, u32[]{:S(2)}, u32[]{:S(2)}) collective-permute-start(bf16[512,128]{1,0:T(8,128)(2,1)S(1)} %get-tuple-element.56.refs_2_), channel_id=1, source_target_pairs={{0,8},{2,10},{4,12},{6,14},{8,16},{10,18},{12,20},{14,22},{16,24},... | collective-permute-start | bytes 393224 | tf_op jit(solution)/shard_map/ppermute | solution.py:329
  44.5 16.5 %collective-permute-start.13 = (bf16[2048,128]{1,0:T(8,128)(2,1)S(1)}, bf16[2048,128]{1,0:T(8,128)(2,1)S(1)}, u32[]{:S(2)}, u32[]{:S(2)}) collective-permute-start(bf16[2048,128]{1,0:T(8,128)(2,1)S(1)} %get-tuple-element.58.refs_10_.refs_7_), channel_id=1, source_target_pairs={{0,4},{2,6},{4,0},{6,2},{8,12},{10,14},{12,8},{14,10},{16,20},{18,... | collective-permute-start | bytes 1572872 | tf_op jit(solution)/shard_map/ppermute | solution.py:329
  44.8 6.4 %collective-permute-start.12 = (bf16[1024,128]{1,0:T(8,128)(2,1)S(1)}, bf16[1024,128]{1,0:T(8,128)(2,1)S(1)}, u32[]{:S(2)}, u32[]{:S(2)}) collective-permute-start(bf16[1024,128]{1,0:T(8,128)(2,1)S(1)} %get-tuple-element.57.refs_6_.refs_3_), channel_id=1, source_target_pairs={{0,24},{2,26},{4,28},{6,30},{8,0},{10,2},{12,4},{14,6},{16,8},{18,... | collective-permute-start | bytes 786440 | tf_op jit(solution)/shard_map/ppermute | solution.py:329
  45.8 7.1 %collective-permute-start.11 = (bf16[1024,128]{1,0:T(8,128)(2,1)S(1)}, bf16[1024,128]{1,0:T(8,128)(2,1)S(1)}, u32[]{:S(2)}, u32[]{:S(2)}) collective-permute-start(bf16[1024,128]{1,0:T(8,128)(2,1)S(1)} %get-tuple-element.57.refs_6_.refs_3_), channel_id=1, source_target_pairs={{0,16},{2,18},{4,20},{6,22},{8,24},{10,26},{12,28},{14,30},{16,0},... | collective-permute-start | bytes 786440 | tf_op jit(solution)/shard_map/ppermute | solution.py:329
  46.1 14.9 %collective-permute-start.10 = (bf16[1024,128]{1,0:T(8,128)(2,1)S(1)}, bf16[1024,128]{1,0:T(8,128)(2,1)S(1)}, u32[]{:S(2)}, u32[]{:S(2)}) collective-permute-start(bf16[1024,128]{1,0:T(8,128)(2,1)S(1)} %get-tuple-element.57.refs_6_.refs_3_), channel_id=1, source_target_pairs={{0,8},{2,10},{4,12},{6,14},{8,16},{10,18},{12,20},{14,22},{16,24},... | collective-permute-start | bytes 786440 | tf_op jit(solution)/shard_map/ppermute | solution.py:329
  65.9 2.7 %collective-permute-start.14 = (bf16[384,256]{1,0:T(8,128)(2,1)S(1)}, bf16[384,256]{1,0:T(8,128)(2,1)S(1)}, u32[]{:S(2)}, u32[]{:S(2)}) collective-permute-start(bf16[384,256]{1,0:T(8,128)(2,1)S(1)} %get-tuple-element.60), channel_id=1, source_target_pairs={{0,2},{2,0},{4,6},{6,4},{8,10},{10,8},{12,14},{14,12},{16,18},{18,... | collective-permute-start | bytes 589832 | tf_op jit(solution)/shard_map/ppermute | solution.py:329
  66.5 3.9 %collective-permute-start.15 = (f32[1,256]{1,0:T(1,128)S(1)}, f32[1,256]{1,0:T(1,128)S(1)}, u32[]{:S(2)}, u32[]{:S(2)}) collective-permute-start(f32[1,256]{1,0:T(1,128)S(1)} %get-tuple-element.62.refs_0_), channel_id=1, source_target_pairs={{0,4},{2,6},{4,0},{6,2},{8,12},{10,14},{12,8},{14,10},{16,20},{18,... | collective-permute-start | bytes 3080 | tf_op jit(solution)/shard_map/ppermute | solution.py:329
  70.5 16.8 %collective-permute-start.21 = (bf16[1024,256]{1,0:T(8,128)(2,1)S(1)}, bf16[1024,256]{1,0:T(8,128)(2,1)S(1)}, u32[]{:S(2)}, u32[]{:S(2)}) collective-permute-start(bf16[1024,256]{1,0:T(8,128)(2,1)S(1)} %get-tuple-element.81), channel_id=1, source_target_pairs={{0,1},{1,0},{2,3},{3,2},{4,5},{5,4},{6,7},{7,6},{8,9},{9,8},{10,11... | collective-permute-start | bytes 1572872 | tf_op jit(solution)/shard_map/ppermute | solution.py:377
  70.8 16.5 %collective-permute-start.22 = (bf16[1024,256]{1,0:T(8,128)(2,1)S(1)}, bf16[1024,256]{1,0:T(8,128)(2,1)S(1)}, u32[]{:S(2)}, u32[]{:S(2)}) collective-permute-start(bf16[1024,256]{1,0:T(8,128)(2,1)S(1)} %get-tuple-element.82), channel_id=1, source_target_pairs={{0,5},{1,4},{2,7},{3,6},{4,1},{5,0},{6,3},{7,2},{8,13},{9,12},{10,... | collective-permute-start | bytes 1572872 | tf_op jit(solution)/shard_map/ppermute | solution.py:378
  72.8 2.7 %collective-permute-start.16 = (f32[1,256]{1,0:T(1,128)S(1)}, f32[1,256]{1,0:T(1,128)S(1)}, u32[]{:S(2)}, u32[]{:S(2)}) collective-permute-start(f32[1,256]{1,0:T(1,128)S(1)} %get-tuple-element.67.refs_7_.refs_0_), channel_id=1, source_target_pairs={{0,8},{2,10},{4,12},{6,14},{8,0},{10,2},{12,4},{14,6},{16,24},{18,... | collective-permute-start | bytes 3080 | tf_op jit(solution)/shard_map/ppermute | solution.py:329
  75.5 4.7 %collective-permute-start.17 = (f32[1,256]{1,0:T(1,128)S(1)}, f32[1,256]{1,0:T(1,128)S(1)}, u32[]{:S(2)}, u32[]{:S(2)}) collective-permute-start(f32[1,256]{1,0:T(1,128)S(1)} %add.23.refs_9_.refs_0_), channel_id=1, source_target_pairs={{0,16},{2,18},{4,20},{6,22},{8,24},{10,26},{12,28},{14,30},{16,0},... | collective-permute-start | bytes 3080 | tf_op jit(solution)/shard_map/ppermute | solution.py:329
  80.2 7.0 %collective-permute-start.18 = (f32[1,256]{1,0:T(1,128)S(1)}, f32[1,256]{1,0:T(1,128)S(1)}, u32[]{:S(2)}, u32[]{:S(2)}) collective-permute-start(f32[1,256]{1,0:T(1,128)S(1)} %add.24.refs_9_.refs_0_), channel_id=1, source_target_pairs={{0,32},{2,34},{4,36},{6,38},{8,40},{10,42},{12,44},{14,46},{16,48}... | collective-permute-start | bytes 3080 | tf_op jit(solution)/shard_map/ppermute | solution.py:329
  81.4 16.6 %collective-permute-start.20 = (bf16[2048,256]{1,0:T(8,128)(2,1)S(1)}, bf16[2048,256]{1,0:T(8,128)(2,1)S(1)}, u32[]{:S(2)}, u32[]{:S(2)}) collective-permute-start(bf16[2048,256]{1,0:T(8,128)(2,1)S(1)} %get-tuple-element.80.refs_3_), channel_id=1, source_target_pairs={{0,2},{2,0},{4,6},{6,4},{8,10},{10,8},{12,14},{14,12},{16,18},{18,... | collective-permute-start | bytes 3145736 | tf_op jit(solution)/shard_map/ppermute | solution.py:329
  87.3 10.7 %collective-permute-start.23 = (bf16[2048,256]{1,0:T(8,128)(2,1)S(1)}, bf16[2048,256]{1,0:T(8,128)(2,1)S(1)}, u32[]{:S(2)}, u32[]{:S(2)}) collective-permute-start(bf16[2048,256]{1,0:T(8,128)(2,1)S(1)} %join.11.refs_3_.refs_5_), channel_id=1, source_target_pairs={{0,2},{2,0},{4,6},{6,4},{8,10},{10,8},{12,14},{14,12},{16,18},{18,... | collective-permute-start | bytes 3145736 | tf_op jit(solution)/shard_map/ppermute | solution.py:329
  87.7 10.4 %collective-permute-start.19 = (bf16[384,512]{1,0:T(8,128)(2,1)S(1)}, bf16[384,512]{1,0:T(8,128)(2,1)S(1)}, u32[]{:S(2)}, u32[]{:S(2)}) collective-permute-start(bf16[384,512]{1,0:T(8,128)(2,1)S(1)} %get-tuple-element.79.refs_1_), channel_id=1, source_target_pairs={{0,1},{1,0},{2,3},{3,2},{4,5},{5,4},{6,7},{7,6},{8,9},{9,8},{10,11... | collective-permute-start | bytes 1179656 | tf_op jit(solution)/shard_map/ppermute | solution.py:376
  88.0 3.6 %collective-permute-start.24 = (f32[1,256]{1,0:T(1,128)S(1)}, f32[1,256]{1,0:T(1,128)S(1)}, u32[]{:S(2)}, u32[]{:S(2)}) collective-permute-start(f32[1,256]{1,0:T(1,128)S(1)} %add.25.refs_9_.refs_2_.refs_0_), channel_id=1, source_target_pairs={{0,64},{2,66},{4,68},{6,70},{8,72},{10,74},{12,76},{14,78},{16,80}... | collective-permute-start | bytes 3080 | tf_op jit(solution)/shard_map/ppermute | solution.py:329
  91.6 10.3 %collective-permute-start.25 = (f32[1,256]{1,0:T(1,128)S(1)}, f32[1,256]{1,0:T(1,128)S(1)}, u32[]{:S(2)}, u32[]{:S(2)}) collective-permute-start(f32[1,256]{1,0:T(1,128)S(1)} %add.26.refs_7_.refs_0_), channel_id=1, source_target_pairs={{0,128},{2,130},{4,132},{6,134},{8,136},{10,138},{12,140},{14,142}... | collective-permute-start | bytes 3080 | tf_op jit(solution)/shard_map/ppermute | solution.py:329
  102.0 2.1 %collective-permute-start.26 = (f32[1,256]{1,0:T(1,128)S(1)}, f32[1,256]{1,0:T(1,128)S(1)}, u32[]{:S(2)}, u32[]{:S(2)}) collective-permute-start(f32[1,256]{1,0:T(1,128)S(1)} %add.27.refs_1_), channel_id=1, source_target_pairs={{0,2},{2,0},{4,6},{6,4},{8,10},{10,8},{12,14},{14,12},{16,18},{18,... | collective-permute-start | bytes 3080 | tf_op jit(solution)/shard_map/ppermute | solution.py:329

commit v3 on v2

--- a/solution.py
+++ b/solution.py
@@ -212,41 +212,28 @@
                 place(pieces[4 + xi], (k * 8 + zi) * CHIP, zi, k, xi, HEAD)
 
 
-STEP = 512
-
-
 def raw_kernel(at_ref, own_ref, other_ref, dv_own, dv_other, scale_ref, *refs):
-    pieces, (mine_ref, theirs_ref, sums_ref, codes_ref, raw_own, raw_other) = refs[:6], refs[6:]
-    i = pl.program_id(0)
-
-    @pl.when(i == 0)
-    def _():
-        put_in_order(at_ref, pieces, codes_ref)
-        raw_own[...] = jnp.zeros_like(raw_own)
-        raw_other[...] = jnp.zeros_like(raw_other)
-
-    codes = codes_ref[pl.ds(pl.multiple_of(i * STEP, STEP), STEP), :]
-    raw_own[...] += dot(own_ref[...], codes, (1, 0))
-    raw_other[...] += dot(other_ref[...], codes, (1, 0))
-
-    @pl.when(i == pl.num_programs(0) - 1)
-    def _():
-        cols = own_columns(at_ref)
-        scale = scale_ref[:, cols]
-        mine_ref[...] = (raw_own[...] * scale).astype(BF16)
-        theirs_ref[...] = (raw_other[...] * scale).astype(BF16)
-        products = raw_own[...] * dv_own[:, cols] + raw_other[...] * dv_other[:, cols]
-        sums_ref[...] = jnp.sum(products, axis=0, keepdims=True)
+    pieces, (mine_ref, theirs_ref, sums_ref, codes_ref) = refs[:6], refs[6:]
+    put_in_order(at_ref, pieces, codes_ref)
+    cols = own_columns(at_ref)
+    scale = scale_ref[:, cols]
+    sums = jnp.zeros((1, HALF), F32)
+    for hidden_ref, dv_ref, values_ref in ((other_ref, dv_other, theirs_ref), (own_ref, dv_own, mine_ref)):
+        raw = dot(hidden_ref[...], codes_ref[...], (1, 0))
+        values_ref[...] = (raw * scale).astype(BF16)
+        sums += jnp.sum(raw * dv_ref[:, cols], axis=0, keepdims=True)
+    sums_ref[...] = sums
 
 
 def raw_part(at, hidden, hidden_other, dv, dv_other, scale, pieces):
-    block = pl.BlockSpec((COUNT, STEP), lambda i: (0, i))
     return call(
         raw_kernel, "raw_part", [shape(COUNT, HALF), shape(COUNT, HALF), shape(1, HALF, dtype=F32)],
-        [(SMEM, at), (block, hidden), (block, hidden_other), (VMEM, dv), (VMEM, dv_other), (VMEM, scale)] + [(VMEM, p) for p in pieces],
-        grid=(DEPTH // STEP,),
-        scratch_shapes=[pltpu.VMEM((DEPTH, HALF), BF16), pltpu.VMEM((COUNT, HALF), F32), pltpu.VMEM((COUNT, HALF), F32)],
-    )
+        [(SMEM, at)] + [(VMEM, a) for a in [hidden, hidden_other, dv, dv_other, scale] + pieces],
+        scratch_shapes=[pltpu.VMEM((DEPTH, HALF), BF16)],
+    )
+
+
+NEAR = 640
 
 
 def split_kernel(at_ref, dv_ref, scale_ref, *refs):
@@ -255,35 +242,36 @@
     s, half = at_ref[4], DEPTH // 2
     kept_ref[...] = codes_ref[pl.ds(pl.multiple_of(s * half, half), half), :]
     base = (1 - s) * half
-    near_ref[...] = codes_ref[pl.ds(pl.multiple_of(base, half), half // 2), :]
-    beside_ref[...] = codes_ref[pl.ds(pl.multiple_of(base + half // 2, half // 2), half // 2), :]
+    near_ref[...] = codes_ref[pl.ds(pl.multiple_of(base, half), NEAR), :]
+    beside_ref[...] = codes_ref[pl.ds(pl.multiple_of(base + NEAR, 128), half - NEAR), :]
     scaled_ref[...] = (dv_ref[...] * scale_ref[...]).astype(BF16)
 
 
 def split_part(at, dv, scale, pieces, after):
     return call(
-        split_kernel, "split_part", [shape(DEPTH // 2, HALF), shape(DEPTH // 4, HALF), shape(DEPTH // 4, HALF), shape(COUNT, 2 * HALF)],
+        split_kernel, "split_part", [shape(DEPTH // 2, HALF), shape(NEAR, HALF), shape(DEPTH // 2 - NEAR, HALF), shape(COUNT, 2 * HALF)],
         [(SMEM, at), (VMEM, dv), (VMEM, scale)] + [(VMEM, p) for p in pieces], after,
         scratch_shapes=[pltpu.VMEM((DEPTH, HALF), BF16)],
     )
+
+
+BATCH = 512
 
 
 def hidden_kernel(at_ref, own_ref, other_ref, kept_ref, kept_far, near_ref, near_far, out_ref, token_ref):
     mine = own_columns(at_ref)
     rest = pl.ds(pl.multiple_of((1 - at_ref[3]) * HALF, HALF), HALF)
-    total = dot(own_ref[:, mine], kept_ref[...], (1, 1)) + dot(own_ref[:, rest], kept_far[...], (1, 1))
-    total += dot(other_ref[:, mine], near_ref[...], (1, 1)) + dot(other_ref[:, rest], near_far[...], (1, 1))
-    out_ref[...] = total.astype(BF16)
+    terms = ((own_ref, mine, kept_ref), (own_ref, rest, kept_far), (other_ref, mine, near_ref), (other_ref, rest, near_far))
+    for i in range(0, DEPTH // 2, BATCH):
+        rows = pl.ds(i, BATCH)
+        out_ref[:, rows] = sum(dot(a[:, cols], b[rows, :], (1, 1)) for a, cols, b in terms).astype(BF16)
     token_ref[...] = jnp.zeros_like(token_ref)
 
 
-def hidden_part(at, own, other, kept, kept_far, near, near_far, after):
-    block = pl.BlockSpec((STEP, HALF), lambda i: (i, 0))
+def hidden_part(at, *arrays, after):
     return call(
         hidden_kernel, "hidden_part", [shape(COUNT, DEPTH // 2), TOKEN],
-        [(SMEM, at), (VMEM, own), (VMEM, other), (block, kept), (block, kept_far), (block, near), (block, near_far)], after,
-        grid=(DEPTH // 2 // STEP,),
-        out_specs=[pl.BlockSpec((COUNT, STEP), lambda i: (0, i)), VMEM],
+        [(SMEM, at)] + [(VMEM, a) for a in arrays], after,
     )
 
 
@@ -335,36 +323,33 @@
     scale = value_scale.reshape(1, -1)
 
     rows = call(first_join, "join", shape(CHIP, HALF), [(SMEM, at), (VMEM, value_codes), (VMEM, send(value_codes, C_SWAP))])
-    hidden = call(
-        copy_kernel, "copy", shape(*hidden.shape), [(ANY, hidden)], (rows,),
-        out_specs=[ANY], scratch_shapes=[pltpu.SemaphoreType.DMA],
-    )
     probs, dv = [], None
-    for bit, heads in ((4, (0,)), (2, (1,)), (1, (2, 3))):
+    for g, bit in enumerate((4, 2, 1)):
         got = send(rows, z_swap(bit))
-        for g in heads:
-            p, dv = probs_part(g, lengths, queries, keys, upstream, dv, (rows,))
-            probs.append(p)
+        p, dv = probs_part(g, lengths, queries, keys, upstream, dv, (rows,))
+        probs.append(p)
         n = rows.shape[0]
         ins = [(VMEM, rows), (VMEM, got)]
-        if bit == 4:
-            rows, hidden = call(join_kernel, "join", shape(2 * n, HALF), ins, (p,), (hidden,))
-            hidden_other = send(hidden, C_SWAP)
-        elif bit == 2:
+        if bit > 1:
             rows = call(join_kernel, "join", shape(2 * n, HALF), ins, (p,))
         else:
-            first, second, dv = call(join_split_kernel, "join", [shape(2 * n, HEAD)] * 2, ins, (p,), (dv,))
-    dv_other = send(dv, C_SWAP)
+            hidden = call(
+                copy_kernel, "copy", shape(*hidden.shape), [(ANY, hidden)], (rows,),
+                out_specs=[ANY], scratch_shapes=[pltpu.SemaphoreType.DMA],
+            )
+            first, second, hidden = call(join_split_kernel, "join", [shape(2 * n, HEAD)] * 2, ins, (p,), (hidden,))
     first_x = send(first, X_SWAP)
     second_y = [send(second, y_shift(k)) for k in (1, 2, 3)]
+    hidden_other = send(hidden, C_SWAP)
+    p, dv = probs_part(3, lengths, queries, keys, upstream, dv, (first,))
+    probs.append(p)
     n = first.shape[0]
-    first, second = call(
+    first, second, dv = call(
         two_joins_kernel, "join", [shape(2 * n, HEAD), shape(4 * n, HEAD)],
-        [(VMEM, a) for a in [first, first_x, second] + second_y], (hidden_other, dv_other),
+        [(VMEM, a) for a in [first, first_x, second] + second_y], (hidden_other,), (dv,),
     )
     pieces = [first] + [send(first, y_shift(k)) for k in (1, 2, 3)] + [second, send(second, X_SWAP)]
-
-    mine, theirs, sums = raw_part(at, hidden, hidden_other, dv, dv_other, scale, pieces)
+    mine, theirs, sums = raw_part(at, hidden, hidden_other, dv, send(dv, C_SWAP), scale, pieces)
 
     got = send(sums, X_SWAP)
     values_far = send(theirs, C_SWAP)
@@ -379,7 +364,7 @@
     held = None
     for g, perm in enumerate((y_swap(1), y_swap(2), z_swap(1), z_swap(2))):
         got = send(sums, perm)
-        *held, token = grads_part(g, at, queries, keys, upstream, mine, values_far, probs[g], held, (sums,))
+        *held, token = grads_part(g, at, queries, keys, upstream, mine, values_far, probs[g], held, (sums, scaled_other) if g == 2 else (sums,))
         after = (token,)
         if g == 3:
             near = call(join_kernel, "join", shape(DEPTH // 2, HALF), [(VMEM, near), (VMEM, beside)], (sums,))
@@ -387,7 +372,7 @@
             after += (near,)
         sums = call(add_kernel, "add", shape(1, HALF, dtype=F32), [(VMEM, sums), (VMEM, got)], after)
     got = send(sums, z_swap(4))
-    grad_hidden, token = hidden_part(at, scaled, scaled_other, kept, kept_far, near, near_far, (sums,))
+    grad_hidden, token = hidden_part(at, scaled, scaled_other, kept, kept_far, near, near_far, after=(sums,))
     sums = call(add_kernel, "add", shape(1, HALF, dtype=F32), [(VMEM, sums), (VMEM, got)], (token,))
     last = call(
         last_kernel, "last", shape(1, 2 * HALF, dtype=F32),

time: 105 us -> 105 us (level)
  Pallas kernels: 31.2 us -> 28.7 us
  local copies, waits for them, and re-layouts: 3.15 us -> 5.33 us
  waiting for transfers between devices: 31.2 us -> 29.1 us
  starting transfers between devices: 38.8 us -> 40.8 us
    ppermute x1, waiting for transfers between devices: 3.65 us -> 0.01 us  [shards(): scaled_other = lax.ppermute(scaled, 'seq', SEQ_SWAP)]
    pallas_call x25, Pallas kernels: 31.2 us -> 28.7 us  [call(): pl.pallas_call(run, in_specs=list(specs) + [ANY] * (len(after) + len(thro...]
    unnamed x14 -> x20, local copies, waits for them, and re-layouts: 3.07 us -> 5.24 us
    ppermute x1, starting transfers between devices: 0.31 us -> 1.46 us  [shards(): near = lax.ppermute(near, 'seq', SEQ_SWAP)]
  transfers between devices with their start and end apart: 27 -> 27, of which waited for: 13 -> 14; matrix products, arithmetic and copies ran while one was open for 0% -> 0% of each run, Pallas kernels for 23% -> 23%
where the time goes in v3:
time: 105 us
  starting transfers between devices  40.8 us (39%)
  waiting for transfers between devices  29.1 us (28%)
  Pallas kernels  28.7 us (27%)
  local copies, waits for them, and re-layouts  5.33 us (5%)
    ppermute x24, starting transfers between devices, send(): return lax.ppermute(x, 'dp', perm)  36.8 us
    pallas_call x25, Pallas kernels, call(): pl.pallas_call(run, in_specs=list(specs) + [ANY] * (len(after) + len(thro...  28.7 us
    ppermute x24, waiting for transfers between devices, send(): return lax.ppermute(x, 'dp', perm)  28 us
    unnamed x20, local copies, waits for them, and re-layouts  5.24 us
    ppermute x1, starting transfers between devices, shards(): beside = lax.ppermute(beside, ('dp', 'seq'), BESIDE)  2.48 us
  transfers between devices with their start and end apart: 27, of which 14 were waited for; matrix products, arithmetic and copies ran while one was open for 0% of the time, Pallas kernels for 23%

profile of v3, /device:TPU:1, one launch (start us, length us, event | category | flops | bytes accessed | tf_op | source)
XLA Modules:
  0.0 104.6 jit_solution(9009510035798232370)
XLA Ops:
  0.6 3.3 %collective-permute-start = (bf16[32,512]{1,0:T(8,128)(2,1)}, bf16[32,512]{1,0:T(8,128)(2,1)S(1)}, u32[]{:S(2)}, u32[]{:S(2)}) collective-permute-start(bf16[32,512]{1,0:T(8,128)(2,1)} %refs_1_.9), channel_id=1, source_target_pairs={{0,2},{2,0},{4,6},{6,4},{8,10},{10,8},{12,14},{14,12},{16,18},{18,... | collective-permute-start | bytes 98312 | tf_op jit(solution)/shard_map/ppermute | solution.py:317
  4.0 1.0 collective-permute-done.refs_2_
  5.0 0.8 copy-done.7
  5.8 0.5 join.6.refs_4_.refs_0_
  6.3 5.3 %collective-permute-start.1 = (bf16[64,256]{1,0:T(8,128)(2,1)S(1)}, bf16[64,256]{1,0:T(8,128)(2,1)S(1)}, u32[]{:S(2)}, u32[]{:S(2)}) collective-permute-start(bf16[64,256]{1,0:T(8,128)(2,1)S(1)} %join.6.refs_4_.refs_0_), channel_id=1, source_target_pairs={{0,128},{2,130},{4,132},{6,134},{8,136},{10,138},{12,140},{14,142}... | collective-permute-start | bytes 98312 | tf_op jit(solution)/shard_map/ppermute | solution.py:317
  11.6 1.4 %copy-done = bf16[384,2048]{1,0:T(8,128)(2,1)S(1)} copy-done((bf16[384,2048]{1,0:T(8,128)(2,1)S(1)}, bf16[384,2048]{1,0:T(8,128)(2,1)}, u32[]{:S(2)}) %copy-start) | copy-done | bytes 1572888
  13.0 1.4 %copy-done.2 = bf16[384,2048]{1,0:T(8,128)(2,1)S(1)} copy-done((bf16[384,2048]{1,0:T(8,128)(2,1)S(1)}, bf16[384,2048]{1,0:T(8,128)(2,1)}, u32[]{:S(2)}) %copy-start.2) | copy-done | bytes 1572888
  14.4 1.0 copy-done.4
  15.4 0.7 copy-done.9
  16.1 2.2 %probs_part.4 = (bf16[4,384,384]{2,1,0:T(8,128)(2,1)S(1)}, f32[384,512]{1,0:T(8,128)S(1)}) custom-call(s32[1,4]{1,0:T(1,128)S(1)} %copy-done.9, bf16[384,2048]{1,0:T(8,128)(2,1)S(1)} %copy-done, bf16[384,512]{1,0:T(8,128)(2,1)S(1)} %copy-done.4, bf16[384,2048]{1,0:T(8,128)(2,1)S(1)} %copy-done.2, bf16[64,256]{1,0:T(8,128)(2,1)S(1)} %join.6.refs_4_.refs_0_), custom_call_target="tpu_custom_call" | custom-call | flops 1000 | bytes 1000 | tf_op jit(solution)/shard_map/probs_part/pallas_call | solution.py:51
  18.3 1.3 %collective-permute-start.2 = (bf16[128,256]{1,0:T(8,128)(2,1)S(1)}, bf16[128,256]{1,0:T(8,128)(2,1)S(1)}, u32[]{:S(2)}, u32[]{:S(2)}) collective-permute-start(bf16[128,256]{1,0:T(8,128)(2,1)S(1)} %join.7.refs_5_.refs_0_), channel_id=1, source_target_pairs={{0,64},{2,66},{4,68},{6,70},{8,72},{10,74},{12,76},{14,78},{16,80}... | collective-permute-start | bytes 196616 | tf_op jit(solution)/shard_map/ppermute | solution.py:317
  19.6 2.2 %probs_part.5 = (bf16[4,384,384]{2,1,0:T(8,128)(2,1)S(1)}, f32[384,512]{1,0:T(8,128)S(1)}) custom-call(s32[1,4]{1,0:T(1,128)S(1)} %copy-done.9, bf16[384,2048]{1,0:T(8,128)(2,1)S(1)} %copy-done.1, bf16[384,512]{1,0:T(8,128)(2,1)S(1)} %copy-done.4, bf16[384,2048]{1,0:T(8,128)(2,1)S(1)} %copy-done.3, ...), custom_call_target="tpu_custom_call", output_to_operand_aliasing={{1}: (4, {})} | custom-call | flops 1000 | bytes 1000 | tf_op jit(solution)/shard_map/probs_part/pallas_call | solution.py:51
  21.8 1.8 %collective-permute-done.2.refs_1_ = bf16[128,256]{1,0:T(8,128)(2,1)S(1)} collective-permute-done((bf16[128,256]{1,0:T(8,128)(2,1)S(1)}, bf16[128,256]{1,0:T(8,128)(2,1)S(1)}, u32[]{:S(2)}, u32[]{:S(2)}) %collective-permute-start.2) | collective-permute-done | bytes 65568 | tf_op jit(solution)/shard_map/ppermute | solution.py:317
  23.6 2.2 %probs_part.6 = (bf16[4,384,384]{2,1,0:T(8,128)(2,1)S(1)}, f32[384,512]{1,0:T(8,128)S(1)}) custom-call(s32[1,4]{1,0:T(1,128)S(1)} %copy-done.9, bf16[384,2048]{1,0:T(8,128)(2,1)S(1)} %copy-done.1, bf16[384,512]{1,0:T(8,128)(2,1)S(1)} %copy-done.4, bf16[384,2048]{1,0:T(8,128)(2,1)S(1)} %copy-done.3, ...), custom_call_target="tpu_custom_call", output_to_operand_aliasing={{1}: (4, {})} | custom-call | flops 1000 | bytes 1000 | tf_op jit(solution)/shard_map/probs_part/pallas_call | solution.py:51
  26.1 1.4 %collective-permute-done.3.refs_1_ = bf16[256,256]{1,0:T(8,128)(2,1)S(1)} collective-permute-done((bf16[256,256]{1,0:T(8,128)(2,1)S(1)}, bf16[256,256]{1,0:T(8,128)(2,1)S(1)}, u32[]{:S(2)}, u32[]{:S(2)}) %collective-permute-start.3) | collective-permute-done | bytes 131104 | tf_op jit(solution)/shard_map/ppermute | solution.py:317
  27.5 2.9 %collective-permute-start.4 = (bf16[384,4096]{1,0:T(8,128)(2,1)S(1)}, bf16[384,4096]{1,0:T(8,128)(2,1)S(1)}, u32[]{:S(2)}, u32[]{:S(2)}) collective-permute-start(bf16[384,4096]{1,0:T(8,128)(2,1)S(1)} %get-tuple-element.49.refs_1_), channel_id=1, source_target_pairs={{0,2},{2,0},{4,6},{6,4},{8,10},{10,8},{12,14},{14,12},{16,18},{18,... | collective-permute-start | bytes 9437192 | tf_op jit(solution)/shard_map/ppermute | solution.py:317
  30.4 2.8 %collective-permute-start.5 = (bf16[512,128]{1,0:T(8,128)(2,1)S(1)}, bf16[512,128]{1,0:T(8,128)(2,1)S(1)}, u32[]{:S(2)}, u32[]{:S(2)}) collective-permute-start(bf16[512,128]{1,0:T(8,128)(2,1)S(1)} %get-tuple-element.50.refs_5_.refs_0_), channel_id=1, source_target_pairs={{0,4},{2,6},{4,0},{6,2},{8,12},{10,14},{12,8},{14,10},{16,20},{18,... | collective-permute-start | bytes 393224 | tf_op jit(solution)/shard_map/ppermute | solution.py:317
  33.2 2.7 %collective-permute-start.8 = (bf16[512,128]{1,0:T(8,128)(2,1)S(1)}, bf16[512,128]{1,0:T(8,128)(2,1)S(1)}, u32[]{:S(2)}, u32[]{:S(2)}) collective-permute-start(bf16[512,128]{1,0:T(8,128)(2,1)S(1)} %get-tuple-element.51.refs_2_), channel_id=1, source_target_pairs={{0,24},{2,26},{4,28},{6,30},{8,0},{10,2},{12,4},{14,6},{16,8},{18,... | collective-permute-start | bytes 393224 | tf_op jit(solution)/shard_map/ppermute | solution.py:317
  36.2 0.7 collective-permute-start.6
  36.9 2.2 %probs_part.7 = (bf16[4,384,384]{2,1,0:T(8,128)(2,1)S(1)}, f32[384,512]{1,0:T(8,128)S(1)}) custom-call(s32[1,4]{1,0:T(1,128)S(1)} %copy-done.9, bf16[384,2048]{1,0:T(8,128)(2,1)S(1)} %copy-done.1, bf16[384,512]{1,0:T(8,128)(2,1)S(1)} %copy-done.5, bf16[384,2048]{1,0:T(8,128)(2,1)S(1)} %copy-done.3, ...), custom_call_target="tpu_custom_call", output_to_operand_aliasing={{1}: (4, {})} | custom-call | flops 1000 | bytes 1000 | tf_op jit(solution)/shard_map/probs_part/pallas_call | solution.py:51
  39.1 1.9 %collective-permute-done.8.refs_5_ = bf16[512,128]{1,0:T(8,128)(2,1)S(1)} collective-permute-done((bf16[512,128]{1,0:T(8,128)(2,1)S(1)}, bf16[512,128]{1,0:T(8,128)(2,1)S(1)}, u32[]{:S(2)}, u32[]{:S(2)}) %collective-permute-start.8) | collective-permute-done | bytes 131104 | tf_op jit(solution)/shard_map/ppermute | solution.py:317
  41.1 0.7 collective-permute-done.7.refs_4_
  41.8 3.8 %collective-permute-done.6.refs_3_ = bf16[512,128]{1,0:T(8,128)(2,1)S(1)} collective-permute-done((bf16[512,128]{1,0:T(8,128)(2,1)S(1)}, bf16[512,128]{1,0:T(8,128)(2,1)S(1)}, u32[]{:S(2)}, u32[]{:S(2)}) %collective-permute-start.6) | collective-permute-done | bytes 131104 | tf_op jit(solution)/shard_map/ppermute | solution.py:317
  45.7 0.6 collective-permute-start.9
  47.1 0.8 collective-permute-start.10
  48.0 5.8 %collective-permute-done.12.refs_9_.refs_6_ = bf16[1024,128]{1,0:T(8,128)(2,1)S(1)} collective-permute-done((bf16[1024,128]{1,0:T(8,128)(2,1)S(1)}, bf16[1024,128]{1,0:T(8,128)(2,1)S(1)}, u32[]{:S(2)}, u32[]{:S(2)}) %collective-permute-start.12) | collective-permute-done | bytes 262176 | tf_op jit(solution)/shard_map/ppermute | solution.py:317
  53.8 1.5 %collective-permute-done.11.refs_8_.refs_5_ = bf16[1024,128]{1,0:T(8,128)(2,1)S(1)} collective-permute-done((bf16[1024,128]{1,0:T(8,128)(2,1)S(1)}, bf16[1024,128]{1,0:T(8,128)(2,1)S(1)}, u32[]{:S(2)}, u32[]{:S(2)}) %collective-permute-start.11) | collective-permute-done | bytes 262176 | tf_op jit(solution)/shard_map/ppermute | solution.py:317
  55.3 6.8 %collective-permute-done.10.refs_7_.refs_4_ = bf16[1024,128]{1,0:T(8,128)(2,1)S(1)} collective-permute-done((bf16[1024,128]{1,0:T(8,128)(2,1)S(1)}, bf16[1024,128]{1,0:T(8,128)(2,1)S(1)}, u32[]{:S(2)}, u32[]{:S(2)}) %collective-permute-start.10) | collective-permute-done | bytes 262176 | tf_op jit(solution)/shard_map/ppermute | solution.py:317
  62.2 2.7 %raw_part.1 = (bf16[384,256]{1,0:T(8,128)(2,1)S(1)}, bf16[384,256]{1,0:T(8,128)(2,1)S(1)}, f32[1,256]{1,0:T(1,128)S(1)}) custom-call(s32[5]{0:T(128)S(1)} %stack.23.refs_0_, bf16[384,4096]{1,0:T(8,128)(2,1)S(1)} %get-tuple-element.49.refs_1_, bf16[384,4096]{1,0:T(8,128)(2,1)S(1)} %collective-permute-done.4.refs_6_.refs_2_, ...), custom_call_target="tpu_custom_call" | custom-call | flops 1000 | bytes 1000 | tf_op jit(solution)/shard_map/raw_part/pallas_call | solution.py:51
  64.9 0.6 collective-permute-start.14
  65.5 2.8 %collective-permute-start.15 = (f32[1,256]{1,0:T(1,128)S(1)}, f32[1,256]{1,0:T(1,128)S(1)}, u32[]{:S(2)}, u32[]{:S(2)}) collective-permute-start(f32[1,256]{1,0:T(1,128)S(1)} %get-tuple-element.60.refs_0_), channel_id=1, source_target_pairs={{0,4},{2,6},{4,0},{6,2},{8,12},{10,14},{12,8},{14,10},{16,20},{18,... | collective-permute-start | bytes 3080 | tf_op jit(solution)/shard_map/ppermute | solution.py:317
  68.2 1.1 %split_part.1 = (bf16[2048,256]{1,0:T(8,128)(2,1)S(1)}, bf16[640,256]{1,0:T(8,128)(2,1)S(1)}, bf16[1408,256]{1,0:T(8,128)(2,1)S(1)}, bf16[384,512]{1,0:T(8,128)(2,1)S(1)}) custom-call(s32[5]{0:T(128)S(1)} %stack.23.refs_0_, f32[384,512]{1,0:T(8,128)S(1)} %get-tuple-element.54.refs_3_.refs_1_, f32[1,512]{1,0:T(1,128)S(1)} %bitcast.8, ...), custom_call_target="tpu_custom_call" | custom-call | flops 1000 | bytes 1000 | tf_op jit(solution)/shard_map/split_part/pallas_call | solution.py:51
  69.4 2.5 %collective-permute-start.22 = (bf16[1408,256]{1,0:T(8,128)(2,1)S(1)}, bf16[1408,256]{1,0:T(8,128)(2,1)S(1)}, u32[]{:S(2)}, u32[]{:S(2)}) collective-permute-start(bf16[1408,256]{1,0:T(8,128)(2,1)S(1)} %get-tuple-element.80), channel_id=1, source_target_pairs={{0,5},{1,4},{2,7},{3,6},{4,1},{5,0},{6,3},{7,2},{8,13},{9,12},{10,... | collective-permute-start | bytes 2162696 | tf_op jit(solution)/shard_map/ppermute | solution.py:363
  71.9 1.5 %collective-permute-start.21 = (bf16[640,256]{1,0:T(8,128)(2,1)S(1)}, bf16[640,256]{1,0:T(8,128)(2,1)S(1)}, u32[]{:S(2)}, u32[]{:S(2)}) collective-permute-start(bf16[640,256]{1,0:T(8,128)(2,1)S(1)} %get-tuple-element.79), channel_id=1, source_target_pairs={{0,1},{1,0},{2,3},{3,2},{4,5},{5,4},{6,7},{7,6},{8,9},{9,8},{10,11... | collective-permute-start | bytes 983048 | tf_op jit(solution)/shard_map/ppermute | solution.py:362
  73.4 2.6 %grads_part.4 = (bf16[384,2048]{1,0:T(8,128)(2,1)}, bf16[384,512]{1,0:T(8,128)(2,1)}, f32[8,128]{1,0:T(8,128)S(1)}) custom-call(s32[5]{0:T(128)S(1)} %stack.23.refs_0_, bf16[384,2048]{1,0:T(8,128)(2,1)S(1)} %copy-done.1, bf16[384,512]{1,0:T(8,128)(2,1)S(1)} %copy-done.5, bf16[384,2048]{1,0:T(8,128)(2,1)S(1)} %copy-done.3, ...), custom_call_target="tpu_custom_call" | custom-call | flops 1000 | bytes 1000 | tf_op jit(solution)/shard_map/grads_part/pallas_call | solution.py:51
  76.1 1.8 %collective-permute-start.17 = (f32[1,256]{1,0:T(1,128)S(1)}, f32[1,256]{1,0:T(1,128)S(1)}, u32[]{:S(2)}, u32[]{:S(2)}) collective-permute-start(f32[1,256]{1,0:T(1,128)S(1)} %add.23.refs_9_.refs_0_), channel_id=1, source_target_pairs={{0,16},{2,18},{4,20},{6,22},{8,24},{10,26},{12,28},{14,30},{16,0},... | collective-permute-start | bytes 3080 | tf_op jit(solution)/shard_map/ppermute | solution.py:317
  77.9 2.6 %grads_part.5 = (bf16[384,2048]{1,0:T(8,128)(2,1)}, bf16[384,512]{1,0:T(8,128)(2,1)}, f32[8,128]{1,0:T(8,128)S(1)}) custom-call(s32[5]{0:T(128)S(1)} %stack.23.refs_0_, bf16[384,2048]{1,0:T(8,128)(2,1)S(1)} %copy-done.1, bf16[384,512]{1,0:T(8,128)(2,1)S(1)} %copy-done.5, ...), custom_call_target="tpu_custom_call", output_to_operand_aliasing={{0}: (7, {}), {1}: (8, {})} | custom-call | flops 1000 | bytes 1000 | tf_op jit(solution)/shard_map/grads_part/pallas_call | solution.py:51
  80.6 3.8 %collective-permute-start.20 = (bf16[2048,256]{1,0:T(8,128)(2,1)S(1)}, bf16[2048,256]{1,0:T(8,128)(2,1)S(1)}, u32[]{:S(2)}, u32[]{:S(2)}) collective-permute-start(bf16[2048,256]{1,0:T(8,128)(2,1)S(1)} %get-tuple-element.78.refs_3_), channel_id=1, source_target_pairs={{0,2},{2,0},{4,6},{6,4},{8,10},{10,8},{12,14},{14,12},{16,18},{18,... | collective-permute-start | bytes 3145736 | tf_op jit(solution)/shard_map/ppermute | solution.py:317
  84.4 2.6 %grads_part.6 = (bf16[384,2048]{1,0:T(8,128)(2,1)}, bf16[384,512]{1,0:T(8,128)(2,1)}, f32[8,128]{1,0:T(8,128)S(1)}) custom-call(s32[5]{0:T(128)S(1)} %stack.23.refs_0_, bf16[384,2048]{1,0:T(8,128)(2,1)S(1)} %copy-done.1, bf16[384,512]{1,0:T(8,128)(2,1)S(1)} %copy-done.5, ...), custom_call_target="tpu_custom_call", output_to_operand_aliasing={{0}: (7, {}), {1}: (8, {})} | custom-call | flops 1000 | bytes 1000 | tf_op jit(solution)/shard_map/grads_part/pallas_call | solution.py:51
  87.0 1.0 collective-permute-done.21.refs_0_
  88.1 2.5 %collective-permute-start.23 = (bf16[2048,256]{1,0:T(8,128)(2,1)S(1)}, bf16[2048,256]{1,0:T(8,128)(2,1)S(1)}, u32[]{:S(2)}, u32[]{:S(2)}) collective-permute-start(bf16[2048,256]{1,0:T(8,128)(2,1)S(1)} %join.11.refs_3_.refs_5_), channel_id=1, source_target_pairs={{0,2},{2,0},{4,6},{6,4},{8,10},{10,8},{12,14},{14,12},{16,18},{18,... | collective-permute-start | bytes 3145736 | tf_op jit(solution)/shard_map/ppermute | solution.py:317
  91.1 2.6 %grads_part.7 = (bf16[384,2048]{1,0:T(8,128)(2,1)}, bf16[384,512]{1,0:T(8,128)(2,1)}, f32[8,128]{1,0:T(8,128)S(1)}) custom-call(s32[5]{0:T(128)S(1)} %stack.23.refs_0_, bf16[384,2048]{1,0:T(8,128)(2,1)S(1)} %copy-done.1, bf16[384,512]{1,0:T(8,128)(2,1)S(1)} %copy-done.5, ...), custom_call_target="tpu_custom_call", output_to_operand_aliasing={{0}: (7, {}), {1}: (8, {})} | custom-call | flops 1000 | bytes 1000 | tf_op jit(solution)/shard_map/grads_part/pallas_call | solution.py:51
  94.0 0.8 collective-permute-start.25
  94.8 3.5 %hidden_part.1 = (bf16[384,2048]{1,0:T(8,128)(2,1)}, f32[8,128]{1,0:T(8,128)S(1)}) custom-call(s32[5]{0:T(128)S(1)} %stack.23.refs_0_, bf16[384,512]{1,0:T(8,128)(2,1)S(1)} %get-tuple-element.72.refs_1_, bf16[384,512]{1,0:T(8,128)(2,1)S(1)} %collective-permute-done.18.refs_10_.refs_2_, bf16[2048,256]{1,0:T(8,128)(2,1)S(1)} %get-tuple-element.78.refs_3_, ...), custom_call_target="tpu_custom_call" | custom-call | flops 1000 | bytes 1000 | tf_op jit(solution)/shard_map/hidden_part/pallas_call | solution.py:51
  98.3 2.0 %collective-permute-done.25.refs_1_ = f32[1,256]{1,0:T(1,128)S(1)} collective-permute-done((f32[1,256]{1,0:T(1,128)S(1)}, f32[1,256]{1,0:T(1,128)S(1)}, u32[]{:S(2)}, u32[]{:S(2)}) %collective-permute-start.25) | collective-permute-done | bytes 1056 | tf_op jit(solution)/shard_map/ppermute | solution.py:317
  100.3 2.4 %collective-permute-start.26 = (f32[1,256]{1,0:T(1,128)S(1)}, f32[1,256]{1,0:T(1,128)S(1)}, u32[]{:S(2)}, u32[]{:S(2)}) collective-permute-start(f32[1,256]{1,0:T(1,128)S(1)} %add.27.refs_1_), channel_id=1, source_target_pairs={{0,2},{2,0},{4,6},{6,4},{8,10},{10,8},{12,14},{14,12},{16,18},{18,... | collective-permute-start | bytes 3080 | tf_op jit(solution)/shard_map/ppermute | solution.py:317
  102.7 0.8 collective-permute-done.26.refs_2_
  103.5 1.1 %last.1 = f32[1,512]{1,0:T(1,128)} custom-call(s32[5]{0:T(128)S(1)} %stack.23.refs_0_, f32[1,256]{1,0:T(1,128)S(1)} %add.27.refs_1_, f32[1,256]{1,0:T(1,128)S(1)} %collective-permute-done.26.refs_2_, f32[1,512]{1,0:T(1,128)S(1)} %bitcast.9), custom_call_target="tpu_custom_call" | custom-call | flops 1000 | bytes 1000 | tf_op jit(solution)/shard_map/last/pallas_call | solution.py:51
  (52 shorter events, 2.8 us)
Async XLA Ops:
  0.6 4.4 %collective-permute-start = (bf16[32,512]{1,0:T(8,128)(2,1)}, bf16[32,512]{1,0:T(8,128)(2,1)S(1)}, u32[]{:S(2)}, u32[]{:S(2)}) collective-permute-start(bf16[32,512]{1,0:T(8,128)(2,1)} %refs_1_.9), channel_id=1, source_target_pairs={{0,2},{2,0},{4,6},{6,4},{8,10},{10,8},{12,14},{14,12},{16,18},{18,... | collective-permute-start | bytes 98312 | tf_op jit(solution)/shard_map/ppermute | solution.py:317
  5.0 0.8 copy-start.7
  6.3 11.9 %collective-permute-start.1 = (bf16[64,256]{1,0:T(8,128)(2,1)S(1)}, bf16[64,256]{1,0:T(8,128)(2,1)S(1)}, u32[]{:S(2)}, u32[]{:S(2)}) collective-permute-start(bf16[64,256]{1,0:T(8,128)(2,1)S(1)} %join.6.refs_4_.refs_0_), channel_id=1, source_target_pairs={{0,128},{2,130},{4,132},{6,134},{8,136},{10,138},{12,140},{14,142}... | collective-permute-start | bytes 98312 | tf_op jit(solution)/shard_map/ppermute | solution.py:317
  11.6 1.4 %copy-start = (bf16[384,2048]{1,0:T(8,128)(2,1)S(1)}, bf16[384,2048]{1,0:T(8,128)(2,1)}, u32[]{:S(2)}) copy-start(bf16[384,2048]{1,0:T(8,128)(2,1)} %refs_1_.17) | copy-start | bytes 4718596
  13.0 1.4 %copy-start.2 = (bf16[384,2048]{1,0:T(8,128)(2,1)S(1)}, bf16[384,2048]{1,0:T(8,128)(2,1)}, u32[]{:S(2)}) copy-start(bf16[384,2048]{1,0:T(8,128)(2,1)} %refs_3_.15) | copy-start | bytes 4718596
  14.4 1.0 copy-start.4
  15.4 0.7 copy-start.9
  16.1 3.5 %copy-start.1 = (bf16[384,2048]{1,0:T(8,128)(2,1)S(1)}, bf16[384,2048]{1,0:T(8,128)(2,1)}, u32[]{:S(2)}) copy-start(bf16[384,2048]{1,0:T(8,128)(2,1)} %refs_1_.17) | copy-start | bytes 4718596
  16.1 3.5 %copy-start.3 = (bf16[384,2048]{1,0:T(8,128)(2,1)S(1)}, bf16[384,2048]{1,0:T(8,128)(2,1)}, u32[]{:S(2)}) copy-start(bf16[384,2048]{1,0:T(8,128)(2,1)} %refs_3_.15) | copy-start | bytes 4718596
  18.3 5.2 %collective-permute-start.2 = (bf16[128,256]{1,0:T(8,128)(2,1)S(1)}, bf16[128,256]{1,0:T(8,128)(2,1)S(1)}, u32[]{:S(2)}, u32[]{:S(2)}) collective-permute-start(bf16[128,256]{1,0:T(8,128)(2,1)S(1)} %join.7.refs_5_.refs_0_), channel_id=1, source_target_pairs={{0,64},{2,66},{4,68},{6,70},{8,72},{10,74},{12,76},{14,78},{16,80}... | collective-permute-start | bytes 196616 | tf_op jit(solution)/shard_map/ppermute | solution.py:317
  23.5 3.9 %collective-permute-start.3 = (bf16[256,256]{1,0:T(8,128)(2,1)S(1)}, bf16[256,256]{1,0:T(8,128)(2,1)S(1)}, u32[]{:S(2)}, u32[]{:S(2)}) collective-permute-start(bf16[256,256]{1,0:T(8,128)(2,1)S(1)} %join.8.refs_5_.refs_1_.refs_0_), channel_id=1, source_target_pairs={{0,32},{2,34},{4,36},{6,38},{8,40},{10,42},{12,44},{14,46},{16,48}... | collective-permute-start | bytes 393224 | tf_op jit(solution)/shard_map/ppermute | solution.py:317
  23.6 2.2 %copy-start.6 = (bf16[384,4096]{1,0:T(8,128)(2,1)S(1)}, bf16[384,4096]{1,0:T(8,128)(2,1)}, u32[]{:S(2)}) copy-start(bf16[384,4096]{1,0:T(8,128)(2,1)} %refs_0_.8) | copy-start | bytes 9437188
  27.4 9.5 %copy-start.5 = (bf16[384,512]{1,0:T(8,128)(2,1)S(1)}, bf16[384,512]{1,0:T(8,128)(2,1)}, u32[]{:S(2)}) copy-start(bf16[384,512]{1,0:T(8,128)(2,1)} %refs_2_.15) | copy-start | bytes 1179652
  27.5 18.1 %collective-permute-start.4 = (bf16[384,4096]{1,0:T(8,128)(2,1)S(1)}, bf16[384,4096]{1,0:T(8,128)(2,1)S(1)}, u32[]{:S(2)}, u32[]{:S(2)}) collective-permute-start(bf16[384,4096]{1,0:T(8,128)(2,1)S(1)} %get-tuple-element.49.refs_1_), channel_id=1, source_target_pairs={{0,2},{2,0},{4,6},{6,4},{8,10},{10,8},{12,14},{14,12},{16,18},{18,... | collective-permute-start | bytes 9437192 | tf_op jit(solution)/shard_map/ppermute | solution.py:317
  30.4 8.7 %collective-permute-start.5 = (bf16[512,128]{1,0:T(8,128)(2,1)S(1)}, bf16[512,128]{1,0:T(8,128)(2,1)S(1)}, u32[]{:S(2)}, u32[]{:S(2)}) collective-permute-start(bf16[512,128]{1,0:T(8,128)(2,1)S(1)} %get-tuple-element.50.refs_5_.refs_0_), channel_id=1, source_target_pairs={{0,4},{2,6},{4,0},{6,2},{8,12},{10,14},{12,8},{14,10},{16,20},{18,... | collective-permute-start | bytes 393224 | tf_op jit(solution)/shard_map/ppermute | solution.py:317
  33.2 7.9 %collective-permute-start.8 = (bf16[512,128]{1,0:T(8,128)(2,1)S(1)}, bf16[512,128]{1,0:T(8,128)(2,1)S(1)}, u32[]{:S(2)}, u32[]{:S(2)}) collective-permute-start(bf16[512,128]{1,0:T(8,128)(2,1)S(1)} %get-tuple-element.51.refs_2_), channel_id=1, source_target_pairs={{0,24},{2,26},{4,28},{6,30},{8,0},{10,2},{12,4},{14,6},{16,8},{18,... | collective-permute-start | bytes 393224 | tf_op jit(solution)/shard_map/ppermute | solution.py:317
  35.9 5.9 %collective-permute-start.7 = (bf16[512,128]{1,0:T(8,128)(2,1)S(1)}, bf16[512,128]{1,0:T(8,128)(2,1)S(1)}, u32[]{:S(2)}, u32[]{:S(2)}) collective-permute-start(bf16[512,128]{1,0:T(8,128)(2,1)S(1)} %get-tuple-element.51.refs_2_), channel_id=1, source_target_pairs={{0,16},{2,18},{4,20},{6,22},{8,24},{10,26},{12,28},{14,30},{16,0},... | collective-permute-start | bytes 393224 | tf_op jit(solution)/shard_map/ppermute | solution.py:317
  36.2 9.4 %collective-permute-start.6 = (bf16[512,128]{1,0:T(8,128)(2,1)S(1)}, bf16[512,128]{1,0:T(8,128)(2,1)S(1)}, u32[]{:S(2)}, u32[]{:S(2)}) collective-permute-start(bf16[512,128]{1,0:T(8,128)(2,1)S(1)} %get-tuple-element.51.refs_2_), channel_id=1, source_target_pairs={{0,8},{2,10},{4,12},{6,14},{8,16},{10,18},{12,20},{14,22},{16,24},... | collective-permute-start | bytes 393224 | tf_op jit(solution)/shard_map/ppermute | solution.py:317
  45.6 16.5 %copy-start.8 = (f32[512]{0:T(512)S(1)}, f32[512]{0:T(512)}, u32[]{:S(2)}) copy-start(f32[512]{0:T(512)} %param.11) | copy-start | bytes 6148
  45.7 16.5 %collective-permute-start.9 = (f32[384,512]{1,0:T(8,128)S(1)}, f32[384,512]{1,0:T(8,128)S(1)}, u32[]{:S(2)}, u32[]{:S(2)}) collective-permute-start(f32[384,512]{1,0:T(8,128)S(1)} %get-tuple-element.54.refs_3_.refs_1_), channel_id=1, source_target_pairs={{0,2},{2,0},{4,6},{6,4},{8,10},{10,8},{12,14},{14,12},{16,18},{18,... | collective-permute-start | bytes 2359304 | tf_op jit(solution)/shard_map/ppermute | solution.py:317
  46.3 15.9 %collective-permute-start.13 = (bf16[2048,128]{1,0:T(8,128)(2,1)S(1)}, bf16[2048,128]{1,0:T(8,128)(2,1)S(1)}, u32[]{:S(2)}, u32[]{:S(2)}) collective-permute-start(bf16[2048,128]{1,0:T(8,128)(2,1)S(1)} %get-tuple-element.56.refs_10_.refs_7_), channel_id=1, source_target_pairs={{0,4},{2,6},{4,0},{6,2},{8,12},{10,14},{12,8},{14,10},{16,20},{18,... | collective-permute-start | bytes 1572872 | tf_op jit(solution)/shard_map/ppermute | solution.py:317
  46.5 7.3 %collective-permute-start.12 = (bf16[1024,128]{1,0:T(8,128)(2,1)S(1)}, bf16[1024,128]{1,0:T(8,128)(2,1)S(1)}, u32[]{:S(2)}, u32[]{:S(2)}) collective-permute-start(bf16[1024,128]{1,0:T(8,128)(2,1)S(1)} %get-tuple-element.55.refs_6_.refs_3_), channel_id=1, source_target_pairs={{0,24},{2,26},{4,28},{6,30},{8,0},{10,2},{12,4},{14,6},{16,8},{18,... | collective-permute-start | bytes 786440 | tf_op jit(solution)/shard_map/ppermute | solution.py:317
  46.8 8.5 %collective-permute-start.11 = (bf16[1024,128]{1,0:T(8,128)(2,1)S(1)}, bf16[1024,128]{1,0:T(8,128)(2,1)S(1)}, u32[]{:S(2)}, u32[]{:S(2)}) collective-permute-start(bf16[1024,128]{1,0:T(8,128)(2,1)S(1)} %get-tuple-element.55.refs_6_.refs_3_), channel_id=1, source_target_pairs={{0,16},{2,18},{4,20},{6,22},{8,24},{10,26},{12,28},{14,30},{16,0},... | collective-permute-start | bytes 786440 | tf_op jit(solution)/shard_map/ppermute | solution.py:317
  47.1 15.0 %collective-permute-start.10 = (bf16[1024,128]{1,0:T(8,128)(2,1)S(1)}, bf16[1024,128]{1,0:T(8,128)(2,1)S(1)}, u32[]{:S(2)}, u32[]{:S(2)}) collective-permute-start(bf16[1024,128]{1,0:T(8,128)(2,1)S(1)} %get-tuple-element.55.refs_6_.refs_3_), channel_id=1, source_target_pairs={{0,8},{2,10},{4,12},{6,14},{8,16},{10,18},{12,20},{14,22},{16,24},... | collective-permute-start | bytes 786440 | tf_op jit(solution)/shard_map/ppermute | solution.py:317
  64.9 3.3 %collective-permute-start.14 = (bf16[384,256]{1,0:T(8,128)(2,1)S(1)}, bf16[384,256]{1,0:T(8,128)(2,1)S(1)}, u32[]{:S(2)}, u32[]{:S(2)}) collective-permute-start(bf16[384,256]{1,0:T(8,128)(2,1)S(1)} %get-tuple-element.58), channel_id=1, source_target_pairs={{0,2},{2,0},{4,6},{6,4},{8,10},{10,8},{12,14},{14,12},{16,18},{18,... | collective-permute-start | bytes 589832 | tf_op jit(solution)/shard_map/ppermute | solution.py:317
  65.5 3.9 %collective-permute-start.15 = (f32[1,256]{1,0:T(1,128)S(1)}, f32[1,256]{1,0:T(1,128)S(1)}, u32[]{:S(2)}, u32[]{:S(2)}) collective-permute-start(f32[1,256]{1,0:T(1,128)S(1)} %get-tuple-element.60.refs_0_), channel_id=1, source_target_pairs={{0,4},{2,6},{4,0},{6,2},{8,12},{10,14},{12,8},{14,10},{16,20},{18,... | collective-permute-start | bytes 3080 | tf_op jit(solution)/shard_map/ppermute | solution.py:317
  69.4 18.6 %collective-permute-start.22 = (bf16[1408,256]{1,0:T(8,128)(2,1)S(1)}, bf16[1408,256]{1,0:T(8,128)(2,1)S(1)}, u32[]{:S(2)}, u32[]{:S(2)}) collective-permute-start(bf16[1408,256]{1,0:T(8,128)(2,1)S(1)} %get-tuple-element.80), channel_id=1, source_target_pairs={{0,5},{1,4},{2,7},{3,6},{4,1},{5,0},{6,3},{7,2},{8,13},{9,12},{10,... | collective-permute-start | bytes 2162696 | tf_op jit(solution)/shard_map/ppermute | solution.py:363
  71.9 12.5 %collective-permute-start.18 = (bf16[384,512]{1,0:T(8,128)(2,1)S(1)}, bf16[384,512]{1,0:T(8,128)(2,1)S(1)}, u32[]{:S(2)}, u32[]{:S(2)}) collective-permute-start(bf16[384,512]{1,0:T(8,128)(2,1)S(1)} %get-tuple-element.72.refs_1_), channel_id=1, source_target_pairs={{0,1},{1,0},{2,3},{3,2},{4,5},{5,4},{6,7},{7,6},{8,9},{9,8},{10,11... | collective-permute-start | bytes 1179656 | tf_op jit(solution)/shard_map/ppermute | solution.py:361
  71.9 16.1 %collective-permute-start.21 = (bf16[640,256]{1,0:T(8,128)(2,1)S(1)}, bf16[640,256]{1,0:T(8,128)(2,1)S(1)}, u32[]{:S(2)}, u32[]{:S(2)}) collective-permute-start(bf16[640,256]{1,0:T(8,128)(2,1)S(1)} %get-tuple-element.79), channel_id=1, source_target_pairs={{0,1},{1,0},{2,3},{3,2},{4,5},{5,4},{6,7},{7,6},{8,9},{9,8},{10,11... | collective-permute-start | bytes 983048 | tf_op jit(solution)/shard_map/ppermute | solution.py:362
  73.4 2.7 %collective-permute-start.16 = (f32[1,256]{1,0:T(1,128)S(1)}, f32[1,256]{1,0:T(1,128)S(1)}, u32[]{:S(2)}, u32[]{:S(2)}) collective-permute-start(f32[1,256]{1,0:T(1,128)S(1)} %get-tuple-element.65.refs_7_.refs_0_), channel_id=1, source_target_pairs={{0,8},{2,10},{4,12},{6,14},{8,0},{10,2},{12,4},{14,6},{16,24},{18,... | collective-permute-start | bytes 3080 | tf_op jit(solution)/shard_map/ppermute | solution.py:317
  76.1 4.4 %collective-permute-start.17 = (f32[1,256]{1,0:T(1,128)S(1)}, f32[1,256]{1,0:T(1,128)S(1)}, u32[]{:S(2)}, u32[]{:S(2)}) collective-permute-start(f32[1,256]{1,0:T(1,128)S(1)} %add.23.refs_9_.refs_0_), channel_id=1, source_target_pairs={{0,16},{2,18},{4,20},{6,22},{8,24},{10,26},{12,28},{14,30},{16,0},... | collective-permute-start | bytes 3080 | tf_op jit(solution)/shard_map/ppermute | solution.py:317
  80.5 6.5 %collective-permute-start.19 = (f32[1,256]{1,0:T(1,128)S(1)}, f32[1,256]{1,0:T(1,128)S(1)}, u32[]{:S(2)}, u32[]{:S(2)}) collective-permute-start(f32[1,256]{1,0:T(1,128)S(1)} %add.24.refs_9_.refs_0_), channel_id=1, source_target_pairs={{0,32},{2,34},{4,36},{6,38},{8,40},{10,42},{12,44},{14,46},{16,48}... | collective-permute-start | bytes 3080 | tf_op jit(solution)/shard_map/ppermute | solution.py:317
  80.6 14.2 %collective-permute-start.20 = (bf16[2048,256]{1,0:T(8,128)(2,1)S(1)}, bf16[2048,256]{1,0:T(8,128)(2,1)S(1)}, u32[]{:S(2)}, u32[]{:S(2)}) collective-permute-start(bf16[2048,256]{1,0:T(8,128)(2,1)S(1)} %get-tuple-element.78.refs_3_), channel_id=1, source_target_pairs={{0,2},{2,0},{4,6},{6,4},{8,10},{10,8},{12,14},{14,12},{16,18},{18,... | collective-permute-start | bytes 3145736 | tf_op jit(solution)/shard_map/ppermute | solution.py:317
  88.1 6.7 %collective-permute-start.23 = (bf16[2048,256]{1,0:T(8,128)(2,1)S(1)}, bf16[2048,256]{1,0:T(8,128)(2,1)S(1)}, u32[]{:S(2)}, u32[]{:S(2)}) collective-permute-start(bf16[2048,256]{1,0:T(8,128)(2,1)S(1)} %join.11.refs_3_.refs_5_), channel_id=1, source_target_pairs={{0,2},{2,0},{4,6},{6,4},{8,10},{10,8},{12,14},{14,12},{16,18},{18,... | collective-permute-start | bytes 3145736 | tf_op jit(solution)/shard_map/ppermute | solution.py:317
  90.6 3.3 %collective-permute-start.24 = (f32[1,256]{1,0:T(1,128)S(1)}, f32[1,256]{1,0:T(1,128)S(1)}, u32[]{:S(2)}, u32[]{:S(2)}) collective-permute-start(f32[1,256]{1,0:T(1,128)S(1)} %add.25.refs_9_.refs_2_.refs_0_), channel_id=1, source_target_pairs={{0,64},{2,66},{4,68},{6,70},{8,72},{10,74},{12,76},{14,78},{16,80}... | collective-permute-start | bytes 3080 | tf_op jit(solution)/shard_map/ppermute | solution.py:317
  94.0 6.3 %collective-permute-start.25 = (f32[1,256]{1,0:T(1,128)S(1)}, f32[1,256]{1,0:T(1,128)S(1)}, u32[]{:S(2)}, u32[]{:S(2)}) collective-permute-start(f32[1,256]{1,0:T(1,128)S(1)} %add.26.refs_7_.refs_0_), channel_id=1, source_target_pairs={{0,128},{2,130},{4,132},{6,134},{8,136},{10,138},{12,140},{14,142}... | collective-permute-start | bytes 3080 | tf_op jit(solution)/shard_map/ppermute | solution.py:317
  100.3 3.2 %collective-permute-start.26 = (f32[1,256]{1,0:T(1,128)S(1)}, f32[1,256]{1,0:T(1,128)S(1)}, u32[]{:S(2)}, u32[]{:S(2)}) collective-permute-start(f32[1,256]{1,0:T(1,128)S(1)} %add.27.refs_1_), channel_id=1, source_target_pairs={{0,2},{2,0},{4,6},{6,4},{8,10},{10,8},{12,14},{14,12},{16,18},{18,... | collective-permute-start | bytes 3080 | tf_op jit(solution)/shard_map/ppermute | solution.py:317

commit v4 on v3

--- a/solution.py
+++ b/solution.py
@@ -26,12 +26,14 @@
 VMEM = pl.BlockSpec(memory_space=pltpu.VMEM)
 SMEM = pl.BlockSpec(memory_space=pltpu.SMEM)
 ANY = pl.BlockSpec(memory_space=pl.ANY)
+HBM = pl.BlockSpec(memory_space=pltpu.HBM)
 TOKEN = jax.ShapeDtypeStruct((8, 128), F32)
 WIDE = GROUP * HEAD
 
 
 def call(kernel, name, out_shape, ins, after=(), through=(), **kw):
     specs, args = zip(*ins)
+    args = tuple(pltpu.with_memory_space_constraint(a, pltpu.HBM) if spec is HBM else a for spec, a in ins)
     n_in = len(args) + len(after)
     single = not isinstance(out_shape, (list, tuple))
     outs = [out_shape] if single else list(out_shape)
@@ -64,13 +66,13 @@
     return jax.ShapeDtypeStruct(dims, dtype)
 
 
-def probs_kernel(lengths_ref, q_ref, k_ref, up_ref, p_ref, dv_ref, bias_ref, s_ref, dv_acc):
+def probs_kernel(at_ref, q_ref, k_ref, up_ref, p_ref, dv_ref, bias_ref, s_ref, dv_acc):
     rows = lax.broadcasted_iota(jnp.int32, (COUNT, COUNT), 0)
     cols = lax.broadcasted_iota(jnp.int32, (COUNT, COUNT), 1)
     start = jnp.zeros((COUNT, COUNT), jnp.int32)
     end = jnp.int32(0)
     for doc in range(3):
-        end = end + lengths_ref[0, doc]
+        end = end + at_ref[5 + doc]
         start = jnp.where(rows >= end, end, start)
     bias_ref[...] = jnp.where((cols <= rows) & (cols >= start), 0.0, -1e30).astype(F32)
     dv_acc[...] = jnp.zeros_like(dv_acc)
@@ -90,22 +92,38 @@
     dv_ref[...] = dv_acc[...].T
 
 
-def probs_part(g, lengths, queries, keys, upstream, dv, after):
+PROBS_SCRATCH = [pltpu.VMEM((COUNT, COUNT), F32), pltpu.VMEM((GROUP * BLOCK, COUNT), F32), pltpu.VMEM((HEAD, COUNT), F32)]
+
+
+def first_probs_kernel(at_ref, q_hbm, k_hbm, up_hbm, p_ref, dv_ref, q_ref, k_ref, up_ref, sems, *scratch):
+    copies = [
+        pltpu.make_async_copy(a.at[:, pl.ds(0, b.shape[1])], b, sems.at[j])
+        for j, (a, b) in enumerate(((q_hbm, q_ref), (k_hbm, k_ref), (up_hbm, up_ref)))
+    ]
+    for copy in copies:
+        copy.start()
+    for copy in copies:
+        copy.wait()
+    probs_kernel(at_ref, q_ref, k_ref, up_ref, p_ref, dv_ref, *scratch)
+
+
+def probs_part(g, at, queries, keys, upstream, dv, after):
     wide = pl.BlockSpec((COUNT, WIDE), lambda i: (0, g))
     narrow = pl.BlockSpec((COUNT, HEAD), lambda i: (0, g))
-    ins = [(SMEM, lengths), (wide, queries), (narrow, keys), (wide, upstream)]
+    outs = [shape(GROUP, COUNT, COUNT), shape(COUNT, 4 * HEAD, dtype=F32)]
+    if g == 0:
+        blocks = [pltpu.VMEM((COUNT, WIDE), BF16), pltpu.VMEM((COUNT, HEAD), BF16), pltpu.VMEM((COUNT, WIDE), BF16)]
+        return call(
+            first_probs_kernel, "probs_part", outs, [(SMEM, at), (HBM, queries), (HBM, keys), (HBM, upstream)], after,
+            out_specs=[VMEM, narrow], grid=(1,), scratch_shapes=blocks + [pltpu.SemaphoreType.DMA((3,))] + PROBS_SCRATCH,
+        )
 
     def kernel(*refs):
-        probs_kernel(*refs[:4], *refs[len(refs) - 5 :])
-
-    extra = {}
-    if dv is not None:
-        ins.append((ANY, dv))
-        extra["input_output_aliases"] = {4: 1}
+        probs_kernel(*refs[:4], *refs[5:])
+
     return call(
-        kernel, "probs_part", [shape(GROUP, COUNT, COUNT), shape(COUNT, 4 * HEAD, dtype=F32)], ins, after,
-        out_specs=[VMEM, narrow], grid=(1,),
-        scratch_shapes=[pltpu.VMEM((COUNT, COUNT), F32), pltpu.VMEM((GROUP * BLOCK, COUNT), F32), pltpu.VMEM((HEAD, COUNT), F32)], **extra,
+        kernel, "probs_part", outs, [(SMEM, at), (wide, queries), (narrow, keys), (wide, upstream), (ANY, dv)], after,
+        out_specs=[VMEM, narrow], grid=(1,), scratch_shapes=PROBS_SCRATCH, input_output_aliases={4: 1},
     )
 
 
@@ -164,10 +182,14 @@
     return pl.ds(pl.multiple_of(at_ref[3] * HALF, HALF), HALF)
 
 
-def first_join(at_ref, own_ref, other_ref, out_ref):
+def first_join(at_ref, own_hbm, other_ref, out_ref, sem):
     c, cols = at_ref[3], own_columns(at_ref)
-    out_ref[pl.ds(pl.multiple_of(c * SHARD, SHARD), SHARD), :] = own_ref[:, cols]
+    copy = pltpu.make_async_copy(
+        own_hbm.at[:, cols], out_ref.at[pl.ds(pl.multiple_of(c * SHARD, SHARD), SHARD), :], sem
+    )
+    copy.start()
     out_ref[pl.ds(pl.multiple_of((1 - c) * SHARD, SHARD), SHARD), :] = other_ref[:, cols]
+    copy.wait()
 
 
 def copy_kernel(in_ref, out_ref, sem):
@@ -182,38 +204,47 @@
     out_ref[n:, :] = other_ref[...]
 
 
-def join_split_kernel(own_ref, other_ref, first_ref, second_ref):
+def core_join_kernel(at_ref, own_ref, got1, got2, got3, first_ref, second_ref):
     n = own_ref.shape[0]
-    for j, out_ref in enumerate((first_ref, second_ref)):
-        out_ref[:n, :] = own_ref[:, HEAD * j : HEAD * (j + 1)]
-        out_ref[n:, :] = other_ref[:, HEAD * j : HEAD * (j + 1)]
-
-
-def two_joins_kernel(a0, a1, b0, b1, b2, b3, first_ref, second_ref):
-    n = a0.shape[0]
-    for j, part in enumerate((a0, a1)):
-        first_ref[n * j : n * (j + 1), :] = part[...]
-    for j, part in enumerate((b0, b1, b2, b3)):
-        second_ref[n * j : n * (j + 1), :] = part[...]
+    first_ref[:n, :] = own_ref[...]
+    first_ref[n:, :] = got1[...]
+
+    @pl.when(at_ref[3] == 0)
+    def _():
+        second_ref[:n, :] = own_ref[...]
+        second_ref[n:, :] = got1[...]
+
+    @pl.when(at_ref[3] == 1)
+    def _():
+        second_ref[:n, :] = got2[...]
+        second_ref[n:, :] = got3[...]
 
 
 def put_in_order(at_ref, pieces, codes_ref):
-    z, y, x = at_ref[0], at_ref[1], at_ref[2]
-
-    def place(piece, row, zi, k, xi, col):
-        to = ((z ^ Z_ORDER[zi]) * 4 + ((y + 4 - k) & 3)) * 2 + (x ^ xi)
-        rows = pl.ds(pl.multiple_of(to * CHIP, CHIP), CHIP)
-        codes_ref[rows, pl.ds(col, HEAD)] = piece[pl.ds(row, CHIP), :]
-
-    for k in range(4):
-        for xi in range(2):
-            for zi in range(8):
-                place(pieces[k], (xi * 8 + zi) * CHIP, zi, k, xi, 0)
-                place(pieces[4 + xi], (k * 8 + zi) * CHIP, zi, k, xi, HEAD)
+    z, y, x, c = at_ref[0], at_ref[1], at_ref[2], at_ref[3]
+    first, second, got1, got2, got3 = pieces
+
+    def place(piece, half, k, xi):
+        for zi in range(8):
+            to = ((z ^ Z_ORDER[zi]) * 4 + ((y + 4 - k) & 3)) * 2 + (x ^ xi)
+            rows = pl.ds(pl.multiple_of(to * CHIP, CHIP), CHIP)
+            codes_ref[rows, :] = piece[pl.ds((half * 8 + zi) * CHIP, CHIP), :]
+
+    @pl.when(c == 0)
+    def _():
+        for k, piece in enumerate((first, got1, got2, got3)):
+            for xi in range(2):
+                place(piece, xi, k, xi)
+
+    @pl.when(c == 1)
+    def _():
+        for j, piece in enumerate((first, second, got1, got2)):
+            for half in range(2):
+                place(piece, half, 2 * (j % 2) + half, j // 2)
 
 
 def raw_kernel(at_ref, own_ref, other_ref, dv_own, dv_other, scale_ref, *refs):
-    pieces, (mine_ref, theirs_ref, sums_ref, codes_ref) = refs[:6], refs[6:]
+    pieces, (mine_ref, theirs_ref, sums_ref, codes_ref) = refs[:5], refs[5:]
     put_in_order(at_ref, pieces, codes_ref)
     cols = own_columns(at_ref)
     scale = scale_ref[:, cols]
@@ -234,37 +265,51 @@
 
 
 NEAR = 640
+BESIDES = DEPTH // 2 - NEAR
 
 
 def split_kernel(at_ref, dv_ref, scale_ref, *refs):
-    pieces, (kept_ref, near_ref, beside_ref, scaled_ref, codes_ref) = refs[:6], refs[6:]
+    pieces, (kept_ref, near_ref, beside_ref, codes_ref) = refs[:5], refs[5:]
     put_in_order(at_ref, pieces, codes_ref)
     s, half = at_ref[4], DEPTH // 2
     kept_ref[...] = codes_ref[pl.ds(pl.multiple_of(s * half, half), half), :]
     base = (1 - s) * half
-    near_ref[...] = codes_ref[pl.ds(pl.multiple_of(base, half), NEAR), :]
-    beside_ref[...] = codes_ref[pl.ds(pl.multiple_of(base + NEAR, 128), half - NEAR), :]
-    scaled_ref[...] = (dv_ref[...] * scale_ref[...]).astype(BF16)
+    for j in range(2):
+        cols = pl.ds(j * HALF, HALF)
+        near_ref[pl.ds(j * COUNT, COUNT), :] = (dv_ref[:, cols] * scale_ref[:, cols]).astype(BF16)
+    near_ref[2 * COUNT :, :] = codes_ref[pl.ds(pl.multiple_of(base, half), NEAR), :]
+    beside_ref[...] = codes_ref[pl.ds(pl.multiple_of(base + NEAR, 128), BESIDES), :]
 
 
 def split_part(at, dv, scale, pieces, after):
     return call(
-        split_kernel, "split_part", [shape(DEPTH // 2, HALF), shape(NEAR, HALF), shape(DEPTH // 2 - NEAR, HALF), shape(COUNT, 2 * HALF)],
+        split_kernel, "split_part", [shape(DEPTH // 2, HALF), shape(2 * COUNT + NEAR, HALF), shape(BESIDES, HALF)],
         [(SMEM, at), (VMEM, dv), (VMEM, scale)] + [(VMEM, p) for p in pieces], after,
         scratch_shapes=[pltpu.VMEM((DEPTH, HALF), BF16)],
     )
 
 
+def codes_join_kernel(kept_ref, near_ref, beside_ref, out_ref):
+    half = DEPTH // 2
+    out_ref[:half, :] = kept_ref[...]
+    out_ref[half : half + NEAR, :] = near_ref[2 * COUNT :, :]
+    out_ref[half + NEAR :, :] = beside_ref[...]
+
+
 BATCH = 512
 
 
-def hidden_kernel(at_ref, own_ref, other_ref, kept_ref, kept_far, near_ref, near_far, out_ref, token_ref):
-    mine = own_columns(at_ref)
-    rest = pl.ds(pl.multiple_of((1 - at_ref[3]) * HALF, HALF), HALF)
-    terms = ((own_ref, mine, kept_ref), (own_ref, rest, kept_far), (other_ref, mine, near_ref), (other_ref, rest, near_far))
+def hidden_kernel(at_ref, dv_ref, scale_ref, near_ref, codes_ref, far_ref, out_ref, token_ref):
+    c = at_ref[3]
+    terms = []
+    for other, ref in enumerate((codes_ref, far_ref)):
+        cols = pl.ds(pl.multiple_of((c ^ other) * HALF, HALF), HALF)
+        own = (dv_ref[:, cols] * scale_ref[:, cols]).astype(BF16)
+        rows = pl.ds(pl.multiple_of((c ^ other) * COUNT, COUNT), COUNT)
+        terms += [(own, ref, 0), (near_ref[rows, :], ref, DEPTH // 2)]
     for i in range(0, DEPTH // 2, BATCH):
-        rows = pl.ds(i, BATCH)
-        out_ref[:, rows] = sum(dot(a[:, cols], b[rows, :], (1, 1)) for a, cols, b in terms).astype(BF16)
+        total = sum(dot(a, b[pl.ds(base + i, BATCH), :], (1, 1)) for a, b, base in terms)
+        out_ref[:, pl.ds(i, BATCH)] = total.astype(BF16)
     token_ref[...] = jnp.zeros_like(token_ref)
 
 
@@ -307,6 +352,10 @@
     return pairs(lambda z, y, x, c: (z, y ^ bit, x, c))
 
 
+def core_pairs(move0, move1):
+    return [move for c, moves in enumerate((move0, move1)) for move in moves if move[0] % 2 == c]
+
+
 X_SWAP = pairs(lambda z, y, x, c: (z, y, x ^ 1, c))
 C_SWAP = pairs(lambda z, y, x, c: (z, y, x, c ^ 1))
 SEQ_SWAP = [(0, 1), (1, 0)]
@@ -319,14 +368,18 @@
 
 def shards(hidden, queries, keys, value_codes, value_scale, upstream, lengths):
     me, s = lax.axis_index("dp"), lax.axis_index("seq")
-    at = jnp.stack([me // 16, me // 4 % 4, me // 2 % 2, me % 2, s]).astype(jnp.int32)
+    place = jnp.stack([me // 16, me // 4 % 4, me // 2 % 2, me % 2, s]).astype(jnp.int32)
+    at = jnp.concatenate([place, lengths[0, :3]])
     scale = value_scale.reshape(1, -1)
 
-    rows = call(first_join, "join", shape(CHIP, HALF), [(SMEM, at), (VMEM, value_codes), (VMEM, send(value_codes, C_SWAP))])
+    rows = call(
+        first_join, "join", shape(CHIP, HALF), [(SMEM, at), (HBM, value_codes), (VMEM, send(value_codes, C_SWAP))],
+        scratch_shapes=[pltpu.SemaphoreType.DMA],
+    )
     probs, dv = [], None
     for g, bit in enumerate((4, 2, 1)):
         got = send(rows, z_swap(bit))
-        p, dv = probs_part(g, lengths, queries, keys, upstream, dv, (rows,))
+        p, dv = probs_part(g, at, queries, keys, upstream, dv, (rows,))
         probs.append(p)
         n = rows.shape[0]
         ins = [(VMEM, rows), (VMEM, got)]
@@ -337,42 +390,43 @@
                 copy_kernel, "copy", shape(*hidden.shape), [(ANY, hidden)], (rows,),
                 out_specs=[ANY], scratch_shapes=[pltpu.SemaphoreType.DMA],
             )
-            first, second, hidden = call(join_split_kernel, "join", [shape(2 * n, HEAD)] * 2, ins, (p,), (hidden,))
-    first_x = send(first, X_SWAP)
-    second_y = [send(second, y_shift(k)) for k in (1, 2, 3)]
+            rows, hidden = call(join_kernel, "join", shape(2 * n, HALF), ins, (p,), (hidden,))
+    got = [send(rows, core_pairs(X_SWAP if k == 1 else [], y_shift(k))) for k in (1, 2, 3)]
     hidden_other = send(hidden, C_SWAP)
-    p, dv = probs_part(3, lengths, queries, keys, upstream, dv, (first,))
+    p, dv = probs_part(3, at, queries, keys, upstream, dv, (rows,))
     probs.append(p)
-    n = first.shape[0]
+    n = rows.shape[0]
     first, second, dv = call(
-        two_joins_kernel, "join", [shape(2 * n, HEAD), shape(4 * n, HEAD)],
-        [(VMEM, a) for a in [first, first_x, second] + second_y], (hidden_other,), (dv,),
-    )
-    pieces = [first] + [send(first, y_shift(k)) for k in (1, 2, 3)] + [second, send(second, X_SWAP)]
+        core_join_kernel, "join", [shape(2 * n, HALF)] * 2,
+        [(SMEM, at)] + [(VMEM, a) for a in [rows] + got], (hidden_other, p), (dv,),
+    )
+    pieces = [first, second]
+    for k, rows in enumerate((first, second, first), 1):
+        pieces.append(send(rows, core_pairs(y_shift(k), X_SWAP if k < 3 else [])))
     mine, theirs, sums = raw_part(at, hidden, hidden_other, dv, send(dv, C_SWAP), scale, pieces)
 
     got = send(sums, X_SWAP)
     values_far = send(theirs, C_SWAP)
-    kept, near, beside, scaled = split_part(at, dv, scale, pieces, (values_far,))
-    sums, kept, near, beside, scaled = call(
-        add_kernel, "add", shape(1, HALF, dtype=F32), [(VMEM, sums), (VMEM, got)], (), (kept, near, beside, scaled)
-    )
-    kept_far = send(kept, C_SWAP)
-    scaled_other = lax.ppermute(scaled, "seq", SEQ_SWAP)
+    kept, near, beside = split_part(at, dv, scale, pieces, (values_far,))
+    sums, near, beside = call(
+        add_kernel, "add", shape(1, HALF, dtype=F32), [(VMEM, sums), (VMEM, got)], (kept,), (near, beside)
+    )
     near = lax.ppermute(near, "seq", SEQ_SWAP)
     beside = lax.ppermute(beside, ("dp", "seq"), BESIDE)
     held = None
     for g, perm in enumerate((y_swap(1), y_swap(2), z_swap(1), z_swap(2))):
         got = send(sums, perm)
-        *held, token = grads_part(g, at, queries, keys, upstream, mine, values_far, probs[g], held, (sums, scaled_other) if g == 2 else (sums,))
+        *held, token = grads_part(g, at, queries, keys, upstream, mine, values_far, probs[g], held, (sums,))
         after = (token,)
         if g == 3:
-            near = call(join_kernel, "join", shape(DEPTH // 2, HALF), [(VMEM, near), (VMEM, beside)], (sums,))
-            near_far = send(near, C_SWAP)
-            after += (near,)
+            codes = call(
+                codes_join_kernel, "join", shape(DEPTH, HALF), [(VMEM, kept), (VMEM, near), (VMEM, beside)], (sums,)
+            )
+            codes_far = send(codes, C_SWAP)
+            after += (codes,)
         sums = call(add_kernel, "add", shape(1, HALF, dtype=F32), [(VMEM, sums), (VMEM, got)], after)
     got = send(sums, z_swap(4))
-    grad_hidden, token = hidden_part(at, scaled, scaled_other, kept, kept_far, near, near_far, after=(sums,))
+    grad_hidden, token = hidden_part(at, dv, scale, near, codes, codes_far, after=(sums,))
     sums = call(add_kernel, "add", shape(1, HALF, dtype=F32), [(VMEM, sums), (VMEM, got)], (token,))
     last = call(
         last_kernel, "last", shape(1, 2 * HALF, dtype=F32),

time: 105 us -> 103 us (0.981)
  local copies, waits for them, and re-layouts: 5.33 us -> 0.77 us
  Pallas kernels: 28.7 us -> 31 us
    ppermute x24 -> x21, waiting for transfers between devices: 28 us -> 22.5 us  [send(): return lax.ppermute(x, 'dp', perm)]
    unnamed x20 -> x10, local copies, waits for them, and re-layouts: 5.24 us -> 0.03 us
    ppermute x1, waiting for transfers between devices: 1.02 us -> 3.71 us  [shards(): near = lax.ppermute(near, 'seq', SEQ_SWAP)]
    pallas_call x25, Pallas kernels: 28.7 us -> 31 us  [call(): pl.pallas_call(run, in_specs=list(specs) + [ANY] * (len(after) + len(thro...]
    ppermute x1, waiting for transfers between devices: 0.01 us -> 2.14 us  [shards(): beside = lax.ppermute(beside, ('dp', 'seq'), BESIDE)]
    ppermute x24 -> x21, starting transfers between devices: 36.8 us -> 38.6 us  [send(): return lax.ppermute(x, 'dp', perm)]
  transfers between devices with their start and end apart: 27 -> 23, of which waited for: 14 -> 14; matrix products, arithmetic and copies ran while one was open for 0% -> 1% of each run, Pallas kernels for 23% -> 24%
where the time goes in v4:
time: 103 us
  starting transfers between devices  41.7 us (40%)
  Pallas kernels  31 us (30%)
  waiting for transfers between devices  28.4 us (28%)
    ppermute x21, starting transfers between devices, send(): return lax.ppermute(x, 'dp', perm)  38.6 us
    pallas_call x25, Pallas kernels, call(): pl.pallas_call(run, in_specs=list(specs) + [ANY] * (len(after) + len(thro...  31 us
    ppermute x21, waiting for transfers between devices, send(): return lax.ppermute(x, 'dp', perm)  22.5 us
    ppermute x1, waiting for transfers between devices, shards(): near = lax.ppermute(near, 'seq', SEQ_SWAP)  3.71 us
    ppermute x1, waiting for transfers between devices, shards(): beside = lax.ppermute(beside, ('dp', 'seq'), BESIDE)  2.14 us
  transfers between devices with their start and end apart: 23, of which 14 were waited for; matrix products, arithmetic and copies ran while one was open for 1% of the time, Pallas kernels for 24%

profile of v4, /device:TPU:1, one launch (start us, length us, event | category | flops | bytes accessed | tf_op | source)
XLA Modules:
  0.0 102.7 jit_solution(9657539250934840021)
XLA Ops:
  0.6 3.3 %collective-permute-start = (bf16[32,512]{1,0:T(8,128)(2,1)}, bf16[32,512]{1,0:T(8,128)(2,1)S(1)}, u32[]{:S(2)}, u32[]{:S(2)}) collective-permute-start(bf16[32,512]{1,0:T(8,128)(2,1)} %refs_1_.9), channel_id=1, source_target_pairs={{0,2},{2,0},{4,6},{6,4},{8,10},{10,8},{12,14},{14,12},{16,18},{18,... | collective-permute-start | bytes 98312 | tf_op jit(solution)/shard_map/ppermute | solution.py:366
  4.0 0.7 slice_bitcast_fusion
  4.7 0.3 collective-permute-done.refs_2_
  5.0 1.3 %join.6.refs_4_.refs_0_ = bf16[64,256]{1,0:T(8,128)(2,1)S(1)} custom-call(s32[8]{0:T(128)S(1)} %concatenate.3.refs_0_, bf16[32,512]{1,0:T(8,128)(2,1)} %refs_1_.9, bf16[32,512]{1,0:T(8,128)(2,1)S(1)} %collective-permute-done.refs_2_), custom_call_target="tpu_custom_call" | custom-call | flops 1000 | bytes 1000 | tf_op jit(solution)/shard_map/join/pallas_call | solution.py:53
  6.3 5.3 %collective-permute-start.1 = (bf16[64,256]{1,0:T(8,128)(2,1)S(1)}, bf16[64,256]{1,0:T(8,128)(2,1)S(1)}, u32[]{:S(2)}, u32[]{:S(2)}) collective-permute-start(bf16[64,256]{1,0:T(8,128)(2,1)S(1)} %join.6.refs_4_.refs_0_), channel_id=1, source_target_pairs={{0,128},{2,130},{4,132},{6,134},{8,136},{10,138},{12,140},{14,142}... | collective-permute-start | bytes 98312 | tf_op jit(solution)/shard_map/ppermute | solution.py:366
  11.6 3.4 %probs_part.4 = (bf16[4,384,384]{2,1,0:T(8,128)(2,1)S(1)}, f32[384,512]{1,0:T(8,128)S(1)}) custom-call(s32[8]{0:T(128)S(1)} %concatenate.3.refs_0_, bf16[384,2048]{1,0:T(8,128)(2,1)} %refs_1_.17, bf16[384,512]{1,0:T(8,128)(2,1)} %refs_2_.15, bf16[384,2048]{1,0:T(8,128)(2,1)} %refs_3_.15, bf16[64,256]{1,0:T(8,128)(2,1)S(1)} %join.6.refs_4_.refs_0_), custom_call_target="tpu_custom_call" | custom-call | flops 1000 | bytes 1000 | tf_op jit(solution)/shard_map/probs_part/pallas_call | solution.py:53
  15.0 1.3 %collective-permute-start.2 = (bf16[128,256]{1,0:T(8,128)(2,1)S(1)}, bf16[128,256]{1,0:T(8,128)(2,1)S(1)}, u32[]{:S(2)}, u32[]{:S(2)}) collective-permute-start(bf16[128,256]{1,0:T(8,128)(2,1)S(1)} %join.7.refs_5_.refs_0_), channel_id=1, source_target_pairs={{0,64},{2,66},{4,68},{6,70},{8,72},{10,74},{12,76},{14,78},{16,80}... | collective-permute-start | bytes 196616 | tf_op jit(solution)/shard_map/ppermute | solution.py:366
  16.3 2.2 %probs_part.5 = (bf16[4,384,384]{2,1,0:T(8,128)(2,1)S(1)}, f32[384,512]{1,0:T(8,128)S(1)}) custom-call(s32[8]{0:T(128)S(1)} %concatenate.3.refs_0_, bf16[384,2048]{1,0:T(8,128)(2,1)S(1)} %copy-done, bf16[384,512]{1,0:T(8,128)(2,1)S(1)} %copy-done.2, bf16[384,2048]{1,0:T(8,128)(2,1)S(1)} %copy-done.1, ...), custom_call_target="tpu_custom_call", output_to_operand_aliasing={{1}: (4, {})} | custom-call | flops 1000 | bytes 1000 | tf_op jit(solution)/shard_map/probs_part/pallas_call | solution.py:53
  18.5 1.8 %collective-permute-done.2.refs_1_ = bf16[128,256]{1,0:T(8,128)(2,1)S(1)} collective-permute-done((bf16[128,256]{1,0:T(8,128)(2,1)S(1)}, bf16[128,256]{1,0:T(8,128)(2,1)S(1)}, u32[]{:S(2)}, u32[]{:S(2)}) %collective-permute-start.2) | collective-permute-done | bytes 65568 | tf_op jit(solution)/shard_map/ppermute | solution.py:366
  20.4 2.2 %probs_part.6 = (bf16[4,384,384]{2,1,0:T(8,128)(2,1)S(1)}, f32[384,512]{1,0:T(8,128)S(1)}) custom-call(s32[8]{0:T(128)S(1)} %concatenate.3.refs_0_, bf16[384,2048]{1,0:T(8,128)(2,1)S(1)} %copy-done, bf16[384,512]{1,0:T(8,128)(2,1)S(1)} %copy-done.2, bf16[384,2048]{1,0:T(8,128)(2,1)S(1)} %copy-done.1, ...), custom_call_target="tpu_custom_call", output_to_operand_aliasing={{1}: (4, {})} | custom-call | flops 1000 | bytes 1000 | tf_op jit(solution)/shard_map/probs_part/pallas_call | solution.py:53
  22.6 0.2 copy.38.refs_3_
  22.8 1.4 %collective-permute-done.3.refs_1_ = bf16[256,256]{1,0:T(8,128)(2,1)S(1)} collective-permute-done((bf16[256,256]{1,0:T(8,128)(2,1)S(1)}, bf16[256,256]{1,0:T(8,128)(2,1)S(1)}, u32[]{:S(2)}, u32[]{:S(2)}) %collective-permute-start.3) | collective-permute-done | bytes 131104 | tf_op jit(solution)/shard_map/ppermute | solution.py:366
  24.2 2.9 %collective-permute-start.4 = (bf16[384,4096]{1,0:T(8,128)(2,1)S(1)}, bf16[384,4096]{1,0:T(8,128)(2,1)S(1)}, u32[]{:S(2)}, u32[]{:S(2)}) collective-permute-start(bf16[384,4096]{1,0:T(8,128)(2,1)S(1)} %get-tuple-element.45.refs_1_), channel_id=1, source_target_pairs={{0,2},{2,0},{4,6},{6,4},{8,10},{10,8},{12,14},{14,12},{16,18},{18,... | collective-permute-start | bytes 9437192 | tf_op jit(solution)/shard_map/ppermute | solution.py:366
  27.1 4.6 %collective-permute-start.7 = (bf16[512,256]{1,0:T(8,128)(2,1)S(1)}, bf16[512,256]{1,0:T(8,128)(2,1)S(1)}, u32[]{:S(2)}, u32[]{:S(2)}) collective-permute-start(bf16[512,256]{1,0:T(8,128)(2,1)S(1)} %get-tuple-element.46.refs_5_.refs_1_), channel_id=1, source_target_pairs={{2,26},{6,30},{10,2},{14,6},{18,10},{22,14},{26,18},{30,22},{34,58... | collective-permute-start | bytes 786440 | tf_op jit(solution)/shard_map/ppermute | solution.py:366
  31.7 2.3 %collective-permute-start.6 = (bf16[512,256]{1,0:T(8,128)(2,1)S(1)}, bf16[512,256]{1,0:T(8,128)(2,1)S(1)}, u32[]{:S(2)}, u32[]{:S(2)}) collective-permute-start(bf16[512,256]{1,0:T(8,128)(2,1)S(1)} %get-tuple-element.46.refs_5_.refs_1_), channel_id=1, source_target_pairs={{2,18},{6,22},{10,26},{14,30},{18,2},{22,6},{26,10},{30,14},{34,50... | collective-permute-start | bytes 786440 | tf_op jit(solution)/shard_map/ppermute | solution.py:366
  34.0 0.8 collective-permute-start.5
  34.8 2.2 %probs_part.7 = (bf16[4,384,384]{2,1,0:T(8,128)(2,1)S(1)}, f32[384,512]{1,0:T(8,128)S(1)}) custom-call(s32[8]{0:T(128)S(1)} %concatenate.3.refs_0_, bf16[384,2048]{1,0:T(8,128)(2,1)S(1)} %copy-done, bf16[384,512]{1,0:T(8,128)(2,1)S(1)} %copy-done.2, bf16[384,2048]{1,0:T(8,128)(2,1)S(1)} %copy-done.1, ...), custom_call_target="tpu_custom_call", output_to_operand_aliasing={{1}: (4, {})} | custom-call | flops 1000 | bytes 1000 | tf_op jit(solution)/shard_map/probs_part/pallas_call | solution.py:53
  37.0 3.5 %collective-permute-done.6.refs_3_ = bf16[512,256]{1,0:T(8,128)(2,1)S(1)} collective-permute-done((bf16[512,256]{1,0:T(8,128)(2,1)S(1)}, bf16[512,256]{1,0:T(8,128)(2,1)S(1)}, u32[]{:S(2)}, u32[]{:S(2)}) %collective-permute-start.6) | collective-permute-done | bytes 262176 | tf_op jit(solution)/shard_map/ppermute | solution.py:366
  40.5 2.7 %collective-permute-done.5.refs_2_ = bf16[512,256]{1,0:T(8,128)(2,1)S(1)} collective-permute-done((bf16[512,256]{1,0:T(8,128)(2,1)S(1)}, bf16[512,256]{1,0:T(8,128)(2,1)S(1)}, u32[]{:S(2)}, u32[]{:S(2)}) %collective-permute-start.5) | collective-permute-done | bytes 262176 | tf_op jit(solution)/shard_map/ppermute | solution.py:366
  43.2 0.6 join.10
  43.9 2.8 %collective-permute-start.10 = (bf16[1024,256]{1,0:T(8,128)(2,1)S(1)}, bf16[1024,256]{1,0:T(8,128)(2,1)S(1)}, u32[]{:S(2)}, u32[]{:S(2)}) collective-permute-start(bf16[1024,256]{1,0:T(8,128)(2,1)S(1)} %get-tuple-element.52.refs_7_.refs_4_), channel_id=1, source_target_pairs={{0,16},{4,20},{8,24},{12,28},{16,0},{20,4},{24,8},{28,12},{32,48},... | collective-permute-start | bytes 1572872 | tf_op jit(solution)/shard_map/ppermute | solution.py:366
  46.7 0.7 collective-permute-start.11
  47.4 0.3 collective-permute-start.9
  47.7 6.1 %collective-permute-done.10.refs_9_.refs_6_ = bf16[1024,256]{1,0:T(8,128)(2,1)S(1)} collective-permute-done((bf16[1024,256]{1,0:T(8,128)(2,1)S(1)}, bf16[1024,256]{1,0:T(8,128)(2,1)S(1)}, u32[]{:S(2)}, u32[]{:S(2)}) %collective-permute-start.10) | collective-permute-done | bytes 524320 | tf_op jit(solution)/shard_map/ppermute | solution.py:366
  53.8 5.3 %collective-permute-done.9.refs_8_.refs_5_ = bf16[1024,256]{1,0:T(8,128)(2,1)S(1)} collective-permute-done((bf16[1024,256]{1,0:T(8,128)(2,1)S(1)}, bf16[1024,256]{1,0:T(8,128)(2,1)S(1)}, u32[]{:S(2)}, u32[]{:S(2)}) %collective-permute-start.9) | collective-permute-done | bytes 524320 | tf_op jit(solution)/shard_map/ppermute | solution.py:366
  59.1 2.7 %raw_part.1 = (bf16[384,256]{1,0:T(8,128)(2,1)S(1)}, bf16[384,256]{1,0:T(8,128)(2,1)S(1)}, f32[1,256]{1,0:T(1,128)S(1)}) custom-call(s32[8]{0:T(128)S(1)} %concatenate.3.refs_0_, bf16[384,4096]{1,0:T(8,128)(2,1)S(1)} %get-tuple-element.45.refs_1_, bf16[384,4096]{1,0:T(8,128)(2,1)S(1)} %collective-permute-done.4.refs_5_.refs_2_, ...), custom_call_target="tpu_custom_call" | custom-call | flops 1000 | bytes 1000 | tf_op jit(solution)/shard_map/raw_part/pallas_call | solution.py:53
  61.9 1.6 %collective-permute-start.12 = (bf16[384,256]{1,0:T(8,128)(2,1)S(1)}, bf16[384,256]{1,0:T(8,128)(2,1)S(1)}, u32[]{:S(2)}, u32[]{:S(2)}) collective-permute-start(bf16[384,256]{1,0:T(8,128)(2,1)S(1)} %get-tuple-element.54), channel_id=1, source_target_pairs={{0,2},{2,0},{4,6},{6,4},{8,10},{10,8},{12,14},{14,12},{16,18},{18,... | collective-permute-start | bytes 589832 | tf_op jit(solution)/shard_map/ppermute | solution.py:366
  63.5 2.8 %collective-permute-start.13 = (f32[1,256]{1,0:T(1,128)S(1)}, f32[1,256]{1,0:T(1,128)S(1)}, u32[]{:S(2)}, u32[]{:S(2)}) collective-permute-start(f32[1,256]{1,0:T(1,128)S(1)} %get-tuple-element.55.refs_0_), channel_id=1, source_target_pairs={{0,4},{2,6},{4,0},{6,2},{8,12},{10,14},{12,8},{14,10},{16,20},{18,... | collective-permute-start | bytes 3080 | tf_op jit(solution)/shard_map/ppermute | solution.py:366
  66.3 0.9 split_part.1
  67.2 0.2 collective-permute-done.13.refs_1_
  67.5 1.2 %collective-permute-start.17 = (bf16[1408,256]{1,0:T(8,128)(2,1)S(1)}, bf16[1408,256]{1,0:T(8,128)(2,1)S(1)}, u32[]{:S(2)}, u32[]{:S(2)}) collective-permute-start(bf16[1408,256]{1,0:T(8,128)(2,1)S(1)} %get-tuple-element.71), channel_id=1, source_target_pairs={{0,1},{1,0},{2,3},{3,2},{4,5},{5,4},{6,7},{7,6},{8,9},{9,8},{10,11... | collective-permute-start | bytes 2162696 | tf_op jit(solution)/shard_map/ppermute | solution.py:414
  68.7 1.8 %collective-permute-start.18 = (bf16[1408,256]{1,0:T(8,128)(2,1)S(1)}, bf16[1408,256]{1,0:T(8,128)(2,1)S(1)}, u32[]{:S(2)}, u32[]{:S(2)}) collective-permute-start(bf16[1408,256]{1,0:T(8,128)(2,1)S(1)} %get-tuple-element.72), channel_id=1, source_target_pairs={{0,5},{1,4},{2,7},{3,6},{4,1},{5,0},{6,3},{7,2},{8,13},{9,12},{10,... | collective-permute-start | bytes 2162696 | tf_op jit(solution)/shard_map/ppermute | solution.py:415
  70.5 2.6 %grads_part.4 = (bf16[384,2048]{1,0:T(8,128)(2,1)}, bf16[384,512]{1,0:T(8,128)(2,1)}, f32[8,128]{1,0:T(8,128)S(1)}) custom-call(s32[8]{0:T(128)S(1)} %concatenate.3.refs_0_, bf16[384,2048]{1,0:T(8,128)(2,1)S(1)} %copy-done, bf16[384,512]{1,0:T(8,128)(2,1)S(1)} %copy-done.2, bf16[384,2048]{1,0:T(8,128)(2,1)S(1)} %copy-done.1, ...), custom_call_target="tpu_custom_call" | custom-call | flops 1000 | bytes 1000 | tf_op jit(solution)/shard_map/grads_part/pallas_call | solution.py:53
  73.2 1.5 %collective-permute-start.15 = (f32[1,256]{1,0:T(1,128)S(1)}, f32[1,256]{1,0:T(1,128)S(1)}, u32[]{:S(2)}, u32[]{:S(2)}) collective-permute-start(f32[1,256]{1,0:T(1,128)S(1)} %add.23.refs_9_.refs_0_), channel_id=1, source_target_pairs={{0,16},{2,18},{4,20},{6,22},{8,24},{10,26},{12,28},{14,30},{16,0},... | collective-permute-start | bytes 3080 | tf_op jit(solution)/shard_map/ppermute | solution.py:366
  74.8 2.6 %grads_part.5 = (bf16[384,2048]{1,0:T(8,128)(2,1)}, bf16[384,512]{1,0:T(8,128)(2,1)}, f32[8,128]{1,0:T(8,128)S(1)}) custom-call(s32[8]{0:T(128)S(1)} %concatenate.3.refs_0_, bf16[384,2048]{1,0:T(8,128)(2,1)S(1)} %copy-done, bf16[384,512]{1,0:T(8,128)(2,1)S(1)} %copy-done.2, ...), custom_call_target="tpu_custom_call", output_to_operand_aliasing={{0}: (7, {}), {1}: (8, {})} | custom-call | flops 1000 | bytes 1000 | tf_op jit(solution)/shard_map/grads_part/pallas_call | solution.py:53
  77.5 2.6 %grads_part.6 = (bf16[384,2048]{1,0:T(8,128)(2,1)}, bf16[384,512]{1,0:T(8,128)(2,1)}, f32[8,128]{1,0:T(8,128)S(1)}) custom-call(s32[8]{0:T(128)S(1)} %concatenate.3.refs_0_, bf16[384,2048]{1,0:T(8,128)(2,1)S(1)} %copy-done, bf16[384,512]{1,0:T(8,128)(2,1)S(1)} %copy-done.2, ...), custom_call_target="tpu_custom_call", output_to_operand_aliasing={{0}: (7, {}), {1}: (8, {})} | custom-call | flops 1000 | bytes 1000 | tf_op jit(solution)/shard_map/grads_part/pallas_call | solution.py:53
  80.2 3.7 %collective-permute-done.17.refs_1_.refs_3_ = bf16[1408,256]{1,0:T(8,128)(2,1)S(1)} collective-permute-done((bf16[1408,256]{1,0:T(8,128)(2,1)S(1)}, bf16[1408,256]{1,0:T(8,128)(2,1)S(1)}, u32[]{:S(2)}, u32[]{:S(2)}) %collective-permute-start.17) | collective-permute-done | bytes 720928 | tf_op jit(solution)/shard_map/ppermute | solution.py:414
  83.9 2.1 %collective-permute-done.18.refs_2_ = bf16[1408,256]{1,0:T(8,128)(2,1)S(1)} collective-permute-done((bf16[1408,256]{1,0:T(8,128)(2,1)S(1)}, bf16[1408,256]{1,0:T(8,128)(2,1)S(1)}, u32[]{:S(2)}, u32[]{:S(2)}) %collective-permute-start.18) | collective-permute-done | bytes 720928 | tf_op jit(solution)/shard_map/ppermute | solution.py:415
  86.0 0.1 join.11.refs_3_.refs_4_
  86.2 2.5 %collective-permute-start.19 = (bf16[4096,256]{1,0:T(8,128)(2,1)S(1)}, bf16[4096,256]{1,0:T(8,128)(2,1)S(1)}, u32[]{:S(2)}, u32[]{:S(2)}) collective-permute-start(bf16[4096,256]{1,0:T(8,128)(2,1)S(1)} %join.11.refs_3_.refs_4_), channel_id=1, source_target_pairs={{0,2},{2,0},{4,6},{6,4},{8,10},{10,8},{12,14},{14,12},{16,18},{18,... | collective-permute-start | bytes 6291464 | tf_op jit(solution)/shard_map/ppermute | solution.py:366
  88.7 0.5 collective-permute-start.20
  89.2 2.6 %grads_part.7 = (bf16[384,2048]{1,0:T(8,128)(2,1)}, bf16[384,512]{1,0:T(8,128)(2,1)}, f32[8,128]{1,0:T(8,128)S(1)}) custom-call(s32[8]{0:T(128)S(1)} %concatenate.3.refs_0_, bf16[384,2048]{1,0:T(8,128)(2,1)S(1)} %copy-done, bf16[384,512]{1,0:T(8,128)(2,1)S(1)} %copy-done.2, ...), custom_call_target="tpu_custom_call", output_to_operand_aliasing={{0}: (7, {}), {1}: (8, {})} | custom-call | flops 1000 | bytes 1000 | tf_op jit(solution)/shard_map/grads_part/pallas_call | solution.py:53
  91.8 0.2 collective-permute-done.20.refs_1_
  92.0 3.9 %collective-permute-start.21 = (f32[1,256]{1,0:T(1,128)S(1)}, f32[1,256]{1,0:T(1,128)S(1)}, u32[]{:S(2)}, u32[]{:S(2)}) collective-permute-start(f32[1,256]{1,0:T(1,128)S(1)} %add.26.refs_6_.refs_0_), channel_id=1, source_target_pairs={{0,128},{2,130},{4,132},{6,134},{8,136},{10,138},{12,140},{14,142}... | collective-permute-start | bytes 3080 | tf_op jit(solution)/shard_map/ppermute | solution.py:366
  96.0 3.5 %hidden_part.1 = (bf16[384,2048]{1,0:T(8,128)(2,1)}, f32[8,128]{1,0:T(8,128)S(1)}) custom-call(s32[8]{0:T(128)S(1)} %concatenate.3.refs_0_, f32[384,512]{1,0:T(8,128)S(1)} %get-tuple-element.50.refs_3_.refs_1_, f32[1,512]{1,0:T(1,128)S(1)} %bitcast.11, bf16[1408,256]{1,0:T(8,128)(2,1)S(1)} %collective-permute-done.17.refs_1_.refs_3_, ...), custom_call_target="tpu_custom_call" | custom-call | flops 1000 | bytes 1000 | tf_op jit(solution)/shard_map/hidden_part/pallas_call | solution.py:53
  99.5 1.2 %collective-permute-start.22 = (f32[1,256]{1,0:T(1,128)S(1)}, f32[1,256]{1,0:T(1,128)S(1)}, u32[]{:S(2)}, u32[]{:S(2)}) collective-permute-start(f32[1,256]{1,0:T(1,128)S(1)} %add.27.refs_1_), channel_id=1, source_target_pairs={{0,2},{2,0},{4,6},{6,4},{8,10},{10,8},{12,14},{14,12},{16,18},{18,... | collective-permute-start | bytes 3080 | tf_op jit(solution)/shard_map/ppermute | solution.py:366
  100.7 0.8 collective-permute-done.22.refs_2_
  101.6 1.1 %last.1 = f32[1,512]{1,0:T(1,128)} custom-call(s32[8]{0:T(128)S(1)} %concatenate.3.refs_0_, f32[1,256]{1,0:T(1,128)S(1)} %add.27.refs_1_, f32[1,256]{1,0:T(1,128)S(1)} %collective-permute-done.22.refs_2_, f32[1,512]{1,0:T(1,128)S(1)} %bitcast.12), custom_call_target="tpu_custom_call" | custom-call | flops 1000 | bytes 1000 | tf_op jit(solution)/shard_map/last/pallas_call | solution.py:53
  (35 shorter events, 0.6 us)
Async XLA Ops:
  0.6 4.4 %collective-permute-start = (bf16[32,512]{1,0:T(8,128)(2,1)}, bf16[32,512]{1,0:T(8,128)(2,1)S(1)}, u32[]{:S(2)}, u32[]{:S(2)}) collective-permute-start(bf16[32,512]{1,0:T(8,128)(2,1)} %refs_1_.9), channel_id=1, source_target_pairs={{0,2},{2,0},{4,6},{6,4},{8,10},{10,8},{12,14},{14,12},{16,18},{18,... | collective-permute-start | bytes 98312 | tf_op jit(solution)/shard_map/ppermute | solution.py:366
  6.3 10.0 %copy-start = (bf16[384,2048]{1,0:T(8,128)(2,1)S(1)}, bf16[384,2048]{1,0:T(8,128)(2,1)}, u32[]{:S(2)}) copy-start(bf16[384,2048]{1,0:T(8,128)(2,1)} %refs_1_.17) | copy-start | bytes 4718596
  6.3 10.0 %copy-start.1 = (bf16[384,2048]{1,0:T(8,128)(2,1)S(1)}, bf16[384,2048]{1,0:T(8,128)(2,1)}, u32[]{:S(2)}) copy-start(bf16[384,2048]{1,0:T(8,128)(2,1)} %refs_3_.15) | copy-start | bytes 4718596
  6.3 10.0 %copy-start.2 = (bf16[384,512]{1,0:T(8,128)(2,1)S(1)}, bf16[384,512]{1,0:T(8,128)(2,1)}, u32[]{:S(2)}) copy-start(bf16[384,512]{1,0:T(8,128)(2,1)} %refs_2_.15) | copy-start | bytes 1179652
  6.3 8.7 %collective-permute-start.1 = (bf16[64,256]{1,0:T(8,128)(2,1)S(1)}, bf16[64,256]{1,0:T(8,128)(2,1)S(1)}, u32[]{:S(2)}, u32[]{:S(2)}) collective-permute-start(bf16[64,256]{1,0:T(8,128)(2,1)S(1)} %join.6.refs_4_.refs_0_), channel_id=1, source_target_pairs={{0,128},{2,130},{4,132},{6,134},{8,136},{10,138},{12,140},{14,142}... | collective-permute-start | bytes 98312 | tf_op jit(solution)/shard_map/ppermute | solution.py:366
  15.0 5.2 %collective-permute-start.2 = (bf16[128,256]{1,0:T(8,128)(2,1)S(1)}, bf16[128,256]{1,0:T(8,128)(2,1)S(1)}, u32[]{:S(2)}, u32[]{:S(2)}) collective-permute-start(bf16[128,256]{1,0:T(8,128)(2,1)S(1)} %join.7.refs_5_.refs_0_), channel_id=1, source_target_pairs={{0,64},{2,66},{4,68},{6,70},{8,72},{10,74},{12,76},{14,78},{16,80}... | collective-permute-start | bytes 196616 | tf_op jit(solution)/shard_map/ppermute | solution.py:366
  20.3 3.9 %collective-permute-start.3 = (bf16[256,256]{1,0:T(8,128)(2,1)S(1)}, bf16[256,256]{1,0:T(8,128)(2,1)S(1)}, u32[]{:S(2)}, u32[]{:S(2)}) collective-permute-start(bf16[256,256]{1,0:T(8,128)(2,1)S(1)} %join.8.refs_5_.refs_1_.refs_0_), channel_id=1, source_target_pairs={{0,32},{2,34},{4,36},{6,38},{8,40},{10,42},{12,44},{14,46},{16,48}... | collective-permute-start | bytes 393224 | tf_op jit(solution)/shard_map/ppermute | solution.py:366
  20.4 2.2 %copy-start.3 = (bf16[384,4096]{1,0:T(8,128)(2,1)S(1)}, bf16[384,4096]{1,0:T(8,128)(2,1)}, u32[]{:S(2)}) copy-start(bf16[384,4096]{1,0:T(8,128)(2,1)} %refs_0_.1) | copy-start | bytes 9437188
  24.2 19.0 %collective-permute-start.4 = (bf16[384,4096]{1,0:T(8,128)(2,1)S(1)}, bf16[384,4096]{1,0:T(8,128)(2,1)S(1)}, u32[]{:S(2)}, u32[]{:S(2)}) collective-permute-start(bf16[384,4096]{1,0:T(8,128)(2,1)S(1)} %get-tuple-element.45.refs_1_), channel_id=1, source_target_pairs={{0,2},{2,0},{4,6},{6,4},{8,10},{10,8},{12,14},{14,12},{16,18},{18,... | collective-permute-start | bytes 9437192 | tf_op jit(solution)/shard_map/ppermute | solution.py:366
  27.1 9.9 %collective-permute-start.7 = (bf16[512,256]{1,0:T(8,128)(2,1)S(1)}, bf16[512,256]{1,0:T(8,128)(2,1)S(1)}, u32[]{:S(2)}, u32[]{:S(2)}) collective-permute-start(bf16[512,256]{1,0:T(8,128)(2,1)S(1)} %get-tuple-element.46.refs_5_.refs_1_), channel_id=1, source_target_pairs={{2,26},{6,30},{10,2},{14,6},{18,10},{22,14},{26,18},{30,22},{34,58... | collective-permute-start | bytes 786440 | tf_op jit(solution)/shard_map/ppermute | solution.py:366
  31.7 8.7 %collective-permute-start.6 = (bf16[512,256]{1,0:T(8,128)(2,1)S(1)}, bf16[512,256]{1,0:T(8,128)(2,1)S(1)}, u32[]{:S(2)}, u32[]{:S(2)}) collective-permute-start(bf16[512,256]{1,0:T(8,128)(2,1)S(1)} %get-tuple-element.46.refs_5_.refs_1_), channel_id=1, source_target_pairs={{2,18},{6,22},{10,26},{14,30},{18,2},{22,6},{26,10},{30,14},{34,50... | collective-permute-start | bytes 786440 | tf_op jit(solution)/shard_map/ppermute | solution.py:366
  34.0 9.2 %collective-permute-start.5 = (bf16[512,256]{1,0:T(8,128)(2,1)S(1)}, bf16[512,256]{1,0:T(8,128)(2,1)S(1)}, u32[]{:S(2)}, u32[]{:S(2)}) collective-permute-start(bf16[512,256]{1,0:T(8,128)(2,1)S(1)} %get-tuple-element.46.refs_5_.refs_1_), channel_id=1, source_target_pairs={{0,4},{4,0},{8,12},{12,8},{16,20},{20,16},{24,28},{28,24},{32,36},... | collective-permute-start | bytes 786440 | tf_op jit(solution)/shard_map/ppermute | solution.py:366
  43.2 16.0 %copy-start.4 = (f32[512]{0:T(512)S(1)}, f32[512]{0:T(512)}, u32[]{:S(2)}) copy-start(f32[512]{0:T(512)} %param.11) | copy-start | bytes 6148
  43.8 15.3 %collective-permute-start.8 = (f32[384,512]{1,0:T(8,128)S(1)}, f32[384,512]{1,0:T(8,128)S(1)}, u32[]{:S(2)}, u32[]{:S(2)}) collective-permute-start(f32[384,512]{1,0:T(8,128)S(1)} %get-tuple-element.50.refs_3_.refs_1_), channel_id=1, source_target_pairs={{0,2},{2,0},{4,6},{6,4},{8,10},{10,8},{12,14},{14,12},{16,18},{18,... | collective-permute-start | bytes 2359304 | tf_op jit(solution)/shard_map/ppermute | solution.py:366
  43.9 9.9 %collective-permute-start.10 = (bf16[1024,256]{1,0:T(8,128)(2,1)S(1)}, bf16[1024,256]{1,0:T(8,128)(2,1)S(1)}, u32[]{:S(2)}, u32[]{:S(2)}) collective-permute-start(bf16[1024,256]{1,0:T(8,128)(2,1)S(1)} %get-tuple-element.52.refs_7_.refs_4_), channel_id=1, source_target_pairs={{0,16},{4,20},{8,24},{12,28},{16,0},{20,4},{24,8},{28,12},{32,48},... | collective-permute-start | bytes 1572872 | tf_op jit(solution)/shard_map/ppermute | solution.py:366
  46.7 7.1 %collective-permute-start.11 = (bf16[1024,256]{1,0:T(8,128)(2,1)S(1)}, bf16[1024,256]{1,0:T(8,128)(2,1)S(1)}, u32[]{:S(2)}, u32[]{:S(2)}) collective-permute-start(bf16[1024,256]{1,0:T(8,128)(2,1)S(1)} %get-tuple-element.51.refs_6_.refs_3_), channel_id=1, source_target_pairs={{0,24},{4,28},{8,0},{12,4},{16,8},{20,12},{24,16},{28,20},{32,56},... | collective-permute-start | bytes 1572872 | tf_op jit(solution)/shard_map/ppermute | solution.py:366
  47.4 11.7 %collective-permute-start.9 = (bf16[1024,256]{1,0:T(8,128)(2,1)S(1)}, bf16[1024,256]{1,0:T(8,128)(2,1)S(1)}, u32[]{:S(2)}, u32[]{:S(2)}) collective-permute-start(bf16[1024,256]{1,0:T(8,128)(2,1)S(1)} %get-tuple-element.51.refs_6_.refs_3_), channel_id=1, source_target_pairs={{0,8},{4,12},{8,16},{12,20},{16,24},{20,28},{24,0},{28,4},{32,40},... | collective-permute-start | bytes 1572872 | tf_op jit(solution)/shard_map/ppermute | solution.py:366
  61.9 4.4 %collective-permute-start.12 = (bf16[384,256]{1,0:T(8,128)(2,1)S(1)}, bf16[384,256]{1,0:T(8,128)(2,1)S(1)}, u32[]{:S(2)}, u32[]{:S(2)}) collective-permute-start(bf16[384,256]{1,0:T(8,128)(2,1)S(1)} %get-tuple-element.54), channel_id=1, source_target_pairs={{0,2},{2,0},{4,6},{6,4},{8,10},{10,8},{12,14},{14,12},{16,18},{18,... | collective-permute-start | bytes 589832 | tf_op jit(solution)/shard_map/ppermute | solution.py:366
  63.5 3.9 %collective-permute-start.13 = (f32[1,256]{1,0:T(1,128)S(1)}, f32[1,256]{1,0:T(1,128)S(1)}, u32[]{:S(2)}, u32[]{:S(2)}) collective-permute-start(f32[1,256]{1,0:T(1,128)S(1)} %get-tuple-element.55.refs_0_), channel_id=1, source_target_pairs={{0,4},{2,6},{4,0},{6,2},{8,12},{10,14},{12,8},{14,10},{16,20},{18,... | collective-permute-start | bytes 3080 | tf_op jit(solution)/shard_map/ppermute | solution.py:366
  67.5 16.4 %collective-permute-start.17 = (bf16[1408,256]{1,0:T(8,128)(2,1)S(1)}, bf16[1408,256]{1,0:T(8,128)(2,1)S(1)}, u32[]{:S(2)}, u32[]{:S(2)}) collective-permute-start(bf16[1408,256]{1,0:T(8,128)(2,1)S(1)} %get-tuple-element.71), channel_id=1, source_target_pairs={{0,1},{1,0},{2,3},{3,2},{4,5},{5,4},{6,7},{7,6},{8,9},{9,8},{10,11... | collective-permute-start | bytes 2162696 | tf_op jit(solution)/shard_map/ppermute | solution.py:414
  68.7 17.3 %collective-permute-start.18 = (bf16[1408,256]{1,0:T(8,128)(2,1)S(1)}, bf16[1408,256]{1,0:T(8,128)(2,1)S(1)}, u32[]{:S(2)}, u32[]{:S(2)}) collective-permute-start(bf16[1408,256]{1,0:T(8,128)(2,1)S(1)} %get-tuple-element.72), channel_id=1, source_target_pairs={{0,5},{1,4},{2,7},{3,6},{4,1},{5,0},{6,3},{7,2},{8,13},{9,12},{10,... | collective-permute-start | bytes 2162696 | tf_op jit(solution)/shard_map/ppermute | solution.py:415
  70.5 2.7 %collective-permute-start.14 = (f32[1,256]{1,0:T(1,128)S(1)}, f32[1,256]{1,0:T(1,128)S(1)}, u32[]{:S(2)}, u32[]{:S(2)}) collective-permute-start(f32[1,256]{1,0:T(1,128)S(1)} %get-tuple-element.59.refs_7_.refs_0_), channel_id=1, source_target_pairs={{0,8},{2,10},{4,12},{6,14},{8,0},{10,2},{12,4},{14,6},{16,24},{18,... | collective-permute-start | bytes 3080 | tf_op jit(solution)/shard_map/ppermute | solution.py:366
  73.2 4.1 %collective-permute-start.15 = (f32[1,256]{1,0:T(1,128)S(1)}, f32[1,256]{1,0:T(1,128)S(1)}, u32[]{:S(2)}, u32[]{:S(2)}) collective-permute-start(f32[1,256]{1,0:T(1,128)S(1)} %add.23.refs_9_.refs_0_), channel_id=1, source_target_pairs={{0,16},{2,18},{4,20},{6,22},{8,24},{10,26},{12,28},{14,30},{16,0},... | collective-permute-start | bytes 3080 | tf_op jit(solution)/shard_map/ppermute | solution.py:366
  77.4 2.8 %collective-permute-start.16 = (f32[1,256]{1,0:T(1,128)S(1)}, f32[1,256]{1,0:T(1,128)S(1)}, u32[]{:S(2)}, u32[]{:S(2)}) collective-permute-start(f32[1,256]{1,0:T(1,128)S(1)} %add.24.refs_9_.refs_0_), channel_id=1, source_target_pairs={{0,32},{2,34},{4,36},{6,38},{8,40},{10,42},{12,44},{14,46},{16,48}... | collective-permute-start | bytes 3080 | tf_op jit(solution)/shard_map/ppermute | solution.py:366
  86.2 9.8 %collective-permute-start.19 = (bf16[4096,256]{1,0:T(8,128)(2,1)S(1)}, bf16[4096,256]{1,0:T(8,128)(2,1)S(1)}, u32[]{:S(2)}, u32[]{:S(2)}) collective-permute-start(bf16[4096,256]{1,0:T(8,128)(2,1)S(1)} %join.11.refs_3_.refs_4_), channel_id=1, source_target_pairs={{0,2},{2,0},{4,6},{6,4},{8,10},{10,8},{12,14},{14,12},{16,18},{18,... | collective-permute-start | bytes 6291464 | tf_op jit(solution)/shard_map/ppermute | solution.py:366
  88.7 3.3 %collective-permute-start.20 = (f32[1,256]{1,0:T(1,128)S(1)}, f32[1,256]{1,0:T(1,128)S(1)}, u32[]{:S(2)}, u32[]{:S(2)}) collective-permute-start(f32[1,256]{1,0:T(1,128)S(1)} %add.25.refs_9_.refs_3_.refs_0_), channel_id=1, source_target_pairs={{0,64},{2,66},{4,68},{6,70},{8,72},{10,74},{12,76},{14,78},{16,80}... | collective-permute-start | bytes 3080 | tf_op jit(solution)/shard_map/ppermute | solution.py:366
  92.0 7.5 %collective-permute-start.21 = (f32[1,256]{1,0:T(1,128)S(1)}, f32[1,256]{1,0:T(1,128)S(1)}, u32[]{:S(2)}, u32[]{:S(2)}) collective-permute-start(f32[1,256]{1,0:T(1,128)S(1)} %add.26.refs_6_.refs_0_), channel_id=1, source_target_pairs={{0,128},{2,130},{4,132},{6,134},{8,136},{10,138},{12,140},{14,142}... | collective-permute-start | bytes 3080 | tf_op jit(solution)/shard_map/ppermute | solution.py:366
  99.5 2.1 %collective-permute-start.22 = (f32[1,256]{1,0:T(1,128)S(1)}, f32[1,256]{1,0:T(1,128)S(1)}, u32[]{:S(2)}, u32[]{:S(2)}) collective-permute-start(f32[1,256]{1,0:T(1,128)S(1)} %add.27.refs_1_), channel_id=1, source_target_pairs={{0,2},{2,0},{4,6},{6,4},{8,10},{10,8},{12,14},{14,12},{16,18},{18,... | collective-permute-start | bytes 3080 | tf_op jit(solution)/shard_map/ppermute | solution.py:366

commit v5 on v4

--- a/solution.py
+++ b/solution.py
@@ -32,7 +32,7 @@
 
 
 def call(kernel, name, out_shape, ins, after=(), through=(), **kw):
-    specs, args = zip(*ins)
+    specs = [spec for spec, _ in ins]
     args = tuple(pltpu.with_memory_space_constraint(a, pltpu.HBM) if spec is HBM else a for spec, a in ins)
     n_in = len(args) + len(after)
     single = not isinstance(out_shape, (list, tuple))
@@ -182,14 +182,16 @@
     return pl.ds(pl.multiple_of(at_ref[3] * HALF, HALF), HALF)
 
 
-def first_join(at_ref, own_hbm, other_ref, out_ref, sem):
-    c, cols = at_ref[3], own_columns(at_ref)
-    copy = pltpu.make_async_copy(
-        own_hbm.at[:, cols], out_ref.at[pl.ds(pl.multiple_of(c * SHARD, SHARD), SHARD), :], sem
-    )
+def own_part(at_ref, own_hbm, out_ref, sem):
+    copy = pltpu.make_async_copy(own_hbm.at[:, own_columns(at_ref)], out_ref, sem)
     copy.start()
-    out_ref[pl.ds(pl.multiple_of((1 - c) * SHARD, SHARD), SHARD), :] = other_ref[:, cols]
     copy.wait()
+
+
+def first_join(at_ref, own_ref, other_ref, out_ref):
+    c = at_ref[3]
+    out_ref[pl.ds(pl.multiple_of(c * SHARD, SHARD), SHARD), :] = own_ref[...]
+    out_ref[pl.ds(pl.multiple_of((1 - c) * SHARD, SHARD), SHARD), :] = other_ref[:, own_columns(at_ref)]
 
 
 def copy_kernel(in_ref, out_ref, sem):
@@ -243,8 +245,12 @@
                 place(piece, half, 2 * (j % 2) + half, j // 2)
 
 
+NEAR = 640
+BESIDES = DEPTH // 2 - NEAR
+
+
 def raw_kernel(at_ref, own_ref, other_ref, dv_own, dv_other, scale_ref, *refs):
-    pieces, (mine_ref, theirs_ref, sums_ref, codes_ref) = refs[:5], refs[5:]
+    pieces, (mine_ref, theirs_ref, sums_ref, kept_ref, near_ref, beside_ref, codes_ref) = refs[:5], refs[5:]
     put_in_order(at_ref, pieces, codes_ref)
     cols = own_columns(at_ref)
     scale = scale_ref[:, cols]
@@ -254,37 +260,22 @@
         values_ref[...] = (raw * scale).astype(BF16)
         sums += jnp.sum(raw * dv_ref[:, cols], axis=0, keepdims=True)
     sums_ref[...] = sums
-
-
-def raw_part(at, hidden, hidden_other, dv, dv_other, scale, pieces):
-    return call(
-        raw_kernel, "raw_part", [shape(COUNT, HALF), shape(COUNT, HALF), shape(1, HALF, dtype=F32)],
-        [(SMEM, at)] + [(VMEM, a) for a in [hidden, hidden_other, dv, dv_other, scale] + pieces],
-        scratch_shapes=[pltpu.VMEM((DEPTH, HALF), BF16)],
-    )
-
-
-NEAR = 640
-BESIDES = DEPTH // 2 - NEAR
-
-
-def split_kernel(at_ref, dv_ref, scale_ref, *refs):
-    pieces, (kept_ref, near_ref, beside_ref, codes_ref) = refs[:5], refs[5:]
-    put_in_order(at_ref, pieces, codes_ref)
     s, half = at_ref[4], DEPTH // 2
     kept_ref[...] = codes_ref[pl.ds(pl.multiple_of(s * half, half), half), :]
     base = (1 - s) * half
     for j in range(2):
-        cols = pl.ds(j * HALF, HALF)
-        near_ref[pl.ds(j * COUNT, COUNT), :] = (dv_ref[:, cols] * scale_ref[:, cols]).astype(BF16)
+        part = pl.ds(j * HALF, HALF)
+        near_ref[pl.ds(j * COUNT, COUNT), :] = (dv_own[:, part] * scale_ref[:, part]).astype(BF16)
     near_ref[2 * COUNT :, :] = codes_ref[pl.ds(pl.multiple_of(base, half), NEAR), :]
     beside_ref[...] = codes_ref[pl.ds(pl.multiple_of(base + NEAR, 128), BESIDES), :]
 
 
-def split_part(at, dv, scale, pieces, after):
+def raw_part(at, hidden, hidden_other, dv, dv_other, scale, pieces):
+    outs = [shape(COUNT, HALF), shape(COUNT, HALF), shape(1, HALF, dtype=F32)]
+    outs += [shape(DEPTH // 2, HALF), shape(2 * COUNT + NEAR, HALF), shape(BESIDES, HALF)]
     return call(
-        split_kernel, "split_part", [shape(DEPTH // 2, HALF), shape(2 * COUNT + NEAR, HALF), shape(BESIDES, HALF)],
-        [(SMEM, at), (VMEM, dv), (VMEM, scale)] + [(VMEM, p) for p in pieces], after,
+        raw_kernel, "raw_part", outs,
+        [(SMEM, at)] + [(VMEM, a) for a in [hidden, hidden_other, dv, dv_other, scale] + pieces],
         scratch_shapes=[pltpu.VMEM((DEPTH, HALF), BF16)],
     )
 
@@ -324,14 +315,6 @@
     out_ref[...] = a_ref[...] + b_ref[...]
 
 
-def last_kernel(at_ref, own_ref, other_ref, scale_ref, out_ref):
-    c = at_ref[3]
-    low = jnp.where(c == 0, own_ref[...], other_ref[...])
-    high = jnp.where(c == 0, other_ref[...], own_ref[...])
-    out_ref[:, :HALF] = low * scale_ref[:, :HALF]
-    out_ref[:, HALF:] = high * scale_ref[:, HALF:]
-
-
 def pairs(move):
     out = []
     for i in range(128):
@@ -372,15 +355,17 @@
     at = jnp.concatenate([place, lengths[0, :3]])
     scale = value_scale.reshape(1, -1)
 
-    rows = call(
-        first_join, "join", shape(CHIP, HALF), [(SMEM, at), (HBM, value_codes), (VMEM, send(value_codes, C_SWAP))],
-        scratch_shapes=[pltpu.SemaphoreType.DMA],
-    )
+    own = call(
+        own_part, "own", shape(SHARD, HALF), [(SMEM, at), (HBM, value_codes)], scratch_shapes=[pltpu.SemaphoreType.DMA]
+    )
+    other = send(value_codes, C_SWAP)
+    rows = call(first_join, "join", shape(CHIP, HALF), [(SMEM, at), (VMEM, own), (VMEM, other)])
     probs, dv = [], None
-    for g, bit in enumerate((4, 2, 1)):
+    for bit, heads in ((4, (0,)), (2, (1, 2)), (1, (3,))):
         got = send(rows, z_swap(bit))
-        p, dv = probs_part(g, at, queries, keys, upstream, dv, (rows,))
-        probs.append(p)
+        for g in heads:
+            p, dv = probs_part(g, at, queries, keys, upstream, dv, (rows,))
+            probs.append(p)
         n = rows.shape[0]
         ins = [(VMEM, rows), (VMEM, got)]
         if bit > 1:
@@ -390,49 +375,46 @@
                 copy_kernel, "copy", shape(*hidden.shape), [(ANY, hidden)], (rows,),
                 out_specs=[ANY], scratch_shapes=[pltpu.SemaphoreType.DMA],
             )
-            rows, hidden = call(join_kernel, "join", shape(2 * n, HALF), ins, (p,), (hidden,))
+            rows, hidden, dv = call(join_kernel, "join", shape(2 * n, HALF), ins, (p,), (hidden, dv))
     got = [send(rows, core_pairs(X_SWAP if k == 1 else [], y_shift(k))) for k in (1, 2, 3)]
-    hidden_other = send(hidden, C_SWAP)
-    p, dv = probs_part(3, at, queries, keys, upstream, dv, (rows,))
-    probs.append(p)
+    hidden_other, dv_other = send(hidden, C_SWAP), send(dv, C_SWAP)
     n = rows.shape[0]
-    first, second, dv = call(
-        core_join_kernel, "join", [shape(2 * n, HALF)] * 2,
-        [(SMEM, at)] + [(VMEM, a) for a in [rows] + got], (hidden_other, p), (dv,),
+    first, second = call(
+        core_join_kernel, "join", [shape(2 * n, HALF)] * 2, [(SMEM, at)] + [(VMEM, a) for a in [rows] + got],
+        (dv_other,),
     )
     pieces = [first, second]
     for k, rows in enumerate((first, second, first), 1):
         pieces.append(send(rows, core_pairs(y_shift(k), X_SWAP if k < 3 else [])))
-    mine, theirs, sums = raw_part(at, hidden, hidden_other, dv, send(dv, C_SWAP), scale, pieces)
-
-    got = send(sums, X_SWAP)
+    mine, theirs, sums, kept, near, beside = raw_part(at, hidden, hidden_other, dv, dv_other, scale, pieces)
+
     values_far = send(theirs, C_SWAP)
-    kept, near, beside = split_part(at, dv, scale, pieces, (values_far,))
-    sums, near, beside = call(
-        add_kernel, "add", shape(1, HALF, dtype=F32), [(VMEM, sums), (VMEM, got)], (kept,), (near, beside)
-    )
-    near = lax.ppermute(near, "seq", SEQ_SWAP)
-    beside = lax.ppermute(beside, ("dp", "seq"), BESIDE)
     held = None
-    for g, perm in enumerate((y_swap(1), y_swap(2), z_swap(1), z_swap(2))):
+    for step, perm in enumerate((X_SWAP, y_swap(1), y_swap(2), z_swap(1), z_swap(2), z_swap(4))):
+        if step == 1:
+            near = lax.ppermute(near, "seq", SEQ_SWAP)
+            beside = lax.ppermute(beside, ("dp", "seq"), BESIDE)
         got = send(sums, perm)
-        *held, token = grads_part(g, at, queries, keys, upstream, mine, values_far, probs[g], held, (sums,))
-        after = (token,)
-        if g == 3:
-            codes = call(
+        through = ()
+        if step < 4:
+            *held, token = grads_part(step, at, queries, keys, upstream, mine, values_far, probs[step], held, (sums,))
+            if step == 0:
+                through = (near, beside)
+        elif step == 4:
+            token = codes = call(
                 codes_join_kernel, "join", shape(DEPTH, HALF), [(VMEM, kept), (VMEM, near), (VMEM, beside)], (sums,)
             )
             codes_far = send(codes, C_SWAP)
-            after += (codes,)
-        sums = call(add_kernel, "add", shape(1, HALF, dtype=F32), [(VMEM, sums), (VMEM, got)], after)
-    got = send(sums, z_swap(4))
-    grad_hidden, token = hidden_part(at, dv, scale, near, codes, codes_far, after=(sums,))
-    sums = call(add_kernel, "add", shape(1, HALF, dtype=F32), [(VMEM, sums), (VMEM, got)], (token,))
-    last = call(
-        last_kernel, "last", shape(1, 2 * HALF, dtype=F32),
-        [(SMEM, at), (VMEM, sums), (VMEM, send(sums, C_SWAP)), (VMEM, scale)],
-    )
-    return held[0], held[1], grad_hidden, last.reshape(-1)
+        else:
+            grad_hidden, token = hidden_part(at, dv, scale, near, codes, codes_far, after=(sums,))
+        ins = [(VMEM, sums), (VMEM, got)]
+        if through:
+            sums, near, beside = call(add_kernel, "add", shape(1, HALF, dtype=F32), ins, (token,), through)
+        else:
+            sums = call(add_kernel, "add", shape(1, HALF, dtype=F32), ins, (token,))
+    far = send(sums, C_SWAP)
+    both = jnp.concatenate([jnp.where(me % 2 == 0, sums, far), jnp.where(me % 2 == 0, far, sums)], axis=1)
+    return held[0], held[1], grad_hidden, (both * scale).reshape(-1)
 
 
 def solution(mesh):

time: 103 us -> 103 us (level)
  waiting for transfers between devices: 28.4 us -> 32.1 us
  starting transfers between devices: 41.7 us -> 39.2 us
  Pallas kernels: 31 us -> 29.7 us
    ppermute x21, waiting for transfers between devices: 22.5 us -> 25.9 us  [send(): return lax.ppermute(x, 'dp', perm)]
    ppermute x1, waiting for transfers between devices: 3.71 us -> 5.36 us  [shards(): near = lax.ppermute(near, 'seq', SEQ_SWAP)]
    pallas_call x25 -> x24, Pallas kernels: 31 us -> 29.7 us  [call(): pl.pallas_call(run, in_specs=list(specs) + [ANY] * (len(after) + len(thro...]
    ppermute x1, waiting for transfers between devices: 2.14 us -> 0.85 us  [shards(): beside = lax.ppermute(beside, ('dp', 'seq'), BESIDE)]
    ppermute x21, starting transfers between devices: 38.6 us -> 37.5 us  [send(): return lax.ppermute(x, 'dp', perm)]
  transfers between devices with their start and end apart: 23 -> 23, of which waited for: 14 -> 12; matrix products, arithmetic and copies ran while one was open for 1% -> 1% of each run, Pallas kernels for 24% -> 25%
where the time goes in v5:
time: 103 us
  starting transfers between devices  39.2 us (38%)
  waiting for transfers between devices  32.1 us (31%)
  Pallas kernels  29.7 us (29%)
    ppermute x21, starting transfers between devices, send(): return lax.ppermute(x, 'dp', perm)  37.5 us
    pallas_call x24, Pallas kernels, call(): pl.pallas_call(run, in_specs=list(specs) + [ANY] * (len(after) + len(thro...  29.7 us
    ppermute x21, waiting for transfers between devices, send(): return lax.ppermute(x, 'dp', perm)  25.9 us
    ppermute x1, waiting for transfers between devices, shards(): near = lax.ppermute(near, 'seq', SEQ_SWAP)  5.36 us
  transfers between devices with their start and end apart: 23, of which 12 were waited for; matrix products, arithmetic and copies ran while one was open for 1% of the time, Pallas kernels for 25%

profile of v5, /device:TPU:1, one launch (start us, length us, event | category | flops | bytes accessed | tf_op | source)
XLA Modules:
  0.0 103.2 jit_solution(7574125671530632712)
XLA Ops:
  0.6 3.3 %collective-permute-start = (bf16[32,512]{1,0:T(8,128)(2,1)}, bf16[32,512]{1,0:T(8,128)(2,1)S(1)}, u32[]{:S(2)}, u32[]{:S(2)}) collective-permute-start(bf16[32,512]{1,0:T(8,128)(2,1)} %refs_1_.9), channel_id=1, source_target_pairs={{0,2},{2,0},{4,6},{6,4},{8,10},{10,8},{12,14},{14,12},{16,18},{18,... | collective-permute-start | bytes 98312 | tf_op jit(solution)/shard_map/ppermute | solution.py:349
  4.0 0.7 slice_bitcast_fusion
  4.7 1.3 %own.1.refs_1_ = bf16[32,256]{1,0:T(8,128)(2,1)S(1)} custom-call(s32[8]{0:T(128)S(1)} %concatenate.11.refs_0_, bf16[32,512]{1,0:T(8,128)(2,1)} %refs_1_.9), custom_call_target="tpu_custom_call" | custom-call | flops 1000 | bytes 1000 | tf_op jit(solution)/shard_map/own/pallas_call | solution.py:53
  6.0 0.5 join.6.refs_4_.refs_0_
  6.6 5.3 %collective-permute-start.1 = (bf16[64,256]{1,0:T(8,128)(2,1)S(1)}, bf16[64,256]{1,0:T(8,128)(2,1)S(1)}, u32[]{:S(2)}, u32[]{:S(2)}) collective-permute-start(bf16[64,256]{1,0:T(8,128)(2,1)S(1)} %join.6.refs_4_.refs_0_), channel_id=1, source_target_pairs={{0,128},{2,130},{4,132},{6,134},{8,136},{10,138},{12,140},{14,142}... | collective-permute-start | bytes 98312 | tf_op jit(solution)/shard_map/ppermute | solution.py:349
  11.8 3.4 %probs_part.4 = (bf16[4,384,384]{2,1,0:T(8,128)(2,1)S(1)}, f32[384,512]{1,0:T(8,128)S(1)}) custom-call(s32[8]{0:T(128)S(1)} %concatenate.11.refs_0_, bf16[384,2048]{1,0:T(8,128)(2,1)} %refs_1_.17, bf16[384,512]{1,0:T(8,128)(2,1)} %refs_2_.15, bf16[384,2048]{1,0:T(8,128)(2,1)} %refs_3_.15, bf16[64,256]{1,0:T(8,128)(2,1)S(1)} %join.6.refs_4_.refs_0_), custom_call_target="tpu_custom_call" | custom-call | flops 1000 | bytes 1000 | tf_op jit(solution)/shard_map/probs_part/pallas_call | solution.py:53
  15.3 1.3 %collective-permute-start.2 = (bf16[128,256]{1,0:T(8,128)(2,1)S(1)}, bf16[128,256]{1,0:T(8,128)(2,1)S(1)}, u32[]{:S(2)}, u32[]{:S(2)}) collective-permute-start(bf16[128,256]{1,0:T(8,128)(2,1)S(1)} %join.7.refs_5_.refs_0_), channel_id=1, source_target_pairs={{0,64},{2,66},{4,68},{6,70},{8,72},{10,74},{12,76},{14,78},{16,80}... | collective-permute-start | bytes 196616 | tf_op jit(solution)/shard_map/ppermute | solution.py:349
  16.6 2.2 %probs_part.5 = (bf16[4,384,384]{2,1,0:T(8,128)(2,1)S(1)}, f32[384,512]{1,0:T(8,128)S(1)}) custom-call(s32[8]{0:T(128)S(1)} %concatenate.11.refs_0_, bf16[384,2048]{1,0:T(8,128)(2,1)S(1)} %copy-done, bf16[384,512]{1,0:T(8,128)(2,1)S(1)} %copy-done.2, bf16[384,2048]{1,0:T(8,128)(2,1)S(1)} %copy-done.1, ...), custom_call_target="tpu_custom_call", output_to_operand_aliasing={{1}: (4, {})} | custom-call | flops 1000 | bytes 1000 | tf_op jit(solution)/shard_map/probs_part/pallas_call | solution.py:53
  18.7 2.2 %probs_part.6 = (bf16[4,384,384]{2,1,0:T(8,128)(2,1)S(1)}, f32[384,512]{1,0:T(8,128)S(1)}) custom-call(s32[8]{0:T(128)S(1)} %concatenate.11.refs_0_, bf16[384,2048]{1,0:T(8,128)(2,1)S(1)} %copy-done, bf16[384,512]{1,0:T(8,128)(2,1)S(1)} %copy-done.2, bf16[384,2048]{1,0:T(8,128)(2,1)S(1)} %copy-done.1, ...), custom_call_target="tpu_custom_call", output_to_operand_aliasing={{1}: (4, {})} | custom-call | flops 1000 | bytes 1000 | tf_op jit(solution)/shard_map/probs_part/pallas_call | solution.py:53
  20.9 0.3 collective-permute-done.2.refs_1_
  21.3 0.5 collective-permute-start.3
  21.8 2.2 %probs_part.7 = (bf16[4,384,384]{2,1,0:T(8,128)(2,1)S(1)}, f32[384,512]{1,0:T(8,128)S(1)}) custom-call(s32[8]{0:T(128)S(1)} %concatenate.11.refs_0_, bf16[384,2048]{1,0:T(8,128)(2,1)S(1)} %copy-done, bf16[384,512]{1,0:T(8,128)(2,1)S(1)} %copy-done.2, bf16[384,2048]{1,0:T(8,128)(2,1)S(1)} %copy-done.1, ...), custom_call_target="tpu_custom_call", output_to_operand_aliasing={{1}: (4, {})} | custom-call | flops 1000 | bytes 1000 | tf_op jit(solution)/shard_map/probs_part/pallas_call | solution.py:53
  24.0 0.2 copy.38.refs_3_
  24.2 1.0 collective-permute-done.3.refs_1_
  25.2 2.2 %collective-permute-start.4 = (bf16[384,4096]{1,0:T(8,128)(2,1)S(1)}, bf16[384,4096]{1,0:T(8,128)(2,1)S(1)}, u32[]{:S(2)}, u32[]{:S(2)}) collective-permute-start(bf16[384,4096]{1,0:T(8,128)(2,1)S(1)} %get-tuple-element.47.refs_1_), channel_id=1, source_target_pairs={{0,2},{2,0},{4,6},{6,4},{8,10},{10,8},{12,14},{14,12},{16,18},{18,... | collective-permute-start | bytes 9437192 | tf_op jit(solution)/shard_map/ppermute | solution.py:349
  27.5 4.6 %collective-permute-start.8 = (bf16[512,256]{1,0:T(8,128)(2,1)S(1)}, bf16[512,256]{1,0:T(8,128)(2,1)S(1)}, u32[]{:S(2)}, u32[]{:S(2)}) collective-permute-start(bf16[512,256]{1,0:T(8,128)(2,1)S(1)} %get-tuple-element.49.refs_1_), channel_id=1, source_target_pairs={{2,26},{6,30},{10,2},{14,6},{18,10},{22,14},{26,18},{30,22},{34,58... | collective-permute-start | bytes 786440 | tf_op jit(solution)/shard_map/ppermute | solution.py:349
  32.1 2.3 %collective-permute-start.7 = (bf16[512,256]{1,0:T(8,128)(2,1)S(1)}, bf16[512,256]{1,0:T(8,128)(2,1)S(1)}, u32[]{:S(2)}, u32[]{:S(2)}) collective-permute-start(bf16[512,256]{1,0:T(8,128)(2,1)S(1)} %get-tuple-element.49.refs_1_), channel_id=1, source_target_pairs={{2,18},{6,22},{10,26},{14,30},{18,2},{22,6},{26,10},{30,14},{34,50... | collective-permute-start | bytes 786440 | tf_op jit(solution)/shard_map/ppermute | solution.py:349
  34.4 0.8 collective-permute-start.6
  35.2 0.3 collective-permute-done.8.refs_4_
  35.4 5.4 %collective-permute-done.7.refs_3_ = bf16[512,256]{1,0:T(8,128)(2,1)S(1)} collective-permute-done((bf16[512,256]{1,0:T(8,128)(2,1)S(1)}, bf16[512,256]{1,0:T(8,128)(2,1)S(1)}, u32[]{:S(2)}, u32[]{:S(2)}) %collective-permute-start.7) | collective-permute-done | bytes 262176 | tf_op jit(solution)/shard_map/ppermute | solution.py:349
  40.9 4.2 %collective-permute-done.6.refs_2_ = bf16[512,256]{1,0:T(8,128)(2,1)S(1)} collective-permute-done((bf16[512,256]{1,0:T(8,128)(2,1)S(1)}, bf16[512,256]{1,0:T(8,128)(2,1)S(1)}, u32[]{:S(2)}, u32[]{:S(2)}) %collective-permute-start.6) | collective-permute-done | bytes 262176 | tf_op jit(solution)/shard_map/ppermute | solution.py:349
  45.0 0.6 join.10
  45.7 2.8 %collective-permute-start.10 = (bf16[1024,256]{1,0:T(8,128)(2,1)S(1)}, bf16[1024,256]{1,0:T(8,128)(2,1)S(1)}, u32[]{:S(2)}, u32[]{:S(2)}) collective-permute-start(bf16[1024,256]{1,0:T(8,128)(2,1)S(1)} %get-tuple-element.51.refs_7_), channel_id=1, source_target_pairs={{0,16},{4,20},{8,24},{12,28},{16,0},{20,4},{24,8},{28,12},{32,48},... | collective-permute-start | bytes 1572872 | tf_op jit(solution)/shard_map/ppermute | solution.py:349
  48.5 0.7 collective-permute-start.11
  49.2 0.3 collective-permute-start.9
  49.5 5.8 %collective-permute-done.10.refs_9_ = bf16[1024,256]{1,0:T(8,128)(2,1)S(1)} collective-permute-done((bf16[1024,256]{1,0:T(8,128)(2,1)S(1)}, bf16[1024,256]{1,0:T(8,128)(2,1)S(1)}, u32[]{:S(2)}, u32[]{:S(2)}) %collective-permute-start.10) | collective-permute-done | bytes 524320 | tf_op jit(solution)/shard_map/ppermute | solution.py:349
  55.3 5.6 %collective-permute-done.9.refs_8_ = bf16[1024,256]{1,0:T(8,128)(2,1)S(1)} collective-permute-done((bf16[1024,256]{1,0:T(8,128)(2,1)S(1)}, bf16[1024,256]{1,0:T(8,128)(2,1)S(1)}, u32[]{:S(2)}, u32[]{:S(2)}) %collective-permute-start.9) | collective-permute-done | bytes 524320 | tf_op jit(solution)/shard_map/ppermute | solution.py:349
  60.9 2.9 %raw_part.1 = (bf16[384,256]{1,0:T(8,128)(2,1)S(1)}, bf16[384,256]{1,0:T(8,128)(2,1)S(1)}, f32[1,256]{1,0:T(1,128)S(1)}, bf16[2048,256]{1,0:T(8,128)(2,1)S(1)}, ...) custom-call(s32[8]{0:T(128)S(1)} %concatenate.11.refs_0_, bf16[384,4096]{1,0:T(8,128)(2,1)S(1)} %get-tuple-element.47.refs_1_, ...), custom_call_target="tpu_custom_call" | custom-call | flops 1000 | bytes 1000 | tf_op jit(solution)/shard_map/raw_part/pallas_call | solution.py:53
  63.9 2.8 %collective-permute-start.13 = (f32[1,256]{1,0:T(1,128)S(1)}, f32[1,256]{1,0:T(1,128)S(1)}, u32[]{:S(2)}, u32[]{:S(2)}) collective-permute-start(f32[1,256]{1,0:T(1,128)S(1)} %get-tuple-element.55.refs_7_.refs_0_), channel_id=1, source_target_pairs={{0,4},{2,6},{4,0},{6,2},{8,12},{10,14},{12,8},{14,10},{16,20},{18,... | collective-permute-start | bytes 3080 | tf_op jit(solution)/shard_map/ppermute | solution.py:349
  66.8 2.6 %grads_part.4 = (bf16[384,2048]{1,0:T(8,128)(2,1)}, bf16[384,512]{1,0:T(8,128)(2,1)}, f32[8,128]{1,0:T(8,128)S(1)}) custom-call(s32[8]{0:T(128)S(1)} %concatenate.11.refs_0_, bf16[384,2048]{1,0:T(8,128)(2,1)S(1)} %copy-done, bf16[384,512]{1,0:T(8,128)(2,1)S(1)} %copy-done.2, bf16[384,2048]{1,0:T(8,128)(2,1)S(1)} %copy-done.1, ...), custom_call_target="tpu_custom_call" | custom-call | flops 1000 | bytes 1000 | tf_op jit(solution)/shard_map/grads_part/pallas_call | solution.py:53
  69.4 0.4 collective-permute-start.16
  69.7 1.3 %collective-permute-start.17 = (bf16[1408,256]{1,0:T(8,128)(2,1)S(1)}, bf16[1408,256]{1,0:T(8,128)(2,1)S(1)}, u32[]{:S(2)}, u32[]{:S(2)}) collective-permute-start(bf16[1408,256]{1,0:T(8,128)(2,1)S(1)} %get-tuple-element.72), channel_id=1, source_target_pairs={{0,5},{1,4},{2,7},{3,6},{4,1},{5,0},{6,3},{7,2},{8,13},{9,12},{10,... | collective-permute-start | bytes 2162696 | tf_op jit(solution)/shard_map/ppermute | solution.py:396
  71.1 2.6 %grads_part.5 = (bf16[384,2048]{1,0:T(8,128)(2,1)}, bf16[384,512]{1,0:T(8,128)(2,1)}, f32[8,128]{1,0:T(8,128)S(1)}) custom-call(s32[8]{0:T(128)S(1)} %concatenate.11.refs_0_, bf16[384,2048]{1,0:T(8,128)(2,1)S(1)} %copy-done, bf16[384,512]{1,0:T(8,128)(2,1)S(1)} %copy-done.2, ...), custom_call_target="tpu_custom_call", output_to_operand_aliasing={{0}: (7, {}), {1}: (8, {})} | custom-call | flops 1000 | bytes 1000 | tf_op jit(solution)/shard_map/grads_part/pallas_call | solution.py:53
  73.8 1.5 %collective-permute-start.15 = (f32[1,256]{1,0:T(1,128)S(1)}, f32[1,256]{1,0:T(1,128)S(1)}, u32[]{:S(2)}, u32[]{:S(2)}) collective-permute-start(f32[1,256]{1,0:T(1,128)S(1)} %add.25.refs_9_.refs_0_), channel_id=1, source_target_pairs={{0,16},{2,18},{4,20},{6,22},{8,24},{10,26},{12,28},{14,30},{16,0},... | collective-permute-start | bytes 3080 | tf_op jit(solution)/shard_map/ppermute | solution.py:349
  75.3 2.6 %grads_part.6 = (bf16[384,2048]{1,0:T(8,128)(2,1)}, bf16[384,512]{1,0:T(8,128)(2,1)}, f32[8,128]{1,0:T(8,128)S(1)}) custom-call(s32[8]{0:T(128)S(1)} %concatenate.11.refs_0_, bf16[384,2048]{1,0:T(8,128)(2,1)S(1)} %copy-done, bf16[384,512]{1,0:T(8,128)(2,1)S(1)} %copy-done.2, ...), custom_call_target="tpu_custom_call", output_to_operand_aliasing={{0}: (7, {}), {1}: (8, {})} | custom-call | flops 1000 | bytes 1000 | tf_op jit(solution)/shard_map/grads_part/pallas_call | solution.py:53
  78.0 0.5 collective-permute-start.18
  78.5 2.6 %grads_part.7 = (bf16[384,2048]{1,0:T(8,128)(2,1)}, bf16[384,512]{1,0:T(8,128)(2,1)}, f32[8,128]{1,0:T(8,128)S(1)}) custom-call(s32[8]{0:T(128)S(1)} %concatenate.11.refs_0_, bf16[384,2048]{1,0:T(8,128)(2,1)S(1)} %copy-done, bf16[384,512]{1,0:T(8,128)(2,1)S(1)} %copy-done.2, ...), custom_call_target="tpu_custom_call", output_to_operand_aliasing={{0}: (7, {}), {1}: (8, {})} | custom-call | flops 1000 | bytes 1000 | tf_op jit(solution)/shard_map/grads_part/pallas_call | solution.py:53
  81.1 5.4 %collective-permute-done.16.refs_1_.refs_3_ = bf16[1408,256]{1,0:T(8,128)(2,1)S(1)} collective-permute-done((bf16[1408,256]{1,0:T(8,128)(2,1)S(1)}, bf16[1408,256]{1,0:T(8,128)(2,1)S(1)}, u32[]{:S(2)}, u32[]{:S(2)}) %collective-permute-start.16) | collective-permute-done | bytes 720928 | tf_op jit(solution)/shard_map/ppermute | solution.py:395
  86.5 0.9 collective-permute-done.17.refs_2_
  87.3 0.1 join.11.refs_2_.refs_4_
  87.5 2.3 %collective-permute-start.19 = (bf16[4096,256]{1,0:T(8,128)(2,1)S(1)}, bf16[4096,256]{1,0:T(8,128)(2,1)S(1)}, u32[]{:S(2)}, u32[]{:S(2)}) collective-permute-start(bf16[4096,256]{1,0:T(8,128)(2,1)S(1)} %join.11.refs_2_.refs_4_), channel_id=1, source_target_pairs={{0,2},{2,0},{4,6},{6,4},{8,10},{10,8},{12,14},{14,12},{16,18},{18,... | collective-permute-start | bytes 6291464 | tf_op jit(solution)/shard_map/ppermute | solution.py:349
  89.7 0.9 collective-permute-start.20
  90.7 2.4 %collective-permute-done.20.refs_1_ = f32[1,256]{1,0:T(1,128)S(1)} collective-permute-done((f32[1,256]{1,0:T(1,128)S(1)}, f32[1,256]{1,0:T(1,128)S(1)}, u32[]{:S(2)}, u32[]{:S(2)}) %collective-permute-start.20) | collective-permute-done | bytes 1056 | tf_op jit(solution)/shard_map/ppermute | solution.py:349
  93.1 3.5 %collective-permute-start.21 = (f32[1,256]{1,0:T(1,128)S(1)}, f32[1,256]{1,0:T(1,128)S(1)}, u32[]{:S(2)}, u32[]{:S(2)}) collective-permute-start(f32[1,256]{1,0:T(1,128)S(1)} %add.28.refs_6_.refs_0_), channel_id=1, source_target_pairs={{0,128},{2,130},{4,132},{6,134},{8,136},{10,138},{12,140},{14,142}... | collective-permute-start | bytes 3080 | tf_op jit(solution)/shard_map/ppermute | solution.py:349
  96.6 3.5 %hidden_part.1 = (bf16[384,2048]{1,0:T(8,128)(2,1)}, f32[8,128]{1,0:T(8,128)S(1)}) custom-call(s32[8]{0:T(128)S(1)} %concatenate.11.refs_0_, f32[384,512]{1,0:T(8,128)S(1)} %get-tuple-element.48.refs_3_.refs_1_, f32[1,512]{1,0:T(1,128)S(1)} %bitcast.11, bf16[1408,256]{1,0:T(8,128)(2,1)S(1)} %collective-permute-done.16.refs_1_.refs_3_, ...), custom_call_target="tpu_custom_call" | custom-call | flops 1000 | bytes 1000 | tf_op jit(solution)/shard_map/hidden_part/pallas_call | solution.py:53
  100.1 1.7 %collective-permute-start.22 = (f32[1,256]{1,0:T(1,128)S(1)}, f32[1,256]{1,0:T(1,128)S(1)}, u32[]{:S(2)}, u32[]{:S(2)}) collective-permute-start(f32[1,256]{1,0:T(1,128)S(1)} %add.29), channel_id=1, source_target_pairs={{0,2},{2,0},{4,6},{6,4},{8,10},{10,8},{12,14},{14,12},{16,18},{18,... | collective-permute-start | bytes 3080 | tf_op jit(solution)/shard_map/ppermute | solution.py:349
  101.8 0.8 collective-permute-done.22
  102.6 0.6 maximum_multiply_fusion
  (36 shorter events, 0.5 us)
Async XLA Ops:
  0.6 5.4 %collective-permute-start = (bf16[32,512]{1,0:T(8,128)(2,1)}, bf16[32,512]{1,0:T(8,128)(2,1)S(1)}, u32[]{:S(2)}, u32[]{:S(2)}) collective-permute-start(bf16[32,512]{1,0:T(8,128)(2,1)} %refs_1_.9), channel_id=1, source_target_pairs={{0,2},{2,0},{4,6},{6,4},{8,10},{10,8},{12,14},{14,12},{16,18},{18,... | collective-permute-start | bytes 98312 | tf_op jit(solution)/shard_map/ppermute | solution.py:349
  6.5 10.0 %copy-start = (bf16[384,2048]{1,0:T(8,128)(2,1)S(1)}, bf16[384,2048]{1,0:T(8,128)(2,1)}, u32[]{:S(2)}) copy-start(bf16[384,2048]{1,0:T(8,128)(2,1)} %refs_1_.17) | copy-start | bytes 4718596
  6.6 10.0 %copy-start.1 = (bf16[384,2048]{1,0:T(8,128)(2,1)S(1)}, bf16[384,2048]{1,0:T(8,128)(2,1)}, u32[]{:S(2)}) copy-start(bf16[384,2048]{1,0:T(8,128)(2,1)} %refs_3_.15) | copy-start | bytes 4718596
  6.6 10.0 %copy-start.2 = (bf16[384,512]{1,0:T(8,128)(2,1)S(1)}, bf16[384,512]{1,0:T(8,128)(2,1)}, u32[]{:S(2)}) copy-start(bf16[384,512]{1,0:T(8,128)(2,1)} %refs_2_.15) | copy-start | bytes 1179652
  6.6 8.7 %collective-permute-start.1 = (bf16[64,256]{1,0:T(8,128)(2,1)S(1)}, bf16[64,256]{1,0:T(8,128)(2,1)S(1)}, u32[]{:S(2)}, u32[]{:S(2)}) collective-permute-start(bf16[64,256]{1,0:T(8,128)(2,1)S(1)} %join.6.refs_4_.refs_0_), channel_id=1, source_target_pairs={{0,128},{2,130},{4,132},{6,134},{8,136},{10,138},{12,140},{14,142}... | collective-permute-start | bytes 98312 | tf_op jit(solution)/shard_map/ppermute | solution.py:349
  15.3 6.0 %collective-permute-start.2 = (bf16[128,256]{1,0:T(8,128)(2,1)S(1)}, bf16[128,256]{1,0:T(8,128)(2,1)S(1)}, u32[]{:S(2)}, u32[]{:S(2)}) collective-permute-start(bf16[128,256]{1,0:T(8,128)(2,1)S(1)} %join.7.refs_5_.refs_0_), channel_id=1, source_target_pairs={{0,64},{2,66},{4,68},{6,70},{8,72},{10,74},{12,76},{14,78},{16,80}... | collective-permute-start | bytes 196616 | tf_op jit(solution)/shard_map/ppermute | solution.py:349
  21.3 3.9 %collective-permute-start.3 = (bf16[256,256]{1,0:T(8,128)(2,1)S(1)}, bf16[256,256]{1,0:T(8,128)(2,1)S(1)}, u32[]{:S(2)}, u32[]{:S(2)}) collective-permute-start(bf16[256,256]{1,0:T(8,128)(2,1)S(1)} %join.8.refs_5_.refs_1_.refs_0_), channel_id=1, source_target_pairs={{0,32},{2,34},{4,36},{6,38},{8,40},{10,42},{12,44},{14,46},{16,48}... | collective-permute-start | bytes 393224 | tf_op jit(solution)/shard_map/ppermute | solution.py:349
  21.8 2.2 %copy-start.3 = (bf16[384,4096]{1,0:T(8,128)(2,1)S(1)}, bf16[384,4096]{1,0:T(8,128)(2,1)}, u32[]{:S(2)}) copy-start(bf16[384,4096]{1,0:T(8,128)(2,1)} %refs_0_.1) | copy-start | bytes 9437188
  25.2 35.7 %copy-start.4 = (f32[512]{0:T(512)S(1)}, f32[512]{0:T(512)}, u32[]{:S(2)}) copy-start(f32[512]{0:T(512)} %param.11) | copy-start | bytes 6148
  25.2 35.7 %collective-permute-start.4 = (bf16[384,4096]{1,0:T(8,128)(2,1)S(1)}, bf16[384,4096]{1,0:T(8,128)(2,1)S(1)}, u32[]{:S(2)}, u32[]{:S(2)}) collective-permute-start(bf16[384,4096]{1,0:T(8,128)(2,1)S(1)} %get-tuple-element.47.refs_1_), channel_id=1, source_target_pairs={{0,2},{2,0},{4,6},{6,4},{8,10},{10,8},{12,14},{14,12},{16,18},{18,... | collective-permute-start | bytes 9437192 | tf_op jit(solution)/shard_map/ppermute | solution.py:349
  27.4 17.7 %collective-permute-start.5 = (f32[384,512]{1,0:T(8,128)S(1)}, f32[384,512]{1,0:T(8,128)S(1)}, u32[]{:S(2)}, u32[]{:S(2)}) collective-permute-start(f32[384,512]{1,0:T(8,128)S(1)} %get-tuple-element.48.refs_3_.refs_1_), channel_id=1, source_target_pairs={{0,2},{2,0},{4,6},{6,4},{8,10},{10,8},{12,14},{14,12},{16,18},{18,... | collective-permute-start | bytes 2359304 | tf_op jit(solution)/shard_map/ppermute | solution.py:349
  27.5 7.9 %collective-permute-start.8 = (bf16[512,256]{1,0:T(8,128)(2,1)S(1)}, bf16[512,256]{1,0:T(8,128)(2,1)S(1)}, u32[]{:S(2)}, u32[]{:S(2)}) collective-permute-start(bf16[512,256]{1,0:T(8,128)(2,1)S(1)} %get-tuple-element.49.refs_1_), channel_id=1, source_target_pairs={{2,26},{6,30},{10,2},{14,6},{18,10},{22,14},{26,18},{30,22},{34,58... | collective-permute-start | bytes 786440 | tf_op jit(solution)/shard_map/ppermute | solution.py:349
  32.1 8.7 %collective-permute-start.7 = (bf16[512,256]{1,0:T(8,128)(2,1)S(1)}, bf16[512,256]{1,0:T(8,128)(2,1)S(1)}, u32[]{:S(2)}, u32[]{:S(2)}) collective-permute-start(bf16[512,256]{1,0:T(8,128)(2,1)S(1)} %get-tuple-element.49.refs_1_), channel_id=1, source_target_pairs={{2,18},{6,22},{10,26},{14,30},{18,2},{22,6},{26,10},{30,14},{34,50... | collective-permute-start | bytes 786440 | tf_op jit(solution)/shard_map/ppermute | solution.py:349
  34.4 10.6 %collective-permute-start.6 = (bf16[512,256]{1,0:T(8,128)(2,1)S(1)}, bf16[512,256]{1,0:T(8,128)(2,1)S(1)}, u32[]{:S(2)}, u32[]{:S(2)}) collective-permute-start(bf16[512,256]{1,0:T(8,128)(2,1)S(1)} %get-tuple-element.49.refs_1_), channel_id=1, source_target_pairs={{0,4},{4,0},{8,12},{12,8},{16,20},{20,16},{24,28},{28,24},{32,36},... | collective-permute-start | bytes 786440 | tf_op jit(solution)/shard_map/ppermute | solution.py:349
  45.7 9.6 %collective-permute-start.10 = (bf16[1024,256]{1,0:T(8,128)(2,1)S(1)}, bf16[1024,256]{1,0:T(8,128)(2,1)S(1)}, u32[]{:S(2)}, u32[]{:S(2)}) collective-permute-start(bf16[1024,256]{1,0:T(8,128)(2,1)S(1)} %get-tuple-element.51.refs_7_), channel_id=1, source_target_pairs={{0,16},{4,20},{8,24},{12,28},{16,0},{20,4},{24,8},{28,12},{32,48},... | collective-permute-start | bytes 1572872 | tf_op jit(solution)/shard_map/ppermute | solution.py:349
  48.5 6.8 %collective-permute-start.11 = (bf16[1024,256]{1,0:T(8,128)(2,1)S(1)}, bf16[1024,256]{1,0:T(8,128)(2,1)S(1)}, u32[]{:S(2)}, u32[]{:S(2)}) collective-permute-start(bf16[1024,256]{1,0:T(8,128)(2,1)S(1)} %get-tuple-element.50.refs_6_), channel_id=1, source_target_pairs={{0,24},{4,28},{8,0},{12,4},{16,8},{20,12},{24,16},{28,20},{32,56},... | collective-permute-start | bytes 1572872 | tf_op jit(solution)/shard_map/ppermute | solution.py:349
  49.2 11.7 %collective-permute-start.9 = (bf16[1024,256]{1,0:T(8,128)(2,1)S(1)}, bf16[1024,256]{1,0:T(8,128)(2,1)S(1)}, u32[]{:S(2)}, u32[]{:S(2)}) collective-permute-start(bf16[1024,256]{1,0:T(8,128)(2,1)S(1)} %get-tuple-element.50.refs_6_), channel_id=1, source_target_pairs={{0,8},{4,12},{8,16},{12,20},{16,24},{20,28},{24,0},{28,4},{32,40},... | collective-permute-start | bytes 1572872 | tf_op jit(solution)/shard_map/ppermute | solution.py:349
  63.8 2.9 %collective-permute-start.12 = (bf16[384,256]{1,0:T(8,128)(2,1)S(1)}, bf16[384,256]{1,0:T(8,128)(2,1)S(1)}, u32[]{:S(2)}, u32[]{:S(2)}) collective-permute-start(bf16[384,256]{1,0:T(8,128)(2,1)S(1)} %get-tuple-element.53), channel_id=1, source_target_pairs={{0,2},{2,0},{4,6},{6,4},{8,10},{10,8},{12,14},{14,12},{16,18},{18,... | collective-permute-start | bytes 589832 | tf_op jit(solution)/shard_map/ppermute | solution.py:349
  63.9 5.4 %collective-permute-start.13 = (f32[1,256]{1,0:T(1,128)S(1)}, f32[1,256]{1,0:T(1,128)S(1)}, u32[]{:S(2)}, u32[]{:S(2)}) collective-permute-start(f32[1,256]{1,0:T(1,128)S(1)} %get-tuple-element.55.refs_7_.refs_0_), channel_id=1, source_target_pairs={{0,4},{2,6},{4,0},{6,2},{8,12},{10,14},{12,8},{14,10},{16,20},{18,... | collective-permute-start | bytes 3080 | tf_op jit(solution)/shard_map/ppermute | solution.py:349
  69.4 17.1 %collective-permute-start.16 = (bf16[1408,256]{1,0:T(8,128)(2,1)S(1)}, bf16[1408,256]{1,0:T(8,128)(2,1)S(1)}, u32[]{:S(2)}, u32[]{:S(2)}) collective-permute-start(bf16[1408,256]{1,0:T(8,128)(2,1)S(1)} %get-tuple-element.70), channel_id=1, source_target_pairs={{0,1},{1,0},{2,3},{3,2},{4,5},{5,4},{6,7},{7,6},{8,9},{9,8},{10,11... | collective-permute-start | bytes 2162696 | tf_op jit(solution)/shard_map/ppermute | solution.py:395
  69.7 17.6 %collective-permute-start.17 = (bf16[1408,256]{1,0:T(8,128)(2,1)S(1)}, bf16[1408,256]{1,0:T(8,128)(2,1)S(1)}, u32[]{:S(2)}, u32[]{:S(2)}) collective-permute-start(bf16[1408,256]{1,0:T(8,128)(2,1)S(1)} %get-tuple-element.72), channel_id=1, source_target_pairs={{0,5},{1,4},{2,7},{3,6},{4,1},{5,0},{6,3},{7,2},{8,13},{9,12},{10,... | collective-permute-start | bytes 2162696 | tf_op jit(solution)/shard_map/ppermute | solution.py:396
  71.1 2.7 %collective-permute-start.14 = (f32[1,256]{1,0:T(1,128)S(1)}, f32[1,256]{1,0:T(1,128)S(1)}, u32[]{:S(2)}, u32[]{:S(2)}) collective-permute-start(f32[1,256]{1,0:T(1,128)S(1)} %get-tuple-element.61.refs_9_.refs_0_), channel_id=1, source_target_pairs={{0,8},{2,10},{4,12},{6,14},{8,0},{10,2},{12,4},{14,6},{16,24},{18,... | collective-permute-start | bytes 3080 | tf_op jit(solution)/shard_map/ppermute | solution.py:349
  73.8 4.1 %collective-permute-start.15 = (f32[1,256]{1,0:T(1,128)S(1)}, f32[1,256]{1,0:T(1,128)S(1)}, u32[]{:S(2)}, u32[]{:S(2)}) collective-permute-start(f32[1,256]{1,0:T(1,128)S(1)} %add.25.refs_9_.refs_0_), channel_id=1, source_target_pairs={{0,16},{2,18},{4,20},{6,22},{8,24},{10,26},{12,28},{14,30},{16,0},... | collective-permute-start | bytes 3080 | tf_op jit(solution)/shard_map/ppermute | solution.py:349
  78.0 3.1 %collective-permute-start.18 = (f32[1,256]{1,0:T(1,128)S(1)}, f32[1,256]{1,0:T(1,128)S(1)}, u32[]{:S(2)}, u32[]{:S(2)}) collective-permute-start(f32[1,256]{1,0:T(1,128)S(1)} %add.26.refs_9_.refs_0_), channel_id=1, source_target_pairs={{0,32},{2,34},{4,36},{6,38},{8,40},{10,42},{12,44},{14,46},{16,48}... | collective-permute-start | bytes 3080 | tf_op jit(solution)/shard_map/ppermute | solution.py:349
  87.5 9.1 %collective-permute-start.19 = (bf16[4096,256]{1,0:T(8,128)(2,1)S(1)}, bf16[4096,256]{1,0:T(8,128)(2,1)S(1)}, u32[]{:S(2)}, u32[]{:S(2)}) collective-permute-start(bf16[4096,256]{1,0:T(8,128)(2,1)S(1)} %join.11.refs_2_.refs_4_), channel_id=1, source_target_pairs={{0,2},{2,0},{4,6},{6,4},{8,10},{10,8},{12,14},{14,12},{16,18},{18,... | collective-permute-start | bytes 6291464 | tf_op jit(solution)/shard_map/ppermute | solution.py:349
  89.7 3.3 %collective-permute-start.20 = (f32[1,256]{1,0:T(1,128)S(1)}, f32[1,256]{1,0:T(1,128)S(1)}, u32[]{:S(2)}, u32[]{:S(2)}) collective-permute-start(f32[1,256]{1,0:T(1,128)S(1)} %add.27.refs_3_.refs_0_), channel_id=1, source_target_pairs={{0,64},{2,66},{4,68},{6,70},{8,72},{10,74},{12,76},{14,78},{16,80}... | collective-permute-start | bytes 3080 | tf_op jit(solution)/shard_map/ppermute | solution.py:349
  93.1 7.0 %collective-permute-start.21 = (f32[1,256]{1,0:T(1,128)S(1)}, f32[1,256]{1,0:T(1,128)S(1)}, u32[]{:S(2)}, u32[]{:S(2)}) collective-permute-start(f32[1,256]{1,0:T(1,128)S(1)} %add.28.refs_6_.refs_0_), channel_id=1, source_target_pairs={{0,128},{2,130},{4,132},{6,134},{8,136},{10,138},{12,140},{14,142}... | collective-permute-start | bytes 3080 | tf_op jit(solution)/shard_map/ppermute | solution.py:349
  100.1 2.5 %collective-permute-start.22 = (f32[1,256]{1,0:T(1,128)S(1)}, f32[1,256]{1,0:T(1,128)S(1)}, u32[]{:S(2)}, u32[]{:S(2)}) collective-permute-start(f32[1,256]{1,0:T(1,128)S(1)} %add.29), channel_id=1, source_target_pairs={{0,2},{2,0},{4,6},{6,4},{8,10},{10,8},{12,14},{14,12},{16,18},{18,... | collective-permute-start | bytes 3080 | tf_op jit(solution)/shard_map/ppermute | solution.py:349

commit v6 on v5

--- a/solution.py
+++ b/solution.py
@@ -67,13 +67,14 @@
 
 
 def probs_kernel(at_ref, q_ref, k_ref, up_ref, p_ref, dv_ref, bias_ref, s_ref, dv_acc):
-    rows = lax.broadcasted_iota(jnp.int32, (COUNT, COUNT), 0)
-    cols = lax.broadcasted_iota(jnp.int32, (COUNT, COUNT), 1)
-    start = jnp.zeros((COUNT, COUNT), jnp.int32)
+    row = lax.broadcasted_iota(jnp.int32, (COUNT, 1), 0)
+    start = jnp.zeros((COUNT, 1), jnp.int32)
     end = jnp.int32(0)
     for doc in range(3):
         end = end + at_ref[5 + doc]
-        start = jnp.where(rows >= end, end, start)
+        start = jnp.where(row >= end, end, start)
+    rows = lax.broadcasted_iota(jnp.int32, (COUNT, COUNT), 0)
+    cols = lax.broadcasted_iota(jnp.int32, (COUNT, COUNT), 1)
     bias_ref[...] = jnp.where((cols <= rows) & (cols >= start), 0.0, -1e30).astype(F32)
     dv_acc[...] = jnp.zeros_like(dv_acc)
     for i in range(BLOCKS):
@@ -95,27 +96,33 @@
 PROBS_SCRATCH = [pltpu.VMEM((COUNT, COUNT), F32), pltpu.VMEM((GROUP * BLOCK, COUNT), F32), pltpu.VMEM((HEAD, COUNT), F32)]
 
 
-def first_probs_kernel(at_ref, q_hbm, k_hbm, up_hbm, p_ref, dv_ref, q_ref, k_ref, up_ref, sems, *scratch):
+def first_probs_kernel(
+    at_ref, q_hbm, k_hbm, up_hbm, hidden_hbm, p_ref, dv_ref, hidden_out, q_ref, k_ref, up_ref, sems, *scratch
+):
     copies = [
         pltpu.make_async_copy(a.at[:, pl.ds(0, b.shape[1])], b, sems.at[j])
         for j, (a, b) in enumerate(((q_hbm, q_ref), (k_hbm, k_ref), (up_hbm, up_ref)))
     ]
     for copy in copies:
         copy.start()
+    whole = pltpu.make_async_copy(hidden_hbm, hidden_out, sems.at[3])
+    whole.start()
     for copy in copies:
         copy.wait()
     probs_kernel(at_ref, q_ref, k_ref, up_ref, p_ref, dv_ref, *scratch)
-
-
-def probs_part(g, at, queries, keys, upstream, dv, after):
+    whole.wait()
+
+
+def probs_part(g, at, queries, keys, upstream, dv, after, hidden=None):
     wide = pl.BlockSpec((COUNT, WIDE), lambda i: (0, g))
     narrow = pl.BlockSpec((COUNT, HEAD), lambda i: (0, g))
     outs = [shape(GROUP, COUNT, COUNT), shape(COUNT, 4 * HEAD, dtype=F32)]
-    if g == 0:
+    if hidden is not None:
         blocks = [pltpu.VMEM((COUNT, WIDE), BF16), pltpu.VMEM((COUNT, HEAD), BF16), pltpu.VMEM((COUNT, WIDE), BF16)]
         return call(
-            first_probs_kernel, "probs_part", outs, [(SMEM, at), (HBM, queries), (HBM, keys), (HBM, upstream)], after,
-            out_specs=[VMEM, narrow], grid=(1,), scratch_shapes=blocks + [pltpu.SemaphoreType.DMA((3,))] + PROBS_SCRATCH,
+            first_probs_kernel, "probs_part", outs + [shape(*hidden.shape)],
+            [(SMEM, at), (HBM, queries), (HBM, keys), (HBM, upstream), (HBM, hidden)], after, out_specs=[VMEM, narrow, ANY],
+            grid=(1,), scratch_shapes=blocks + [pltpu.SemaphoreType.DMA((4,))] + PROBS_SCRATCH,
         )
 
     def kernel(*refs):
@@ -194,16 +201,15 @@
     out_ref[pl.ds(pl.multiple_of((1 - c) * SHARD, SHARD), SHARD), :] = other_ref[:, own_columns(at_ref)]
 
 
-def copy_kernel(in_ref, out_ref, sem):
-    copy = pltpu.make_async_copy(in_ref, out_ref, sem)
-    copy.start()
-    copy.wait()
-
-
 def join_kernel(own_ref, other_ref, out_ref):
     n = own_ref.shape[0]
     out_ref[:n, :] = own_ref[...]
     out_ref[n:, :] = other_ref[...]
+
+
+def join_take_kernel(at_ref, own_ref, other_ref, dv_ref, out_ref, dv_out):
+    join_kernel(own_ref, other_ref, out_ref)
+    dv_out[...] = dv_ref[:, pl.ds(pl.multiple_of((1 - at_ref[3]) * HALF, HALF), HALF)]
 
 
 def core_join_kernel(at_ref, own_ref, got1, got2, got3, first_ref, second_ref):
@@ -255,10 +261,11 @@
     cols = own_columns(at_ref)
     scale = scale_ref[:, cols]
     sums = jnp.zeros((1, HALF), F32)
-    for hidden_ref, dv_ref, values_ref in ((other_ref, dv_other, theirs_ref), (own_ref, dv_own, mine_ref)):
+    terms = ((other_ref, dv_other[...], theirs_ref), (own_ref, dv_own[:, cols], mine_ref))
+    for hidden_ref, dv, values_ref in terms:
         raw = dot(hidden_ref[...], codes_ref[...], (1, 0))
         values_ref[...] = (raw * scale).astype(BF16)
-        sums += jnp.sum(raw * dv_ref[:, cols], axis=0, keepdims=True)
+        sums += jnp.sum(raw * dv, axis=0, keepdims=True)
     sums_ref[...] = sums
     s, half = at_ref[4], DEPTH // 2
     kept_ref[...] = codes_ref[pl.ds(pl.multiple_of(s * half, half), half), :]
@@ -280,35 +287,37 @@
     )
 
 
-def codes_join_kernel(kept_ref, near_ref, beside_ref, out_ref):
-    half = DEPTH // 2
-    out_ref[:half, :] = kept_ref[...]
-    out_ref[half : half + NEAR, :] = near_ref[2 * COUNT :, :]
-    out_ref[half + NEAR :, :] = beside_ref[...]
+def codes_join_kernel(near_ref, beside_ref, out_ref):
+    out_ref[:NEAR, :] = near_ref[2 * COUNT :, :]
+    out_ref[NEAR:, :] = beside_ref[...]
 
 
 BATCH = 512
 
 
-def hidden_kernel(at_ref, dv_ref, scale_ref, near_ref, codes_ref, far_ref, out_ref, token_ref):
+def hidden_terms(c, dv_ref, scale_ref, near_ref, own_codes, seq_codes):
+    cols = pl.ds(pl.multiple_of(c * HALF, HALF), HALF)
+    own = (dv_ref[:, cols] * scale_ref[:, cols]).astype(BF16)
+    far = near_ref[pl.ds(pl.multiple_of(c * COUNT, COUNT), COUNT), :]
+    for i in range(0, DEPTH // 2, BATCH):
+        rows = pl.ds(i, BATCH)
+        yield rows, dot(own, own_codes[rows, :], (1, 1)) + dot(far, seq_codes[rows, :], (1, 1))
+
+
+def own_terms_kernel(at_ref, dv_ref, scale_ref, near_ref, own_codes, seq_codes, out_ref):
+    for rows, total in hidden_terms(at_ref[3], dv_ref, scale_ref, near_ref, own_codes, seq_codes):
+        out_ref[:, rows] = total
+
+
+def last_kernel(
+    at_ref, dv_ref, scale_ref, near_ref, own_codes, seq_codes, part_ref, own0, own1, far0, far1, out_ref, sums_ref
+):
     c = at_ref[3]
-    terms = []
-    for other, ref in enumerate((codes_ref, far_ref)):
-        cols = pl.ds(pl.multiple_of((c ^ other) * HALF, HALF), HALF)
-        own = (dv_ref[:, cols] * scale_ref[:, cols]).astype(BF16)
-        rows = pl.ds(pl.multiple_of((c ^ other) * COUNT, COUNT), COUNT)
-        terms += [(own, ref, 0), (near_ref[rows, :], ref, DEPTH // 2)]
-    for i in range(0, DEPTH // 2, BATCH):
-        total = sum(dot(a, b[pl.ds(base + i, BATCH), :], (1, 1)) for a, b, base in terms)
-        out_ref[:, pl.ds(i, BATCH)] = total.astype(BF16)
-    token_ref[...] = jnp.zeros_like(token_ref)
-
-
-def hidden_part(at, *arrays, after):
-    return call(
-        hidden_kernel, "hidden_part", [shape(COUNT, DEPTH // 2), TOKEN],
-        [(SMEM, at)] + [(VMEM, a) for a in arrays], after,
-    )
+    own, far = own0[...] + own1[...], far0[...] + far1[...]
+    sums_ref[:, :HALF] = jnp.where(c == 0, own, far) * scale_ref[:, :HALF]
+    sums_ref[:, HALF:] = jnp.where(c == 0, far, own) * scale_ref[:, HALF:]
+    for rows, total in hidden_terms(1 - c, dv_ref, scale_ref, near_ref, own_codes, seq_codes):
+        out_ref[:, rows] = (total + part_ref[:, rows]).astype(BF16)
 
 
 def add_kernel(a_ref, b_ref, out_ref):
@@ -364,20 +373,25 @@
     for bit, heads in ((4, (0,)), (2, (1, 2)), (1, (3,))):
         got = send(rows, z_swap(bit))
         for g in heads:
-            p, dv = probs_part(g, at, queries, keys, upstream, dv, (rows,))
+            if g == 0:
+                p, dv, hidden = probs_part(g, at, queries, keys, upstream, dv, (rows,), hidden)
+            else:
+                p, dv = probs_part(g, at, queries, keys, upstream, dv, (rows,))
             probs.append(p)
         n = rows.shape[0]
         ins = [(VMEM, rows), (VMEM, got)]
-        if bit > 1:
+        if bit == 4:
+            rows, hidden = call(join_kernel, "join", shape(2 * n, HALF), ins, (p,), (hidden,))
+            hidden_other = send(hidden, C_SWAP)
+        elif bit == 2:
             rows = call(join_kernel, "join", shape(2 * n, HALF), ins, (p,))
         else:
-            hidden = call(
-                copy_kernel, "copy", shape(*hidden.shape), [(ANY, hidden)], (rows,),
-                out_specs=[ANY], scratch_shapes=[pltpu.SemaphoreType.DMA],
+            rows, dv_half = call(
+                join_take_kernel, "join", [shape(2 * n, HALF), shape(COUNT, HALF, dtype=F32)],
+                [(SMEM, at)] + ins + [(VMEM, dv)], (hidden_other,),
             )
-            rows, hidden, dv = call(join_kernel, "join", shape(2 * n, HALF), ins, (p,), (hidden, dv))
     got = [send(rows, core_pairs(X_SWAP if k == 1 else [], y_shift(k))) for k in (1, 2, 3)]
-    hidden_other, dv_other = send(hidden, C_SWAP), send(dv, C_SWAP)
+    dv_other = send(dv_half, C_SWAP)
     n = rows.shape[0]
     first, second = call(
         core_join_kernel, "join", [shape(2 * n, HALF)] * 2, [(SMEM, at)] + [(VMEM, a) for a in [rows] + got],
@@ -399,22 +413,28 @@
         if step < 4:
             *held, token = grads_part(step, at, queries, keys, upstream, mine, values_far, probs[step], held, (sums,))
             if step == 0:
-                through = (near, beside)
-        elif step == 4:
-            token = codes = call(
-                codes_join_kernel, "join", shape(DEPTH, HALF), [(VMEM, kept), (VMEM, near), (VMEM, beside)], (sums,)
-            )
+                through = (near, beside, kept)
+        elif step == 5:
+            codes = call(codes_join_kernel, "join", shape(DEPTH // 2, HALF), [(VMEM, near), (VMEM, beside)], (sums,))
             codes_far = send(codes, C_SWAP)
+            break
+        ins = [(VMEM, sums), (VMEM, got)]
+        after = () if step == 4 else (token,)
+        if through:
+            sums, near, beside, kept = call(add_kernel, "add", shape(1, HALF, dtype=F32), ins, after, through)
+            kept_far = send(kept, C_SWAP)
         else:
-            grad_hidden, token = hidden_part(at, dv, scale, near, codes, codes_far, after=(sums,))
-        ins = [(VMEM, sums), (VMEM, got)]
-        if through:
-            sums, near, beside = call(add_kernel, "add", shape(1, HALF, dtype=F32), ins, (token,), through)
-        else:
-            sums = call(add_kernel, "add", shape(1, HALF, dtype=F32), ins, (token,))
-    far = send(sums, C_SWAP)
-    both = jnp.concatenate([jnp.where(me % 2 == 0, sums, far), jnp.where(me % 2 == 0, far, sums)], axis=1)
-    return held[0], held[1], grad_hidden, (both * scale).reshape(-1)
+            sums = call(add_kernel, "add", shape(1, HALF, dtype=F32), ins, after)
+    far = [send(sums, C_SWAP), send(sums, pairs(lambda z, y, x, c: (z ^ 4, y, x, c ^ 1)))]
+    base = [(SMEM, at), (VMEM, dv), (VMEM, scale), (VMEM, near)]
+    part = call(
+        own_terms_kernel, "own_terms", shape(COUNT, DEPTH // 2, dtype=F32), base + [(VMEM, kept), (VMEM, codes)], (sums,)
+    )
+    grad_hidden, last = call(
+        last_kernel, "last", [shape(COUNT, DEPTH // 2), shape(1, 2 * HALF, dtype=F32)],
+        base + [(VMEM, a) for a in [kept_far, codes_far, part, sums, got] + far],
+    )
+    return held[0], held[1], grad_hidden, last.reshape(-1)
 
 
 def solution(mesh):

time: 103 us -> 105 us (1.019)
  starting transfers between devices: 39.2 us -> 45.6 us
  waiting for transfers between devices: 32.1 us -> 26.6 us
    ppermute x21 -> x23, starting transfers between devices: 37.5 us -> 43.9 us  [send(): return lax.ppermute(x, 'dp', perm)]
    ppermute x1, waiting for transfers between devices: 5.36 us -> 0.01 us  [shards(): near = lax.ppermute(near, 'seq', SEQ_SWAP)]
    pallas_call x24 -> x23, Pallas kernels: 29.7 us -> 30.7 us  [call(): pl.pallas_call(run, in_specs=list(specs) + [ANY] * (len(after) + len(thro...]
    ppermute x21 -> x23, waiting for transfers between devices: 25.9 us -> 26.3 us  [send(): return lax.ppermute(x, 'dp', perm)]
  transfers between devices with their start and end apart: 23 -> 25, of which waited for: 12 -> 9; matrix products, arithmetic and copies ran while one was open for 1% -> 1% of each run, Pallas kernels for 25% -> 22%
where the time goes in v6:
time: 105 us
  starting transfers between devices  45.6 us (43%)
  Pallas kernels  30.7 us (29%)
  waiting for transfers between devices  26.6 us (25%)
  local copies, waits for them, and re-layouts  1.08 us (1%)
    ppermute x23, starting transfers between devices, send(): return lax.ppermute(x, 'dp', perm)  43.9 us
    pallas_call x23, Pallas kernels, call(): pl.pallas_call(run, in_specs=list(specs) + [ANY] * (len(after) + len(thro...  30.7 us
    ppermute x23, waiting for transfers between devices, send(): return lax.ppermute(x, 'dp', perm)  26.3 us
  transfers between devices with their start and end apart: 25, of which 9 were waited for; matrix products, arithmetic and copies ran while one was open for 1% of the time, Pallas kernels for 22%

profile of v6, /device:TPU:1, one launch (start us, length us, event | category | flops | bytes accessed | tf_op | source)
XLA Modules:
  0.0 104.9 jit_solution(7649290430198208373)
XLA Ops:
  0.6 3.3 %collective-permute-start = (bf16[32,512]{1,0:T(8,128)(2,1)}, bf16[32,512]{1,0:T(8,128)(2,1)S(1)}, u32[]{:S(2)}, u32[]{:S(2)}) collective-permute-start(bf16[32,512]{1,0:T(8,128)(2,1)} %refs_1_.9), channel_id=1, source_target_pairs={{0,2},{2,0},{4,6},{6,4},{8,10},{10,8},{12,14},{14,12},{16,18},{18,... | collective-permute-start | bytes 98312 | tf_op jit(solution)/shard_map/ppermute | solution.py:358
  4.0 0.7 slice_bitcast_fusion
  4.7 1.3 %own.1.refs_1_ = bf16[32,256]{1,0:T(8,128)(2,1)S(1)} custom-call(s32[8]{0:T(128)S(1)} %concatenate.3.refs_0_, bf16[32,512]{1,0:T(8,128)(2,1)} %refs_1_.9), custom_call_target="tpu_custom_call" | custom-call | flops 1000 | bytes 1000 | tf_op jit(solution)/shard_map/own/pallas_call | solution.py:53
  6.0 0.5 join.6.refs_5_.refs_0_
  6.5 5.3 %collective-permute-start.1 = (bf16[64,256]{1,0:T(8,128)(2,1)S(1)}, bf16[64,256]{1,0:T(8,128)(2,1)S(1)}, u32[]{:S(2)}, u32[]{:S(2)}) collective-permute-start(bf16[64,256]{1,0:T(8,128)(2,1)S(1)} %join.6.refs_5_.refs_0_), channel_id=1, source_target_pairs={{0,128},{2,130},{4,132},{6,134},{8,136},{10,138},{12,140},{14,142}... | collective-permute-start | bytes 98312 | tf_op jit(solution)/shard_map/ppermute | solution.py:358
  11.8 3.4 %probs_part.4 = (bf16[4,384,384]{2,1,0:T(8,128)(2,1)S(1)}, f32[384,512]{1,0:T(8,128)S(1)}, bf16[384,4096]{1,0:T(8,128)(2,1)S(1)}) custom-call(s32[8]{0:T(128)S(1)} %concatenate.3.refs_0_, bf16[384,2048]{1,0:T(8,128)(2,1)} %refs_1_.17, bf16[384,512]{1,0:T(8,128)(2,1)} %refs_2_.15, bf16[384,2048]{1,0:T(8,128)(2,1)} %refs_3_.15, bf16[384,4096]{1,0:T(8,128)(2,1)} %refs_4_.1, ...), custom_call_target="tpu_custom_call" | custom-call | flops 1000 | bytes 1000 | tf_op jit(solution)/shard_map/probs_part/pallas_call | solution.py:53
  15.3 0.4 collective-permute-start.2
  15.7 1.2 %collective-permute-start.3 = (bf16[128,256]{1,0:T(8,128)(2,1)S(1)}, bf16[128,256]{1,0:T(8,128)(2,1)S(1)}, u32[]{:S(2)}, u32[]{:S(2)}) collective-permute-start(bf16[128,256]{1,0:T(8,128)(2,1)S(1)} %get-tuple-element.47.refs_5_.refs_0_), channel_id=1, source_target_pairs={{0,64},{2,66},{4,68},{6,70},{8,72},{10,74},{12,76},{14,78},{16,80}... | collective-permute-start | bytes 196616 | tf_op jit(solution)/shard_map/ppermute | solution.py:358
  16.9 0.3 copy-done.1
  17.2 2.2 %probs_part.5 = (bf16[4,384,384]{2,1,0:T(8,128)(2,1)S(1)}, f32[384,512]{1,0:T(8,128)S(1)}) custom-call(s32[8]{0:T(128)S(1)} %concatenate.3.refs_0_, bf16[384,2048]{1,0:T(8,128)(2,1)S(1)} %copy-done, bf16[384,512]{1,0:T(8,128)(2,1)S(1)} %copy-done.2, bf16[384,2048]{1,0:T(8,128)(2,1)S(1)} %copy-done.1, ...), custom_call_target="tpu_custom_call", output_to_operand_aliasing={{1}: (4, {})} | custom-call | flops 1000 | bytes 1000 | tf_op jit(solution)/shard_map/probs_part/pallas_call | solution.py:53
  19.4 2.2 %probs_part.6 = (bf16[4,384,384]{2,1,0:T(8,128)(2,1)S(1)}, f32[384,512]{1,0:T(8,128)S(1)}) custom-call(s32[8]{0:T(128)S(1)} %concatenate.3.refs_0_, bf16[384,2048]{1,0:T(8,128)(2,1)S(1)} %copy-done, bf16[384,512]{1,0:T(8,128)(2,1)S(1)} %copy-done.2, bf16[384,2048]{1,0:T(8,128)(2,1)S(1)} %copy-done.1, ...), custom_call_target="tpu_custom_call", output_to_operand_aliasing={{1}: (4, {})} | custom-call | flops 1000 | bytes 1000 | tf_op jit(solution)/shard_map/probs_part/pallas_call | solution.py:53
  21.6 0.8 collective-permute-start.4
  22.4 2.2 %probs_part.7 = (bf16[4,384,384]{2,1,0:T(8,128)(2,1)S(1)}, f32[384,512]{1,0:T(8,128)S(1)}) custom-call(s32[8]{0:T(128)S(1)} %concatenate.3.refs_0_, bf16[384,2048]{1,0:T(8,128)(2,1)S(1)} %copy-done, bf16[384,512]{1,0:T(8,128)(2,1)S(1)} %copy-done.2, bf16[384,2048]{1,0:T(8,128)(2,1)S(1)} %copy-done.1, ...), custom_call_target="tpu_custom_call", output_to_operand_aliasing={{1}: (4, {})} | custom-call | flops 1000 | bytes 1000 | tf_op jit(solution)/shard_map/probs_part/pallas_call | solution.py:53
  24.6 0.9 collective-permute-done.4.refs_2_
  25.5 0.6 join.9
  26.1 2.2 %collective-permute-start.5 = (f32[384,256]{1,0:T(8,128)S(1)}, f32[384,256]{1,0:T(8,128)S(1)}, u32[]{:S(2)}, u32[]{:S(2)}) collective-permute-start(f32[384,256]{1,0:T(8,128)S(1)} %get-tuple-element.52), channel_id=1, source_target_pairs={{0,2},{2,0},{4,6},{6,4},{8,10},{10,8},{12,14},{14,12},{16,18},{18,... | collective-permute-start | bytes 1179656 | tf_op jit(solution)/shard_map/ppermute | solution.py:358
  28.3 4.6 %collective-permute-start.8 = (bf16[512,256]{1,0:T(8,128)(2,1)S(1)}, bf16[512,256]{1,0:T(8,128)(2,1)S(1)}, u32[]{:S(2)}, u32[]{:S(2)}) collective-permute-start(bf16[512,256]{1,0:T(8,128)(2,1)S(1)} %get-tuple-element.53.refs_1_), channel_id=1, source_target_pairs={{2,26},{6,30},{10,2},{14,6},{18,10},{22,14},{26,18},{30,22},{34,58... | collective-permute-start | bytes 786440 | tf_op jit(solution)/shard_map/ppermute | solution.py:358
  32.9 2.3 %collective-permute-start.7 = (bf16[512,256]{1,0:T(8,128)(2,1)S(1)}, bf16[512,256]{1,0:T(8,128)(2,1)S(1)}, u32[]{:S(2)}, u32[]{:S(2)}) collective-permute-start(bf16[512,256]{1,0:T(8,128)(2,1)S(1)} %get-tuple-element.53.refs_1_), channel_id=1, source_target_pairs={{2,18},{6,22},{10,26},{14,30},{18,2},{22,6},{26,10},{30,14},{34,50... | collective-permute-start | bytes 786440 | tf_op jit(solution)/shard_map/ppermute | solution.py:358
  35.2 0.8 collective-permute-start.6
  36.0 0.3 collective-permute-done.8.refs_4_
  36.2 5.4 %collective-permute-done.7.refs_3_ = bf16[512,256]{1,0:T(8,128)(2,1)S(1)} collective-permute-done((bf16[512,256]{1,0:T(8,128)(2,1)S(1)}, bf16[512,256]{1,0:T(8,128)(2,1)S(1)}, u32[]{:S(2)}, u32[]{:S(2)}) %collective-permute-start.7) | collective-permute-done | bytes 262176 | tf_op jit(solution)/shard_map/ppermute | solution.py:358
  41.7 4.6 %collective-permute-done.6.refs_2_ = bf16[512,256]{1,0:T(8,128)(2,1)S(1)} collective-permute-done((bf16[512,256]{1,0:T(8,128)(2,1)S(1)}, bf16[512,256]{1,0:T(8,128)(2,1)S(1)}, u32[]{:S(2)}, u32[]{:S(2)}) %collective-permute-start.6) | collective-permute-done | bytes 262176 | tf_op jit(solution)/shard_map/ppermute | solution.py:358
  46.2 0.6 join.10
  46.9 2.8 %collective-permute-start.10 = (bf16[1024,256]{1,0:T(8,128)(2,1)S(1)}, bf16[1024,256]{1,0:T(8,128)(2,1)S(1)}, u32[]{:S(2)}, u32[]{:S(2)}) collective-permute-start(bf16[1024,256]{1,0:T(8,128)(2,1)S(1)} %get-tuple-element.55.refs_7_), channel_id=1, source_target_pairs={{0,16},{4,20},{8,24},{12,28},{16,0},{20,4},{24,8},{28,12},{32,48},... | collective-permute-start | bytes 1572872 | tf_op jit(solution)/shard_map/ppermute | solution.py:358
  49.7 0.7 collective-permute-start.11
  50.3 0.3 collective-permute-start.9
  50.7 5.8 %collective-permute-done.10.refs_9_ = bf16[1024,256]{1,0:T(8,128)(2,1)S(1)} collective-permute-done((bf16[1024,256]{1,0:T(8,128)(2,1)S(1)}, bf16[1024,256]{1,0:T(8,128)(2,1)S(1)}, u32[]{:S(2)}, u32[]{:S(2)}) %collective-permute-start.10) | collective-permute-done | bytes 524320 | tf_op jit(solution)/shard_map/ppermute | solution.py:358
  56.5 5.6 %collective-permute-done.9.refs_8_ = bf16[1024,256]{1,0:T(8,128)(2,1)S(1)} collective-permute-done((bf16[1024,256]{1,0:T(8,128)(2,1)S(1)}, bf16[1024,256]{1,0:T(8,128)(2,1)S(1)}, u32[]{:S(2)}, u32[]{:S(2)}) %collective-permute-start.9) | collective-permute-done | bytes 524320 | tf_op jit(solution)/shard_map/ppermute | solution.py:358
  62.1 2.9 %raw_part.1 = (bf16[384,256]{1,0:T(8,128)(2,1)S(1)}, bf16[384,256]{1,0:T(8,128)(2,1)S(1)}, f32[1,256]{1,0:T(1,128)S(1)}, bf16[2048,256]{1,0:T(8,128)(2,1)S(1)}, ...) custom-call(s32[8]{0:T(128)S(1)} %concatenate.3.refs_0_, bf16[384,4096]{1,0:T(8,128)(2,1)S(1)} %get-tuple-element.45.refs_1_, ...), custom_call_target="tpu_custom_call" | custom-call | flops 1000 | bytes 1000 | tf_op jit(solution)/shard_map/raw_part/pallas_call | solution.py:53
  65.1 2.8 %collective-permute-start.13 = (f32[1,256]{1,0:T(1,128)S(1)}, f32[1,256]{1,0:T(1,128)S(1)}, u32[]{:S(2)}, u32[]{:S(2)}) collective-permute-start(f32[1,256]{1,0:T(1,128)S(1)} %get-tuple-element.60.refs_7_.refs_0_), channel_id=1, source_target_pairs={{0,4},{2,6},{4,0},{6,2},{8,12},{10,14},{12,8},{14,10},{16,20},{18,... | collective-permute-start | bytes 3080 | tf_op jit(solution)/shard_map/ppermute | solution.py:358
  67.9 2.6 %grads_part.4 = (bf16[384,2048]{1,0:T(8,128)(2,1)}, bf16[384,512]{1,0:T(8,128)(2,1)}, f32[8,128]{1,0:T(8,128)S(1)}) custom-call(s32[8]{0:T(128)S(1)} %concatenate.3.refs_0_, bf16[384,2048]{1,0:T(8,128)(2,1)S(1)} %copy-done, bf16[384,512]{1,0:T(8,128)(2,1)S(1)} %copy-done.2, bf16[384,2048]{1,0:T(8,128)(2,1)S(1)} %copy-done.1, ...), custom_call_target="tpu_custom_call" | custom-call | flops 1000 | bytes 1000 | tf_op jit(solution)/shard_map/grads_part/pallas_call | solution.py:53
  70.6 0.4 collective-permute-start.16
  70.9 1.3 %collective-permute-start.18 = (bf16[1408,256]{1,0:T(8,128)(2,1)S(1)}, bf16[1408,256]{1,0:T(8,128)(2,1)S(1)}, u32[]{:S(2)}, u32[]{:S(2)}) collective-permute-start(bf16[1408,256]{1,0:T(8,128)(2,1)S(1)} %get-tuple-element.78), channel_id=1, source_target_pairs={{0,5},{1,4},{2,7},{3,6},{4,1},{5,0},{6,3},{7,2},{8,13},{9,12},{10,... | collective-permute-start | bytes 2162696 | tf_op jit(solution)/shard_map/ppermute | solution.py:410
  72.3 2.6 %grads_part.5 = (bf16[384,2048]{1,0:T(8,128)(2,1)}, bf16[384,512]{1,0:T(8,128)(2,1)}, f32[8,128]{1,0:T(8,128)S(1)}) custom-call(s32[8]{0:T(128)S(1)} %concatenate.3.refs_0_, bf16[384,2048]{1,0:T(8,128)(2,1)S(1)} %copy-done, bf16[384,512]{1,0:T(8,128)(2,1)S(1)} %copy-done.2, ...), custom_call_target="tpu_custom_call", output_to_operand_aliasing={{0}: (7, {}), {1}: (8, {})} | custom-call | flops 1000 | bytes 1000 | tf_op jit(solution)/shard_map/grads_part/pallas_call | solution.py:53
  75.0 1.5 %collective-permute-start.15 = (f32[1,256]{1,0:T(1,128)S(1)}, f32[1,256]{1,0:T(1,128)S(1)}, u32[]{:S(2)}, u32[]{:S(2)}) collective-permute-start(f32[1,256]{1,0:T(1,128)S(1)} %add.22.refs_9_.refs_0_), channel_id=1, source_target_pairs={{0,16},{2,18},{4,20},{6,22},{8,24},{10,26},{12,28},{14,30},{16,0},... | collective-permute-start | bytes 3080 | tf_op jit(solution)/shard_map/ppermute | solution.py:358
  76.5 2.6 %grads_part.6 = (bf16[384,2048]{1,0:T(8,128)(2,1)}, bf16[384,512]{1,0:T(8,128)(2,1)}, f32[8,128]{1,0:T(8,128)S(1)}) custom-call(s32[8]{0:T(128)S(1)} %concatenate.3.refs_0_, bf16[384,2048]{1,0:T(8,128)(2,1)S(1)} %copy-done, bf16[384,512]{1,0:T(8,128)(2,1)S(1)} %copy-done.2, ...), custom_call_target="tpu_custom_call", output_to_operand_aliasing={{0}: (7, {}), {1}: (8, {})} | custom-call | flops 1000 | bytes 1000 | tf_op jit(solution)/shard_map/grads_part/pallas_call | solution.py:53
  79.1 0.8 collective-permute-start.19
  80.0 2.6 %grads_part.7 = (bf16[384,2048]{1,0:T(8,128)(2,1)}, bf16[384,512]{1,0:T(8,128)(2,1)}, f32[8,128]{1,0:T(8,128)S(1)}) custom-call(s32[8]{0:T(128)S(1)} %concatenate.3.refs_0_, bf16[384,2048]{1,0:T(8,128)(2,1)S(1)} %copy-done, bf16[384,512]{1,0:T(8,128)(2,1)S(1)} %copy-done.2, ...), custom_call_target="tpu_custom_call", output_to_operand_aliasing={{0}: (7, {}), {1}: (8, {})} | custom-call | flops 1000 | bytes 1000 | tf_op jit(solution)/shard_map/grads_part/pallas_call | solution.py:53
  82.6 1.3 %collective-permute-start.20 = (f32[1,256]{1,0:T(1,128)S(1)}, f32[1,256]{1,0:T(1,128)S(1)}, u32[]{:S(2)}, u32[]{:S(2)}) collective-permute-start(f32[1,256]{1,0:T(1,128)S(1)} %add.24.refs_0_), channel_id=1, source_target_pairs={{0,64},{2,66},{4,68},{6,70},{8,72},{10,74},{12,76},{14,78},{16,80}... | collective-permute-start | bytes 3080 | tf_op jit(solution)/shard_map/ppermute | solution.py:358
  83.9 4.3 %collective-permute-start.17 = (bf16[2048,256]{1,0:T(8,128)(2,1)S(1)}, bf16[2048,256]{1,0:T(8,128)(2,1)S(1)}, u32[]{:S(2)}, u32[]{:S(2)}) collective-permute-start(bf16[2048,256]{1,0:T(8,128)(2,1)S(1)} %get-tuple-element.77.refs_4_), channel_id=1, source_target_pairs={{0,2},{2,0},{4,6},{6,4},{8,10},{10,8},{12,14},{14,12},{16,18},{18,... | collective-permute-start | bytes 3145736 | tf_op jit(solution)/shard_map/ppermute | solution.py:358
  88.2 0.4 collective-permute-done.18.refs_1_
  88.6 2.7 %collective-permute-start.21 = (bf16[2048,256]{1,0:T(8,128)(2,1)S(1)}, bf16[2048,256]{1,0:T(8,128)(2,1)S(1)}, u32[]{:S(2)}, u32[]{:S(2)}) collective-permute-start(bf16[2048,256]{1,0:T(8,128)(2,1)S(1)} %join.11.refs_5_), channel_id=1, source_target_pairs={{0,2},{2,0},{4,6},{6,4},{8,10},{10,8},{12,14},{14,12},{16,18},{18,... | collective-permute-start | bytes 3145736 | tf_op jit(solution)/shard_map/ppermute | solution.py:358
  91.3 4.3 %collective-permute-start.24 = (f32[1,256]{1,0:T(1,128)S(1)}, f32[1,256]{1,0:T(1,128)S(1)}, u32[]{:S(2)}, u32[]{:S(2)}) collective-permute-start(f32[1,256]{1,0:T(1,128)S(1)} %add.25.refs_2_.refs_6_.refs_7_), channel_id=1, source_target_pairs={{0,130},{2,128},{4,134},{6,132},{8,138},{10,136},{12,142},{14,140}... | collective-permute-start | bytes 3080 | tf_op jit(solution)/shard_map/ppermute | solution.py:358
  95.7 0.2 collective-permute-start.23
  95.8 1.2 %collective-permute-start.22 = (f32[1,256]{1,0:T(1,128)S(1)}, f32[1,256]{1,0:T(1,128)S(1)}, u32[]{:S(2)}, u32[]{:S(2)}) collective-permute-start(f32[1,256]{1,0:T(1,128)S(1)} %add.25.refs_2_.refs_6_.refs_7_), channel_id=1, source_target_pairs={{0,128},{2,130},{4,132},{6,134},{8,136},{10,138},{12,140},{14,142}... | collective-permute-start | bytes 3080 | tf_op jit(solution)/shard_map/ppermute | solution.py:358
  97.1 1.5 %own_terms.1.refs_6_ = f32[384,2048]{1,0:T(8,128)S(1)} custom-call(s32[8]{0:T(128)S(1)} %concatenate.3.refs_0_, f32[384,512]{1,0:T(8,128)S(1)} %get-tuple-element.51.refs_3_.refs_1_, f32[1,512]{1,0:T(1,128)S(1)} %bitcast.10, bf16[1408,256]{1,0:T(8,128)(2,1)S(1)} %collective-permute-done.16.refs_0_.refs_3_, bf16[2048,256]{1,0:T(8,128)(2,1)S(1)} %get-tuple-element.77.refs_4_, ...), custom_call_target="tpu_custom_call" | custom-call | flops 1000 | bytes 1000 | tf_op jit(solution)/shard_map/own_terms/pallas_call | solution.py:53
  98.7 3.5 %collective-permute-done.22.refs_8_ = f32[1,256]{1,0:T(1,128)S(1)} collective-permute-done((f32[1,256]{1,0:T(1,128)S(1)}, f32[1,256]{1,0:T(1,128)S(1)}, u32[]{:S(2)}, u32[]{:S(2)}) %collective-permute-start.22) | collective-permute-done | bytes 1056 | tf_op jit(solution)/shard_map/ppermute | solution.py:358
  102.2 2.7 %last.1 = (bf16[384,2048]{1,0:T(8,128)(2,1)}, f32[1,512]{1,0:T(1,128)}) custom-call(s32[8]{0:T(128)S(1)} %concatenate.3.refs_0_, f32[384,512]{1,0:T(8,128)S(1)} %get-tuple-element.51.refs_3_.refs_1_, f32[1,512]{1,0:T(1,128)S(1)} %bitcast.11, bf16[1408,256]{1,0:T(8,128)(2,1)S(1)} %collective-permute-done.16.refs_0_.refs_3_, ...), custom_call_target="tpu_custom_call" | custom-call | flops 1000 | bytes 1000 | tf_op jit(solution)/shard_map/last/pallas_call | solution.py:53
  (35 shorter events, 0.5 us)
Async XLA Ops:
  0.6 5.4 %collective-permute-start = (bf16[32,512]{1,0:T(8,128)(2,1)}, bf16[32,512]{1,0:T(8,128)(2,1)S(1)}, u32[]{:S(2)}, u32[]{:S(2)}) collective-permute-start(bf16[32,512]{1,0:T(8,128)(2,1)} %refs_1_.9), channel_id=1, source_target_pairs={{0,2},{2,0},{4,6},{6,4},{8,10},{10,8},{12,14},{14,12},{16,18},{18,... | collective-permute-start | bytes 98312 | tf_op jit(solution)/shard_map/ppermute | solution.py:358
  6.5 8.7 %collective-permute-start.1 = (bf16[64,256]{1,0:T(8,128)(2,1)S(1)}, bf16[64,256]{1,0:T(8,128)(2,1)S(1)}, u32[]{:S(2)}, u32[]{:S(2)}) collective-permute-start(bf16[64,256]{1,0:T(8,128)(2,1)S(1)} %join.6.refs_5_.refs_0_), channel_id=1, source_target_pairs={{0,128},{2,130},{4,132},{6,134},{8,136},{10,138},{12,140},{14,142}... | collective-permute-start | bytes 98312 | tf_op jit(solution)/shard_map/ppermute | solution.py:358
  15.2 1.6 %copy-start = (bf16[384,2048]{1,0:T(8,128)(2,1)S(1)}, bf16[384,2048]{1,0:T(8,128)(2,1)}, u32[]{:S(2)}) copy-start(bf16[384,2048]{1,0:T(8,128)(2,1)} %refs_1_.17) | copy-start | bytes 4718596
  15.3 1.9 %copy-start.1 = (bf16[384,2048]{1,0:T(8,128)(2,1)S(1)}, bf16[384,2048]{1,0:T(8,128)(2,1)}, u32[]{:S(2)}) copy-start(bf16[384,2048]{1,0:T(8,128)(2,1)} %refs_3_.15) | copy-start | bytes 4718596
  15.3 1.9 %copy-start.2 = (bf16[384,512]{1,0:T(8,128)(2,1)S(1)}, bf16[384,512]{1,0:T(8,128)(2,1)}, u32[]{:S(2)}) copy-start(bf16[384,512]{1,0:T(8,128)(2,1)} %refs_2_.15) | copy-start | bytes 1179652
  15.3 10.2 %collective-permute-start.2 = (bf16[384,4096]{1,0:T(8,128)(2,1)S(1)}, bf16[384,4096]{1,0:T(8,128)(2,1)S(1)}, u32[]{:S(2)}, u32[]{:S(2)}) collective-permute-start(bf16[384,4096]{1,0:T(8,128)(2,1)S(1)} %get-tuple-element.45.refs_1_), channel_id=1, source_target_pairs={{0,2},{2,0},{4,6},{6,4},{8,10},{10,8},{12,14},{14,12},{16,18},{18,... | collective-permute-start | bytes 9437192 | tf_op jit(solution)/shard_map/ppermute | solution.py:358
  15.7 5.9 %collective-permute-start.3 = (bf16[128,256]{1,0:T(8,128)(2,1)S(1)}, bf16[128,256]{1,0:T(8,128)(2,1)S(1)}, u32[]{:S(2)}, u32[]{:S(2)}) collective-permute-start(bf16[128,256]{1,0:T(8,128)(2,1)S(1)} %get-tuple-element.47.refs_5_.refs_0_), channel_id=1, source_target_pairs={{0,64},{2,66},{4,68},{6,70},{8,72},{10,74},{12,76},{14,78},{16,80}... | collective-permute-start | bytes 196616 | tf_op jit(solution)/shard_map/ppermute | solution.py:358
  21.6 3.9 %collective-permute-start.4 = (bf16[256,256]{1,0:T(8,128)(2,1)S(1)}, bf16[256,256]{1,0:T(8,128)(2,1)S(1)}, u32[]{:S(2)}, u32[]{:S(2)}) collective-permute-start(bf16[256,256]{1,0:T(8,128)(2,1)S(1)} %join.8.refs_5_.refs_1_), channel_id=1, source_target_pairs={{0,32},{2,34},{4,36},{6,38},{8,40},{10,42},{12,44},{14,46},{16,48}... | collective-permute-start | bytes 393224 | tf_op jit(solution)/shard_map/ppermute | solution.py:358
  25.5 36.6 %copy-start.3 = (f32[512]{0:T(512)S(1)}, f32[512]{0:T(512)}, u32[]{:S(2)}) copy-start(f32[512]{0:T(512)} %param.11) | copy-start | bytes 6148
  26.1 20.1 %collective-permute-start.5 = (f32[384,256]{1,0:T(8,128)S(1)}, f32[384,256]{1,0:T(8,128)S(1)}, u32[]{:S(2)}, u32[]{:S(2)}) collective-permute-start(f32[384,256]{1,0:T(8,128)S(1)} %get-tuple-element.52), channel_id=1, source_target_pairs={{0,2},{2,0},{4,6},{6,4},{8,10},{10,8},{12,14},{14,12},{16,18},{18,... | collective-permute-start | bytes 1179656 | tf_op jit(solution)/shard_map/ppermute | solution.py:358
  28.3 7.9 %collective-permute-start.8 = (bf16[512,256]{1,0:T(8,128)(2,1)S(1)}, bf16[512,256]{1,0:T(8,128)(2,1)S(1)}, u32[]{:S(2)}, u32[]{:S(2)}) collective-permute-start(bf16[512,256]{1,0:T(8,128)(2,1)S(1)} %get-tuple-element.53.refs_1_), channel_id=1, source_target_pairs={{2,26},{6,30},{10,2},{14,6},{18,10},{22,14},{26,18},{30,22},{34,58... | collective-permute-start | bytes 786440 | tf_op jit(solution)/shard_map/ppermute | solution.py:358
  32.9 8.7 %collective-permute-start.7 = (bf16[512,256]{1,0:T(8,128)(2,1)S(1)}, bf16[512,256]{1,0:T(8,128)(2,1)S(1)}, u32[]{:S(2)}, u32[]{:S(2)}) collective-permute-start(bf16[512,256]{1,0:T(8,128)(2,1)S(1)} %get-tuple-element.53.refs_1_), channel_id=1, source_target_pairs={{2,18},{6,22},{10,26},{14,30},{18,2},{22,6},{26,10},{30,14},{34,50... | collective-permute-start | bytes 786440 | tf_op jit(solution)/shard_map/ppermute | solution.py:358
  35.2 11.0 %collective-permute-start.6 = (bf16[512,256]{1,0:T(8,128)(2,1)S(1)}, bf16[512,256]{1,0:T(8,128)(2,1)S(1)}, u32[]{:S(2)}, u32[]{:S(2)}) collective-permute-start(bf16[512,256]{1,0:T(8,128)(2,1)S(1)} %get-tuple-element.53.refs_1_), channel_id=1, source_target_pairs={{0,4},{4,0},{8,12},{12,8},{16,20},{20,16},{24,28},{28,24},{32,36},... | collective-permute-start | bytes 786440 | tf_op jit(solution)/shard_map/ppermute | solution.py:358
  46.9 9.6 %collective-permute-start.10 = (bf16[1024,256]{1,0:T(8,128)(2,1)S(1)}, bf16[1024,256]{1,0:T(8,128)(2,1)S(1)}, u32[]{:S(2)}, u32[]{:S(2)}) collective-permute-start(bf16[1024,256]{1,0:T(8,128)(2,1)S(1)} %get-tuple-element.55.refs_7_), channel_id=1, source_target_pairs={{0,16},{4,20},{8,24},{12,28},{16,0},{20,4},{24,8},{28,12},{32,48},... | collective-permute-start | bytes 1572872 | tf_op jit(solution)/shard_map/ppermute | solution.py:358
  49.7 6.8 %collective-permute-start.11 = (bf16[1024,256]{1,0:T(8,128)(2,1)S(1)}, bf16[1024,256]{1,0:T(8,128)(2,1)S(1)}, u32[]{:S(2)}, u32[]{:S(2)}) collective-permute-start(bf16[1024,256]{1,0:T(8,128)(2,1)S(1)} %get-tuple-element.54.refs_6_), channel_id=1, source_target_pairs={{0,24},{4,28},{8,0},{12,4},{16,8},{20,12},{24,16},{28,20},{32,56},... | collective-permute-start | bytes 1572872 | tf_op jit(solution)/shard_map/ppermute | solution.py:358
  50.3 11.8 %collective-permute-start.9 = (bf16[1024,256]{1,0:T(8,128)(2,1)S(1)}, bf16[1024,256]{1,0:T(8,128)(2,1)S(1)}, u32[]{:S(2)}, u32[]{:S(2)}) collective-permute-start(bf16[1024,256]{1,0:T(8,128)(2,1)S(1)} %get-tuple-element.54.refs_6_), channel_id=1, source_target_pairs={{0,8},{4,12},{8,16},{12,20},{16,24},{20,28},{24,0},{28,4},{32,40},... | collective-permute-start | bytes 1572872 | tf_op jit(solution)/shard_map/ppermute | solution.py:358
  65.0 2.9 %collective-permute-start.12 = (bf16[384,256]{1,0:T(8,128)(2,1)S(1)}, bf16[384,256]{1,0:T(8,128)(2,1)S(1)}, u32[]{:S(2)}, u32[]{:S(2)}) collective-permute-start(bf16[384,256]{1,0:T(8,128)(2,1)S(1)} %get-tuple-element.57), channel_id=1, source_target_pairs={{0,2},{2,0},{4,6},{6,4},{8,10},{10,8},{12,14},{14,12},{16,18},{18,... | collective-permute-start | bytes 589832 | tf_op jit(solution)/shard_map/ppermute | solution.py:358
  65.1 5.4 %collective-permute-start.13 = (f32[1,256]{1,0:T(1,128)S(1)}, f32[1,256]{1,0:T(1,128)S(1)}, u32[]{:S(2)}, u32[]{:S(2)}) collective-permute-start(f32[1,256]{1,0:T(1,128)S(1)} %get-tuple-element.60.refs_7_.refs_0_), channel_id=1, source_target_pairs={{0,4},{2,6},{4,0},{6,2},{8,12},{10,14},{12,8},{14,10},{16,20},{18,... | collective-permute-start | bytes 3080 | tf_op jit(solution)/shard_map/ppermute | solution.py:358
  70.6 17.6 %collective-permute-start.16 = (bf16[1408,256]{1,0:T(8,128)(2,1)S(1)}, bf16[1408,256]{1,0:T(8,128)(2,1)S(1)}, u32[]{:S(2)}, u32[]{:S(2)}) collective-permute-start(bf16[1408,256]{1,0:T(8,128)(2,1)S(1)} %get-tuple-element.76), channel_id=1, source_target_pairs={{0,1},{1,0},{2,3},{3,2},{4,5},{5,4},{6,7},{7,6},{8,9},{9,8},{10,11... | collective-permute-start | bytes 2162696 | tf_op jit(solution)/shard_map/ppermute | solution.py:409
  70.9 17.6 %collective-permute-start.18 = (bf16[1408,256]{1,0:T(8,128)(2,1)S(1)}, bf16[1408,256]{1,0:T(8,128)(2,1)S(1)}, u32[]{:S(2)}, u32[]{:S(2)}) collective-permute-start(bf16[1408,256]{1,0:T(8,128)(2,1)S(1)} %get-tuple-element.78), channel_id=1, source_target_pairs={{0,5},{1,4},{2,7},{3,6},{4,1},{5,0},{6,3},{7,2},{8,13},{9,12},{10,... | collective-permute-start | bytes 2162696 | tf_op jit(solution)/shard_map/ppermute | solution.py:410
  72.3 2.7 %collective-permute-start.14 = (f32[1,256]{1,0:T(1,128)S(1)}, f32[1,256]{1,0:T(1,128)S(1)}, u32[]{:S(2)}, u32[]{:S(2)}) collective-permute-start(f32[1,256]{1,0:T(1,128)S(1)} %get-tuple-element.67.refs_9_.refs_0_), channel_id=1, source_target_pairs={{0,8},{2,10},{4,12},{6,14},{8,0},{10,2},{12,4},{14,6},{16,24},{18,... | collective-permute-start | bytes 3080 | tf_op jit(solution)/shard_map/ppermute | solution.py:358
  75.0 4.1 %collective-permute-start.15 = (f32[1,256]{1,0:T(1,128)S(1)}, f32[1,256]{1,0:T(1,128)S(1)}, u32[]{:S(2)}, u32[]{:S(2)}) collective-permute-start(f32[1,256]{1,0:T(1,128)S(1)} %add.22.refs_9_.refs_0_), channel_id=1, source_target_pairs={{0,16},{2,18},{4,20},{6,22},{8,24},{10,26},{12,28},{14,30},{16,0},... | collective-permute-start | bytes 3080 | tf_op jit(solution)/shard_map/ppermute | solution.py:358
  79.1 3.5 %collective-permute-start.19 = (f32[1,256]{1,0:T(1,128)S(1)}, f32[1,256]{1,0:T(1,128)S(1)}, u32[]{:S(2)}, u32[]{:S(2)}) collective-permute-start(f32[1,256]{1,0:T(1,128)S(1)} %add.23.refs_9_.refs_0_), channel_id=1, source_target_pairs={{0,32},{2,34},{4,36},{6,38},{8,40},{10,42},{12,44},{14,46},{16,48}... | collective-permute-start | bytes 3080 | tf_op jit(solution)/shard_map/ppermute | solution.py:358
  82.6 5.6 %collective-permute-start.20 = (f32[1,256]{1,0:T(1,128)S(1)}, f32[1,256]{1,0:T(1,128)S(1)}, u32[]{:S(2)}, u32[]{:S(2)}) collective-permute-start(f32[1,256]{1,0:T(1,128)S(1)} %add.24.refs_0_), channel_id=1, source_target_pairs={{0,64},{2,66},{4,68},{6,70},{8,72},{10,74},{12,76},{14,78},{16,80}... | collective-permute-start | bytes 3080 | tf_op jit(solution)/shard_map/ppermute | solution.py:358
  83.9 18.3 %collective-permute-start.17 = (bf16[2048,256]{1,0:T(8,128)(2,1)S(1)}, bf16[2048,256]{1,0:T(8,128)(2,1)S(1)}, u32[]{:S(2)}, u32[]{:S(2)}) collective-permute-start(bf16[2048,256]{1,0:T(8,128)(2,1)S(1)} %get-tuple-element.77.refs_4_), channel_id=1, source_target_pairs={{0,2},{2,0},{4,6},{6,4},{8,10},{10,8},{12,14},{14,12},{16,18},{18,... | collective-permute-start | bytes 3145736 | tf_op jit(solution)/shard_map/ppermute | solution.py:358
  88.6 13.6 %collective-permute-start.21 = (bf16[2048,256]{1,0:T(8,128)(2,1)S(1)}, bf16[2048,256]{1,0:T(8,128)(2,1)S(1)}, u32[]{:S(2)}, u32[]{:S(2)}) collective-permute-start(bf16[2048,256]{1,0:T(8,128)(2,1)S(1)} %join.11.refs_5_), channel_id=1, source_target_pairs={{0,2},{2,0},{4,6},{6,4},{8,10},{10,8},{12,14},{14,12},{16,18},{18,... | collective-permute-start | bytes 3145736 | tf_op jit(solution)/shard_map/ppermute | solution.py:358
  91.3 7.3 %collective-permute-start.24 = (f32[1,256]{1,0:T(1,128)S(1)}, f32[1,256]{1,0:T(1,128)S(1)}, u32[]{:S(2)}, u32[]{:S(2)}) collective-permute-start(f32[1,256]{1,0:T(1,128)S(1)} %add.25.refs_2_.refs_6_.refs_7_), channel_id=1, source_target_pairs={{0,130},{2,128},{4,134},{6,132},{8,138},{10,136},{12,142},{14,140}... | collective-permute-start | bytes 3080 | tf_op jit(solution)/shard_map/ppermute | solution.py:358
  95.7 3.0 %collective-permute-start.23 = (f32[1,256]{1,0:T(1,128)S(1)}, f32[1,256]{1,0:T(1,128)S(1)}, u32[]{:S(2)}, u32[]{:S(2)}) collective-permute-start(f32[1,256]{1,0:T(1,128)S(1)} %add.25.refs_2_.refs_6_.refs_7_), channel_id=1, source_target_pairs={{0,2},{2,0},{4,6},{6,4},{8,10},{10,8},{12,14},{14,12},{16,18},{18,... | collective-permute-start | bytes 3080 | tf_op jit(solution)/shard_map/ppermute | solution.py:358
  95.8 6.3 %collective-permute-start.22 = (f32[1,256]{1,0:T(1,128)S(1)}, f32[1,256]{1,0:T(1,128)S(1)}, u32[]{:S(2)}, u32[]{:S(2)}) collective-permute-start(f32[1,256]{1,0:T(1,128)S(1)} %add.25.refs_2_.refs_6_.refs_7_), channel_id=1, source_target_pairs={{0,128},{2,130},{4,132},{6,134},{8,136},{10,138},{12,140},{14,142}... | collective-permute-start | bytes 3080 | tf_op jit(solution)/shard_map/ppermute | solution.py:358

commit v7 on v6

--- a/solution.py
+++ b/solution.py
@@ -178,7 +178,6 @@
     )
 
 
-Z_ORDER = (0, 4, 2, 6, 1, 5, 3, 7)
 SHARD = 32
 CHIP = 2 * SHARD
 HALF = 256
@@ -189,16 +188,15 @@
     return pl.ds(pl.multiple_of(at_ref[3] * HALF, HALF), HALF)
 
 
-def own_part(at_ref, own_hbm, out_ref, sem):
-    copy = pltpu.make_async_copy(own_hbm.at[:, own_columns(at_ref)], out_ref, sem)
+def first_join(own_hbm, other_ref, out_ref, sem):
+    c = lax.rem(lax.axis_index("dp"), 2)
+    cols = pl.ds(pl.multiple_of(c * HALF, HALF), HALF)
+    copy = pltpu.make_async_copy(
+        own_hbm.at[:, cols], out_ref.at[pl.ds(pl.multiple_of(c * SHARD, SHARD), SHARD), :], sem
+    )
     copy.start()
+    out_ref[pl.ds(pl.multiple_of((1 - c) * SHARD, SHARD), SHARD), :] = other_ref[:, cols]
     copy.wait()
-
-
-def first_join(at_ref, own_ref, other_ref, out_ref):
-    c = at_ref[3]
-    out_ref[pl.ds(pl.multiple_of(c * SHARD, SHARD), SHARD), :] = own_ref[...]
-    out_ref[pl.ds(pl.multiple_of((1 - c) * SHARD, SHARD), SHARD), :] = other_ref[:, own_columns(at_ref)]
 
 
 def join_kernel(own_ref, other_ref, out_ref):
@@ -212,43 +210,14 @@
     dv_out[...] = dv_ref[:, pl.ds(pl.multiple_of((1 - at_ref[3]) * HALF, HALF), HALF)]
 
 
-def core_join_kernel(at_ref, own_ref, got1, got2, got3, first_ref, second_ref):
-    n = own_ref.shape[0]
-    first_ref[:n, :] = own_ref[...]
-    first_ref[n:, :] = got1[...]
-
-    @pl.when(at_ref[3] == 0)
-    def _():
-        second_ref[:n, :] = own_ref[...]
-        second_ref[n:, :] = got1[...]
-
-    @pl.when(at_ref[3] == 1)
-    def _():
-        second_ref[:n, :] = got2[...]
-        second_ref[n:, :] = got3[...]
-
-
 def put_in_order(at_ref, pieces, codes_ref):
-    z, y, x, c = at_ref[0], at_ref[1], at_ref[2], at_ref[3]
-    first, second, got1, got2, got3 = pieces
-
-    def place(piece, half, k, xi):
-        for zi in range(8):
-            to = ((z ^ Z_ORDER[zi]) * 4 + ((y + 4 - k) & 3)) * 2 + (x ^ xi)
+    z, y, x = at_ref[0], at_ref[1], at_ref[2]
+    for k, piece in enumerate(pieces):
+        for i in range(16):
+            zi, xi = (i & 1) * 4 + (i >> 2 & 1) * 2 + (i >> 3), i >> 1 & 1
+            to = ((z ^ zi) * 4 + ((y + 4 - k) & 3)) * 2 + (x ^ xi)
             rows = pl.ds(pl.multiple_of(to * CHIP, CHIP), CHIP)
-            codes_ref[rows, :] = piece[pl.ds((half * 8 + zi) * CHIP, CHIP), :]
-
-    @pl.when(c == 0)
-    def _():
-        for k, piece in enumerate((first, got1, got2, got3)):
-            for xi in range(2):
-                place(piece, xi, k, xi)
-
-    @pl.when(c == 1)
-    def _():
-        for j, piece in enumerate((first, second, got1, got2)):
-            for half in range(2):
-                place(piece, half, 2 * (j % 2) + half, j // 2)
+            codes_ref[rows, :] = piece[pl.ds(i * CHIP, CHIP), :]
 
 
 NEAR = 640
@@ -256,7 +225,7 @@
 
 
 def raw_kernel(at_ref, own_ref, other_ref, dv_own, dv_other, scale_ref, *refs):
-    pieces, (mine_ref, theirs_ref, sums_ref, kept_ref, near_ref, beside_ref, codes_ref) = refs[:5], refs[5:]
+    pieces, (mine_ref, theirs_ref, sums_ref, kept_ref, near_ref, beside_ref, codes_ref) = refs[:4], refs[4:]
     put_in_order(at_ref, pieces, codes_ref)
     cols = own_columns(at_ref)
     scale = scale_ref[:, cols]
@@ -309,14 +278,9 @@
         out_ref[:, rows] = total
 
 
-def last_kernel(
-    at_ref, dv_ref, scale_ref, near_ref, own_codes, seq_codes, part_ref, own0, own1, far0, far1, out_ref, sums_ref
-):
-    c = at_ref[3]
-    own, far = own0[...] + own1[...], far0[...] + far1[...]
-    sums_ref[:, :HALF] = jnp.where(c == 0, own, far) * scale_ref[:, :HALF]
-    sums_ref[:, HALF:] = jnp.where(c == 0, far, own) * scale_ref[:, HALF:]
-    for rows, total in hidden_terms(1 - c, dv_ref, scale_ref, near_ref, own_codes, seq_codes):
+def far_terms_kernel(at_ref, dv_ref, scale_ref, near_ref, own_codes, seq_codes, part_ref, sums_ref, out_ref, sums_out):
+    sums_out[...] = sums_ref[...]
+    for rows, total in hidden_terms(1 - at_ref[3], dv_ref, scale_ref, near_ref, own_codes, seq_codes):
         out_ref[:, rows] = (total + part_ref[:, rows]).astype(BF16)
 
 
@@ -344,10 +308,6 @@
     return pairs(lambda z, y, x, c: (z, y ^ bit, x, c))
 
 
-def core_pairs(move0, move1):
-    return [move for c, moves in enumerate((move0, move1)) for move in moves if move[0] % 2 == c]
-
-
 X_SWAP = pairs(lambda z, y, x, c: (z, y, x ^ 1, c))
 C_SWAP = pairs(lambda z, y, x, c: (z, y, x, c ^ 1))
 SEQ_SWAP = [(0, 1), (1, 0)]
@@ -364,77 +324,69 @@
     at = jnp.concatenate([place, lengths[0, :3]])
     scale = value_scale.reshape(1, -1)
 
-    own = call(
-        own_part, "own", shape(SHARD, HALF), [(SMEM, at), (HBM, value_codes)], scratch_shapes=[pltpu.SemaphoreType.DMA]
-    )
-    other = send(value_codes, C_SWAP)
-    rows = call(first_join, "join", shape(CHIP, HALF), [(SMEM, at), (VMEM, own), (VMEM, other)])
+    rows = call(
+        first_join, "join", shape(CHIP, HALF), [(HBM, value_codes), (VMEM, send(value_codes, C_SWAP))],
+        scratch_shapes=[pltpu.SemaphoreType.DMA],
+    )
     probs, dv = [], None
-    for bit, heads in ((4, (0,)), (2, (1, 2)), (1, (3,))):
-        got = send(rows, z_swap(bit))
+    for step, (perm, heads) in enumerate(((z_swap(4), (0, 1)), (X_SWAP, (2,)), (z_swap(2), (3,)), (z_swap(1), ()))):
+        got = send(rows, perm)
+        after = ()
         for g in heads:
             if g == 0:
                 p, dv, hidden = probs_part(g, at, queries, keys, upstream, dv, (rows,), hidden)
             else:
                 p, dv = probs_part(g, at, queries, keys, upstream, dv, (rows,))
             probs.append(p)
+            after = (p,)
         n = rows.shape[0]
         ins = [(VMEM, rows), (VMEM, got)]
-        if bit == 4:
-            rows, hidden = call(join_kernel, "join", shape(2 * n, HALF), ins, (p,), (hidden,))
+        if step == 0:
+            rows, hidden = call(join_kernel, "join", shape(2 * n, HALF), ins, after, (hidden,))
             hidden_other = send(hidden, C_SWAP)
-        elif bit == 2:
-            rows = call(join_kernel, "join", shape(2 * n, HALF), ins, (p,))
-        else:
+        elif step == 2:
             rows, dv_half = call(
                 join_take_kernel, "join", [shape(2 * n, HALF), shape(COUNT, HALF, dtype=F32)],
-                [(SMEM, at)] + ins + [(VMEM, dv)], (hidden_other,),
+                [(SMEM, at)] + ins + [(VMEM, dv)], after,
             )
-    got = [send(rows, core_pairs(X_SWAP if k == 1 else [], y_shift(k))) for k in (1, 2, 3)]
-    dv_other = send(dv_half, C_SWAP)
-    n = rows.shape[0]
-    first, second = call(
-        core_join_kernel, "join", [shape(2 * n, HALF)] * 2, [(SMEM, at)] + [(VMEM, a) for a in [rows] + got],
-        (dv_other,),
-    )
-    pieces = [first, second]
-    for k, rows in enumerate((first, second, first), 1):
-        pieces.append(send(rows, core_pairs(y_shift(k), X_SWAP if k < 3 else [])))
+            dv_other = send(dv_half, C_SWAP)
+        elif step == 3:
+            rows = call(join_kernel, "join", shape(2 * n, HALF), ins, (hidden_other, dv_other))
+        else:
+            rows = call(join_kernel, "join", shape(2 * n, HALF), ins, after)
+    pieces = [rows] + [send(rows, y_shift(k)) for k in (1, 2, 3)]
     mine, theirs, sums, kept, near, beside = raw_part(at, hidden, hidden_other, dv, dv_other, scale, pieces)
 
-    values_far = send(theirs, C_SWAP)
+    values_far, kept_far = send(theirs, C_SWAP), send(kept, C_SWAP)
+    near = lax.ppermute(near, "seq", SEQ_SWAP)
+    beside = lax.ppermute(beside, ("dp", "seq"), BESIDE)
+    base = [(SMEM, at), (VMEM, dv), (VMEM, scale)]
     held = None
     for step, perm in enumerate((X_SWAP, y_swap(1), y_swap(2), z_swap(1), z_swap(2), z_swap(4))):
-        if step == 1:
-            near = lax.ppermute(near, "seq", SEQ_SWAP)
-            beside = lax.ppermute(beside, ("dp", "seq"), BESIDE)
         got = send(sums, perm)
-        through = ()
-        if step < 4:
-            *held, token = grads_part(step, at, queries, keys, upstream, mine, values_far, probs[step], held, (sums,))
-            if step == 0:
-                through = (near, beside, kept)
-        elif step == 5:
+        after = ()
+        if 1 <= step <= 4:
+            *held, token = grads_part(
+                step - 1, at, queries, keys, upstream, mine, values_far, probs[step - 1], held, (sums,)
+            )
+            after = (token,)
+        if step == 4:
             codes = call(codes_join_kernel, "join", shape(DEPTH // 2, HALF), [(VMEM, near), (VMEM, beside)], (sums,))
             codes_far = send(codes, C_SWAP)
-            break
-        ins = [(VMEM, sums), (VMEM, got)]
-        after = () if step == 4 else (token,)
-        if through:
-            sums, near, beside, kept = call(add_kernel, "add", shape(1, HALF, dtype=F32), ins, after, through)
-            kept_far = send(kept, C_SWAP)
-        else:
-            sums = call(add_kernel, "add", shape(1, HALF, dtype=F32), ins, after)
-    far = [send(sums, C_SWAP), send(sums, pairs(lambda z, y, x, c: (z ^ 4, y, x, c ^ 1)))]
-    base = [(SMEM, at), (VMEM, dv), (VMEM, scale), (VMEM, near)]
-    part = call(
-        own_terms_kernel, "own_terms", shape(COUNT, DEPTH // 2, dtype=F32), base + [(VMEM, kept), (VMEM, codes)], (sums,)
-    )
-    grad_hidden, last = call(
-        last_kernel, "last", [shape(COUNT, DEPTH // 2), shape(1, 2 * HALF, dtype=F32)],
-        base + [(VMEM, a) for a in [kept_far, codes_far, part, sums, got] + far],
-    )
-    return held[0], held[1], grad_hidden, last.reshape(-1)
+        elif step == 5:
+            part = call(
+                own_terms_kernel, "own_terms", shape(COUNT, DEPTH // 2, dtype=F32),
+                base + [(VMEM, near), (VMEM, kept), (VMEM, codes)], (sums,),
+            )
+            after = (part,)
+        sums = call(add_kernel, "add", shape(1, HALF, dtype=F32), [(VMEM, sums), (VMEM, got)], after)
+    far = send(sums, C_SWAP)
+    grad_hidden, sums = call(
+        far_terms_kernel, "far_terms", [shape(COUNT, DEPTH // 2), shape(1, HALF, dtype=F32)],
+        base + [(VMEM, a) for a in (near, kept_far, codes_far, part, sums)],
+    )
+    both = jnp.concatenate([jnp.where(me % 2 == 0, sums, far), jnp.where(me % 2 == 0, far, sums)], axis=1)
+    return held[0], held[1], grad_hidden, (both * scale).reshape(-1)
 
 
 def solution(mesh):

time: 105 us -> 127 us (1.21)
  waiting for transfers between devices: 26.6 us -> 58.6 us
  starting transfers between devices: 45.6 us -> 32.5 us
  local copies, waits for them, and re-layouts: 1.08 us -> 2.65 us
    ppermute x23 -> x20, waiting for transfers between devices: 26.3 us -> 58.6 us  [send(): return lax.ppermute(x, 'dp', perm)]
    ppermute x23 -> x20, starting transfers between devices: 43.9 us -> 29.4 us  [send(): return lax.ppermute(x, 'dp', perm)]
    unnamed x8 -> x12, local copies, waits for them, and re-layouts: 0.34 us -> 1.91 us
  transfers between devices with their start and end apart: 25 -> 22, of which waited for: 9 -> 10; matrix products, arithmetic and copies ran while one was open for 1% -> 1% of each run, Pallas kernels for 22% -> 22%
where the time goes in v7:
time: 127 us
  waiting for transfers between devices  58.6 us (46%)
  starting transfers between devices  32.5 us (26%)
  Pallas kernels  31.8 us (25%)
  local copies, waits for them, and re-layouts  2.65 us (2%)
    ppermute x20, waiting for transfers between devices, send(): return lax.ppermute(x, 'dp', perm)  58.6 us
    pallas_call x23, Pallas kernels, call(): pl.pallas_call(run, in_specs=list(specs) + [ANY] * (len(after) + len(thro...  31.8 us
    ppermute x20, starting transfers between devices, send(): return lax.ppermute(x, 'dp', perm)  29.4 us
  transfers between devices with their start and end apart: 22, of which 10 were waited for; matrix products, arithmetic and copies ran while one was open for 1% of the time, Pallas kernels for 22%

profile of v7, /device:TPU:1, one launch (start us, length us, event | category | flops | bytes accessed | tf_op | source)
XLA Modules:
  0.0 126.8 jit_solution(11874424028045744257)
XLA Ops:
  0.6 3.3 %collective-permute-start = (bf16[32,512]{1,0:T(8,128)(2,1)}, bf16[32,512]{1,0:T(8,128)(2,1)S(1)}, u32[]{:S(2)}, u32[]{:S(2)}) collective-permute-start(bf16[32,512]{1,0:T(8,128)(2,1)} %refs_0_.1), channel_id=1, source_target_pairs={{0,2},{2,0},{4,6},{6,4},{8,10},{10,8},{12,14},{14,12},{16,18},{18,... | collective-permute-start | bytes 98312 | tf_op jit(solution)/shard_map/ppermute | solution.py:318
  4.0 1.1 collective-permute-done.refs_1_
  5.0 0.7 join.6.refs_5_.refs_0_
  5.8 5.3 %collective-permute-start.1 = (bf16[64,256]{1,0:T(8,128)(2,1)S(1)}, bf16[64,256]{1,0:T(8,128)(2,1)S(1)}, u32[]{:S(2)}, u32[]{:S(2)}) collective-permute-start(bf16[64,256]{1,0:T(8,128)(2,1)S(1)} %join.6.refs_5_.refs_0_), channel_id=1, source_target_pairs={{0,128},{2,130},{4,132},{6,134},{8,136},{10,138},{12,140},{14,142}... | collective-permute-start | bytes 98312 | tf_op jit(solution)/shard_map/ppermute | solution.py:318
  11.0 0.7 slice_bitcast_fusion
  11.7 0.1 concatenate.11.refs_0_
  11.8 3.7 %probs_part.4 = (bf16[4,384,384]{2,1,0:T(8,128)(2,1)S(1)}, f32[384,512]{1,0:T(8,128)S(1)}, bf16[384,4096]{1,0:T(8,128)(2,1)S(1)}) custom-call(s32[8]{0:T(128)S(1)} %concatenate.11.refs_0_, bf16[384,2048]{1,0:T(8,128)(2,1)} %refs_1_.15, bf16[384,512]{1,0:T(8,128)(2,1)} %refs_2_.15, bf16[384,2048]{1,0:T(8,128)(2,1)} %refs_3_.15, bf16[384,4096]{1,0:T(8,128)(2,1)} %refs_4_.1, ...), custom_call_target="tpu_custom_call" | custom-call | flops 1000 | bytes 1000 | tf_op jit(solution)/shard_map/probs_part/pallas_call | solution.py:53
  15.5 2.2 %probs_part.5 = (bf16[4,384,384]{2,1,0:T(8,128)(2,1)S(1)}, f32[384,512]{1,0:T(8,128)S(1)}) custom-call(s32[8]{0:T(128)S(1)} %concatenate.11.refs_0_, bf16[384,2048]{1,0:T(8,128)(2,1)S(1)} %copy-done, bf16[384,512]{1,0:T(8,128)(2,1)S(1)} %copy-done.4, bf16[384,2048]{1,0:T(8,128)(2,1)S(1)} %copy-done.1, ...), custom_call_target="tpu_custom_call", output_to_operand_aliasing={{1}: (4, {})} | custom-call | flops 1000 | bytes 1000 | tf_op jit(solution)/shard_map/probs_part/pallas_call | solution.py:53
  17.7 0.7 collective-permute-start.2
  18.4 2.8 %collective-permute-start.3 = (bf16[128,256]{1,0:T(8,128)(2,1)S(1)}, bf16[128,256]{1,0:T(8,128)(2,1)S(1)}, u32[]{:S(2)}, u32[]{:S(2)}) collective-permute-start(bf16[128,256]{1,0:T(8,128)(2,1)S(1)} %get-tuple-element.42.refs_5_.refs_0_), channel_id=1, source_target_pairs={{0,4},{2,6},{4,0},{6,2},{8,12},{10,14},{12,8},{14,10},{16,20},{18,... | collective-permute-start | bytes 196616 | tf_op jit(solution)/shard_map/ppermute | solution.py:318
  21.2 2.2 %probs_part.6 = (bf16[4,384,384]{2,1,0:T(8,128)(2,1)S(1)}, f32[384,512]{1,0:T(8,128)S(1)}) custom-call(s32[8]{0:T(128)S(1)} %concatenate.11.refs_0_, bf16[384,2048]{1,0:T(8,128)(2,1)S(1)} %copy-done, bf16[384,512]{1,0:T(8,128)(2,1)S(1)} %copy-done.4, bf16[384,2048]{1,0:T(8,128)(2,1)S(1)} %copy-done.1, ...), custom_call_target="tpu_custom_call", output_to_operand_aliasing={{1}: (4, {})} | custom-call | flops 1000 | bytes 1000 | tf_op jit(solution)/shard_map/probs_part/pallas_call | solution.py:53
  23.4 0.2 collective-permute-done.3.refs_1_
  23.6 1.3 %collective-permute-start.4 = (bf16[256,256]{1,0:T(8,128)(2,1)S(1)}, bf16[256,256]{1,0:T(8,128)(2,1)S(1)}, u32[]{:S(2)}, u32[]{:S(2)}) collective-permute-start(bf16[256,256]{1,0:T(8,128)(2,1)S(1)} %join.8.refs_5_.refs_1_), channel_id=1, source_target_pairs={{0,64},{2,66},{4,68},{6,70},{8,72},{10,74},{12,76},{14,78},{16,80}... | collective-permute-start | bytes 393224 | tf_op jit(solution)/shard_map/ppermute | solution.py:318
  24.9 2.2 %probs_part.7 = (bf16[4,384,384]{2,1,0:T(8,128)(2,1)S(1)}, f32[384,512]{1,0:T(8,128)S(1)}) custom-call(s32[8]{0:T(128)S(1)} %concatenate.11.refs_0_, bf16[384,2048]{1,0:T(8,128)(2,1)S(1)} %copy-done, bf16[384,512]{1,0:T(8,128)(2,1)S(1)} %copy-done.4, bf16[384,2048]{1,0:T(8,128)(2,1)S(1)} %copy-done.1, ...), custom_call_target="tpu_custom_call", output_to_operand_aliasing={{1}: (4, {})} | custom-call | flops 1000 | bytes 1000 | tf_op jit(solution)/shard_map/probs_part/pallas_call | solution.py:53
  27.1 5.2 %collective-permute-done.4.refs_2_ = bf16[256,256]{1,0:T(8,128)(2,1)S(1)} collective-permute-done((bf16[256,256]{1,0:T(8,128)(2,1)S(1)}, bf16[256,256]{1,0:T(8,128)(2,1)S(1)}, u32[]{:S(2)}, u32[]{:S(2)}) %collective-permute-start.4) | collective-permute-done | bytes 131104 | tf_op jit(solution)/shard_map/ppermute | solution.py:318
  32.3 0.6 join.9
  32.9 1.1 collective-permute-start.5
  34.0 7.9 %collective-permute-done.6.refs_1_ = bf16[512,256]{1,0:T(8,128)(2,1)S(1)} collective-permute-done((bf16[512,256]{1,0:T(8,128)(2,1)S(1)}, bf16[512,256]{1,0:T(8,128)(2,1)S(1)}, u32[]{:S(2)}, u32[]{:S(2)}) %collective-permute-start.6) | collective-permute-done | bytes 262176 | tf_op jit(solution)/shard_map/ppermute | solution.py:318
  41.9 2.8 %collective-permute-start.9 = (bf16[1024,256]{1,0:T(8,128)(2,1)S(1)}, bf16[1024,256]{1,0:T(8,128)(2,1)S(1)}, u32[]{:S(2)}, u32[]{:S(2)}) collective-permute-start(bf16[1024,256]{1,0:T(8,128)(2,1)S(1)} %join.10.refs_6_), channel_id=1, source_target_pairs={{0,24},{2,26},{4,28},{6,30},{8,0},{10,2},{12,4},{14,6},{16,8},{18,... | collective-permute-start | bytes 1572872 | tf_op jit(solution)/shard_map/ppermute | solution.py:318
  44.7 0.3 collective-permute-start.8
  45.1 0.7 collective-permute-start.7
  45.8 10.4 %collective-permute-done.9.refs_9_ = bf16[1024,256]{1,0:T(8,128)(2,1)S(1)} collective-permute-done((bf16[1024,256]{1,0:T(8,128)(2,1)S(1)}, bf16[1024,256]{1,0:T(8,128)(2,1)S(1)}, u32[]{:S(2)}, u32[]{:S(2)}) %collective-permute-start.9) | collective-permute-done | bytes 524320 | tf_op jit(solution)/shard_map/ppermute | solution.py:318
  56.1 2.4 %collective-permute-done.8.refs_8_ = bf16[1024,256]{1,0:T(8,128)(2,1)S(1)} collective-permute-done((bf16[1024,256]{1,0:T(8,128)(2,1)S(1)}, bf16[1024,256]{1,0:T(8,128)(2,1)S(1)}, u32[]{:S(2)}, u32[]{:S(2)}) %collective-permute-start.8) | collective-permute-done | bytes 524320 | tf_op jit(solution)/shard_map/ppermute | solution.py:318
  58.5 12.8 %collective-permute-done.7.refs_7_ = bf16[1024,256]{1,0:T(8,128)(2,1)S(1)} collective-permute-done((bf16[1024,256]{1,0:T(8,128)(2,1)S(1)}, bf16[1024,256]{1,0:T(8,128)(2,1)S(1)}, u32[]{:S(2)}, u32[]{:S(2)}) %collective-permute-start.7) | collective-permute-done | bytes 524320 | tf_op jit(solution)/shard_map/ppermute | solution.py:318
  71.3 3.6 %raw_part.1 = (bf16[384,256]{1,0:T(8,128)(2,1)S(1)}, bf16[384,256]{1,0:T(8,128)(2,1)S(1)}, f32[1,256]{1,0:T(1,128)S(1)}, bf16[2048,256]{1,0:T(8,128)(2,1)}, bf16...) custom-call(s32[8]{0:T(128)S(1)} %concatenate.11.refs_0_, bf16[384,4096]{1,0:T(8,128)(2,1)S(1)} %get-tuple-element.40.refs_1_, ...), custom_call_target="tpu_custom_call" | custom-call | flops 1000 | bytes 1000 | tf_op jit(solution)/shard_map/raw_part/pallas_call | solution.py:53
  75.0 1.2 collective-permute-start.15
  76.2 1.8 %collective-permute-start.17 = (bf16[1408,256]{1,0:T(8,128)(2,1)S(1)}, bf16[1408,256]{1,0:T(8,128)(2,1)S(1)}, u32[]{:S(2)}, u32[]{:S(2)}) collective-permute-start(bf16[1408,256]{1,0:T(8,128)(2,1)S(1)} %get-tuple-element.66), channel_id=1, source_target_pairs={{0,5},{1,4},{2,7},{3,6},{4,1},{5,0},{6,3},{7,2},{8,13},{9,12},{10,... | collective-permute-start | bytes 2162696 | tf_op jit(solution)/shard_map/ppermute | solution.py:362
  78.0 1.0 collective-permute-start.10
  79.0 0.4 collective-permute-start.11
  79.4 14.7 %collective-permute-done.11.refs_1_ = f32[1,256]{1,0:T(1,128)S(1)} collective-permute-done((f32[1,256]{1,0:T(1,128)S(1)}, f32[1,256]{1,0:T(1,128)S(1)}, u32[]{:S(2)}, u32[]{:S(2)}) %collective-permute-start.11) | collective-permute-done | bytes 1056 | tf_op jit(solution)/shard_map/ppermute | solution.py:318
  94.1 2.6 %grads_part.4 = (bf16[384,2048]{1,0:T(8,128)(2,1)}, bf16[384,512]{1,0:T(8,128)(2,1)}, f32[8,128]{1,0:T(8,128)S(1)}) custom-call(s32[8]{0:T(128)S(1)} %concatenate.11.refs_0_, bf16[384,2048]{1,0:T(8,128)(2,1)S(1)} %copy-done, bf16[384,512]{1,0:T(8,128)(2,1)S(1)} %copy-done.4, bf16[384,2048]{1,0:T(8,128)(2,1)S(1)} %copy-done.1, ...), custom_call_target="tpu_custom_call" | custom-call | flops 1000 | bytes 1000 | tf_op jit(solution)/shard_map/grads_part/pallas_call | solution.py:53
  96.7 0.4 collective-permute-start.13
  97.2 2.6 %grads_part.5 = (bf16[384,2048]{1,0:T(8,128)(2,1)}, bf16[384,512]{1,0:T(8,128)(2,1)}, f32[8,128]{1,0:T(8,128)S(1)}) custom-call(s32[8]{0:T(128)S(1)} %concatenate.11.refs_0_, bf16[384,2048]{1,0:T(8,128)(2,1)S(1)} %copy-done, bf16[384,512]{1,0:T(8,128)(2,1)S(1)} %copy-done.4, ...), custom_call_target="tpu_custom_call", output_to_operand_aliasing={{0}: (7, {}), {1}: (8, {})} | custom-call | flops 1000 | bytes 1000 | tf_op jit(solution)/shard_map/grads_part/pallas_call | solution.py:53
  99.8 1.0 collective-permute-done.13.refs_1_
  100.8 0.1 collective-permute-start.14
  100.9 3.9 %collective-permute-start.16 = (bf16[2048,256]{1,0:T(8,128)(2,1)}, bf16[2048,256]{1,0:T(8,128)(2,1)}, u32[]{:S(2)}, u32[]{:S(2)}) collective-permute-start(bf16[2048,256]{1,0:T(8,128)(2,1)} %get-tuple-element.65.refs_4_), channel_id=1, source_target_pairs={{0,2},{2,0},{4,6},{6,4},{8,10},{10,8},{12,14},{14,12},{16,18},{18,... | collective-permute-start | bytes 3145736 | tf_op jit(solution)/shard_map/ppermute | solution.py:318
  104.8 2.6 %grads_part.6 = (bf16[384,2048]{1,0:T(8,128)(2,1)}, bf16[384,512]{1,0:T(8,128)(2,1)}, f32[8,128]{1,0:T(8,128)S(1)}) custom-call(s32[8]{0:T(128)S(1)} %concatenate.11.refs_0_, bf16[384,2048]{1,0:T(8,128)(2,1)S(1)} %copy-done, bf16[384,512]{1,0:T(8,128)(2,1)S(1)} %copy-done.4, ...), custom_call_target="tpu_custom_call", output_to_operand_aliasing={{0}: (7, {}), {1}: (8, {})} | custom-call | flops 1000 | bytes 1000 | tf_op jit(solution)/shard_map/grads_part/pallas_call | solution.py:53
  107.5 0.1 join.11.refs_5_
  107.5 0.6 collective-permute-start.18
  108.1 1.4 %collective-permute-start.19 = (f32[1,256]{1,0:T(1,128)S(1)}, f32[1,256]{1,0:T(1,128)S(1)}, u32[]{:S(2)}, u32[]{:S(2)}) collective-permute-start(f32[1,256]{1,0:T(1,128)S(1)} %add.27.refs_9_.refs_2_.refs_0_), channel_id=1, source_target_pairs={{0,64},{2,66},{4,68},{6,70},{8,72},{10,74},{12,76},{14,78},{16,80}... | collective-permute-start | bytes 3080 | tf_op jit(solution)/shard_map/ppermute | solution.py:318
  109.5 2.6 %grads_part.7 = (bf16[384,2048]{1,0:T(8,128)(2,1)}, bf16[384,512]{1,0:T(8,128)(2,1)}, f32[8,128]{1,0:T(8,128)S(1)}) custom-call(s32[8]{0:T(128)S(1)} %concatenate.11.refs_0_, bf16[384,2048]{1,0:T(8,128)(2,1)S(1)} %copy-done, bf16[384,512]{1,0:T(8,128)(2,1)S(1)} %copy-done.4, ...), custom_call_target="tpu_custom_call", output_to_operand_aliasing={{0}: (7, {}), {1}: (8, {})} | custom-call | flops 1000 | bytes 1000 | tf_op jit(solution)/shard_map/grads_part/pallas_call | solution.py:53
  112.1 1.5 %collective-permute-start.20 = (f32[1,256]{1,0:T(1,128)S(1)}, f32[1,256]{1,0:T(1,128)S(1)}, u32[]{:S(2)}, u32[]{:S(2)}) collective-permute-start(f32[1,256]{1,0:T(1,128)S(1)} %add.28.refs_6_.refs_0_), channel_id=1, source_target_pairs={{0,128},{2,130},{4,132},{6,134},{8,136},{10,138},{12,140},{14,142}... | collective-permute-start | bytes 3080 | tf_op jit(solution)/shard_map/ppermute | solution.py:318
  113.6 2.2 %own_terms.1.refs_2_.refs_6_ = f32[384,2048]{1,0:T(8,128)S(1)} custom-call(s32[8]{0:T(128)S(1)} %concatenate.11.refs_0_, f32[384,512]{1,0:T(8,128)S(1)} %get-tuple-element.45.refs_3_.refs_1_, f32[1,512]{1,0:T(1,128)S(1)} %bitcast.11, bf16[1408,256]{1,0:T(8,128)(2,1)S(1)} %collective-permute-done.15.refs_0_.refs_3_, ...), custom_call_target="tpu_custom_call" | custom-call | flops 1000 | bytes 1000 | tf_op jit(solution)/shard_map/own_terms/pallas_call | solution.py:53
  115.8 2.9 %collective-permute-done.20.refs_1_ = f32[1,256]{1,0:T(1,128)S(1)} collective-permute-done((f32[1,256]{1,0:T(1,128)S(1)}, f32[1,256]{1,0:T(1,128)S(1)}, u32[]{:S(2)}, u32[]{:S(2)}) %collective-permute-start.20) | collective-permute-done | bytes 1056 | tf_op jit(solution)/shard_map/ppermute | solution.py:318
  118.8 1.8 %collective-permute-start.21 = (f32[1,256]{1,0:T(1,128)S(1)}, f32[1,256]{1,0:T(1,128)S(1)}, u32[]{:S(2)}, u32[]{:S(2)}) collective-permute-start(f32[1,256]{1,0:T(1,128)S(1)} %add.29.refs_7_), channel_id=1, source_target_pairs={{0,2},{2,0},{4,6},{6,4},{8,10},{10,8},{12,14},{14,12},{16,18},{18,... | collective-permute-start | bytes 3080 | tf_op jit(solution)/shard_map/ppermute | solution.py:318
  120.6 1.9 %copy-done.3 = f32[384,2048]{1,0:T(8,128)S(1)} copy-done((f32[384,2048]{1,0:T(8,128)S(1)}, f32[384,2048]{1,0:T(8,128)}, u32[]{:S(2)}) %copy-start.3) | copy-done | bytes 3145752
  122.5 3.8 %far_terms.1 = (bf16[384,2048]{1,0:T(8,128)(2,1)}, f32[1,256]{1,0:T(1,128)S(1)}) custom-call(s32[8]{0:T(128)S(1)} %concatenate.11.refs_0_, f32[384,512]{1,0:T(8,128)S(1)} %get-tuple-element.45.refs_3_.refs_1_, f32[1,512]{1,0:T(1,128)S(1)} %bitcast.12, bf16[1408,256]{1,0:T(8,128)(2,1)S(1)} %collective-permute-done.15.refs_0_.refs_3_, ...), custom_call_target="tpu_custom_call" | custom-call | flops 1000 | bytes 1000 | tf_op jit(solution)/shard_map/far_terms/pallas_call | solution.py:53
  126.3 0.6 maximum_multiply_fusion
  (35 shorter events, 0.1 us)
Async XLA Ops:
  0.6 4.4 %collective-permute-start = (bf16[32,512]{1,0:T(8,128)(2,1)}, bf16[32,512]{1,0:T(8,128)(2,1)S(1)}, u32[]{:S(2)}, u32[]{:S(2)}) collective-permute-start(bf16[32,512]{1,0:T(8,128)(2,1)} %refs_0_.1), channel_id=1, source_target_pairs={{0,2},{2,0},{4,6},{6,4},{8,10},{10,8},{12,14},{14,12},{16,18},{18,... | collective-permute-start | bytes 98312 | tf_op jit(solution)/shard_map/ppermute | solution.py:318
  5.8 11.9 %collective-permute-start.1 = (bf16[64,256]{1,0:T(8,128)(2,1)S(1)}, bf16[64,256]{1,0:T(8,128)(2,1)S(1)}, u32[]{:S(2)}, u32[]{:S(2)}) collective-permute-start(bf16[64,256]{1,0:T(8,128)(2,1)S(1)} %join.6.refs_5_.refs_0_), channel_id=1, source_target_pairs={{0,128},{2,130},{4,132},{6,134},{8,136},{10,138},{12,140},{14,142}... | collective-permute-start | bytes 98312 | tf_op jit(solution)/shard_map/ppermute | solution.py:318
  11.8 3.7 %copy-start = (bf16[384,2048]{1,0:T(8,128)(2,1)S(1)}, bf16[384,2048]{1,0:T(8,128)(2,1)}, u32[]{:S(2)}) copy-start(bf16[384,2048]{1,0:T(8,128)(2,1)} %refs_1_.15) | copy-start | bytes 4718596
  11.8 3.7 %copy-start.1 = (bf16[384,2048]{1,0:T(8,128)(2,1)S(1)}, bf16[384,2048]{1,0:T(8,128)(2,1)}, u32[]{:S(2)}) copy-start(bf16[384,2048]{1,0:T(8,128)(2,1)} %refs_3_.15) | copy-start | bytes 4718596
  11.8 3.7 %copy-start.4 = (bf16[384,512]{1,0:T(8,128)(2,1)S(1)}, bf16[384,512]{1,0:T(8,128)(2,1)}, u32[]{:S(2)}) copy-start(bf16[384,512]{1,0:T(8,128)(2,1)} %refs_2_.15) | copy-start | bytes 1179652
  17.7 24.2 %collective-permute-start.2 = (bf16[384,4096]{1,0:T(8,128)(2,1)S(1)}, bf16[384,4096]{1,0:T(8,128)(2,1)S(1)}, u32[]{:S(2)}, u32[]{:S(2)}) collective-permute-start(bf16[384,4096]{1,0:T(8,128)(2,1)S(1)} %get-tuple-element.40.refs_1_), channel_id=1, source_target_pairs={{0,2},{2,0},{4,6},{6,4},{8,10},{10,8},{12,14},{14,12},{16,18},{18,... | collective-permute-start | bytes 9437192 | tf_op jit(solution)/shard_map/ppermute | solution.py:318
  18.4 5.2 %collective-permute-start.3 = (bf16[128,256]{1,0:T(8,128)(2,1)S(1)}, bf16[128,256]{1,0:T(8,128)(2,1)S(1)}, u32[]{:S(2)}, u32[]{:S(2)}) collective-permute-start(bf16[128,256]{1,0:T(8,128)(2,1)S(1)} %get-tuple-element.42.refs_5_.refs_0_), channel_id=1, source_target_pairs={{0,4},{2,6},{4,0},{6,2},{8,12},{10,14},{12,8},{14,10},{16,20},{18,... | collective-permute-start | bytes 196616 | tf_op jit(solution)/shard_map/ppermute | solution.py:318
  23.6 8.7 %collective-permute-start.4 = (bf16[256,256]{1,0:T(8,128)(2,1)S(1)}, bf16[256,256]{1,0:T(8,128)(2,1)S(1)}, u32[]{:S(2)}, u32[]{:S(2)}) collective-permute-start(bf16[256,256]{1,0:T(8,128)(2,1)S(1)} %join.8.refs_5_.refs_1_), channel_id=1, source_target_pairs={{0,64},{2,66},{4,68},{6,70},{8,72},{10,74},{12,76},{14,78},{16,80}... | collective-permute-start | bytes 393224 | tf_op jit(solution)/shard_map/ppermute | solution.py:318
  32.9 9.0 %collective-permute-start.5 = (f32[384,256]{1,0:T(8,128)S(1)}, f32[384,256]{1,0:T(8,128)S(1)}, u32[]{:S(2)}, u32[]{:S(2)}) collective-permute-start(f32[384,256]{1,0:T(8,128)S(1)} %get-tuple-element.47), channel_id=1, source_target_pairs={{0,2},{2,0},{4,6},{6,4},{8,10},{10,8},{12,14},{14,12},{16,18},{18,... | collective-permute-start | bytes 1179656 | tf_op jit(solution)/shard_map/ppermute | solution.py:318
  34.0 37.3 %copy-start.5 = (f32[512]{0:T(512)S(1)}, f32[512]{0:T(512)}, u32[]{:S(2)}) copy-start(f32[512]{0:T(512)} %param.11) | copy-start | bytes 6148
  34.0 7.9 %collective-permute-start.6 = (bf16[512,256]{1,0:T(8,128)(2,1)S(1)}, bf16[512,256]{1,0:T(8,128)(2,1)S(1)}, u32[]{:S(2)}, u32[]{:S(2)}) collective-permute-start(bf16[512,256]{1,0:T(8,128)(2,1)S(1)} %get-tuple-element.48.refs_0_), channel_id=1, source_target_pairs={{0,32},{2,34},{4,36},{6,38},{8,40},{10,42},{12,44},{14,46},{16,48}... | collective-permute-start | bytes 786440 | tf_op jit(solution)/shard_map/ppermute | solution.py:318
  41.9 14.2 %collective-permute-start.9 = (bf16[1024,256]{1,0:T(8,128)(2,1)S(1)}, bf16[1024,256]{1,0:T(8,128)(2,1)S(1)}, u32[]{:S(2)}, u32[]{:S(2)}) collective-permute-start(bf16[1024,256]{1,0:T(8,128)(2,1)S(1)} %join.10.refs_6_), channel_id=1, source_target_pairs={{0,24},{2,26},{4,28},{6,30},{8,0},{10,2},{12,4},{14,6},{16,8},{18,... | collective-permute-start | bytes 1572872 | tf_op jit(solution)/shard_map/ppermute | solution.py:318
  44.7 13.8 %collective-permute-start.8 = (bf16[1024,256]{1,0:T(8,128)(2,1)S(1)}, bf16[1024,256]{1,0:T(8,128)(2,1)S(1)}, u32[]{:S(2)}, u32[]{:S(2)}) collective-permute-start(bf16[1024,256]{1,0:T(8,128)(2,1)S(1)} %join.10.refs_6_), channel_id=1, source_target_pairs={{0,16},{2,18},{4,20},{6,22},{8,24},{10,26},{12,28},{14,30},{16,0},... | collective-permute-start | bytes 1572872 | tf_op jit(solution)/shard_map/ppermute | solution.py:318
  45.1 26.2 %collective-permute-start.7 = (bf16[1024,256]{1,0:T(8,128)(2,1)S(1)}, bf16[1024,256]{1,0:T(8,128)(2,1)S(1)}, u32[]{:S(2)}, u32[]{:S(2)}) collective-permute-start(bf16[1024,256]{1,0:T(8,128)(2,1)S(1)} %join.10.refs_6_), channel_id=1, source_target_pairs={{0,8},{2,10},{4,12},{6,14},{8,16},{10,18},{12,20},{14,22},{16,24},... | collective-permute-start | bytes 1572872 | tf_op jit(solution)/shard_map/ppermute | solution.py:318
  75.0 32.5 %collective-permute-start.15 = (bf16[1408,256]{1,0:T(8,128)(2,1)S(1)}, bf16[1408,256]{1,0:T(8,128)(2,1)S(1)}, u32[]{:S(2)}, u32[]{:S(2)}) collective-permute-start(bf16[1408,256]{1,0:T(8,128)(2,1)S(1)} %get-tuple-element.64), channel_id=1, source_target_pairs={{0,1},{1,0},{2,3},{3,2},{4,5},{5,4},{6,7},{7,6},{8,9},{9,8},{10,11... | collective-permute-start | bytes 2162696 | tf_op jit(solution)/shard_map/ppermute | solution.py:361
  76.2 31.3 %collective-permute-start.17 = (bf16[1408,256]{1,0:T(8,128)(2,1)S(1)}, bf16[1408,256]{1,0:T(8,128)(2,1)S(1)}, u32[]{:S(2)}, u32[]{:S(2)}) collective-permute-start(bf16[1408,256]{1,0:T(8,128)(2,1)S(1)} %get-tuple-element.66), channel_id=1, source_target_pairs={{0,5},{1,4},{2,7},{3,6},{4,1},{5,0},{6,3},{7,2},{8,13},{9,12},{10,... | collective-permute-start | bytes 2162696 | tf_op jit(solution)/shard_map/ppermute | solution.py:362
  78.0 16.1 %collective-permute-start.10 = (bf16[384,256]{1,0:T(8,128)(2,1)S(1)}, bf16[384,256]{1,0:T(8,128)(2,1)S(1)}, u32[]{:S(2)}, u32[]{:S(2)}) collective-permute-start(bf16[384,256]{1,0:T(8,128)(2,1)S(1)} %get-tuple-element.50), channel_id=1, source_target_pairs={{0,2},{2,0},{4,6},{6,4},{8,10},{10,8},{12,14},{14,12},{16,18},{18,... | collective-permute-start | bytes 589832 | tf_op jit(solution)/shard_map/ppermute | solution.py:318
  79.0 15.1 %collective-permute-start.11 = (f32[1,256]{1,0:T(1,128)S(1)}, f32[1,256]{1,0:T(1,128)S(1)}, u32[]{:S(2)}, u32[]{:S(2)}) collective-permute-start(f32[1,256]{1,0:T(1,128)S(1)} %get-tuple-element.52.refs_0_), channel_id=1, source_target_pairs={{0,4},{2,6},{4,0},{6,2},{8,12},{10,14},{12,8},{14,10},{16,20},{18,... | collective-permute-start | bytes 3080 | tf_op jit(solution)/shard_map/ppermute | solution.py:318
  94.1 2.6 %collective-permute-start.12 = (f32[1,256]{1,0:T(1,128)S(1)}, f32[1,256]{1,0:T(1,128)S(1)}, u32[]{:S(2)}, u32[]{:S(2)}) collective-permute-start(f32[1,256]{1,0:T(1,128)S(1)} %add.24.refs_7_.refs_0_), channel_id=1, source_target_pairs={{0,8},{2,10},{4,12},{6,14},{8,0},{10,2},{12,4},{14,6},{16,24},{18,... | collective-permute-start | bytes 3080 | tf_op jit(solution)/shard_map/ppermute | solution.py:318
  96.7 4.0 %collective-permute-start.13 = (f32[1,256]{1,0:T(1,128)S(1)}, f32[1,256]{1,0:T(1,128)S(1)}, u32[]{:S(2)}, u32[]{:S(2)}) collective-permute-start(f32[1,256]{1,0:T(1,128)S(1)} %add.25.refs_9_.refs_0_), channel_id=1, source_target_pairs={{0,16},{2,18},{4,20},{6,22},{8,24},{10,26},{12,28},{14,30},{16,0},... | collective-permute-start | bytes 3080 | tf_op jit(solution)/shard_map/ppermute | solution.py:318
  100.8 6.7 %collective-permute-start.14 = (f32[1,256]{1,0:T(1,128)S(1)}, f32[1,256]{1,0:T(1,128)S(1)}, u32[]{:S(2)}, u32[]{:S(2)}) collective-permute-start(f32[1,256]{1,0:T(1,128)S(1)} %add.26.refs_9_.refs_0_), channel_id=1, source_target_pairs={{0,32},{2,34},{4,36},{6,38},{8,40},{10,42},{12,44},{14,46},{16,48}... | collective-permute-start | bytes 3080 | tf_op jit(solution)/shard_map/ppermute | solution.py:318
  100.9 19.7 %collective-permute-start.16 = (bf16[2048,256]{1,0:T(8,128)(2,1)}, bf16[2048,256]{1,0:T(8,128)(2,1)}, u32[]{:S(2)}, u32[]{:S(2)}) collective-permute-start(bf16[2048,256]{1,0:T(8,128)(2,1)} %get-tuple-element.65.refs_4_), channel_id=1, source_target_pairs={{0,2},{2,0},{4,6},{6,4},{8,10},{10,8},{12,14},{14,12},{16,18},{18,... | collective-permute-start | bytes 3145736 | tf_op jit(solution)/shard_map/ppermute | solution.py:318
  107.5 13.1 %collective-permute-start.18 = (bf16[2048,256]{1,0:T(8,128)(2,1)S(1)}, bf16[2048,256]{1,0:T(8,128)(2,1)}, u32[]{:S(2)}, u32[]{:S(2)}) collective-permute-start(bf16[2048,256]{1,0:T(8,128)(2,1)S(1)} %join.11.refs_5_), channel_id=1, source_target_pairs={{0,2},{2,0},{4,6},{6,4},{8,10},{10,8},{12,14},{14,12},{16,18},{18,... | collective-permute-start | bytes 3145736 | tf_op jit(solution)/shard_map/ppermute | solution.py:318
  108.1 4.0 %collective-permute-start.19 = (f32[1,256]{1,0:T(1,128)S(1)}, f32[1,256]{1,0:T(1,128)S(1)}, u32[]{:S(2)}, u32[]{:S(2)}) collective-permute-start(f32[1,256]{1,0:T(1,128)S(1)} %add.27.refs_9_.refs_2_.refs_0_), channel_id=1, source_target_pairs={{0,64},{2,66},{4,68},{6,70},{8,72},{10,74},{12,76},{14,78},{16,80}... | collective-permute-start | bytes 3080 | tf_op jit(solution)/shard_map/ppermute | solution.py:318
  112.1 6.6 %collective-permute-start.20 = (f32[1,256]{1,0:T(1,128)S(1)}, f32[1,256]{1,0:T(1,128)S(1)}, u32[]{:S(2)}, u32[]{:S(2)}) collective-permute-start(f32[1,256]{1,0:T(1,128)S(1)} %add.28.refs_6_.refs_0_), channel_id=1, source_target_pairs={{0,128},{2,130},{4,132},{6,134},{8,136},{10,138},{12,140},{14,142}... | collective-permute-start | bytes 3080 | tf_op jit(solution)/shard_map/ppermute | solution.py:318
  115.8 2.9 %copy-start.2 = (f32[384,2048]{1,0:T(8,128)}, f32[384,2048]{1,0:T(8,128)S(1)}, u32[]{:S(2)}) copy-start(f32[384,2048]{1,0:T(8,128)S(1)} %own_terms.1.refs_2_.refs_6_) | copy-start | bytes 9437188
  118.8 7.5 %collective-permute-start.21 = (f32[1,256]{1,0:T(1,128)S(1)}, f32[1,256]{1,0:T(1,128)S(1)}, u32[]{:S(2)}, u32[]{:S(2)}) collective-permute-start(f32[1,256]{1,0:T(1,128)S(1)} %add.29.refs_7_), channel_id=1, source_target_pairs={{0,2},{2,0},{4,6},{6,4},{8,10},{10,8},{12,14},{14,12},{16,18},{18,... | collective-permute-start | bytes 3080 | tf_op jit(solution)/shard_map/ppermute | solution.py:318
  120.6 1.9 %copy-start.3 = (f32[384,2048]{1,0:T(8,128)S(1)}, f32[384,2048]{1,0:T(8,128)}, u32[]{:S(2)}) copy-start(f32[384,2048]{1,0:T(8,128)} %copy-done.2) | copy-start | bytes 9437188

commit v8 on v7

--- a/solution.py
+++ b/solution.py
@@ -17,7 +17,7 @@
 LOG2E = math.log2(math.e)
 BF16 = jnp.bfloat16
 F32 = jnp.float32
-VMEM_LIMIT = 20 * 1024 * 1024
+VMEM_LIMIT = 14 * 1024 * 1024
 
 
 def dot(a, b, dims):
@@ -138,7 +138,7 @@
     token_ref[...] = jnp.zeros_like(token_ref)
     dk_acc[...] = jnp.zeros_like(dk_acc)
     col = pl.ds(HEAD * (g % 2), HEAD)
-    all_values = jnp.where(at_ref[3] == g // 2, mine_ref[:, col], theirs_ref[:, col])
+    all_values = jnp.where(at_ref[3] == g // 2, mine_ref[:, col], theirs_ref[:COUNT, col])
     for i in range(BLOCKS):
         width = BLOCK * (i + 1)
         at = pl.ds(BLOCK * i, BLOCK)
@@ -205,19 +205,36 @@
     out_ref[n:, :] = other_ref[...]
 
 
-def join_take_kernel(at_ref, own_ref, other_ref, dv_ref, out_ref, dv_out):
-    join_kernel(own_ref, other_ref, out_ref)
+def join_split_kernel(at_ref, own_ref, other_ref, dv_ref, first_ref, second_ref, dv_out):
+    n = own_ref.shape[0]
+    for j, out_ref in enumerate((first_ref, second_ref)):
+        out_ref[:n, :] = own_ref[:, HEAD * j : HEAD * (j + 1)]
+        out_ref[n:, :] = other_ref[:, HEAD * j : HEAD * (j + 1)]
     dv_out[...] = dv_ref[:, pl.ds(pl.multiple_of((1 - at_ref[3]) * HALF, HALF), HALF)]
+
+
+def two_joins_kernel(a0, a1, b0, b1, b2, b3, first_ref, second_ref):
+    n = a0.shape[0]
+    for j, part in enumerate((a0, a1)):
+        first_ref[n * j : n * (j + 1), :] = part[...]
+    for j, part in enumerate((b0, b1, b2, b3)):
+        second_ref[n * j : n * (j + 1), :] = part[...]
 
 
 def put_in_order(at_ref, pieces, codes_ref):
     z, y, x = at_ref[0], at_ref[1], at_ref[2]
-    for k, piece in enumerate(pieces):
-        for i in range(16):
-            zi, xi = (i & 1) * 4 + (i >> 2 & 1) * 2 + (i >> 3), i >> 1 & 1
-            to = ((z ^ zi) * 4 + ((y + 4 - k) & 3)) * 2 + (x ^ xi)
-            rows = pl.ds(pl.multiple_of(to * CHIP, CHIP), CHIP)
-            codes_ref[rows, :] = piece[pl.ds(i * CHIP, CHIP), :]
+
+    def place(piece, row, i, k, xi, col):
+        zi = (i & 1) * 4 + (i & 2) + (i >> 2)
+        to = ((z ^ zi) * 4 + ((y + 4 - k) & 3)) * 2 + (x ^ xi)
+        rows = pl.ds(pl.multiple_of(to * CHIP, CHIP), CHIP)
+        codes_ref[rows, pl.ds(col, HEAD)] = piece[pl.ds(row, CHIP), :]
+
+    for k in range(4):
+        for xi in range(2):
+            for i in range(8):
+                place(pieces[k], (xi * 8 + i) * CHIP, i, k, xi, 0)
+                place(pieces[4 + xi], (k * 8 + i) * CHIP, i, k, xi, HEAD)
 
 
 NEAR = 640
@@ -225,19 +242,19 @@
 
 
 def raw_kernel(at_ref, own_ref, other_ref, dv_own, dv_other, scale_ref, *refs):
-    pieces, (mine_ref, theirs_ref, sums_ref, kept_ref, near_ref, beside_ref, codes_ref) = refs[:4], refs[4:]
+    pieces, (mine_ref, core_ref, sums_ref, near_ref, beside_ref, codes_ref) = refs[:6], refs[6:]
     put_in_order(at_ref, pieces, codes_ref)
     cols = own_columns(at_ref)
     scale = scale_ref[:, cols]
     sums = jnp.zeros((1, HALF), F32)
-    terms = ((other_ref, dv_other[...], theirs_ref), (own_ref, dv_own[:, cols], mine_ref))
+    terms = ((other_ref, dv_other[...], core_ref), (own_ref, dv_own[:, cols], mine_ref))
     for hidden_ref, dv, values_ref in terms:
         raw = dot(hidden_ref[...], codes_ref[...], (1, 0))
-        values_ref[...] = (raw * scale).astype(BF16)
+        values_ref[:COUNT, :] = (raw * scale).astype(BF16)
         sums += jnp.sum(raw * dv, axis=0, keepdims=True)
     sums_ref[...] = sums
     s, half = at_ref[4], DEPTH // 2
-    kept_ref[...] = codes_ref[pl.ds(pl.multiple_of(s * half, half), half), :]
+    core_ref[COUNT:, :] = codes_ref[pl.ds(pl.multiple_of(s * half, half), half), :]
     base = (1 - s) * half
     for j in range(2):
         part = pl.ds(j * HALF, HALF)
@@ -247,8 +264,8 @@
 
 
 def raw_part(at, hidden, hidden_other, dv, dv_other, scale, pieces):
-    outs = [shape(COUNT, HALF), shape(COUNT, HALF), shape(1, HALF, dtype=F32)]
-    outs += [shape(DEPTH // 2, HALF), shape(2 * COUNT + NEAR, HALF), shape(BESIDES, HALF)]
+    outs = [shape(COUNT, HALF), shape(COUNT + DEPTH // 2, HALF), shape(1, HALF, dtype=F32)]
+    outs += [shape(2 * COUNT + NEAR, HALF), shape(BESIDES, HALF)]
     return call(
         raw_kernel, "raw_part", outs,
         [(SMEM, at)] + [(VMEM, a) for a in [hidden, hidden_other, dv, dv_other, scale] + pieces],
@@ -264,23 +281,23 @@
 BATCH = 512
 
 
-def hidden_terms(c, dv_ref, scale_ref, near_ref, own_codes, seq_codes):
+def hidden_terms(c, dv_ref, scale_ref, near_ref, core_codes, seq_codes):
     cols = pl.ds(pl.multiple_of(c * HALF, HALF), HALF)
     own = (dv_ref[:, cols] * scale_ref[:, cols]).astype(BF16)
     far = near_ref[pl.ds(pl.multiple_of(c * COUNT, COUNT), COUNT), :]
     for i in range(0, DEPTH // 2, BATCH):
-        rows = pl.ds(i, BATCH)
-        yield rows, dot(own, own_codes[rows, :], (1, 1)) + dot(far, seq_codes[rows, :], (1, 1))
-
-
-def own_terms_kernel(at_ref, dv_ref, scale_ref, near_ref, own_codes, seq_codes, out_ref):
-    for rows, total in hidden_terms(at_ref[3], dv_ref, scale_ref, near_ref, own_codes, seq_codes):
+        total = dot(own, core_codes[COUNT + i : COUNT + i + BATCH, :], (1, 1))
+        yield pl.ds(i, BATCH), total + dot(far, seq_codes[i : i + BATCH, :], (1, 1))
+
+
+def own_terms_kernel(at_ref, dv_ref, scale_ref, near_ref, core_codes, seq_codes, out_ref):
+    for rows, total in hidden_terms(at_ref[3], dv_ref, scale_ref, near_ref, core_codes, seq_codes):
         out_ref[:, rows] = total
 
 
-def far_terms_kernel(at_ref, dv_ref, scale_ref, near_ref, own_codes, seq_codes, part_ref, sums_ref, out_ref, sums_out):
+def far_terms_kernel(at_ref, dv_ref, scale_ref, near_ref, core_codes, seq_codes, part_ref, sums_ref, out_ref, sums_out):
     sums_out[...] = sums_ref[...]
-    for rows, total in hidden_terms(1 - at_ref[3], dv_ref, scale_ref, near_ref, own_codes, seq_codes):
+    for rows, total in hidden_terms(1 - at_ref[3], dv_ref, scale_ref, near_ref, core_codes, seq_codes):
         out_ref[:, rows] = (total + part_ref[:, rows]).astype(BF16)
 
 
@@ -325,65 +342,69 @@
     scale = value_scale.reshape(1, -1)
 
     rows = call(
-        first_join, "join", shape(CHIP, HALF), [(HBM, value_codes), (VMEM, send(value_codes, C_SWAP))],
+        first_join, "join", shape(CHIP, HALF), [(HBM, value_codes), (VMEM, send(value_codes, C_SWAP))], (at,),
         scratch_shapes=[pltpu.SemaphoreType.DMA],
     )
     probs, dv = [], None
-    for step, (perm, heads) in enumerate(((z_swap(4), (0, 1)), (X_SWAP, (2,)), (z_swap(2), (3,)), (z_swap(1), ()))):
-        got = send(rows, perm)
-        after = ()
+    for bit, heads in ((4, (0,)), (2, (1, 2)), (1, (3,))):
+        got = send(rows, z_swap(bit))
         for g in heads:
             if g == 0:
                 p, dv, hidden = probs_part(g, at, queries, keys, upstream, dv, (rows,), hidden)
             else:
                 p, dv = probs_part(g, at, queries, keys, upstream, dv, (rows,))
             probs.append(p)
-            after = (p,)
         n = rows.shape[0]
         ins = [(VMEM, rows), (VMEM, got)]
-        if step == 0:
-            rows, hidden = call(join_kernel, "join", shape(2 * n, HALF), ins, after, (hidden,))
+        if bit == 4:
+            rows, hidden = call(join_kernel, "join", shape(2 * n, HALF), ins, (p,), (hidden,))
             hidden_other = send(hidden, C_SWAP)
-        elif step == 2:
-            rows, dv_half = call(
-                join_take_kernel, "join", [shape(2 * n, HALF), shape(COUNT, HALF, dtype=F32)],
-                [(SMEM, at)] + ins + [(VMEM, dv)], after,
+        elif bit == 2:
+            rows = call(join_kernel, "join", shape(2 * n, HALF), ins, (p,))
+        else:
+            first, second, dv_half = call(
+                join_split_kernel, "join", [shape(2 * n, HEAD)] * 2 + [shape(COUNT, HALF, dtype=F32)],
+                [(SMEM, at)] + ins + [(VMEM, dv)], (hidden_other,),
             )
-            dv_other = send(dv_half, C_SWAP)
-        elif step == 3:
-            rows = call(join_kernel, "join", shape(2 * n, HALF), ins, (hidden_other, dv_other))
-        else:
-            rows = call(join_kernel, "join", shape(2 * n, HALF), ins, after)
-    pieces = [rows] + [send(rows, y_shift(k)) for k in (1, 2, 3)]
-    mine, theirs, sums, kept, near, beside = raw_part(at, hidden, hidden_other, dv, dv_other, scale, pieces)
-
-    values_far, kept_far = send(theirs, C_SWAP), send(kept, C_SWAP)
-    near = lax.ppermute(near, "seq", SEQ_SWAP)
-    beside = lax.ppermute(beside, ("dp", "seq"), BESIDE)
+    first_x = send(first, X_SWAP)
+    second_y = [send(second, y_shift(k)) for k in (1, 2, 3)]
+    dv_other = send(dv_half, C_SWAP)
+    n = first.shape[0]
+    first, second = call(
+        two_joins_kernel, "join", [shape(2 * n, HEAD), shape(4 * n, HEAD)],
+        [(VMEM, a) for a in [first, first_x, second] + second_y], (dv_other,),
+    )
+    pieces = [first] + [send(first, y_shift(k)) for k in (1, 2, 3)] + [second, send(second, X_SWAP)]
+    mine, core, sums, near, beside = raw_part(at, hidden, hidden_other, dv, dv_other, scale, pieces)
+
+    core_far = send(core, C_SWAP)
     base = [(SMEM, at), (VMEM, dv), (VMEM, scale)]
     held = None
     for step, perm in enumerate((X_SWAP, y_swap(1), y_swap(2), z_swap(1), z_swap(2), z_swap(4))):
         got = send(sums, perm)
-        after = ()
-        if 1 <= step <= 4:
-            *held, token = grads_part(
-                step - 1, at, queries, keys, upstream, mine, values_far, probs[step - 1], held, (sums,)
-            )
+        ins, after = [(VMEM, sums), (VMEM, got)], ()
+        if step == 0:
+            sums, near, beside = call(add_kernel, "add", shape(1, HALF, dtype=F32), ins, after, (near, beside))
+            near = lax.ppermute(near, "seq", SEQ_SWAP)
+            beside = lax.ppermute(beside, ("dp", "seq"), BESIDE)
+            continue
+        if step <= 4:
+            g = step - 1
+            *held, token = grads_part(g, at, queries, keys, upstream, mine, core_far, probs[g], held, (sums,))
             after = (token,)
-        if step == 4:
+        else:
             codes = call(codes_join_kernel, "join", shape(DEPTH // 2, HALF), [(VMEM, near), (VMEM, beside)], (sums,))
             codes_far = send(codes, C_SWAP)
-        elif step == 5:
             part = call(
                 own_terms_kernel, "own_terms", shape(COUNT, DEPTH // 2, dtype=F32),
-                base + [(VMEM, near), (VMEM, kept), (VMEM, codes)], (sums,),
+                base + [(VMEM, near), (VMEM, core), (VMEM, codes)], (sums,),
             )
             after = (part,)
-        sums = call(add_kernel, "add", shape(1, HALF, dtype=F32), [(VMEM, sums), (VMEM, got)], after)
+        sums = call(add_kernel, "add", shape(1, HALF, dtype=F32), ins, after)
     far = send(sums, C_SWAP)
     grad_hidden, sums = call(
         far_terms_kernel, "far_terms", [shape(COUNT, DEPTH // 2), shape(1, HALF, dtype=F32)],
-        base + [(VMEM, a) for a in (near, kept_far, codes_far, part, sums)],
+        base + [(VMEM, a) for a in (near, core_far, codes_far, part, sums)],
     )
     both = jnp.concatenate([jnp.where(me % 2 == 0, sums, far), jnp.where(me % 2 == 0, far, sums)], axis=1)
     return held[0], held[1], grad_hidden, (both * scale).reshape(-1)

time: 127 us -> 104 us (0.82)
  waiting for transfers between devices: 58.6 us -> 26.7 us
  starting transfers between devices: 32.5 us -> 39.4 us
  local copies, waits for them, and re-layouts: 2.65 us -> 4.28 us
    ppermute x20 -> x23, waiting for transfers between devices: 58.6 us -> 26.2 us  [send(): return lax.ppermute(x, 'dp', perm)]
    ppermute x20 -> x23, starting transfers between devices: 29.4 us -> 36.4 us  [send(): return lax.ppermute(x, 'dp', perm)]
    unnamed x12, local copies, waits for them, and re-layouts: 1.91 us -> 3.53 us
  transfers between devices with their start and end apart: 22 -> 25, of which waited for: 10 -> 12; matrix products, arithmetic and copies ran while one was open for 1% -> 1% of each run, Pallas kernels for 22% -> 25%
where the time goes in v8:
time: 104 us; the launch traced here: 103 us
  starting transfers between devices  39.4 us (38%)
  Pallas kernels  31.5 us (30%)
  waiting for transfers between devices  26.7 us (26%)
  local copies, waits for them, and re-layouts  4.28 us (4%)
    ppermute x23, starting transfers between devices, send(): return lax.ppermute(x, 'dp', perm)  36.4 us
    pallas_call x23, Pallas kernels, call(): pl.pallas_call(run, in_specs=list(specs) + [ANY] * (len(after) + len(thro...  31.5 us
    ppermute x23, waiting for transfers between devices, send(): return lax.ppermute(x, 'dp', perm)  26.2 us
    unnamed x12, local copies, waits for them, and re-layouts  3.53 us
  transfers between devices with their start and end apart: 25, of which 12 were waited for; matrix products, arithmetic and copies ran while one was open for 1% of the time, Pallas kernels for 25%

profile of v8, /device:TPU:1, one launch (start us, length us, event | category | flops | bytes accessed | tf_op | source)
XLA Modules:
  0.0 103.3 jit_solution(3105659584220055998)
XLA Ops:
  0.6 3.3 %collective-permute-start = (bf16[32,512]{1,0:T(8,128)(2,1)}, bf16[32,512]{1,0:T(8,128)(2,1)S(1)}, u32[]{:S(2)}, u32[]{:S(2)}) collective-permute-start(bf16[32,512]{1,0:T(8,128)(2,1)} %refs_0_.1), channel_id=1, source_target_pairs={{0,2},{2,0},{4,6},{6,4},{8,10},{10,8},{12,14},{14,12},{16,18},{18,... | collective-permute-start | bytes 98312 | tf_op jit(solution)/shard_map/ppermute | solution.py:335
  4.0 0.7 slice_bitcast_fusion
  5.0 0.7 join.6.refs_5_.refs_0_
  5.8 5.3 %collective-permute-start.1 = (bf16[64,256]{1,0:T(8,128)(2,1)S(1)}, bf16[64,256]{1,0:T(8,128)(2,1)S(1)}, u32[]{:S(2)}, u32[]{:S(2)}) collective-permute-start(bf16[64,256]{1,0:T(8,128)(2,1)S(1)} %join.6.refs_5_.refs_0_), channel_id=1, source_target_pairs={{0,128},{2,130},{4,132},{6,134},{8,136},{10,138},{12,140},{14,142}... | collective-permute-start | bytes 98312 | tf_op jit(solution)/shard_map/ppermute | solution.py:335
  11.0 3.4 %probs_part.4 = (bf16[4,384,384]{2,1,0:T(8,128)(2,1)S(1)}, f32[384,512]{1,0:T(8,128)S(1)}, bf16[384,4096]{1,0:T(8,128)(2,1)S(1)}) custom-call(s32[8]{0:T(128)S(1)} %concatenate.11.refs_2_.refs_0_, bf16[384,2048]{1,0:T(8,128)(2,1)} %refs_1_.15, bf16[384,512]{1,0:T(8,128)(2,1)} %refs_2_.15, bf16[384,2048]{1,0:T(8,128)(2,1)} %refs_3_.15, ...), custom_call_target="tpu_custom_call" | custom-call | flops 1000 | bytes 1000 | tf_op jit(solution)/shard_map/probs_part/pallas_call | solution.py:53
  14.5 0.7 collective-permute-start.2
  15.2 1.2 %collective-permute-start.3 = (bf16[128,256]{1,0:T(8,128)(2,1)S(1)}, bf16[128,256]{1,0:T(8,128)(2,1)S(1)}, u32[]{:S(2)}, u32[]{:S(2)}) collective-permute-start(bf16[128,256]{1,0:T(8,128)(2,1)S(1)} %get-tuple-element.46.refs_5_.refs_0_), channel_id=1, source_target_pairs={{0,64},{2,66},{4,68},{6,70},{8,72},{10,74},{12,76},{14,78},{16,80}... | collective-permute-start | bytes 196616 | tf_op jit(solution)/shard_map/ppermute | solution.py:335
  16.4 2.2 %probs_part.5 = (bf16[4,384,384]{2,1,0:T(8,128)(2,1)S(1)}, f32[384,512]{1,0:T(8,128)S(1)}) custom-call(s32[8]{0:T(128)S(1)} %concatenate.11.refs_2_.refs_0_, bf16[384,2048]{1,0:T(8,128)(2,1)S(1)} %copy-done, bf16[384,512]{1,0:T(8,128)(2,1)S(1)} %copy-done.4, bf16[384,2048]{1,0:T(8,128)(2,1)S(1)} %copy-done.1, ...), custom_call_target="tpu_custom_call", output_to_operand_aliasing={{1}: (4, {})} | custom-call | flops 1000 | bytes 1000 | tf_op jit(solution)/shard_map/probs_part/pallas_call | solution.py:53
  18.6 2.2 %probs_part.6 = (bf16[4,384,384]{2,1,0:T(8,128)(2,1)S(1)}, f32[384,512]{1,0:T(8,128)S(1)}) custom-call(s32[8]{0:T(128)S(1)} %concatenate.11.refs_2_.refs_0_, bf16[384,2048]{1,0:T(8,128)(2,1)S(1)} %copy-done, bf16[384,512]{1,0:T(8,128)(2,1)S(1)} %copy-done.4, bf16[384,2048]{1,0:T(8,128)(2,1)S(1)} %copy-done.1, ...), custom_call_target="tpu_custom_call", output_to_operand_aliasing={{1}: (4, {})} | custom-call | flops 1000 | bytes 1000 | tf_op jit(solution)/shard_map/probs_part/pallas_call | solution.py:53
  20.8 0.4 collective-permute-done.3.refs_1_
  21.2 0.5 collective-permute-start.4
  21.7 2.2 %probs_part.7 = (bf16[4,384,384]{2,1,0:T(8,128)(2,1)S(1)}, f32[384,512]{1,0:T(8,128)S(1)}) custom-call(s32[8]{0:T(128)S(1)} %concatenate.11.refs_2_.refs_0_, bf16[384,2048]{1,0:T(8,128)(2,1)S(1)} %copy-done, bf16[384,512]{1,0:T(8,128)(2,1)S(1)} %copy-done.4, bf16[384,2048]{1,0:T(8,128)(2,1)S(1)} %copy-done.1, ...), custom_call_target="tpu_custom_call", output_to_operand_aliasing={{1}: (4, {})} | custom-call | flops 1000 | bytes 1000 | tf_op jit(solution)/shard_map/probs_part/pallas_call | solution.py:53
  23.9 1.6 %collective-permute-done.4.refs_2_ = bf16[256,256]{1,0:T(8,128)(2,1)S(1)} collective-permute-done((bf16[256,256]{1,0:T(8,128)(2,1)S(1)}, bf16[256,256]{1,0:T(8,128)(2,1)S(1)}, u32[]{:S(2)}, u32[]{:S(2)}) %collective-permute-start.4) | collective-permute-done | bytes 131104 | tf_op jit(solution)/shard_map/ppermute | solution.py:335
  25.5 0.6 join.9
  26.1 1.8 %collective-permute-start.5 = (f32[384,256]{1,0:T(8,128)S(1)}, f32[384,256]{1,0:T(8,128)S(1)}, u32[]{:S(2)}, u32[]{:S(2)}) collective-permute-start(f32[384,256]{1,0:T(8,128)S(1)} %get-tuple-element.51), channel_id=1, source_target_pairs={{0,2},{2,0},{4,6},{6,4},{8,10},{10,8},{12,14},{14,12},{16,18},{18,... | collective-permute-start | bytes 1179656 | tf_op jit(solution)/shard_map/ppermute | solution.py:335
  27.9 2.8 %collective-permute-start.6 = (bf16[512,128]{1,0:T(8,128)(2,1)S(1)}, bf16[512,128]{1,0:T(8,128)(2,1)S(1)}, u32[]{:S(2)}, u32[]{:S(2)}) collective-permute-start(bf16[512,128]{1,0:T(8,128)(2,1)S(1)} %get-tuple-element.52.refs_0_), channel_id=1, source_target_pairs={{0,4},{2,6},{4,0},{6,2},{8,12},{10,14},{12,8},{14,10},{16,20},{18,... | collective-permute-start | bytes 393224 | tf_op jit(solution)/shard_map/ppermute | solution.py:335
  30.7 2.7 %collective-permute-start.9 = (bf16[512,128]{1,0:T(8,128)(2,1)S(1)}, bf16[512,128]{1,0:T(8,128)(2,1)S(1)}, u32[]{:S(2)}, u32[]{:S(2)}) collective-permute-start(bf16[512,128]{1,0:T(8,128)(2,1)S(1)} %get-tuple-element.53.refs_2_), channel_id=1, source_target_pairs={{0,24},{2,26},{4,28},{6,30},{8,0},{10,2},{12,4},{14,6},{16,8},{18,... | collective-permute-start | bytes 393224 | tf_op jit(solution)/shard_map/ppermute | solution.py:335
  33.8 0.7 collective-permute-start.7
  34.5 4.1 %collective-permute-done.9.refs_5_ = bf16[512,128]{1,0:T(8,128)(2,1)S(1)} collective-permute-done((bf16[512,128]{1,0:T(8,128)(2,1)S(1)}, bf16[512,128]{1,0:T(8,128)(2,1)S(1)}, u32[]{:S(2)}, u32[]{:S(2)}) %collective-permute-start.9) | collective-permute-done | bytes 131104 | tf_op jit(solution)/shard_map/ppermute | solution.py:335
  38.6 0.7 collective-permute-done.8.refs_4_
  39.3 3.8 %collective-permute-done.7.refs_3_ = bf16[512,128]{1,0:T(8,128)(2,1)S(1)} collective-permute-done((bf16[512,128]{1,0:T(8,128)(2,1)S(1)}, bf16[512,128]{1,0:T(8,128)(2,1)S(1)}, u32[]{:S(2)}, u32[]{:S(2)}) %collective-permute-start.7) | collective-permute-done | bytes 131104 | tf_op jit(solution)/shard_map/ppermute | solution.py:335
  43.2 0.5 collective-permute-start.13
  43.7 1.5 %collective-permute-start.10 = (bf16[1024,128]{1,0:T(8,128)(2,1)S(1)}, bf16[1024,128]{1,0:T(8,128)(2,1)S(1)}, u32[]{:S(2)}, u32[]{:S(2)}) collective-permute-start(bf16[1024,128]{1,0:T(8,128)(2,1)S(1)} %get-tuple-element.54.refs_6_), channel_id=1, source_target_pairs={{0,8},{2,10},{4,12},{6,14},{8,16},{10,18},{12,20},{14,22},{16,24},... | collective-permute-start | bytes 786440 | tf_op jit(solution)/shard_map/ppermute | solution.py:335
  45.2 5.6 %collective-permute-done.12.refs_9_ = bf16[1024,128]{1,0:T(8,128)(2,1)S(1)} collective-permute-done((bf16[1024,128]{1,0:T(8,128)(2,1)S(1)}, bf16[1024,128]{1,0:T(8,128)(2,1)S(1)}, u32[]{:S(2)}, u32[]{:S(2)}) %collective-permute-start.12) | collective-permute-done | bytes 262176 | tf_op jit(solution)/shard_map/ppermute | solution.py:335
  50.8 0.9 collective-permute-done.11.refs_8_
  51.7 7.4 %collective-permute-done.10.refs_7_ = bf16[1024,128]{1,0:T(8,128)(2,1)S(1)} collective-permute-done((bf16[1024,128]{1,0:T(8,128)(2,1)S(1)}, bf16[1024,128]{1,0:T(8,128)(2,1)S(1)}, u32[]{:S(2)}, u32[]{:S(2)}) %collective-permute-start.10) | collective-permute-done | bytes 262176 | tf_op jit(solution)/shard_map/ppermute | solution.py:335
  59.1 2.9 %raw_part.1 = (bf16[384,256]{1,0:T(8,128)(2,1)S(1)}, bf16[2432,256]{1,0:T(8,128)(2,1)S(1)}, f32[1,256]{1,0:T(1,128)S(1)}, bf16[1408,256]{1,0:T(8,128)(2,1)S(1)}, bf16[1408,256]{1,0:T(8,128)(2,1)S(1)}) custom-call(s32[8]{0:T(128)S(1)} %concatenate.11.refs_2_.refs_0_, bf16[384,4096]{1,0:T(8,128)(2,1)S(1)} %get-tuple-element.44.refs_1_, ...), custom_call_target="tpu_custom_call" | custom-call | flops 1000 | bytes 1000 | tf_op jit(solution)/shard_map/raw_part/pallas_call | solution.py:53
  62.0 0.6 collective-permute-start.14
  62.5 2.8 %collective-permute-start.15 = (f32[1,256]{1,0:T(1,128)S(1)}, f32[1,256]{1,0:T(1,128)S(1)}, u32[]{:S(2)}, u32[]{:S(2)}) collective-permute-start(f32[1,256]{1,0:T(1,128)S(1)} %get-tuple-element.60.refs_0_), channel_id=1, source_target_pairs={{0,4},{2,6},{4,0},{6,2},{8,12},{10,14},{12,8},{14,10},{16,20},{18,... | collective-permute-start | bytes 3080 | tf_op jit(solution)/shard_map/ppermute | solution.py:335
  65.3 1.2 %collective-permute-done.15.refs_1_ = f32[1,256]{1,0:T(1,128)S(1)} collective-permute-done((f32[1,256]{1,0:T(1,128)S(1)}, f32[1,256]{1,0:T(1,128)S(1)}, u32[]{:S(2)}, u32[]{:S(2)}) %collective-permute-start.15) | collective-permute-done | bytes 1056 | tf_op jit(solution)/shard_map/ppermute | solution.py:335
  66.5 1.2 %collective-permute-start.19 = (bf16[1408,256]{1,0:T(8,128)(2,1)S(1)}, bf16[1408,256]{1,0:T(8,128)(2,1)S(1)}, u32[]{:S(2)}, u32[]{:S(2)}) collective-permute-start(bf16[1408,256]{1,0:T(8,128)(2,1)S(1)} %get-tuple-element.75), channel_id=1, source_target_pairs={{0,1},{1,0},{2,3},{3,2},{4,5},{5,4},{6,7},{7,6},{8,9},{9,8},{10,11... | collective-permute-start | bytes 2162696 | tf_op jit(solution)/shard_map/ppermute | solution.py:388
  67.7 1.8 %collective-permute-start.20 = (bf16[1408,256]{1,0:T(8,128)(2,1)S(1)}, bf16[1408,256]{1,0:T(8,128)(2,1)S(1)}, u32[]{:S(2)}, u32[]{:S(2)}) collective-permute-start(bf16[1408,256]{1,0:T(8,128)(2,1)S(1)} %get-tuple-element.76), channel_id=1, source_target_pairs={{0,5},{1,4},{2,7},{3,6},{4,1},{5,0},{6,3},{7,2},{8,13},{9,12},{10,... | collective-permute-start | bytes 2162696 | tf_op jit(solution)/shard_map/ppermute | solution.py:389
  69.5 2.6 %grads_part.4 = (bf16[384,2048]{1,0:T(8,128)(2,1)}, bf16[384,512]{1,0:T(8,128)(2,1)}, f32[8,128]{1,0:T(8,128)S(1)}) custom-call(s32[8]{0:T(128)S(1)} %concatenate.11.refs_2_.refs_0_, bf16[384,2048]{1,0:T(8,128)(2,1)S(1)} %copy-done, bf16[384,512]{1,0:T(8,128)(2,1)S(1)} %copy-done.4, bf16[384,2048]{1,0:T(8,128)(2,1)S(1)} %copy-done.1, ...), custom_call_target="tpu_custom_call" | custom-call | flops 1000 | bytes 1000 | tf_op jit(solution)/shard_map/grads_part/pallas_call | solution.py:53
  72.2 2.1 %collective-permute-start.17 = (f32[1,256]{1,0:T(1,128)S(1)}, f32[1,256]{1,0:T(1,128)S(1)}, u32[]{:S(2)}, u32[]{:S(2)}) collective-permute-start(f32[1,256]{1,0:T(1,128)S(1)} %add.25.refs_9_.refs_0_), channel_id=1, source_target_pairs={{0,16},{2,18},{4,20},{6,22},{8,24},{10,26},{12,28},{14,30},{16,0},... | collective-permute-start | bytes 3080 | tf_op jit(solution)/shard_map/ppermute | solution.py:335
  74.3 2.6 %grads_part.5 = (bf16[384,2048]{1,0:T(8,128)(2,1)}, bf16[384,512]{1,0:T(8,128)(2,1)}, f32[8,128]{1,0:T(8,128)S(1)}) custom-call(s32[8]{0:T(128)S(1)} %concatenate.11.refs_2_.refs_0_, bf16[384,2048]{1,0:T(8,128)(2,1)S(1)} %copy-done, bf16[384,512]{1,0:T(8,128)(2,1)S(1)} %copy-done.4, ...), custom_call_target="tpu_custom_call", output_to_operand_aliasing={{0}: (7, {}), {1}: (8, {})} | custom-call | flops 1000 | bytes 1000 | tf_op jit(solution)/shard_map/grads_part/pallas_call | solution.py:53
  76.9 0.5 collective-permute-start.18
  77.4 2.6 %grads_part.6 = (bf16[384,2048]{1,0:T(8,128)(2,1)}, bf16[384,512]{1,0:T(8,128)(2,1)}, f32[8,128]{1,0:T(8,128)S(1)}) custom-call(s32[8]{0:T(128)S(1)} %concatenate.11.refs_2_.refs_0_, bf16[384,2048]{1,0:T(8,128)(2,1)S(1)} %copy-done, bf16[384,512]{1,0:T(8,128)(2,1)S(1)} %copy-done.4, ...), custom_call_target="tpu_custom_call", output_to_operand_aliasing={{0}: (7, {}), {1}: (8, {})} | custom-call | flops 1000 | bytes 1000 | tf_op jit(solution)/shard_map/grads_part/pallas_call | solution.py:53
  80.0 1.8 %collective-permute-start.21 = (f32[1,256]{1,0:T(1,128)S(1)}, f32[1,256]{1,0:T(1,128)S(1)}, u32[]{:S(2)}, u32[]{:S(2)}) collective-permute-start(f32[1,256]{1,0:T(1,128)S(1)} %add.27.refs_9_.refs_0_), channel_id=1, source_target_pairs={{0,64},{2,66},{4,68},{6,70},{8,72},{10,74},{12,76},{14,78},{16,80}... | collective-permute-start | bytes 3080 | tf_op jit(solution)/shard_map/ppermute | solution.py:335
  81.9 2.6 %grads_part.7 = (bf16[384,2048]{1,0:T(8,128)(2,1)}, bf16[384,512]{1,0:T(8,128)(2,1)}, f32[8,128]{1,0:T(8,128)S(1)}) custom-call(s32[8]{0:T(128)S(1)} %concatenate.11.refs_2_.refs_0_, bf16[384,2048]{1,0:T(8,128)(2,1)S(1)} %copy-done, bf16[384,512]{1,0:T(8,128)(2,1)S(1)} %copy-done.4, ...), custom_call_target="tpu_custom_call", output_to_operand_aliasing={{0}: (7, {}), {1}: (8, {})} | custom-call | flops 1000 | bytes 1000 | tf_op jit(solution)/shard_map/grads_part/pallas_call | solution.py:53
  84.5 0.5 collective-permute-done.20.refs_1_
  85.0 1.0 %join.11.refs_5_ = bf16[2048,256]{1,0:T(8,128)(2,1)} custom-call(bf16[1408,256]{1,0:T(8,128)(2,1)S(1)} %collective-permute-done.19.refs_0_.refs_3_, bf16[1408,256]{1,0:T(8,128)(2,1)S(1)} %collective-permute-done.20.refs_1_, f32[1,256]{1,0:T(1,128)S(1)} %add.28.refs_2_.refs_6_.refs_0_), custom_call_target="tpu_custom_call" | custom-call | flops 1000 | bytes 1000 | tf_op jit(solution)/shard_map/join/pallas_call | solution.py:53
  86.1 3.0 %collective-permute-start.22 = (bf16[2048,256]{1,0:T(8,128)(2,1)}, bf16[2048,256]{1,0:T(8,128)(2,1)}, u32[]{:S(2)}, u32[]{:S(2)}) collective-permute-start(bf16[2048,256]{1,0:T(8,128)(2,1)} %join.11.refs_5_), channel_id=1, source_target_pairs={{0,2},{2,0},{4,6},{6,4},{8,10},{10,8},{12,14},{14,12},{16,18},{18,... | collective-permute-start | bytes 3145736 | tf_op jit(solution)/shard_map/ppermute | solution.py:335
  89.1 4.1 %collective-permute-start.23 = (f32[1,256]{1,0:T(1,128)S(1)}, f32[1,256]{1,0:T(1,128)S(1)}, u32[]{:S(2)}, u32[]{:S(2)}) collective-permute-start(f32[1,256]{1,0:T(1,128)S(1)} %add.28.refs_2_.refs_6_.refs_0_), channel_id=1, source_target_pairs={{0,128},{2,130},{4,132},{6,134},{8,136},{10,138},{12,140},{14,142}... | collective-permute-start | bytes 3080 | tf_op jit(solution)/shard_map/ppermute | solution.py:335
  93.2 2.2 %own_terms.1.refs_2_.refs_6_ = f32[384,2048]{1,0:T(8,128)S(1)} custom-call(s32[8]{0:T(128)S(1)} %concatenate.11.refs_2_.refs_0_, f32[384,512]{1,0:T(8,128)S(1)} %get-tuple-element.50.refs_3_.refs_1_, f32[1,512]{1,0:T(1,128)S(1)} %bitcast.11, bf16[1408,256]{1,0:T(8,128)(2,1)S(1)} %collective-permute-done.19.refs_0_.refs_3_, ...), custom_call_target="tpu_custom_call" | custom-call | flops 1000 | bytes 1000 | tf_op jit(solution)/shard_map/own_terms/pallas_call | solution.py:53
  95.4 1.6 %copy-done.2 = f32[384,2048]{1,0:T(8,128)} copy-done((f32[384,2048]{1,0:T(8,128)}, f32[384,2048]{1,0:T(8,128)S(1)}, u32[]{:S(2)}) %copy-start.2) | copy-done | bytes 3145752
  97.3 1.9 %copy-done.3 = f32[384,2048]{1,0:T(8,128)S(1)} copy-done((f32[384,2048]{1,0:T(8,128)S(1)}, f32[384,2048]{1,0:T(8,128)}, u32[]{:S(2)}) %copy-start.3) | copy-done | bytes 3145752
  99.2 3.5 %far_terms.1 = (bf16[384,2048]{1,0:T(8,128)(2,1)}, f32[1,256]{1,0:T(1,128)S(1)}) custom-call(s32[8]{0:T(128)S(1)} %concatenate.11.refs_2_.refs_0_, f32[384,512]{1,0:T(8,128)S(1)} %get-tuple-element.50.refs_3_.refs_1_, f32[1,512]{1,0:T(1,128)S(1)} %bitcast.12, bf16[1408,256]{1,0:T(8,128)(2,1)S(1)} %collective-permute-done.19.refs_0_.refs_3_, ...), custom_call_target="tpu_custom_call" | custom-call | flops 1000 | bytes 1000 | tf_op jit(solution)/shard_map/far_terms/pallas_call | solution.py:53
  102.7 0.6 maximum_multiply_fusion
  (41 shorter events, 1.3 us)
Async XLA Ops:
  0.6 4.4 %collective-permute-start = (bf16[32,512]{1,0:T(8,128)(2,1)}, bf16[32,512]{1,0:T(8,128)(2,1)S(1)}, u32[]{:S(2)}, u32[]{:S(2)}) collective-permute-start(bf16[32,512]{1,0:T(8,128)(2,1)} %refs_0_.1), channel_id=1, source_target_pairs={{0,2},{2,0},{4,6},{6,4},{8,10},{10,8},{12,14},{14,12},{16,18},{18,... | collective-permute-start | bytes 98312 | tf_op jit(solution)/shard_map/ppermute | solution.py:335
  5.8 8.7 %collective-permute-start.1 = (bf16[64,256]{1,0:T(8,128)(2,1)S(1)}, bf16[64,256]{1,0:T(8,128)(2,1)S(1)}, u32[]{:S(2)}, u32[]{:S(2)}) collective-permute-start(bf16[64,256]{1,0:T(8,128)(2,1)S(1)} %join.6.refs_5_.refs_0_), channel_id=1, source_target_pairs={{0,128},{2,130},{4,132},{6,134},{8,136},{10,138},{12,140},{14,142}... | collective-permute-start | bytes 98312 | tf_op jit(solution)/shard_map/ppermute | solution.py:335
  14.5 2.0 %copy-start = (bf16[384,2048]{1,0:T(8,128)(2,1)S(1)}, bf16[384,2048]{1,0:T(8,128)(2,1)}, u32[]{:S(2)}) copy-start(bf16[384,2048]{1,0:T(8,128)(2,1)} %refs_1_.15) | copy-start | bytes 4718596
  14.5 2.0 %copy-start.1 = (bf16[384,2048]{1,0:T(8,128)(2,1)S(1)}, bf16[384,2048]{1,0:T(8,128)(2,1)}, u32[]{:S(2)}) copy-start(bf16[384,2048]{1,0:T(8,128)(2,1)} %refs_3_.15) | copy-start | bytes 4718596
  14.5 2.0 %copy-start.4 = (bf16[384,512]{1,0:T(8,128)(2,1)S(1)}, bf16[384,512]{1,0:T(8,128)(2,1)}, u32[]{:S(2)}) copy-start(bf16[384,512]{1,0:T(8,128)(2,1)} %refs_2_.15) | copy-start | bytes 1179652
  14.5 10.9 %collective-permute-start.2 = (bf16[384,4096]{1,0:T(8,128)(2,1)S(1)}, bf16[384,4096]{1,0:T(8,128)(2,1)S(1)}, u32[]{:S(2)}, u32[]{:S(2)}) collective-permute-start(bf16[384,4096]{1,0:T(8,128)(2,1)S(1)} %get-tuple-element.44.refs_1_), channel_id=1, source_target_pairs={{0,2},{2,0},{4,6},{6,4},{8,10},{10,8},{12,14},{14,12},{16,18},{18,... | collective-permute-start | bytes 9437192 | tf_op jit(solution)/shard_map/ppermute | solution.py:335
  15.2 6.0 %collective-permute-start.3 = (bf16[128,256]{1,0:T(8,128)(2,1)S(1)}, bf16[128,256]{1,0:T(8,128)(2,1)S(1)}, u32[]{:S(2)}, u32[]{:S(2)}) collective-permute-start(bf16[128,256]{1,0:T(8,128)(2,1)S(1)} %get-tuple-element.46.refs_5_.refs_0_), channel_id=1, source_target_pairs={{0,64},{2,66},{4,68},{6,70},{8,72},{10,74},{12,76},{14,78},{16,80}... | collective-permute-start | bytes 196616 | tf_op jit(solution)/shard_map/ppermute | solution.py:335
  21.2 4.2 %collective-permute-start.4 = (bf16[256,256]{1,0:T(8,128)(2,1)S(1)}, bf16[256,256]{1,0:T(8,128)(2,1)S(1)}, u32[]{:S(2)}, u32[]{:S(2)}) collective-permute-start(bf16[256,256]{1,0:T(8,128)(2,1)S(1)} %join.8.refs_5_.refs_1_), channel_id=1, source_target_pairs={{0,32},{2,34},{4,36},{6,38},{8,40},{10,42},{12,44},{14,46},{16,48}... | collective-permute-start | bytes 393224 | tf_op jit(solution)/shard_map/ppermute | solution.py:335
  25.5 33.6 %copy-start.5 = (f32[512]{0:T(512)S(1)}, f32[512]{0:T(512)}, u32[]{:S(2)}) copy-start(f32[512]{0:T(512)} %param.11) | copy-start | bytes 6148
  26.1 17.1 %collective-permute-start.5 = (f32[384,256]{1,0:T(8,128)S(1)}, f32[384,256]{1,0:T(8,128)S(1)}, u32[]{:S(2)}, u32[]{:S(2)}) collective-permute-start(f32[384,256]{1,0:T(8,128)S(1)} %get-tuple-element.51), channel_id=1, source_target_pairs={{0,2},{2,0},{4,6},{6,4},{8,10},{10,8},{12,14},{14,12},{16,18},{18,... | collective-permute-start | bytes 1179656 | tf_op jit(solution)/shard_map/ppermute | solution.py:335
  27.9 6.6 %collective-permute-start.6 = (bf16[512,128]{1,0:T(8,128)(2,1)S(1)}, bf16[512,128]{1,0:T(8,128)(2,1)S(1)}, u32[]{:S(2)}, u32[]{:S(2)}) collective-permute-start(bf16[512,128]{1,0:T(8,128)(2,1)S(1)} %get-tuple-element.52.refs_0_), channel_id=1, source_target_pairs={{0,4},{2,6},{4,0},{6,2},{8,12},{10,14},{12,8},{14,10},{16,20},{18,... | collective-permute-start | bytes 393224 | tf_op jit(solution)/shard_map/ppermute | solution.py:335
  30.7 7.9 %collective-permute-start.9 = (bf16[512,128]{1,0:T(8,128)(2,1)S(1)}, bf16[512,128]{1,0:T(8,128)(2,1)S(1)}, u32[]{:S(2)}, u32[]{:S(2)}) collective-permute-start(bf16[512,128]{1,0:T(8,128)(2,1)S(1)} %get-tuple-element.53.refs_2_), channel_id=1, source_target_pairs={{0,24},{2,26},{4,28},{6,30},{8,0},{10,2},{12,4},{14,6},{16,8},{18,... | collective-permute-start | bytes 393224 | tf_op jit(solution)/shard_map/ppermute | solution.py:335
  33.4 5.9 %collective-permute-start.8 = (bf16[512,128]{1,0:T(8,128)(2,1)S(1)}, bf16[512,128]{1,0:T(8,128)(2,1)S(1)}, u32[]{:S(2)}, u32[]{:S(2)}) collective-permute-start(bf16[512,128]{1,0:T(8,128)(2,1)S(1)} %get-tuple-element.53.refs_2_), channel_id=1, source_target_pairs={{0,16},{2,18},{4,20},{6,22},{8,24},{10,26},{12,28},{14,30},{16,0},... | collective-permute-start | bytes 393224 | tf_op jit(solution)/shard_map/ppermute | solution.py:335
  33.8 9.4 %collective-permute-start.7 = (bf16[512,128]{1,0:T(8,128)(2,1)S(1)}, bf16[512,128]{1,0:T(8,128)(2,1)S(1)}, u32[]{:S(2)}, u32[]{:S(2)}) collective-permute-start(bf16[512,128]{1,0:T(8,128)(2,1)S(1)} %get-tuple-element.53.refs_2_), channel_id=1, source_target_pairs={{0,8},{2,10},{4,12},{6,14},{8,16},{10,18},{12,20},{14,22},{16,24},... | collective-permute-start | bytes 393224 | tf_op jit(solution)/shard_map/ppermute | solution.py:335
  43.2 15.9 %collective-permute-start.13 = (bf16[2048,128]{1,0:T(8,128)(2,1)S(1)}, bf16[2048,128]{1,0:T(8,128)(2,1)S(1)}, u32[]{:S(2)}, u32[]{:S(2)}) collective-permute-start(bf16[2048,128]{1,0:T(8,128)(2,1)S(1)} %get-tuple-element.55.refs_10_), channel_id=1, source_target_pairs={{0,4},{2,6},{4,0},{6,2},{8,12},{10,14},{12,8},{14,10},{16,20},{18,... | collective-permute-start | bytes 1572872 | tf_op jit(solution)/shard_map/ppermute | solution.py:335
  43.7 7.1 %collective-permute-start.12 = (bf16[1024,128]{1,0:T(8,128)(2,1)S(1)}, bf16[1024,128]{1,0:T(8,128)(2,1)S(1)}, u32[]{:S(2)}, u32[]{:S(2)}) collective-permute-start(bf16[1024,128]{1,0:T(8,128)(2,1)S(1)} %get-tuple-element.54.refs_6_), channel_id=1, source_target_pairs={{0,24},{2,26},{4,28},{6,30},{8,0},{10,2},{12,4},{14,6},{16,8},{18,... | collective-permute-start | bytes 786440 | tf_op jit(solution)/shard_map/ppermute | solution.py:335
  43.7 8.0 %collective-permute-start.11 = (bf16[1024,128]{1,0:T(8,128)(2,1)S(1)}, bf16[1024,128]{1,0:T(8,128)(2,1)S(1)}, u32[]{:S(2)}, u32[]{:S(2)}) collective-permute-start(bf16[1024,128]{1,0:T(8,128)(2,1)S(1)} %get-tuple-element.54.refs_6_), channel_id=1, source_target_pairs={{0,16},{2,18},{4,20},{6,22},{8,24},{10,26},{12,28},{14,30},{16,0},... | collective-permute-start | bytes 786440 | tf_op jit(solution)/shard_map/ppermute | solution.py:335
  43.7 15.3 %collective-permute-start.10 = (bf16[1024,128]{1,0:T(8,128)(2,1)S(1)}, bf16[1024,128]{1,0:T(8,128)(2,1)S(1)}, u32[]{:S(2)}, u32[]{:S(2)}) collective-permute-start(bf16[1024,128]{1,0:T(8,128)(2,1)S(1)} %get-tuple-element.54.refs_6_), channel_id=1, source_target_pairs={{0,8},{2,10},{4,12},{6,14},{8,16},{10,18},{12,20},{14,22},{16,24},... | collective-permute-start | bytes 786440 | tf_op jit(solution)/shard_map/ppermute | solution.py:335
  62.0 7.5 %collective-permute-start.14 = (bf16[2432,256]{1,0:T(8,128)(2,1)S(1)}, bf16[2432,256]{1,0:T(8,128)(2,1)S(1)}, u32[]{:S(2)}, u32[]{:S(2)}) collective-permute-start(bf16[2432,256]{1,0:T(8,128)(2,1)S(1)} %get-tuple-element.57.refs_4_), channel_id=1, source_target_pairs={{0,2},{2,0},{4,6},{6,4},{8,10},{10,8},{12,14},{14,12},{16,18},{18,... | collective-permute-start | bytes 3735560 | tf_op jit(solution)/shard_map/ppermute | solution.py:335
  62.5 3.9 %collective-permute-start.15 = (f32[1,256]{1,0:T(1,128)S(1)}, f32[1,256]{1,0:T(1,128)S(1)}, u32[]{:S(2)}, u32[]{:S(2)}) collective-permute-start(f32[1,256]{1,0:T(1,128)S(1)} %get-tuple-element.60.refs_0_), channel_id=1, source_target_pairs={{0,4},{2,6},{4,0},{6,2},{8,12},{10,14},{12,8},{14,10},{16,20},{18,... | collective-permute-start | bytes 3080 | tf_op jit(solution)/shard_map/ppermute | solution.py:335
  66.5 18.0 %collective-permute-start.19 = (bf16[1408,256]{1,0:T(8,128)(2,1)S(1)}, bf16[1408,256]{1,0:T(8,128)(2,1)S(1)}, u32[]{:S(2)}, u32[]{:S(2)}) collective-permute-start(bf16[1408,256]{1,0:T(8,128)(2,1)S(1)} %get-tuple-element.75), channel_id=1, source_target_pairs={{0,1},{1,0},{2,3},{3,2},{4,5},{5,4},{6,7},{7,6},{8,9},{9,8},{10,11... | collective-permute-start | bytes 2162696 | tf_op jit(solution)/shard_map/ppermute | solution.py:388
  67.7 17.3 %collective-permute-start.20 = (bf16[1408,256]{1,0:T(8,128)(2,1)S(1)}, bf16[1408,256]{1,0:T(8,128)(2,1)S(1)}, u32[]{:S(2)}, u32[]{:S(2)}) collective-permute-start(bf16[1408,256]{1,0:T(8,128)(2,1)S(1)} %get-tuple-element.76), channel_id=1, source_target_pairs={{0,5},{1,4},{2,7},{3,6},{4,1},{5,0},{6,3},{7,2},{8,13},{9,12},{10,... | collective-permute-start | bytes 2162696 | tf_op jit(solution)/shard_map/ppermute | solution.py:389
  69.5 2.7 %collective-permute-start.16 = (f32[1,256]{1,0:T(1,128)S(1)}, f32[1,256]{1,0:T(1,128)S(1)}, u32[]{:S(2)}, u32[]{:S(2)}) collective-permute-start(f32[1,256]{1,0:T(1,128)S(1)} %get-tuple-element.63.refs_7_.refs_0_), channel_id=1, source_target_pairs={{0,8},{2,10},{4,12},{6,14},{8,0},{10,2},{12,4},{14,6},{16,24},{18,... | collective-permute-start | bytes 3080 | tf_op jit(solution)/shard_map/ppermute | solution.py:335
  72.2 4.7 %collective-permute-start.17 = (f32[1,256]{1,0:T(1,128)S(1)}, f32[1,256]{1,0:T(1,128)S(1)}, u32[]{:S(2)}, u32[]{:S(2)}) collective-permute-start(f32[1,256]{1,0:T(1,128)S(1)} %add.25.refs_9_.refs_0_), channel_id=1, source_target_pairs={{0,16},{2,18},{4,20},{6,22},{8,24},{10,26},{12,28},{14,30},{16,0},... | collective-permute-start | bytes 3080 | tf_op jit(solution)/shard_map/ppermute | solution.py:335
  76.9 3.1 %collective-permute-start.18 = (f32[1,256]{1,0:T(1,128)S(1)}, f32[1,256]{1,0:T(1,128)S(1)}, u32[]{:S(2)}, u32[]{:S(2)}) collective-permute-start(f32[1,256]{1,0:T(1,128)S(1)} %add.26.refs_9_.refs_0_), channel_id=1, source_target_pairs={{0,32},{2,34},{4,36},{6,38},{8,40},{10,42},{12,44},{14,46},{16,48}... | collective-permute-start | bytes 3080 | tf_op jit(solution)/shard_map/ppermute | solution.py:335
  80.0 4.5 %collective-permute-start.21 = (f32[1,256]{1,0:T(1,128)S(1)}, f32[1,256]{1,0:T(1,128)S(1)}, u32[]{:S(2)}, u32[]{:S(2)}) collective-permute-start(f32[1,256]{1,0:T(1,128)S(1)} %add.27.refs_9_.refs_0_), channel_id=1, source_target_pairs={{0,64},{2,66},{4,68},{6,70},{8,72},{10,74},{12,76},{14,78},{16,80}... | collective-permute-start | bytes 3080 | tf_op jit(solution)/shard_map/ppermute | solution.py:335
  86.1 11.3 %collective-permute-start.22 = (bf16[2048,256]{1,0:T(8,128)(2,1)}, bf16[2048,256]{1,0:T(8,128)(2,1)}, u32[]{:S(2)}, u32[]{:S(2)}) collective-permute-start(bf16[2048,256]{1,0:T(8,128)(2,1)} %join.11.refs_5_), channel_id=1, source_target_pairs={{0,2},{2,0},{4,6},{6,4},{8,10},{10,8},{12,14},{14,12},{16,18},{18,... | collective-permute-start | bytes 3145736 | tf_op jit(solution)/shard_map/ppermute | solution.py:335
  89.1 6.3 %collective-permute-start.23 = (f32[1,256]{1,0:T(1,128)S(1)}, f32[1,256]{1,0:T(1,128)S(1)}, u32[]{:S(2)}, u32[]{:S(2)}) collective-permute-start(f32[1,256]{1,0:T(1,128)S(1)} %add.28.refs_2_.refs_6_.refs_0_), channel_id=1, source_target_pairs={{0,128},{2,130},{4,132},{6,134},{8,136},{10,138},{12,140},{14,142}... | collective-permute-start | bytes 3080 | tf_op jit(solution)/shard_map/ppermute | solution.py:335
  95.4 1.7 %copy-start.2 = (f32[384,2048]{1,0:T(8,128)}, f32[384,2048]{1,0:T(8,128)S(1)}, u32[]{:S(2)}) copy-start(f32[384,2048]{1,0:T(8,128)S(1)} %own_terms.1.refs_2_.refs_6_) | copy-start | bytes 9437188
  97.1 5.6 %collective-permute-start.24 = (f32[1,256]{1,0:T(1,128)S(1)}, f32[1,256]{1,0:T(1,128)S(1)}, u32[]{:S(2)}, u32[]{:S(2)}) collective-permute-start(f32[1,256]{1,0:T(1,128)S(1)} %add.29.refs_7_), channel_id=1, source_target_pairs={{0,2},{2,0},{4,6},{6,4},{8,10},{10,8},{12,14},{14,12},{16,18},{18,... | collective-permute-start | bytes 3080 | tf_op jit(solution)/shard_map/ppermute | solution.py:335
  97.3 1.9 %copy-start.3 = (f32[384,2048]{1,0:T(8,128)S(1)}, f32[384,2048]{1,0:T(8,128)}, u32[]{:S(2)}) copy-start(f32[384,2048]{1,0:T(8,128)} %copy-done.2) | copy-start | bytes 9437188

commit v9 on v8

--- a/solution.py
+++ b/solution.py
@@ -17,7 +17,7 @@
 LOG2E = math.log2(math.e)
 BF16 = jnp.bfloat16
 F32 = jnp.float32
-VMEM_LIMIT = 14 * 1024 * 1024
+VMEM_LIMIT = 16 * 1024 * 1024
 
 
 def dot(a, b, dims):
@@ -138,7 +138,7 @@
     token_ref[...] = jnp.zeros_like(token_ref)
     dk_acc[...] = jnp.zeros_like(dk_acc)
     col = pl.ds(HEAD * (g % 2), HEAD)
-    all_values = jnp.where(at_ref[3] == g // 2, mine_ref[:, col], theirs_ref[:COUNT, col])
+    all_values = jnp.where(at_ref[3] == g // 2, mine_ref[:, col], theirs_ref[:, col])
     for i in range(BLOCKS):
         width = BLOCK * (i + 1)
         at = pl.ds(BLOCK * i, BLOCK)
@@ -242,19 +242,19 @@
 
 
 def raw_kernel(at_ref, own_ref, other_ref, dv_own, dv_other, scale_ref, *refs):
-    pieces, (mine_ref, core_ref, sums_ref, near_ref, beside_ref, codes_ref) = refs[:6], refs[6:]
+    pieces, (mine_ref, theirs_ref, sums_ref, kept_ref, near_ref, beside_ref, codes_ref) = refs[:6], refs[6:]
     put_in_order(at_ref, pieces, codes_ref)
     cols = own_columns(at_ref)
     scale = scale_ref[:, cols]
     sums = jnp.zeros((1, HALF), F32)
-    terms = ((other_ref, dv_other[...], core_ref), (own_ref, dv_own[:, cols], mine_ref))
+    terms = ((other_ref, dv_other[...], theirs_ref), (own_ref, dv_own[:, cols], mine_ref))
     for hidden_ref, dv, values_ref in terms:
         raw = dot(hidden_ref[...], codes_ref[...], (1, 0))
-        values_ref[:COUNT, :] = (raw * scale).astype(BF16)
+        values_ref[...] = (raw * scale).astype(BF16)
         sums += jnp.sum(raw * dv, axis=0, keepdims=True)
     sums_ref[...] = sums
     s, half = at_ref[4], DEPTH // 2
-    core_ref[COUNT:, :] = codes_ref[pl.ds(pl.multiple_of(s * half, half), half), :]
+    kept_ref[...] = codes_ref[pl.ds(pl.multiple_of(s * half, half), half), :]
     base = (1 - s) * half
     for j in range(2):
         part = pl.ds(j * HALF, HALF)
@@ -264,8 +264,8 @@
 
 
 def raw_part(at, hidden, hidden_other, dv, dv_other, scale, pieces):
-    outs = [shape(COUNT, HALF), shape(COUNT + DEPTH // 2, HALF), shape(1, HALF, dtype=F32)]
-    outs += [shape(2 * COUNT + NEAR, HALF), shape(BESIDES, HALF)]
+    outs = [shape(COUNT, HALF), shape(COUNT, HALF), shape(1, HALF, dtype=F32)]
+    outs += [shape(DEPTH // 2, HALF), shape(2 * COUNT + NEAR, HALF), shape(BESIDES, HALF)]
     return call(
         raw_kernel, "raw_part", outs,
         [(SMEM, at)] + [(VMEM, a) for a in [hidden, hidden_other, dv, dv_other, scale] + pieces],
@@ -273,32 +273,30 @@
     )
 
 
-def codes_join_kernel(near_ref, beside_ref, out_ref):
-    out_ref[:NEAR, :] = near_ref[2 * COUNT :, :]
-    out_ref[NEAR:, :] = beside_ref[...]
-
-
 BATCH = 512
 
 
-def hidden_terms(c, dv_ref, scale_ref, near_ref, core_codes, seq_codes):
-    cols = pl.ds(pl.multiple_of(c * HALF, HALF), HALF)
-    own = (dv_ref[:, cols] * scale_ref[:, cols]).astype(BF16)
-    far = near_ref[pl.ds(pl.multiple_of(c * COUNT, COUNT), COUNT), :]
-    for i in range(0, DEPTH // 2, BATCH):
-        total = dot(own, core_codes[COUNT + i : COUNT + i + BATCH, :], (1, 1))
-        yield pl.ds(i, BATCH), total + dot(far, seq_codes[i : i + BATCH, :], (1, 1))
-
-
-def own_terms_kernel(at_ref, dv_ref, scale_ref, near_ref, core_codes, seq_codes, out_ref):
-    for rows, total in hidden_terms(at_ref[3], dv_ref, scale_ref, near_ref, core_codes, seq_codes):
-        out_ref[:, rows] = total
-
-
-def far_terms_kernel(at_ref, dv_ref, scale_ref, near_ref, core_codes, seq_codes, part_ref, sums_ref, out_ref, sums_out):
-    sums_out[...] = sums_ref[...]
-    for rows, total in hidden_terms(1 - at_ref[3], dv_ref, scale_ref, near_ref, core_codes, seq_codes):
-        out_ref[:, rows] = (total + part_ref[:, rows]).astype(BF16)
+def hidden_kernel(
+    at_ref, dv_ref, scale_ref, near_ref, beside_ref, kept_ref, near_far, beside_far, kept_far, out_ref, token_ref
+):
+    token_ref[...] = jnp.zeros_like(token_ref)
+    sides = []
+    for other, near, beside, kept in ((0, near_ref, beside_ref, kept_ref), (1, near_far, beside_far, kept_far)):
+        c = at_ref[3] ^ other
+        cols = pl.ds(pl.multiple_of(c * HALF, HALF), HALF)
+        own = (dv_ref[:, cols] * scale_ref[:, cols]).astype(BF16)
+        seq = near_ref[pl.ds(pl.multiple_of(c * COUNT, COUNT), COUNT), :]
+        sides.append((own, seq, near, beside, kept))
+    at = 0
+    while at < DEPTH // 2:
+        end = min(at + BATCH, NEAR if at < NEAR else DEPTH // 2)
+        total = 0.0
+        for own, seq, near, beside, kept in sides:
+            total += dot(own, kept[at:end, :], (1, 1))
+            codes = near[2 * COUNT + at : 2 * COUNT + end, :] if at < NEAR else beside[at - NEAR : end - NEAR, :]
+            total += dot(seq, codes, (1, 1))
+        out_ref[:, at:end] = total.astype(BF16)
+        at = end
 
 
 def add_kernel(a_ref, b_ref, out_ref):
@@ -375,37 +373,35 @@
         [(VMEM, a) for a in [first, first_x, second] + second_y], (dv_other,),
     )
     pieces = [first] + [send(first, y_shift(k)) for k in (1, 2, 3)] + [second, send(second, X_SWAP)]
-    mine, core, sums, near, beside = raw_part(at, hidden, hidden_other, dv, dv_other, scale, pieces)
-
-    core_far = send(core, C_SWAP)
-    base = [(SMEM, at), (VMEM, dv), (VMEM, scale)]
+    mine, theirs, sums, kept, near, beside = raw_part(at, hidden, hidden_other, dv, dv_other, scale, pieces)
+
+    values_far = send(theirs, C_SWAP)
+    near = lax.ppermute(near, "seq", SEQ_SWAP)
+    beside = lax.ppermute(beside, ("dp", "seq"), BESIDE)
     held = None
-    for step, perm in enumerate((X_SWAP, y_swap(1), y_swap(2), z_swap(1), z_swap(2), z_swap(4))):
+    for step, perm in enumerate((y_swap(1), y_swap(2), z_swap(1), z_swap(2), z_swap(4), X_SWAP)):
         got = send(sums, perm)
-        ins, after = [(VMEM, sums), (VMEM, got)], ()
-        if step == 0:
-            sums, near, beside = call(add_kernel, "add", shape(1, HALF, dtype=F32), ins, after, (near, beside))
-            near = lax.ppermute(near, "seq", SEQ_SWAP)
-            beside = lax.ppermute(beside, ("dp", "seq"), BESIDE)
-            continue
-        if step <= 4:
-            g = step - 1
-            *held, token = grads_part(g, at, queries, keys, upstream, mine, core_far, probs[g], held, (sums,))
+        after, through = (), ()
+        if step < 4:
+            *held, token = grads_part(
+                step, at, queries, keys, upstream, mine, values_far, probs[step], held, (sums,)
+            )
             after = (token,)
+            if step == 3:
+                through = (near, beside, kept)
+        elif step == 5:
+            grad_hidden, token = call(
+                hidden_kernel, "hidden_part", [shape(COUNT, DEPTH // 2), TOKEN],
+                [(SMEM, at)] + [(VMEM, a) for a in [dv, scale, near, beside, kept] + far], (sums,),
+            )
+            after = (token,)
+        ins = [(VMEM, sums), (VMEM, got)]
+        if through:
+            sums, near, beside, kept = call(add_kernel, "add", shape(1, HALF, dtype=F32), ins, after, through)
+            far = [send(a, C_SWAP) for a in (near, beside, kept)]
         else:
-            codes = call(codes_join_kernel, "join", shape(DEPTH // 2, HALF), [(VMEM, near), (VMEM, beside)], (sums,))
-            codes_far = send(codes, C_SWAP)
-            part = call(
-                own_terms_kernel, "own_terms", shape(COUNT, DEPTH // 2, dtype=F32),
-                base + [(VMEM, near), (VMEM, core), (VMEM, codes)], (sums,),
-            )
-            after = (part,)
-        sums = call(add_kernel, "add", shape(1, HALF, dtype=F32), ins, after)
+            sums = call(add_kernel, "add", shape(1, HALF, dtype=F32), ins, after)
     far = send(sums, C_SWAP)
-    grad_hidden, sums = call(
-        far_terms_kernel, "far_terms", [shape(COUNT, DEPTH // 2), shape(1, HALF, dtype=F32)],
-        base + [(VMEM, a) for a in (near, core_far, codes_far, part, sums)],
-    )
     both = jnp.concatenate([jnp.where(me % 2 == 0, sums, far), jnp.where(me % 2 == 0, far, sums)], axis=1)
     return held[0], held[1], grad_hidden, (both * scale).reshape(-1)
 

time: 104 us -> 98.3 us (0.945)
  local copies, waits for them, and re-layouts: 4.28 us -> 0.76 us
  Pallas kernels: 31.5 us -> 28.5 us
  waiting for transfers between devices: 26.7 us -> 29.4 us
  starting transfers between devices: 39.4 us -> 38.1 us
    unnamed x12 -> x8, local copies, waits for them, and re-layouts: 3.53 us -> 0.02 us
    ppermute x23 -> x25, waiting for transfers between devices: 26.2 us -> 29.3 us  [send(): return lax.ppermute(x, 'dp', perm)]
    pallas_call x23 -> x21, Pallas kernels: 31.5 us -> 28.5 us  [call(): pl.pallas_call(run, in_specs=list(specs) + [ANY] * (len(after) + len(thro...]
    ppermute x23 -> x25, starting transfers between devices: 36.4 us -> 35 us  [send(): return lax.ppermute(x, 'dp', perm)]
  transfers between devices with their start and end apart: 25 -> 27, of which waited for: 12 -> 14; matrix products, arithmetic and copies ran while one was open for 1% -> 1% of each run, Pallas kernels for 25% -> 25%
where the time goes in v9:
time: 98.3 us; the launch traced here: 98.1 us
  starting transfers between devices  38.1 us (39%)
  waiting for transfers between devices  29.4 us (30%)
  Pallas kernels  28.5 us (29%)
    ppermute x25, starting transfers between devices, send(): return lax.ppermute(x, 'dp', perm)  35 us
    ppermute x25, waiting for transfers between devices, send(): return lax.ppermute(x, 'dp', perm)  29.3 us
    pallas_call x21, Pallas kernels, call(): pl.pallas_call(run, in_specs=list(specs) + [ANY] * (len(after) + len(thro...  28.5 us
  transfers between devices with their start and end apart: 27, of which 14 were waited for; matrix products, arithmetic and copies ran while one was open for 1% of the time, Pallas kernels for 25%

profile of v9, /device:TPU:1, one launch (start us, length us, event | category | flops | bytes accessed | tf_op | source)
XLA Modules:
  0.0 98.1 jit_solution(14018241468376702476)
XLA Ops:
  0.6 3.3 %collective-permute-start = (bf16[32,512]{1,0:T(8,128)(2,1)}, bf16[32,512]{1,0:T(8,128)(2,1)S(1)}, u32[]{:S(2)}, u32[]{:S(2)}) collective-permute-start(bf16[32,512]{1,0:T(8,128)(2,1)} %refs_0_.1), channel_id=1, source_target_pairs={{0,2},{2,0},{4,6},{6,4},{8,10},{10,8},{12,14},{14,12},{16,18},{18,... | collective-permute-start | bytes 98312 | tf_op jit(solution)/shard_map/ppermute | solution.py:333
  4.0 0.7 slice_bitcast_fusion
  5.0 0.7 join.5.refs_5_.refs_0_
  5.8 5.3 %collective-permute-start.1 = (bf16[64,256]{1,0:T(8,128)(2,1)S(1)}, bf16[64,256]{1,0:T(8,128)(2,1)S(1)}, u32[]{:S(2)}, u32[]{:S(2)}) collective-permute-start(bf16[64,256]{1,0:T(8,128)(2,1)S(1)} %join.5.refs_5_.refs_0_), channel_id=1, source_target_pairs={{0,128},{2,130},{4,132},{6,134},{8,136},{10,138},{12,140},{14,142}... | collective-permute-start | bytes 98312 | tf_op jit(solution)/shard_map/ppermute | solution.py:333
  11.0 3.4 %probs_part.4 = (bf16[4,384,384]{2,1,0:T(8,128)(2,1)S(1)}, f32[384,512]{1,0:T(8,128)S(1)}, bf16[384,4096]{1,0:T(8,128)(2,1)S(1)}) custom-call(s32[8]{0:T(128)S(1)} %concatenate.11.refs_2_.refs_0_, bf16[384,2048]{1,0:T(8,128)(2,1)} %refs_1_.15, bf16[384,512]{1,0:T(8,128)(2,1)} %refs_2_.15, bf16[384,2048]{1,0:T(8,128)(2,1)} %refs_3_.15, ...), custom_call_target="tpu_custom_call" | custom-call | flops 1000 | bytes 1000 | tf_op jit(solution)/shard_map/probs_part/pallas_call | solution.py:53
  14.5 0.7 collective-permute-start.2
  15.2 1.2 %collective-permute-start.3 = (bf16[128,256]{1,0:T(8,128)(2,1)S(1)}, bf16[128,256]{1,0:T(8,128)(2,1)S(1)}, u32[]{:S(2)}, u32[]{:S(2)}) collective-permute-start(bf16[128,256]{1,0:T(8,128)(2,1)S(1)} %get-tuple-element.48.refs_5_.refs_0_), channel_id=1, source_target_pairs={{0,64},{2,66},{4,68},{6,70},{8,72},{10,74},{12,76},{14,78},{16,80}... | collective-permute-start | bytes 196616 | tf_op jit(solution)/shard_map/ppermute | solution.py:333
  16.4 2.2 %probs_part.5 = (bf16[4,384,384]{2,1,0:T(8,128)(2,1)S(1)}, f32[384,512]{1,0:T(8,128)S(1)}) custom-call(s32[8]{0:T(128)S(1)} %concatenate.11.refs_2_.refs_0_, bf16[384,2048]{1,0:T(8,128)(2,1)S(1)} %copy-done, bf16[384,512]{1,0:T(8,128)(2,1)S(1)} %copy-done.2, bf16[384,2048]{1,0:T(8,128)(2,1)S(1)} %copy-done.1, ...), custom_call_target="tpu_custom_call", output_to_operand_aliasing={{1}: (4, {})} | custom-call | flops 1000 | bytes 1000 | tf_op jit(solution)/shard_map/probs_part/pallas_call | solution.py:53
  18.6 2.2 %probs_part.6 = (bf16[4,384,384]{2,1,0:T(8,128)(2,1)S(1)}, f32[384,512]{1,0:T(8,128)S(1)}) custom-call(s32[8]{0:T(128)S(1)} %concatenate.11.refs_2_.refs_0_, bf16[384,2048]{1,0:T(8,128)(2,1)S(1)} %copy-done, bf16[384,512]{1,0:T(8,128)(2,1)S(1)} %copy-done.2, bf16[384,2048]{1,0:T(8,128)(2,1)S(1)} %copy-done.1, ...), custom_call_target="tpu_custom_call", output_to_operand_aliasing={{1}: (4, {})} | custom-call | flops 1000 | bytes 1000 | tf_op jit(solution)/shard_map/probs_part/pallas_call | solution.py:53
  20.8 0.4 collective-permute-done.3.refs_1_
  21.2 0.5 collective-permute-start.4
  21.7 2.2 %probs_part.7 = (bf16[4,384,384]{2,1,0:T(8,128)(2,1)S(1)}, f32[384,512]{1,0:T(8,128)S(1)}) custom-call(s32[8]{0:T(128)S(1)} %concatenate.11.refs_2_.refs_0_, bf16[384,2048]{1,0:T(8,128)(2,1)S(1)} %copy-done, bf16[384,512]{1,0:T(8,128)(2,1)S(1)} %copy-done.2, bf16[384,2048]{1,0:T(8,128)(2,1)S(1)} %copy-done.1, ...), custom_call_target="tpu_custom_call", output_to_operand_aliasing={{1}: (4, {})} | custom-call | flops 1000 | bytes 1000 | tf_op jit(solution)/shard_map/probs_part/pallas_call | solution.py:53
  23.9 1.6 %collective-permute-done.4.refs_2_ = bf16[256,256]{1,0:T(8,128)(2,1)S(1)} collective-permute-done((bf16[256,256]{1,0:T(8,128)(2,1)S(1)}, bf16[256,256]{1,0:T(8,128)(2,1)S(1)}, u32[]{:S(2)}, u32[]{:S(2)}) %collective-permute-start.4) | collective-permute-done | bytes 131104 | tf_op jit(solution)/shard_map/ppermute | solution.py:333
  25.5 0.6 join.8
  26.1 1.8 %collective-permute-start.5 = (f32[384,256]{1,0:T(8,128)S(1)}, f32[384,256]{1,0:T(8,128)S(1)}, u32[]{:S(2)}, u32[]{:S(2)}) collective-permute-start(f32[384,256]{1,0:T(8,128)S(1)} %get-tuple-element.53), channel_id=1, source_target_pairs={{0,2},{2,0},{4,6},{6,4},{8,10},{10,8},{12,14},{14,12},{16,18},{18,... | collective-permute-start | bytes 1179656 | tf_op jit(solution)/shard_map/ppermute | solution.py:333
  27.9 2.8 %collective-permute-start.6 = (bf16[512,128]{1,0:T(8,128)(2,1)S(1)}, bf16[512,128]{1,0:T(8,128)(2,1)S(1)}, u32[]{:S(2)}, u32[]{:S(2)}) collective-permute-start(bf16[512,128]{1,0:T(8,128)(2,1)S(1)} %get-tuple-element.54.refs_0_), channel_id=1, source_target_pairs={{0,4},{2,6},{4,0},{6,2},{8,12},{10,14},{12,8},{14,10},{16,20},{18,... | collective-permute-start | bytes 393224 | tf_op jit(solution)/shard_map/ppermute | solution.py:333
  30.7 2.7 %collective-permute-start.9 = (bf16[512,128]{1,0:T(8,128)(2,1)S(1)}, bf16[512,128]{1,0:T(8,128)(2,1)S(1)}, u32[]{:S(2)}, u32[]{:S(2)}) collective-permute-start(bf16[512,128]{1,0:T(8,128)(2,1)S(1)} %get-tuple-element.55.refs_2_), channel_id=1, source_target_pairs={{0,24},{2,26},{4,28},{6,30},{8,0},{10,2},{12,4},{14,6},{16,8},{18,... | collective-permute-start | bytes 393224 | tf_op jit(solution)/shard_map/ppermute | solution.py:333
  33.4 0.4 collective-permute-start.8
  33.8 0.7 collective-permute-start.7
  34.5 4.1 %collective-permute-done.9.refs_5_ = bf16[512,128]{1,0:T(8,128)(2,1)S(1)} collective-permute-done((bf16[512,128]{1,0:T(8,128)(2,1)S(1)}, bf16[512,128]{1,0:T(8,128)(2,1)S(1)}, u32[]{:S(2)}, u32[]{:S(2)}) %collective-permute-start.9) | collective-permute-done | bytes 131104 | tf_op jit(solution)/shard_map/ppermute | solution.py:333
  38.6 0.7 collective-permute-done.8.refs_4_
  39.3 3.8 %collective-permute-done.7.refs_3_ = bf16[512,128]{1,0:T(8,128)(2,1)S(1)} collective-permute-done((bf16[512,128]{1,0:T(8,128)(2,1)S(1)}, bf16[512,128]{1,0:T(8,128)(2,1)S(1)}, u32[]{:S(2)}, u32[]{:S(2)}) %collective-permute-start.7) | collective-permute-done | bytes 131104 | tf_op jit(solution)/shard_map/ppermute | solution.py:333
  43.2 0.5 collective-permute-start.13
  43.7 1.5 %collective-permute-start.10 = (bf16[1024,128]{1,0:T(8,128)(2,1)S(1)}, bf16[1024,128]{1,0:T(8,128)(2,1)S(1)}, u32[]{:S(2)}, u32[]{:S(2)}) collective-permute-start(bf16[1024,128]{1,0:T(8,128)(2,1)S(1)} %get-tuple-element.56.refs_6_), channel_id=1, source_target_pairs={{0,8},{2,10},{4,12},{6,14},{8,16},{10,18},{12,20},{14,22},{16,24},... | collective-permute-start | bytes 786440 | tf_op jit(solution)/shard_map/ppermute | solution.py:333
  45.2 5.6 %collective-permute-done.12.refs_9_ = bf16[1024,128]{1,0:T(8,128)(2,1)S(1)} collective-permute-done((bf16[1024,128]{1,0:T(8,128)(2,1)S(1)}, bf16[1024,128]{1,0:T(8,128)(2,1)S(1)}, u32[]{:S(2)}, u32[]{:S(2)}) %collective-permute-start.12) | collective-permute-done | bytes 262176 | tf_op jit(solution)/shard_map/ppermute | solution.py:333
  50.8 0.9 collective-permute-done.11.refs_8_
  51.7 7.4 %collective-permute-done.10.refs_7_ = bf16[1024,128]{1,0:T(8,128)(2,1)S(1)} collective-permute-done((bf16[1024,128]{1,0:T(8,128)(2,1)S(1)}, bf16[1024,128]{1,0:T(8,128)(2,1)S(1)}, u32[]{:S(2)}, u32[]{:S(2)}) %collective-permute-start.10) | collective-permute-done | bytes 262176 | tf_op jit(solution)/shard_map/ppermute | solution.py:333
  59.1 2.9 %raw_part.1 = (bf16[384,256]{1,0:T(8,128)(2,1)S(1)}, bf16[384,256]{1,0:T(8,128)(2,1)S(1)}, f32[1,256]{1,0:T(1,128)S(1)}, bf16[2048,256]{1,0:T(8,128)(2,1)S(1)}, ...) custom-call(s32[8]{0:T(128)S(1)} %concatenate.11.refs_2_.refs_0_, ...), custom_call_target="tpu_custom_call" | custom-call | flops 1000 | bytes 1000 | tf_op jit(solution)/shard_map/raw_part/pallas_call | solution.py:53
  62.0 1.3 %collective-permute-start.19 = (bf16[1408,256]{1,0:T(8,128)(2,1)S(1)}, bf16[1408,256]{1,0:T(8,128)(2,1)S(1)}, u32[]{:S(2)}, u32[]{:S(2)}) collective-permute-start(bf16[1408,256]{1,0:T(8,128)(2,1)S(1)} %get-tuple-element.75), channel_id=1, source_target_pairs={{0,1},{1,0},{2,3},{3,2},{4,5},{5,4},{6,7},{7,6},{8,9},{9,8},{10,11... | collective-permute-start | bytes 2162696 | tf_op jit(solution)/shard_map/ppermute | solution.py:379
  63.3 1.8 %collective-permute-start.20 = (bf16[1408,256]{1,0:T(8,128)(2,1)S(1)}, bf16[1408,256]{1,0:T(8,128)(2,1)S(1)}, u32[]{:S(2)}, u32[]{:S(2)}) collective-permute-start(bf16[1408,256]{1,0:T(8,128)(2,1)S(1)} %get-tuple-element.76), channel_id=1, source_target_pairs={{0,5},{1,4},{2,7},{3,6},{4,1},{5,0},{6,3},{7,2},{8,13},{9,12},{10,... | collective-permute-start | bytes 2162696 | tf_op jit(solution)/shard_map/ppermute | solution.py:380
  65.1 1.1 %collective-permute-start.14 = (bf16[384,256]{1,0:T(8,128)(2,1)S(1)}, bf16[384,256]{1,0:T(8,128)(2,1)S(1)}, u32[]{:S(2)}, u32[]{:S(2)}) collective-permute-start(bf16[384,256]{1,0:T(8,128)(2,1)S(1)} %get-tuple-element.59), channel_id=1, source_target_pairs={{0,2},{2,0},{4,6},{6,4},{8,10},{10,8},{12,14},{14,12},{16,18},{18,... | collective-permute-start | bytes 589832 | tf_op jit(solution)/shard_map/ppermute | solution.py:333
  66.2 1.1 %collective-permute-done.14.refs_5_ = bf16[384,256]{1,0:T(8,128)(2,1)S(1)} collective-permute-done((bf16[384,256]{1,0:T(8,128)(2,1)S(1)}, bf16[384,256]{1,0:T(8,128)(2,1)S(1)}, u32[]{:S(2)}, u32[]{:S(2)}) %collective-permute-start.14) | collective-permute-done | bytes 196640 | tf_op jit(solution)/shard_map/ppermute | solution.py:333
  67.2 2.6 %grads_part.4 = (bf16[384,2048]{1,0:T(8,128)(2,1)}, bf16[384,512]{1,0:T(8,128)(2,1)}, f32[8,128]{1,0:T(8,128)S(1)}) custom-call(s32[8]{0:T(128)S(1)} %concatenate.11.refs_2_.refs_0_, bf16[384,2048]{1,0:T(8,128)(2,1)S(1)} %copy-done, bf16[384,512]{1,0:T(8,128)(2,1)S(1)} %copy-done.2, bf16[384,2048]{1,0:T(8,128)(2,1)S(1)} %copy-done.1, ...), custom_call_target="tpu_custom_call" | custom-call | flops 1000 | bytes 1000 | tf_op jit(solution)/shard_map/grads_part/pallas_call | solution.py:53
  69.8 1.1 %collective-permute-start.16 = (f32[1,256]{1,0:T(1,128)S(1)}, f32[1,256]{1,0:T(1,128)S(1)}, u32[]{:S(2)}, u32[]{:S(2)}) collective-permute-start(f32[1,256]{1,0:T(1,128)S(1)} %add.24.refs_9_.refs_0_), channel_id=1, source_target_pairs={{0,16},{2,18},{4,20},{6,22},{8,24},{10,26},{12,28},{14,30},{16,0},... | collective-permute-start | bytes 3080 | tf_op jit(solution)/shard_map/ppermute | solution.py:333
  70.9 2.6 %grads_part.5 = (bf16[384,2048]{1,0:T(8,128)(2,1)}, bf16[384,512]{1,0:T(8,128)(2,1)}, f32[8,128]{1,0:T(8,128)S(1)}) custom-call(s32[8]{0:T(128)S(1)} %concatenate.11.refs_2_.refs_0_, bf16[384,2048]{1,0:T(8,128)(2,1)S(1)} %copy-done, bf16[384,512]{1,0:T(8,128)(2,1)S(1)} %copy-done.2, ...), custom_call_target="tpu_custom_call", output_to_operand_aliasing={{0}: (7, {}), {1}: (8, {})} | custom-call | flops 1000 | bytes 1000 | tf_op jit(solution)/shard_map/grads_part/pallas_call | solution.py:53
  73.8 0.4 collective-permute-start.17
  74.2 2.6 %grads_part.6 = (bf16[384,2048]{1,0:T(8,128)(2,1)}, bf16[384,512]{1,0:T(8,128)(2,1)}, f32[8,128]{1,0:T(8,128)S(1)}) custom-call(s32[8]{0:T(128)S(1)} %concatenate.11.refs_2_.refs_0_, bf16[384,2048]{1,0:T(8,128)(2,1)S(1)} %copy-done, bf16[384,512]{1,0:T(8,128)(2,1)S(1)} %copy-done.2, ...), custom_call_target="tpu_custom_call", output_to_operand_aliasing={{0}: (7, {}), {1}: (8, {})} | custom-call | flops 1000 | bytes 1000 | tf_op jit(solution)/shard_map/grads_part/pallas_call | solution.py:53
  76.8 1.8 %collective-permute-start.18 = (f32[1,256]{1,0:T(1,128)S(1)}, f32[1,256]{1,0:T(1,128)S(1)}, u32[]{:S(2)}, u32[]{:S(2)}) collective-permute-start(f32[1,256]{1,0:T(1,128)S(1)} %add.26.refs_9_.refs_0_), channel_id=1, source_target_pairs={{0,64},{2,66},{4,68},{6,70},{8,72},{10,74},{12,76},{14,78},{16,80}... | collective-permute-start | bytes 3080 | tf_op jit(solution)/shard_map/ppermute | solution.py:333
  78.7 2.6 %grads_part.7 = (bf16[384,2048]{1,0:T(8,128)(2,1)}, bf16[384,512]{1,0:T(8,128)(2,1)}, f32[8,128]{1,0:T(8,128)S(1)}) custom-call(s32[8]{0:T(128)S(1)} %concatenate.11.refs_2_.refs_0_, bf16[384,2048]{1,0:T(8,128)(2,1)S(1)} %copy-done, bf16[384,512]{1,0:T(8,128)(2,1)S(1)} %copy-done.2, ...), custom_call_target="tpu_custom_call", output_to_operand_aliasing={{0}: (7, {}), {1}: (8, {})} | custom-call | flops 1000 | bytes 1000 | tf_op jit(solution)/shard_map/grads_part/pallas_call | solution.py:53
  81.4 2.1 %collective-permute-start.23 = (bf16[2048,256]{1,0:T(8,128)(2,1)S(1)}, bf16[2048,256]{1,0:T(8,128)(2,1)S(1)}, u32[]{:S(2)}, u32[]{:S(2)}) collective-permute-start(bf16[2048,256]{1,0:T(8,128)(2,1)S(1)} %get-tuple-element.80.refs_5_), channel_id=1, source_target_pairs={{0,2},{2,0},{4,6},{6,4},{8,10},{10,8},{12,14},{14,12},{16,18},{18,... | collective-permute-start | bytes 3145736 | tf_op jit(solution)/shard_map/ppermute | solution.py:333
  83.6 0.4 collective-permute-start.22
  84.0 4.1 %collective-permute-start.24 = (f32[1,256]{1,0:T(1,128)S(1)}, f32[1,256]{1,0:T(1,128)S(1)}, u32[]{:S(2)}, u32[]{:S(2)}) collective-permute-start(f32[1,256]{1,0:T(1,128)S(1)} %get-tuple-element.81.refs_0_), channel_id=1, source_target_pairs={{0,128},{2,130},{4,132},{6,134},{8,136},{10,138},{12,140},{14,142}... | collective-permute-start | bytes 3080 | tf_op jit(solution)/shard_map/ppermute | solution.py:333
  88.1 2.2 %collective-permute-done.24.refs_1_ = f32[1,256]{1,0:T(1,128)S(1)} collective-permute-done((f32[1,256]{1,0:T(1,128)S(1)}, f32[1,256]{1,0:T(1,128)S(1)}, u32[]{:S(2)}, u32[]{:S(2)}) %collective-permute-start.24) | collective-permute-done | bytes 1056 | tf_op jit(solution)/shard_map/ppermute | solution.py:333
  90.4 0.8 collective-permute-start.25
  91.2 3.7 %hidden_part.1 = (bf16[384,2048]{1,0:T(8,128)(2,1)}, f32[8,128]{1,0:T(8,128)S(1)}) custom-call(s32[8]{0:T(128)S(1)} %concatenate.11.refs_2_.refs_0_, f32[384,512]{1,0:T(8,128)S(1)} %get-tuple-element.52.refs_3_.refs_1_, f32[1,512]{1,0:T(1,128)S(1)} %bitcast.11, bf16[1408,256]{1,0:T(8,128)(2,1)S(1)} %get-tuple-element.78.refs_3_, ...), custom_call_target="tpu_custom_call" | custom-call | flops 1000 | bytes 1000 | tf_op jit(solution)/shard_map/hidden_part/pallas_call | solution.py:53
  94.9 1.8 %collective-permute-start.26 = (f32[1,256]{1,0:T(1,128)S(1)}, f32[1,256]{1,0:T(1,128)S(1)}, u32[]{:S(2)}, u32[]{:S(2)}) collective-permute-start(f32[1,256]{1,0:T(1,128)S(1)} %add.29), channel_id=1, source_target_pairs={{0,2},{2,0},{4,6},{6,4},{8,10},{10,8},{12,14},{14,12},{16,18},{18,... | collective-permute-start | bytes 3080 | tf_op jit(solution)/shard_map/ppermute | solution.py:333
  96.7 0.8 collective-permute-done.26
  97.5 0.6 maximum_multiply_fusion
  (39 shorter events, 1.1 us)
Async XLA Ops:
  0.6 4.4 %collective-permute-start = (bf16[32,512]{1,0:T(8,128)(2,1)}, bf16[32,512]{1,0:T(8,128)(2,1)S(1)}, u32[]{:S(2)}, u32[]{:S(2)}) collective-permute-start(bf16[32,512]{1,0:T(8,128)(2,1)} %refs_0_.1), channel_id=1, source_target_pairs={{0,2},{2,0},{4,6},{6,4},{8,10},{10,8},{12,14},{14,12},{16,18},{18,... | collective-permute-start | bytes 98312 | tf_op jit(solution)/shard_map/ppermute | solution.py:333
  5.8 8.7 %collective-permute-start.1 = (bf16[64,256]{1,0:T(8,128)(2,1)S(1)}, bf16[64,256]{1,0:T(8,128)(2,1)S(1)}, u32[]{:S(2)}, u32[]{:S(2)}) collective-permute-start(bf16[64,256]{1,0:T(8,128)(2,1)S(1)} %join.5.refs_5_.refs_0_), channel_id=1, source_target_pairs={{0,128},{2,130},{4,132},{6,134},{8,136},{10,138},{12,140},{14,142}... | collective-permute-start | bytes 98312 | tf_op jit(solution)/shard_map/ppermute | solution.py:333
  14.5 2.0 %copy-start = (bf16[384,2048]{1,0:T(8,128)(2,1)S(1)}, bf16[384,2048]{1,0:T(8,128)(2,1)}, u32[]{:S(2)}) copy-start(bf16[384,2048]{1,0:T(8,128)(2,1)} %refs_1_.15) | copy-start | bytes 4718596
  14.5 2.0 %copy-start.1 = (bf16[384,2048]{1,0:T(8,128)(2,1)S(1)}, bf16[384,2048]{1,0:T(8,128)(2,1)}, u32[]{:S(2)}) copy-start(bf16[384,2048]{1,0:T(8,128)(2,1)} %refs_3_.15) | copy-start | bytes 4718596
  14.5 2.0 %copy-start.2 = (bf16[384,512]{1,0:T(8,128)(2,1)S(1)}, bf16[384,512]{1,0:T(8,128)(2,1)}, u32[]{:S(2)}) copy-start(bf16[384,512]{1,0:T(8,128)(2,1)} %refs_2_.15) | copy-start | bytes 1179652
  14.5 10.9 %collective-permute-start.2 = (bf16[384,4096]{1,0:T(8,128)(2,1)S(1)}, bf16[384,4096]{1,0:T(8,128)(2,1)S(1)}, u32[]{:S(2)}, u32[]{:S(2)}) collective-permute-start(bf16[384,4096]{1,0:T(8,128)(2,1)S(1)} %get-tuple-element.46.refs_1_), channel_id=1, source_target_pairs={{0,2},{2,0},{4,6},{6,4},{8,10},{10,8},{12,14},{14,12},{16,18},{18,... | collective-permute-start | bytes 9437192 | tf_op jit(solution)/shard_map/ppermute | solution.py:333
  15.2 6.0 %collective-permute-start.3 = (bf16[128,256]{1,0:T(8,128)(2,1)S(1)}, bf16[128,256]{1,0:T(8,128)(2,1)S(1)}, u32[]{:S(2)}, u32[]{:S(2)}) collective-permute-start(bf16[128,256]{1,0:T(8,128)(2,1)S(1)} %get-tuple-element.48.refs_5_.refs_0_), channel_id=1, source_target_pairs={{0,64},{2,66},{4,68},{6,70},{8,72},{10,74},{12,76},{14,78},{16,80}... | collective-permute-start | bytes 196616 | tf_op jit(solution)/shard_map/ppermute | solution.py:333
  21.2 4.2 %collective-permute-start.4 = (bf16[256,256]{1,0:T(8,128)(2,1)S(1)}, bf16[256,256]{1,0:T(8,128)(2,1)S(1)}, u32[]{:S(2)}, u32[]{:S(2)}) collective-permute-start(bf16[256,256]{1,0:T(8,128)(2,1)S(1)} %join.7.refs_5_.refs_1_), channel_id=1, source_target_pairs={{0,32},{2,34},{4,36},{6,38},{8,40},{10,42},{12,44},{14,46},{16,48}... | collective-permute-start | bytes 393224 | tf_op jit(solution)/shard_map/ppermute | solution.py:333
  25.5 33.6 %copy-start.3 = (f32[512]{0:T(512)S(1)}, f32[512]{0:T(512)}, u32[]{:S(2)}) copy-start(f32[512]{0:T(512)} %param.11) | copy-start | bytes 6148
  26.1 17.1 %collective-permute-start.5 = (f32[384,256]{1,0:T(8,128)S(1)}, f32[384,256]{1,0:T(8,128)S(1)}, u32[]{:S(2)}, u32[]{:S(2)}) collective-permute-start(f32[384,256]{1,0:T(8,128)S(1)} %get-tuple-element.53), channel_id=1, source_target_pairs={{0,2},{2,0},{4,6},{6,4},{8,10},{10,8},{12,14},{14,12},{16,18},{18,... | collective-permute-start | bytes 1179656 | tf_op jit(solution)/shard_map/ppermute | solution.py:333
  27.9 6.6 %collective-permute-start.6 = (bf16[512,128]{1,0:T(8,128)(2,1)S(1)}, bf16[512,128]{1,0:T(8,128)(2,1)S(1)}, u32[]{:S(2)}, u32[]{:S(2)}) collective-permute-start(bf16[512,128]{1,0:T(8,128)(2,1)S(1)} %get-tuple-element.54.refs_0_), channel_id=1, source_target_pairs={{0,4},{2,6},{4,0},{6,2},{8,12},{10,14},{12,8},{14,10},{16,20},{18,... | collective-permute-start | bytes 393224 | tf_op jit(solution)/shard_map/ppermute | solution.py:333
  30.7 7.9 %collective-permute-start.9 = (bf16[512,128]{1,0:T(8,128)(2,1)S(1)}, bf16[512,128]{1,0:T(8,128)(2,1)S(1)}, u32[]{:S(2)}, u32[]{:S(2)}) collective-permute-start(bf16[512,128]{1,0:T(8,128)(2,1)S(1)} %get-tuple-element.55.refs_2_), channel_id=1, source_target_pairs={{0,24},{2,26},{4,28},{6,30},{8,0},{10,2},{12,4},{14,6},{16,8},{18,... | collective-permute-start | bytes 393224 | tf_op jit(solution)/shard_map/ppermute | solution.py:333
  33.4 5.9 %collective-permute-start.8 = (bf16[512,128]{1,0:T(8,128)(2,1)S(1)}, bf16[512,128]{1,0:T(8,128)(2,1)S(1)}, u32[]{:S(2)}, u32[]{:S(2)}) collective-permute-start(bf16[512,128]{1,0:T(8,128)(2,1)S(1)} %get-tuple-element.55.refs_2_), channel_id=1, source_target_pairs={{0,16},{2,18},{4,20},{6,22},{8,24},{10,26},{12,28},{14,30},{16,0},... | collective-permute-start | bytes 393224 | tf_op jit(solution)/shard_map/ppermute | solution.py:333
  33.8 9.4 %collective-permute-start.7 = (bf16[512,128]{1,0:T(8,128)(2,1)S(1)}, bf16[512,128]{1,0:T(8,128)(2,1)S(1)}, u32[]{:S(2)}, u32[]{:S(2)}) collective-permute-start(bf16[512,128]{1,0:T(8,128)(2,1)S(1)} %get-tuple-element.55.refs_2_), channel_id=1, source_target_pairs={{0,8},{2,10},{4,12},{6,14},{8,16},{10,18},{12,20},{14,22},{16,24},... | collective-permute-start | bytes 393224 | tf_op jit(solution)/shard_map/ppermute | solution.py:333
  43.2 15.9 %collective-permute-start.13 = (bf16[2048,128]{1,0:T(8,128)(2,1)S(1)}, bf16[2048,128]{1,0:T(8,128)(2,1)S(1)}, u32[]{:S(2)}, u32[]{:S(2)}) collective-permute-start(bf16[2048,128]{1,0:T(8,128)(2,1)S(1)} %get-tuple-element.57.refs_10_), channel_id=1, source_target_pairs={{0,4},{2,6},{4,0},{6,2},{8,12},{10,14},{12,8},{14,10},{16,20},{18,... | collective-permute-start | bytes 1572872 | tf_op jit(solution)/shard_map/ppermute | solution.py:333
  43.7 7.1 %collective-permute-start.12 = (bf16[1024,128]{1,0:T(8,128)(2,1)S(1)}, bf16[1024,128]{1,0:T(8,128)(2,1)S(1)}, u32[]{:S(2)}, u32[]{:S(2)}) collective-permute-start(bf16[1024,128]{1,0:T(8,128)(2,1)S(1)} %get-tuple-element.56.refs_6_), channel_id=1, source_target_pairs={{0,24},{2,26},{4,28},{6,30},{8,0},{10,2},{12,4},{14,6},{16,8},{18,... | collective-permute-start | bytes 786440 | tf_op jit(solution)/shard_map/ppermute | solution.py:333
  43.7 8.0 %collective-permute-start.11 = (bf16[1024,128]{1,0:T(8,128)(2,1)S(1)}, bf16[1024,128]{1,0:T(8,128)(2,1)S(1)}, u32[]{:S(2)}, u32[]{:S(2)}) collective-permute-start(bf16[1024,128]{1,0:T(8,128)(2,1)S(1)} %get-tuple-element.56.refs_6_), channel_id=1, source_target_pairs={{0,16},{2,18},{4,20},{6,22},{8,24},{10,26},{12,28},{14,30},{16,0},... | collective-permute-start | bytes 786440 | tf_op jit(solution)/shard_map/ppermute | solution.py:333
  43.7 15.3 %collective-permute-start.10 = (bf16[1024,128]{1,0:T(8,128)(2,1)S(1)}, bf16[1024,128]{1,0:T(8,128)(2,1)S(1)}, u32[]{:S(2)}, u32[]{:S(2)}) collective-permute-start(bf16[1024,128]{1,0:T(8,128)(2,1)S(1)} %get-tuple-element.56.refs_6_), channel_id=1, source_target_pairs={{0,8},{2,10},{4,12},{6,14},{8,16},{10,18},{12,20},{14,22},{16,24},... | collective-permute-start | bytes 786440 | tf_op jit(solution)/shard_map/ppermute | solution.py:333
  62.0 19.3 %collective-permute-start.19 = (bf16[1408,256]{1,0:T(8,128)(2,1)S(1)}, bf16[1408,256]{1,0:T(8,128)(2,1)S(1)}, u32[]{:S(2)}, u32[]{:S(2)}) collective-permute-start(bf16[1408,256]{1,0:T(8,128)(2,1)S(1)} %get-tuple-element.75), channel_id=1, source_target_pairs={{0,1},{1,0},{2,3},{3,2},{4,5},{5,4},{6,7},{7,6},{8,9},{9,8},{10,11... | collective-permute-start | bytes 2162696 | tf_op jit(solution)/shard_map/ppermute | solution.py:379
  63.3 18.1 %collective-permute-start.20 = (bf16[1408,256]{1,0:T(8,128)(2,1)S(1)}, bf16[1408,256]{1,0:T(8,128)(2,1)S(1)}, u32[]{:S(2)}, u32[]{:S(2)}) collective-permute-start(bf16[1408,256]{1,0:T(8,128)(2,1)S(1)} %get-tuple-element.76), channel_id=1, source_target_pairs={{0,5},{1,4},{2,7},{3,6},{4,1},{5,0},{6,3},{7,2},{8,13},{9,12},{10,... | collective-permute-start | bytes 2162696 | tf_op jit(solution)/shard_map/ppermute | solution.py:380
  65.1 2.1 %collective-permute-start.14 = (bf16[384,256]{1,0:T(8,128)(2,1)S(1)}, bf16[384,256]{1,0:T(8,128)(2,1)S(1)}, u32[]{:S(2)}, u32[]{:S(2)}) collective-permute-start(bf16[384,256]{1,0:T(8,128)(2,1)S(1)} %get-tuple-element.59), channel_id=1, source_target_pairs={{0,2},{2,0},{4,6},{6,4},{8,10},{10,8},{12,14},{14,12},{16,18},{18,... | collective-permute-start | bytes 589832 | tf_op jit(solution)/shard_map/ppermute | solution.py:333
  66.1 3.7 %collective-permute-start.15 = (f32[1,256]{1,0:T(1,128)S(1)}, f32[1,256]{1,0:T(1,128)S(1)}, u32[]{:S(2)}, u32[]{:S(2)}) collective-permute-start(f32[1,256]{1,0:T(1,128)S(1)} %get-tuple-element.62.refs_7_.refs_0_), channel_id=1, source_target_pairs={{0,8},{2,10},{4,12},{6,14},{8,0},{10,2},{12,4},{14,6},{16,24},{18,... | collective-permute-start | bytes 3080 | tf_op jit(solution)/shard_map/ppermute | solution.py:333
  69.8 4.0 %collective-permute-start.16 = (f32[1,256]{1,0:T(1,128)S(1)}, f32[1,256]{1,0:T(1,128)S(1)}, u32[]{:S(2)}, u32[]{:S(2)}) collective-permute-start(f32[1,256]{1,0:T(1,128)S(1)} %add.24.refs_9_.refs_0_), channel_id=1, source_target_pairs={{0,16},{2,18},{4,20},{6,22},{8,24},{10,26},{12,28},{14,30},{16,0},... | collective-permute-start | bytes 3080 | tf_op jit(solution)/shard_map/ppermute | solution.py:333
  73.8 3.0 %collective-permute-start.17 = (f32[1,256]{1,0:T(1,128)S(1)}, f32[1,256]{1,0:T(1,128)S(1)}, u32[]{:S(2)}, u32[]{:S(2)}) collective-permute-start(f32[1,256]{1,0:T(1,128)S(1)} %add.25.refs_9_.refs_0_), channel_id=1, source_target_pairs={{0,32},{2,34},{4,36},{6,38},{8,40},{10,42},{12,44},{14,46},{16,48}... | collective-permute-start | bytes 3080 | tf_op jit(solution)/shard_map/ppermute | solution.py:333
  76.8 4.5 %collective-permute-start.18 = (f32[1,256]{1,0:T(1,128)S(1)}, f32[1,256]{1,0:T(1,128)S(1)}, u32[]{:S(2)}, u32[]{:S(2)}) collective-permute-start(f32[1,256]{1,0:T(1,128)S(1)} %add.26.refs_9_.refs_0_), channel_id=1, source_target_pairs={{0,64},{2,66},{4,68},{6,70},{8,72},{10,74},{12,76},{14,78},{16,80}... | collective-permute-start | bytes 3080 | tf_op jit(solution)/shard_map/ppermute | solution.py:333
  81.4 9.7 %collective-permute-start.23 = (bf16[2048,256]{1,0:T(8,128)(2,1)S(1)}, bf16[2048,256]{1,0:T(8,128)(2,1)S(1)}, u32[]{:S(2)}, u32[]{:S(2)}) collective-permute-start(bf16[2048,256]{1,0:T(8,128)(2,1)S(1)} %get-tuple-element.80.refs_5_), channel_id=1, source_target_pairs={{0,2},{2,0},{4,6},{6,4},{8,10},{10,8},{12,14},{14,12},{16,18},{18,... | collective-permute-start | bytes 3145736 | tf_op jit(solution)/shard_map/ppermute | solution.py:333
  83.5 7.6 %collective-permute-start.21 = (bf16[1408,256]{1,0:T(8,128)(2,1)S(1)}, bf16[1408,256]{1,0:T(8,128)(2,1)S(1)}, u32[]{:S(2)}, u32[]{:S(2)}) collective-permute-start(bf16[1408,256]{1,0:T(8,128)(2,1)S(1)} %get-tuple-element.78.refs_3_), channel_id=1, source_target_pairs={{0,2},{2,0},{4,6},{6,4},{8,10},{10,8},{12,14},{14,12},{16,18},{18,... | collective-permute-start | bytes 2162696 | tf_op jit(solution)/shard_map/ppermute | solution.py:333
  83.6 7.5 %collective-permute-start.22 = (bf16[1408,256]{1,0:T(8,128)(2,1)S(1)}, bf16[1408,256]{1,0:T(8,128)(2,1)S(1)}, u32[]{:S(2)}, u32[]{:S(2)}) collective-permute-start(bf16[1408,256]{1,0:T(8,128)(2,1)S(1)} %get-tuple-element.79.refs_4_), channel_id=1, source_target_pairs={{0,2},{2,0},{4,6},{6,4},{8,10},{10,8},{12,14},{14,12},{16,18},{18,... | collective-permute-start | bytes 2162696 | tf_op jit(solution)/shard_map/ppermute | solution.py:333
  84.0 6.3 %collective-permute-start.24 = (f32[1,256]{1,0:T(1,128)S(1)}, f32[1,256]{1,0:T(1,128)S(1)}, u32[]{:S(2)}, u32[]{:S(2)}) collective-permute-start(f32[1,256]{1,0:T(1,128)S(1)} %get-tuple-element.81.refs_0_), channel_id=1, source_target_pairs={{0,128},{2,130},{4,132},{6,134},{8,136},{10,138},{12,140},{14,142}... | collective-permute-start | bytes 3080 | tf_op jit(solution)/shard_map/ppermute | solution.py:333
  90.4 4.5 %collective-permute-start.25 = (f32[1,256]{1,0:T(1,128)S(1)}, f32[1,256]{1,0:T(1,128)S(1)}, u32[]{:S(2)}, u32[]{:S(2)}) collective-permute-start(f32[1,256]{1,0:T(1,128)S(1)} %add.28.refs_9_.refs_0_), channel_id=1, source_target_pairs={{0,4},{2,6},{4,0},{6,2},{8,12},{10,14},{12,8},{14,10},{16,20},{18,... | collective-permute-start | bytes 3080 | tf_op jit(solution)/shard_map/ppermute | solution.py:333
  94.9 2.6 %collective-permute-start.26 = (f32[1,256]{1,0:T(1,128)S(1)}, f32[1,256]{1,0:T(1,128)S(1)}, u32[]{:S(2)}, u32[]{:S(2)}) collective-permute-start(f32[1,256]{1,0:T(1,128)S(1)} %add.29), channel_id=1, source_target_pairs={{0,2},{2,0},{4,6},{6,4},{8,10},{10,8},{12,14},{14,12},{16,18},{18,... | collective-permute-start | bytes 3080 | tf_op jit(solution)/shard_map/ppermute | solution.py:333

commit v10 on v9

--- a/solution.py
+++ b/solution.py
@@ -205,15 +205,15 @@
     out_ref[n:, :] = other_ref[...]
 
 
-def join_split_kernel(at_ref, own_ref, other_ref, dv_ref, first_ref, second_ref, dv_out):
+def join_split_kernel(own_ref, other_ref, first_ref, second_ref):
     n = own_ref.shape[0]
     for j, out_ref in enumerate((first_ref, second_ref)):
         out_ref[:n, :] = own_ref[:, HEAD * j : HEAD * (j + 1)]
         out_ref[n:, :] = other_ref[:, HEAD * j : HEAD * (j + 1)]
+
+
+def two_joins_kernel(at_ref, dv_ref, a0, a1, b0, b1, b2, b3, first_ref, second_ref, dv_out):
     dv_out[...] = dv_ref[:, pl.ds(pl.multiple_of((1 - at_ref[3]) * HALF, HALF), HALF)]
-
-
-def two_joins_kernel(a0, a1, b0, b1, b2, b3, first_ref, second_ref):
     n = a0.shape[0]
     for j, part in enumerate((a0, a1)):
         first_ref[n * j : n * (j + 1), :] = part[...]
@@ -344,7 +344,7 @@
         scratch_shapes=[pltpu.SemaphoreType.DMA],
     )
     probs, dv = [], None
-    for bit, heads in ((4, (0,)), (2, (1, 2)), (1, (3,))):
+    for bit, heads in ((4, (0,)), (2, (1,)), (1, (2,))):
         got = send(rows, z_swap(bit))
         for g in heads:
             if g == 0:
@@ -360,45 +360,46 @@
         elif bit == 2:
             rows = call(join_kernel, "join", shape(2 * n, HALF), ins, (p,))
         else:
-            first, second, dv_half = call(
-                join_split_kernel, "join", [shape(2 * n, HEAD)] * 2 + [shape(COUNT, HALF, dtype=F32)],
-                [(SMEM, at)] + ins + [(VMEM, dv)], (hidden_other,),
-            )
+            first, second = call(join_split_kernel, "join", [shape(2 * n, HEAD)] * 2, ins, (hidden_other, p))
     first_x = send(first, X_SWAP)
     second_y = [send(second, y_shift(k)) for k in (1, 2, 3)]
+    p, dv = probs_part(3, at, queries, keys, upstream, dv, (first,))
+    probs.append(p)
+    n = first.shape[0]
+    first, second, dv_half = call(
+        two_joins_kernel, "join", [shape(2 * n, HEAD), shape(4 * n, HEAD), shape(COUNT, HALF, dtype=F32)],
+        [(SMEM, at)] + [(VMEM, a) for a in [dv, first, first_x, second] + second_y],
+    )
+    pieces = [first] + [send(first, y_shift(k)) for k in (1, 2, 3)] + [second, send(second, X_SWAP)]
     dv_other = send(dv_half, C_SWAP)
-    n = first.shape[0]
-    first, second = call(
-        two_joins_kernel, "join", [shape(2 * n, HEAD), shape(4 * n, HEAD)],
-        [(VMEM, a) for a in [first, first_x, second] + second_y], (dv_other,),
-    )
-    pieces = [first] + [send(first, y_shift(k)) for k in (1, 2, 3)] + [second, send(second, X_SWAP)]
     mine, theirs, sums, kept, near, beside = raw_part(at, hidden, hidden_other, dv, dv_other, scale, pieces)
 
-    values_far = send(theirs, C_SWAP)
-    near = lax.ppermute(near, "seq", SEQ_SWAP)
-    beside = lax.ppermute(beside, ("dp", "seq"), BESIDE)
-    held = None
+    held, far = None, None
     for step, perm in enumerate((y_swap(1), y_swap(2), z_swap(1), z_swap(2), z_swap(4), X_SWAP)):
         got = send(sums, perm)
         after, through = (), ()
-        if step < 4:
-            *held, token = grads_part(
-                step, at, queries, keys, upstream, mine, values_far, probs[step], held, (sums,)
-            )
+        if step == 0:
+            values_far = send(theirs, C_SWAP)
+            near = lax.ppermute(near, "seq", SEQ_SWAP)
+            beside = lax.ppermute(beside, ("dp", "seq"), BESIDE)
+            after = (values_far,)
+        elif step < 5:
+            g = step - 1
+            if step == 4:
+                far = [send(a, C_SWAP) for a in (near, beside, kept)]
+            *held, token = grads_part(g, at, queries, keys, upstream, mine, values_far, probs[g], held, (sums,))
             after = (token,)
-            if step == 3:
-                through = (near, beside, kept)
-        elif step == 5:
+        else:
             grad_hidden, token = call(
                 hidden_kernel, "hidden_part", [shape(COUNT, DEPTH // 2), TOKEN],
                 [(SMEM, at)] + [(VMEM, a) for a in [dv, scale, near, beside, kept] + far], (sums,),
             )
             after = (token,)
         ins = [(VMEM, sums), (VMEM, got)]
-        if through:
-            sums, near, beside, kept = call(add_kernel, "add", shape(1, HALF, dtype=F32), ins, after, through)
-            far = [send(a, C_SWAP) for a in (near, beside, kept)]
+        if step == 3:
+            sums, near, beside, kept = call(
+                add_kernel, "add", shape(1, HALF, dtype=F32), ins, after, (near, beside, kept)
+            )
         else:
             sums = call(add_kernel, "add", shape(1, HALF, dtype=F32), ins, after)
     far = send(sums, C_SWAP)

time: 98.3 us -> 97.1 us (0.988)
  waiting for transfers between devices: 29.4 us -> 28.4 us
    ppermute x25, waiting for transfers between devices: 29.3 us -> 27 us  [send(): return lax.ppermute(x, 'dp', perm)]
    ppermute x1, waiting for transfers between devices: 0.09 us -> 1.38 us  [shards(): beside = lax.ppermute(beside, ('dp', 'seq'), BESIDE)]
  transfers between devices with their start and end apart: 27 -> 27, of which waited for: 14 -> 12; matrix products, arithmetic and copies ran while one was open for 1% -> 1% of each run, Pallas kernels for 25% -> 25%
where the time goes in v10:
time: 97.1 us; the launch traced here: 96.9 us
  starting transfers between devices  37.9 us (39%)
  Pallas kernels  28.5 us (29%)
  waiting for transfers between devices  28.4 us (29%)
    ppermute x25, starting transfers between devices, send(): return lax.ppermute(x, 'dp', perm)  34.8 us
    pallas_call x21, Pallas kernels, call(): pl.pallas_call(run, in_specs=list(specs) + [ANY] * (len(after) + len(thro...  28.5 us
    ppermute x25, waiting for transfers between devices, send(): return lax.ppermute(x, 'dp', perm)  27 us
  transfers between devices with their start and end apart: 27, of which 12 were waited for; matrix products, arithmetic and copies ran while one was open for 1% of the time, Pallas kernels for 25%

profile of v10, /device:TPU:1, one launch (start us, length us, event | category | flops | bytes accessed | tf_op | source)
XLA Modules:
  0.0 96.9 jit_solution(12526010179445937154)
XLA Ops:
  0.6 3.3 %collective-permute-start = (bf16[32,512]{1,0:T(8,128)(2,1)}, bf16[32,512]{1,0:T(8,128)(2,1)S(1)}, u32[]{:S(2)}, u32[]{:S(2)}) collective-permute-start(bf16[32,512]{1,0:T(8,128)(2,1)} %refs_0_.1), channel_id=1, source_target_pairs={{0,2},{2,0},{4,6},{6,4},{8,10},{10,8},{12,14},{14,12},{16,18},{18,... | collective-permute-start | bytes 98312 | tf_op jit(solution)/shard_map/ppermute | solution.py:333
  4.0 0.7 slice_bitcast_fusion
  4.7 0.3 collective-permute-done.refs_1_
  5.0 0.7 join.5.refs_5_.refs_0_
  5.8 5.3 %collective-permute-start.1 = (bf16[64,256]{1,0:T(8,128)(2,1)S(1)}, bf16[64,256]{1,0:T(8,128)(2,1)S(1)}, u32[]{:S(2)}, u32[]{:S(2)}) collective-permute-start(bf16[64,256]{1,0:T(8,128)(2,1)S(1)} %join.5.refs_5_.refs_0_), channel_id=1, source_target_pairs={{0,128},{2,130},{4,132},{6,134},{8,136},{10,138},{12,140},{14,142}... | collective-permute-start | bytes 98312 | tf_op jit(solution)/shard_map/ppermute | solution.py:333
  11.0 3.4 %probs_part.4 = (bf16[4,384,384]{2,1,0:T(8,128)(2,1)S(1)}, f32[384,512]{1,0:T(8,128)S(1)}, bf16[384,4096]{1,0:T(8,128)(2,1)S(1)}) custom-call(s32[8]{0:T(128)S(1)} %concatenate.11.refs_2_.refs_0_, bf16[384,2048]{1,0:T(8,128)(2,1)} %refs_1_.15, bf16[384,512]{1,0:T(8,128)(2,1)} %refs_2_.15, bf16[384,2048]{1,0:T(8,128)(2,1)} %refs_3_.15, ...), custom_call_target="tpu_custom_call" | custom-call | flops 1000 | bytes 1000 | tf_op jit(solution)/shard_map/probs_part/pallas_call | solution.py:53
  14.5 0.7 collective-permute-start.2
  15.2 1.2 %collective-permute-start.3 = (bf16[128,256]{1,0:T(8,128)(2,1)S(1)}, bf16[128,256]{1,0:T(8,128)(2,1)S(1)}, u32[]{:S(2)}, u32[]{:S(2)}) collective-permute-start(bf16[128,256]{1,0:T(8,128)(2,1)S(1)} %get-tuple-element.48.refs_5_.refs_0_), channel_id=1, source_target_pairs={{0,64},{2,66},{4,68},{6,70},{8,72},{10,74},{12,76},{14,78},{16,80}... | collective-permute-start | bytes 196616 | tf_op jit(solution)/shard_map/ppermute | solution.py:333
  16.4 2.2 %probs_part.5 = (bf16[4,384,384]{2,1,0:T(8,128)(2,1)S(1)}, f32[384,512]{1,0:T(8,128)S(1)}) custom-call(s32[8]{0:T(128)S(1)} %concatenate.11.refs_2_.refs_0_, bf16[384,2048]{1,0:T(8,128)(2,1)S(1)} %copy-done, bf16[384,512]{1,0:T(8,128)(2,1)S(1)} %copy-done.2, bf16[384,2048]{1,0:T(8,128)(2,1)S(1)} %copy-done.1, ...), custom_call_target="tpu_custom_call", output_to_operand_aliasing={{1}: (4, {})} | custom-call | flops 1000 | bytes 1000 | tf_op jit(solution)/shard_map/probs_part/pallas_call | solution.py:53
  18.6 2.6 %collective-permute-done.3.refs_1_ = bf16[128,256]{1,0:T(8,128)(2,1)S(1)} collective-permute-done((bf16[128,256]{1,0:T(8,128)(2,1)S(1)}, bf16[128,256]{1,0:T(8,128)(2,1)S(1)}, u32[]{:S(2)}, u32[]{:S(2)}) %collective-permute-start.3) | collective-permute-done | bytes 65568 | tf_op jit(solution)/shard_map/ppermute | solution.py:333
  21.3 2.2 %probs_part.6 = (bf16[4,384,384]{2,1,0:T(8,128)(2,1)S(1)}, f32[384,512]{1,0:T(8,128)S(1)}) custom-call(s32[8]{0:T(128)S(1)} %concatenate.11.refs_2_.refs_0_, bf16[384,2048]{1,0:T(8,128)(2,1)S(1)} %copy-done, bf16[384,512]{1,0:T(8,128)(2,1)S(1)} %copy-done.2, bf16[384,2048]{1,0:T(8,128)(2,1)S(1)} %copy-done.1, ...), custom_call_target="tpu_custom_call", output_to_operand_aliasing={{1}: (4, {})} | custom-call | flops 1000 | bytes 1000 | tf_op jit(solution)/shard_map/probs_part/pallas_call | solution.py:53
  23.5 1.9 %collective-permute-done.4.refs_1_ = bf16[256,256]{1,0:T(8,128)(2,1)S(1)} collective-permute-done((bf16[256,256]{1,0:T(8,128)(2,1)S(1)}, bf16[256,256]{1,0:T(8,128)(2,1)S(1)}, u32[]{:S(2)}, u32[]{:S(2)}) %collective-permute-start.4) | collective-permute-done | bytes 131104 | tf_op jit(solution)/shard_map/ppermute | solution.py:333
  25.5 2.8 %collective-permute-start.5 = (bf16[512,128]{1,0:T(8,128)(2,1)S(1)}, bf16[512,128]{1,0:T(8,128)(2,1)S(1)}, u32[]{:S(2)}, u32[]{:S(2)}) collective-permute-start(bf16[512,128]{1,0:T(8,128)(2,1)S(1)} %get-tuple-element.53.refs_5_.refs_2_), channel_id=1, source_target_pairs={{0,4},{2,6},{4,0},{6,2},{8,12},{10,14},{12,8},{14,10},{16,20},{18,... | collective-permute-start | bytes 393224 | tf_op jit(solution)/shard_map/ppermute | solution.py:333
  28.3 2.7 %collective-permute-start.8 = (bf16[512,128]{1,0:T(8,128)(2,1)S(1)}, bf16[512,128]{1,0:T(8,128)(2,1)S(1)}, u32[]{:S(2)}, u32[]{:S(2)}) collective-permute-start(bf16[512,128]{1,0:T(8,128)(2,1)S(1)} %get-tuple-element.55.refs_4_), channel_id=1, source_target_pairs={{0,24},{2,26},{4,28},{6,30},{8,0},{10,2},{12,4},{14,6},{16,8},{18,... | collective-permute-start | bytes 393224 | tf_op jit(solution)/shard_map/ppermute | solution.py:333
  31.1 0.4 collective-permute-start.7
  31.4 0.7 collective-permute-start.6
  32.1 2.2 %probs_part.7 = (bf16[4,384,384]{2,1,0:T(8,128)(2,1)S(1)}, f32[384,512]{1,0:T(8,128)S(1)}) custom-call(s32[8]{0:T(128)S(1)} %concatenate.11.refs_2_.refs_0_, bf16[384,2048]{1,0:T(8,128)(2,1)S(1)} %copy-done, bf16[384,512]{1,0:T(8,128)(2,1)S(1)} %copy-done.2, bf16[384,2048]{1,0:T(8,128)(2,1)S(1)} %copy-done.1, ...), custom_call_target="tpu_custom_call", output_to_operand_aliasing={{1}: (4, {})} | custom-call | flops 1000 | bytes 1000 | tf_op jit(solution)/shard_map/probs_part/pallas_call | solution.py:53
  34.3 2.2 %collective-permute-done.7.refs_6_ = bf16[512,128]{1,0:T(8,128)(2,1)S(1)} collective-permute-done((bf16[512,128]{1,0:T(8,128)(2,1)S(1)}, bf16[512,128]{1,0:T(8,128)(2,1)S(1)}, u32[]{:S(2)}, u32[]{:S(2)}) %collective-permute-start.7) | collective-permute-done | bytes 131104 | tf_op jit(solution)/shard_map/ppermute | solution.py:333
  36.5 1.3 %collective-permute-done.6.refs_5_ = bf16[512,128]{1,0:T(8,128)(2,1)S(1)} collective-permute-done((bf16[512,128]{1,0:T(8,128)(2,1)S(1)}, bf16[512,128]{1,0:T(8,128)(2,1)S(1)}, u32[]{:S(2)}, u32[]{:S(2)}) %collective-permute-start.6) | collective-permute-done | bytes 131104 | tf_op jit(solution)/shard_map/ppermute | solution.py:333
  37.8 0.6 join.9
  38.4 0.3 collective-permute-start.13
  38.7 3.8 %collective-permute-start.9 = (f32[384,256]{1,0:T(8,128)S(1)}, f32[384,256]{1,0:T(8,128)S(1)}, u32[]{:S(2)}, u32[]{:S(2)}) collective-permute-start(f32[384,256]{1,0:T(8,128)S(1)} %get-tuple-element.56), channel_id=1, source_target_pairs={{0,2},{2,0},{4,6},{6,4},{8,10},{10,8},{12,14},{14,12},{16,18},{18,... | collective-permute-start | bytes 1179656 | tf_op jit(solution)/shard_map/ppermute | solution.py:333
  42.8 0.3 collective-permute-start.11
  43.1 0.8 collective-permute-start.10
  44.0 6.5 %collective-permute-done.12.refs_9_ = bf16[1024,128]{1,0:T(8,128)(2,1)S(1)} collective-permute-done((bf16[1024,128]{1,0:T(8,128)(2,1)S(1)}, bf16[1024,128]{1,0:T(8,128)(2,1)S(1)}, u32[]{:S(2)}, u32[]{:S(2)}) %collective-permute-start.12) | collective-permute-done | bytes 262176 | tf_op jit(solution)/shard_map/ppermute | solution.py:333
  50.5 1.5 %collective-permute-done.11.refs_8_ = bf16[1024,128]{1,0:T(8,128)(2,1)S(1)} collective-permute-done((bf16[1024,128]{1,0:T(8,128)(2,1)S(1)}, bf16[1024,128]{1,0:T(8,128)(2,1)S(1)}, u32[]{:S(2)}, u32[]{:S(2)}) %collective-permute-start.11) | collective-permute-done | bytes 262176 | tf_op jit(solution)/shard_map/ppermute | solution.py:333
  52.0 6.2 %collective-permute-done.10.refs_7_ = bf16[1024,128]{1,0:T(8,128)(2,1)S(1)} collective-permute-done((bf16[1024,128]{1,0:T(8,128)(2,1)S(1)}, bf16[1024,128]{1,0:T(8,128)(2,1)S(1)}, u32[]{:S(2)}, u32[]{:S(2)}) %collective-permute-start.10) | collective-permute-done | bytes 262176 | tf_op jit(solution)/shard_map/ppermute | solution.py:333
  58.2 2.9 %raw_part.1 = (bf16[384,256]{1,0:T(8,128)(2,1)S(1)}, bf16[384,256]{1,0:T(8,128)(2,1)S(1)}, f32[1,256]{1,0:T(1,128)S(1)}, bf16[2048,256]{1,0:T(8,128)(2,1)S(1)}, ...) custom-call(s32[8]{0:T(128)S(1)} %concatenate.11.refs_2_.refs_0_, ...), custom_call_target="tpu_custom_call" | custom-call | flops 1000 | bytes 1000 | tf_op jit(solution)/shard_map/raw_part/pallas_call | solution.py:53
  61.1 1.3 %collective-permute-start.19 = (bf16[1408,256]{1,0:T(8,128)(2,1)S(1)}, bf16[1408,256]{1,0:T(8,128)(2,1)S(1)}, u32[]{:S(2)}, u32[]{:S(2)}) collective-permute-start(bf16[1408,256]{1,0:T(8,128)(2,1)S(1)} %get-tuple-element.72), channel_id=1, source_target_pairs={{0,1},{1,0},{2,3},{3,2},{4,5},{5,4},{6,7},{7,6},{8,9},{9,8},{10,11... | collective-permute-start | bytes 2162696 | tf_op jit(solution)/shard_map/ppermute | solution.py:383
  62.4 1.8 %collective-permute-start.20 = (bf16[1408,256]{1,0:T(8,128)(2,1)S(1)}, bf16[1408,256]{1,0:T(8,128)(2,1)S(1)}, u32[]{:S(2)}, u32[]{:S(2)}) collective-permute-start(bf16[1408,256]{1,0:T(8,128)(2,1)S(1)} %get-tuple-element.73), channel_id=1, source_target_pairs={{0,5},{1,4},{2,7},{3,6},{4,1},{5,0},{6,3},{7,2},{8,13},{9,12},{10,... | collective-permute-start | bytes 2162696 | tf_op jit(solution)/shard_map/ppermute | solution.py:384
  64.2 1.0 %collective-permute-start.14 = (bf16[384,256]{1,0:T(8,128)(2,1)S(1)}, bf16[384,256]{1,0:T(8,128)(2,1)S(1)}, u32[]{:S(2)}, u32[]{:S(2)}) collective-permute-start(bf16[384,256]{1,0:T(8,128)(2,1)S(1)} %get-tuple-element.60), channel_id=1, source_target_pairs={{0,2},{2,0},{4,6},{6,4},{8,10},{10,8},{12,14},{14,12},{16,18},{18,... | collective-permute-start | bytes 589832 | tf_op jit(solution)/shard_map/ppermute | solution.py:333
  65.3 2.7 %collective-permute-done.15.refs_1_ = f32[1,256]{1,0:T(1,128)S(1)} collective-permute-done((f32[1,256]{1,0:T(1,128)S(1)}, f32[1,256]{1,0:T(1,128)S(1)}, u32[]{:S(2)}, u32[]{:S(2)}) %collective-permute-start.15) | collective-permute-done | bytes 1056 | tf_op jit(solution)/shard_map/ppermute | solution.py:333
  68.0 0.4 collective-permute-start.16
  68.3 2.6 %grads_part.4 = (bf16[384,2048]{1,0:T(8,128)(2,1)}, bf16[384,512]{1,0:T(8,128)(2,1)}, f32[8,128]{1,0:T(8,128)S(1)}) custom-call(s32[8]{0:T(128)S(1)} %concatenate.11.refs_2_.refs_0_, bf16[384,2048]{1,0:T(8,128)(2,1)S(1)} %copy-done, bf16[384,512]{1,0:T(8,128)(2,1)S(1)} %copy-done.2, bf16[384,2048]{1,0:T(8,128)(2,1)S(1)} %copy-done.1, ...), custom_call_target="tpu_custom_call" | custom-call | flops 1000 | bytes 1000 | tf_op jit(solution)/shard_map/grads_part/pallas_call | solution.py:53
  71.0 1.0 collective-permute-done.16.refs_1_
  71.9 0.3 collective-permute-start.17
  72.2 2.6 %grads_part.5 = (bf16[384,2048]{1,0:T(8,128)(2,1)}, bf16[384,512]{1,0:T(8,128)(2,1)}, f32[8,128]{1,0:T(8,128)S(1)}) custom-call(s32[8]{0:T(128)S(1)} %concatenate.11.refs_2_.refs_0_, bf16[384,2048]{1,0:T(8,128)(2,1)S(1)} %copy-done, bf16[384,512]{1,0:T(8,128)(2,1)S(1)} %copy-done.2, ...), custom_call_target="tpu_custom_call", output_to_operand_aliasing={{0}: (7, {}), {1}: (8, {})} | custom-call | flops 1000 | bytes 1000 | tf_op jit(solution)/shard_map/grads_part/pallas_call | solution.py:53
  74.9 1.7 %collective-permute-start.18 = (f32[1,256]{1,0:T(1,128)S(1)}, f32[1,256]{1,0:T(1,128)S(1)}, u32[]{:S(2)}, u32[]{:S(2)}) collective-permute-start(f32[1,256]{1,0:T(1,128)S(1)} %add.26.refs_9_.refs_0_), channel_id=1, source_target_pairs={{0,64},{2,66},{4,68},{6,70},{8,72},{10,74},{12,76},{14,78},{16,80}... | collective-permute-start | bytes 3080 | tf_op jit(solution)/shard_map/ppermute | solution.py:333
  76.5 2.6 %grads_part.6 = (bf16[384,2048]{1,0:T(8,128)(2,1)}, bf16[384,512]{1,0:T(8,128)(2,1)}, f32[8,128]{1,0:T(8,128)S(1)}) custom-call(s32[8]{0:T(128)S(1)} %concatenate.11.refs_2_.refs_0_, bf16[384,2048]{1,0:T(8,128)(2,1)S(1)} %copy-done, bf16[384,512]{1,0:T(8,128)(2,1)S(1)} %copy-done.2, ...), custom_call_target="tpu_custom_call", output_to_operand_aliasing={{0}: (7, {}), {1}: (8, {})} | custom-call | flops 1000 | bytes 1000 | tf_op jit(solution)/shard_map/grads_part/pallas_call | solution.py:53
  79.2 1.4 %collective-permute-done.20.refs_4_ = bf16[1408,256]{1,0:T(8,128)(2,1)S(1)} collective-permute-done((bf16[1408,256]{1,0:T(8,128)(2,1)S(1)}, bf16[1408,256]{1,0:T(8,128)(2,1)S(1)}, u32[]{:S(2)}, u32[]{:S(2)}) %collective-permute-start.20) | collective-permute-done | bytes 720928 | tf_op jit(solution)/shard_map/ppermute | solution.py:384
  80.5 1.6 %collective-permute-start.23 = (bf16[2048,256]{1,0:T(8,128)(2,1)S(1)}, bf16[2048,256]{1,0:T(8,128)(2,1)S(1)}, u32[]{:S(2)}, u32[]{:S(2)}) collective-permute-start(bf16[2048,256]{1,0:T(8,128)(2,1)S(1)} %get-tuple-element.80.refs_5_), channel_id=1, source_target_pairs={{0,2},{2,0},{4,6},{6,4},{8,10},{10,8},{12,14},{14,12},{16,18},{18,... | collective-permute-start | bytes 3145736 | tf_op jit(solution)/shard_map/ppermute | solution.py:333
  82.7 4.0 %collective-permute-start.24 = (f32[1,256]{1,0:T(1,128)S(1)}, f32[1,256]{1,0:T(1,128)S(1)}, u32[]{:S(2)}, u32[]{:S(2)}) collective-permute-start(f32[1,256]{1,0:T(1,128)S(1)} %get-tuple-element.75.refs_9_.refs_0_), channel_id=1, source_target_pairs={{0,128},{2,130},{4,132},{6,134},{8,136},{10,138},{12,140},{14,142}... | collective-permute-start | bytes 3080 | tf_op jit(solution)/shard_map/ppermute | solution.py:333
  86.7 2.6 %grads_part.7 = (bf16[384,2048]{1,0:T(8,128)(2,1)}, bf16[384,512]{1,0:T(8,128)(2,1)}, f32[8,128]{1,0:T(8,128)S(1)}) custom-call(s32[8]{0:T(128)S(1)} %concatenate.11.refs_2_.refs_0_, bf16[384,2048]{1,0:T(8,128)(2,1)S(1)} %copy-done, bf16[384,512]{1,0:T(8,128)(2,1)S(1)} %copy-done.2, ...), custom_call_target="tpu_custom_call", output_to_operand_aliasing={{0}: (7, {}), {1}: (8, {})} | custom-call | flops 1000 | bytes 1000 | tf_op jit(solution)/shard_map/grads_part/pallas_call | solution.py:53
  89.4 1.3 %collective-permute-start.25 = (f32[1,256]{1,0:T(1,128)S(1)}, f32[1,256]{1,0:T(1,128)S(1)}, u32[]{:S(2)}, u32[]{:S(2)}) collective-permute-start(f32[1,256]{1,0:T(1,128)S(1)} %add.28.refs_9_.refs_0_), channel_id=1, source_target_pairs={{0,4},{2,6},{4,0},{6,2},{8,12},{10,14},{12,8},{14,10},{16,20},{18,... | collective-permute-start | bytes 3080 | tf_op jit(solution)/shard_map/ppermute | solution.py:333
  90.7 3.7 %hidden_part.1 = (bf16[384,2048]{1,0:T(8,128)(2,1)}, f32[8,128]{1,0:T(8,128)S(1)}) custom-call(s32[8]{0:T(128)S(1)} %concatenate.11.refs_2_.refs_0_, f32[384,512]{1,0:T(8,128)S(1)} %get-tuple-element.54.refs_1_.refs_3_, f32[1,512]{1,0:T(1,128)S(1)} %bitcast.11, bf16[1408,256]{1,0:T(8,128)(2,1)S(1)} %get-tuple-element.78.refs_3_, ...), custom_call_target="tpu_custom_call" | custom-call | flops 1000 | bytes 1000 | tf_op jit(solution)/shard_map/hidden_part/pallas_call | solution.py:53
  94.5 1.1 %collective-permute-start.26 = (f32[1,256]{1,0:T(1,128)S(1)}, f32[1,256]{1,0:T(1,128)S(1)}, u32[]{:S(2)}, u32[]{:S(2)}) collective-permute-start(f32[1,256]{1,0:T(1,128)S(1)} %add.29), channel_id=1, source_target_pairs={{0,2},{2,0},{4,6},{6,4},{8,10},{10,8},{12,14},{14,12},{16,18},{18,... | collective-permute-start | bytes 3080 | tf_op jit(solution)/shard_map/ppermute | solution.py:333
  95.5 0.8 collective-permute-done.26
  96.4 0.6 maximum_multiply_fusion
  (39 shorter events, 1.1 us)
Async XLA Ops:
  0.6 4.4 %collective-permute-start = (bf16[32,512]{1,0:T(8,128)(2,1)}, bf16[32,512]{1,0:T(8,128)(2,1)S(1)}, u32[]{:S(2)}, u32[]{:S(2)}) collective-permute-start(bf16[32,512]{1,0:T(8,128)(2,1)} %refs_0_.1), channel_id=1, source_target_pairs={{0,2},{2,0},{4,6},{6,4},{8,10},{10,8},{12,14},{14,12},{16,18},{18,... | collective-permute-start | bytes 98312 | tf_op jit(solution)/shard_map/ppermute | solution.py:333
  5.8 8.7 %collective-permute-start.1 = (bf16[64,256]{1,0:T(8,128)(2,1)S(1)}, bf16[64,256]{1,0:T(8,128)(2,1)S(1)}, u32[]{:S(2)}, u32[]{:S(2)}) collective-permute-start(bf16[64,256]{1,0:T(8,128)(2,1)S(1)} %join.5.refs_5_.refs_0_), channel_id=1, source_target_pairs={{0,128},{2,130},{4,132},{6,134},{8,136},{10,138},{12,140},{14,142}... | collective-permute-start | bytes 98312 | tf_op jit(solution)/shard_map/ppermute | solution.py:333
  14.5 2.0 %copy-start = (bf16[384,2048]{1,0:T(8,128)(2,1)S(1)}, bf16[384,2048]{1,0:T(8,128)(2,1)}, u32[]{:S(2)}) copy-start(bf16[384,2048]{1,0:T(8,128)(2,1)} %refs_1_.15) | copy-start | bytes 4718596
  14.5 2.0 %copy-start.1 = (bf16[384,2048]{1,0:T(8,128)(2,1)S(1)}, bf16[384,2048]{1,0:T(8,128)(2,1)}, u32[]{:S(2)}) copy-start(bf16[384,2048]{1,0:T(8,128)(2,1)} %refs_3_.15) | copy-start | bytes 4718596
  14.5 2.0 %copy-start.2 = (bf16[384,512]{1,0:T(8,128)(2,1)S(1)}, bf16[384,512]{1,0:T(8,128)(2,1)}, u32[]{:S(2)}) copy-start(bf16[384,512]{1,0:T(8,128)(2,1)} %refs_2_.15) | copy-start | bytes 1179652
  14.5 10.9 %collective-permute-start.2 = (bf16[384,4096]{1,0:T(8,128)(2,1)S(1)}, bf16[384,4096]{1,0:T(8,128)(2,1)S(1)}, u32[]{:S(2)}, u32[]{:S(2)}) collective-permute-start(bf16[384,4096]{1,0:T(8,128)(2,1)S(1)} %get-tuple-element.46.refs_1_), channel_id=1, source_target_pairs={{0,2},{2,0},{4,6},{6,4},{8,10},{10,8},{12,14},{14,12},{16,18},{18,... | collective-permute-start | bytes 9437192 | tf_op jit(solution)/shard_map/ppermute | solution.py:333
  15.2 6.0 %collective-permute-start.3 = (bf16[128,256]{1,0:T(8,128)(2,1)S(1)}, bf16[128,256]{1,0:T(8,128)(2,1)S(1)}, u32[]{:S(2)}, u32[]{:S(2)}) collective-permute-start(bf16[128,256]{1,0:T(8,128)(2,1)S(1)} %get-tuple-element.48.refs_5_.refs_0_), channel_id=1, source_target_pairs={{0,64},{2,66},{4,68},{6,70},{8,72},{10,74},{12,76},{14,78},{16,80}... | collective-permute-start | bytes 196616 | tf_op jit(solution)/shard_map/ppermute | solution.py:333
  21.2 4.2 %collective-permute-start.4 = (bf16[256,256]{1,0:T(8,128)(2,1)S(1)}, bf16[256,256]{1,0:T(8,128)(2,1)S(1)}, u32[]{:S(2)}, u32[]{:S(2)}) collective-permute-start(bf16[256,256]{1,0:T(8,128)(2,1)S(1)} %join.7.refs_5_.refs_0_), channel_id=1, source_target_pairs={{0,32},{2,34},{4,36},{6,38},{8,40},{10,42},{12,44},{14,46},{16,48}... | collective-permute-start | bytes 393224 | tf_op jit(solution)/shard_map/ppermute | solution.py:333
  25.5 8.8 %collective-permute-start.5 = (bf16[512,128]{1,0:T(8,128)(2,1)S(1)}, bf16[512,128]{1,0:T(8,128)(2,1)S(1)}, u32[]{:S(2)}, u32[]{:S(2)}) collective-permute-start(bf16[512,128]{1,0:T(8,128)(2,1)S(1)} %get-tuple-element.53.refs_5_.refs_2_), channel_id=1, source_target_pairs={{0,4},{2,6},{4,0},{6,2},{8,12},{10,14},{12,8},{14,10},{16,20},{18,... | collective-permute-start | bytes 393224 | tf_op jit(solution)/shard_map/ppermute | solution.py:333
  28.3 6.0 %collective-permute-start.8 = (bf16[512,128]{1,0:T(8,128)(2,1)S(1)}, bf16[512,128]{1,0:T(8,128)(2,1)S(1)}, u32[]{:S(2)}, u32[]{:S(2)}) collective-permute-start(bf16[512,128]{1,0:T(8,128)(2,1)S(1)} %get-tuple-element.55.refs_4_), channel_id=1, source_target_pairs={{0,24},{2,26},{4,28},{6,30},{8,0},{10,2},{12,4},{14,6},{16,8},{18,... | collective-permute-start | bytes 393224 | tf_op jit(solution)/shard_map/ppermute | solution.py:333
  31.1 5.4 %collective-permute-start.7 = (bf16[512,128]{1,0:T(8,128)(2,1)S(1)}, bf16[512,128]{1,0:T(8,128)(2,1)S(1)}, u32[]{:S(2)}, u32[]{:S(2)}) collective-permute-start(bf16[512,128]{1,0:T(8,128)(2,1)S(1)} %get-tuple-element.55.refs_4_), channel_id=1, source_target_pairs={{0,16},{2,18},{4,20},{6,22},{8,24},{10,26},{12,28},{14,30},{16,0},... | collective-permute-start | bytes 393224 | tf_op jit(solution)/shard_map/ppermute | solution.py:333
  31.4 6.4 %collective-permute-start.6 = (bf16[512,128]{1,0:T(8,128)(2,1)S(1)}, bf16[512,128]{1,0:T(8,128)(2,1)S(1)}, u32[]{:S(2)}, u32[]{:S(2)}) collective-permute-start(bf16[512,128]{1,0:T(8,128)(2,1)S(1)} %get-tuple-element.55.refs_4_), channel_id=1, source_target_pairs={{0,8},{2,10},{4,12},{6,14},{8,16},{10,18},{12,20},{14,22},{16,24},... | collective-permute-start | bytes 393224 | tf_op jit(solution)/shard_map/ppermute | solution.py:333
  34.3 23.9 %copy-start.3 = (f32[512]{0:T(512)S(1)}, f32[512]{0:T(512)}, u32[]{:S(2)}) copy-start(f32[512]{0:T(512)} %param.11) | copy-start | bytes 6148
  38.4 19.8 %collective-permute-start.13 = (bf16[2048,128]{1,0:T(8,128)(2,1)S(1)}, bf16[2048,128]{1,0:T(8,128)(2,1)S(1)}, u32[]{:S(2)}, u32[]{:S(2)}) collective-permute-start(bf16[2048,128]{1,0:T(8,128)(2,1)S(1)} %get-tuple-element.58.refs_10_), channel_id=1, source_target_pairs={{0,4},{2,6},{4,0},{6,2},{8,12},{10,14},{12,8},{14,10},{16,20},{18,... | collective-permute-start | bytes 1572872 | tf_op jit(solution)/shard_map/ppermute | solution.py:333
  38.7 19.4 %collective-permute-start.9 = (f32[384,256]{1,0:T(8,128)S(1)}, f32[384,256]{1,0:T(8,128)S(1)}, u32[]{:S(2)}, u32[]{:S(2)}) collective-permute-start(f32[384,256]{1,0:T(8,128)S(1)} %get-tuple-element.56), channel_id=1, source_target_pairs={{0,2},{2,0},{4,6},{6,4},{8,10},{10,8},{12,14},{14,12},{16,18},{18,... | collective-permute-start | bytes 1179656 | tf_op jit(solution)/shard_map/ppermute | solution.py:333
  42.5 7.9 %collective-permute-start.12 = (bf16[1024,128]{1,0:T(8,128)(2,1)S(1)}, bf16[1024,128]{1,0:T(8,128)(2,1)S(1)}, u32[]{:S(2)}, u32[]{:S(2)}) collective-permute-start(bf16[1024,128]{1,0:T(8,128)(2,1)S(1)} %get-tuple-element.57.refs_6_), channel_id=1, source_target_pairs={{0,24},{2,26},{4,28},{6,30},{8,0},{10,2},{12,4},{14,6},{16,8},{18,... | collective-permute-start | bytes 786440 | tf_op jit(solution)/shard_map/ppermute | solution.py:333
  42.8 9.2 %collective-permute-start.11 = (bf16[1024,128]{1,0:T(8,128)(2,1)S(1)}, bf16[1024,128]{1,0:T(8,128)(2,1)S(1)}, u32[]{:S(2)}, u32[]{:S(2)}) collective-permute-start(bf16[1024,128]{1,0:T(8,128)(2,1)S(1)} %get-tuple-element.57.refs_6_), channel_id=1, source_target_pairs={{0,16},{2,18},{4,20},{6,22},{8,24},{10,26},{12,28},{14,30},{16,0},... | collective-permute-start | bytes 786440 | tf_op jit(solution)/shard_map/ppermute | solution.py:333
  43.1 15.0 %collective-permute-start.10 = (bf16[1024,128]{1,0:T(8,128)(2,1)S(1)}, bf16[1024,128]{1,0:T(8,128)(2,1)S(1)}, u32[]{:S(2)}, u32[]{:S(2)}) collective-permute-start(bf16[1024,128]{1,0:T(8,128)(2,1)S(1)} %get-tuple-element.57.refs_6_), channel_id=1, source_target_pairs={{0,8},{2,10},{4,12},{6,14},{8,16},{10,18},{12,20},{14,22},{16,24},... | collective-permute-start | bytes 786440 | tf_op jit(solution)/shard_map/ppermute | solution.py:333
  61.1 18.0 %collective-permute-start.19 = (bf16[1408,256]{1,0:T(8,128)(2,1)S(1)}, bf16[1408,256]{1,0:T(8,128)(2,1)S(1)}, u32[]{:S(2)}, u32[]{:S(2)}) collective-permute-start(bf16[1408,256]{1,0:T(8,128)(2,1)S(1)} %get-tuple-element.72), channel_id=1, source_target_pairs={{0,1},{1,0},{2,3},{3,2},{4,5},{5,4},{6,7},{7,6},{8,9},{9,8},{10,11... | collective-permute-start | bytes 2162696 | tf_op jit(solution)/shard_map/ppermute | solution.py:383
  62.4 18.1 %collective-permute-start.20 = (bf16[1408,256]{1,0:T(8,128)(2,1)S(1)}, bf16[1408,256]{1,0:T(8,128)(2,1)S(1)}, u32[]{:S(2)}, u32[]{:S(2)}) collective-permute-start(bf16[1408,256]{1,0:T(8,128)(2,1)S(1)} %get-tuple-element.73), channel_id=1, source_target_pairs={{0,5},{1,4},{2,7},{3,6},{4,1},{5,0},{6,3},{7,2},{8,13},{9,12},{10,... | collective-permute-start | bytes 2162696 | tf_op jit(solution)/shard_map/ppermute | solution.py:384
  64.2 3.8 %collective-permute-start.14 = (bf16[384,256]{1,0:T(8,128)(2,1)S(1)}, bf16[384,256]{1,0:T(8,128)(2,1)S(1)}, u32[]{:S(2)}, u32[]{:S(2)}) collective-permute-start(bf16[384,256]{1,0:T(8,128)(2,1)S(1)} %get-tuple-element.60), channel_id=1, source_target_pairs={{0,2},{2,0},{4,6},{6,4},{8,10},{10,8},{12,14},{14,12},{16,18},{18,... | collective-permute-start | bytes 589832 | tf_op jit(solution)/shard_map/ppermute | solution.py:333
  65.3 2.7 %collective-permute-start.15 = (f32[1,256]{1,0:T(1,128)S(1)}, f32[1,256]{1,0:T(1,128)S(1)}, u32[]{:S(2)}, u32[]{:S(2)}) collective-permute-start(f32[1,256]{1,0:T(1,128)S(1)} %get-tuple-element.62.refs_0_), channel_id=1, source_target_pairs={{0,8},{2,10},{4,12},{6,14},{8,0},{10,2},{12,4},{14,6},{16,24},{18,... | collective-permute-start | bytes 3080 | tf_op jit(solution)/shard_map/ppermute | solution.py:333
  68.0 3.9 %collective-permute-start.16 = (f32[1,256]{1,0:T(1,128)S(1)}, f32[1,256]{1,0:T(1,128)S(1)}, u32[]{:S(2)}, u32[]{:S(2)}) collective-permute-start(f32[1,256]{1,0:T(1,128)S(1)} %add.24.refs_7_.refs_0_), channel_id=1, source_target_pairs={{0,16},{2,18},{4,20},{6,22},{8,24},{10,26},{12,28},{14,30},{16,0},... | collective-permute-start | bytes 3080 | tf_op jit(solution)/shard_map/ppermute | solution.py:333
  71.9 2.9 %collective-permute-start.17 = (f32[1,256]{1,0:T(1,128)S(1)}, f32[1,256]{1,0:T(1,128)S(1)}, u32[]{:S(2)}, u32[]{:S(2)}) collective-permute-start(f32[1,256]{1,0:T(1,128)S(1)} %add.25.refs_9_.refs_0_), channel_id=1, source_target_pairs={{0,32},{2,34},{4,36},{6,38},{8,40},{10,42},{12,44},{14,46},{16,48}... | collective-permute-start | bytes 3080 | tf_op jit(solution)/shard_map/ppermute | solution.py:333
  74.9 4.3 %collective-permute-start.18 = (f32[1,256]{1,0:T(1,128)S(1)}, f32[1,256]{1,0:T(1,128)S(1)}, u32[]{:S(2)}, u32[]{:S(2)}) collective-permute-start(f32[1,256]{1,0:T(1,128)S(1)} %add.26.refs_9_.refs_0_), channel_id=1, source_target_pairs={{0,64},{2,66},{4,68},{6,70},{8,72},{10,74},{12,76},{14,78},{16,80}... | collective-permute-start | bytes 3080 | tf_op jit(solution)/shard_map/ppermute | solution.py:333
  80.5 10.2 %collective-permute-start.23 = (bf16[2048,256]{1,0:T(8,128)(2,1)S(1)}, bf16[2048,256]{1,0:T(8,128)(2,1)S(1)}, u32[]{:S(2)}, u32[]{:S(2)}) collective-permute-start(bf16[2048,256]{1,0:T(8,128)(2,1)S(1)} %get-tuple-element.80.refs_5_), channel_id=1, source_target_pairs={{0,2},{2,0},{4,6},{6,4},{8,10},{10,8},{12,14},{14,12},{16,18},{18,... | collective-permute-start | bytes 3145736 | tf_op jit(solution)/shard_map/ppermute | solution.py:333
  82.2 8.5 %collective-permute-start.21 = (bf16[1408,256]{1,0:T(8,128)(2,1)S(1)}, bf16[1408,256]{1,0:T(8,128)(2,1)S(1)}, u32[]{:S(2)}, u32[]{:S(2)}) collective-permute-start(bf16[1408,256]{1,0:T(8,128)(2,1)S(1)} %get-tuple-element.78.refs_3_), channel_id=1, source_target_pairs={{0,2},{2,0},{4,6},{6,4},{8,10},{10,8},{12,14},{14,12},{16,18},{18,... | collective-permute-start | bytes 2162696 | tf_op jit(solution)/shard_map/ppermute | solution.py:333
  82.5 8.2 %collective-permute-start.22 = (bf16[1408,256]{1,0:T(8,128)(2,1)S(1)}, bf16[1408,256]{1,0:T(8,128)(2,1)S(1)}, u32[]{:S(2)}, u32[]{:S(2)}) collective-permute-start(bf16[1408,256]{1,0:T(8,128)(2,1)S(1)} %get-tuple-element.79.refs_4_), channel_id=1, source_target_pairs={{0,2},{2,0},{4,6},{6,4},{8,10},{10,8},{12,14},{14,12},{16,18},{18,... | collective-permute-start | bytes 2162696 | tf_op jit(solution)/shard_map/ppermute | solution.py:333
  82.7 6.7 %collective-permute-start.24 = (f32[1,256]{1,0:T(1,128)S(1)}, f32[1,256]{1,0:T(1,128)S(1)}, u32[]{:S(2)}, u32[]{:S(2)}) collective-permute-start(f32[1,256]{1,0:T(1,128)S(1)} %get-tuple-element.75.refs_9_.refs_0_), channel_id=1, source_target_pairs={{0,128},{2,130},{4,132},{6,134},{8,136},{10,138},{12,140},{14,142}... | collective-permute-start | bytes 3080 | tf_op jit(solution)/shard_map/ppermute | solution.py:333
  89.4 5.1 %collective-permute-start.25 = (f32[1,256]{1,0:T(1,128)S(1)}, f32[1,256]{1,0:T(1,128)S(1)}, u32[]{:S(2)}, u32[]{:S(2)}) collective-permute-start(f32[1,256]{1,0:T(1,128)S(1)} %add.28.refs_9_.refs_0_), channel_id=1, source_target_pairs={{0,4},{2,6},{4,0},{6,2},{8,12},{10,14},{12,8},{14,10},{16,20},{18,... | collective-permute-start | bytes 3080 | tf_op jit(solution)/shard_map/ppermute | solution.py:333
  94.5 1.9 %collective-permute-start.26 = (f32[1,256]{1,0:T(1,128)S(1)}, f32[1,256]{1,0:T(1,128)S(1)}, u32[]{:S(2)}, u32[]{:S(2)}) collective-permute-start(f32[1,256]{1,0:T(1,128)S(1)} %add.29), channel_id=1, source_target_pairs={{0,2},{2,0},{4,6},{6,4},{8,10},{10,8},{12,14},{14,12},{16,18},{18,... | collective-permute-start | bytes 3080 | tf_op jit(solution)/shard_map/ppermute | solution.py:333

commit v11 on v10

--- a/solution.py
+++ b/solution.py
@@ -213,7 +213,7 @@
 
 
 def two_joins_kernel(at_ref, dv_ref, a0, a1, b0, b1, b2, b3, first_ref, second_ref, dv_out):
-    dv_out[...] = dv_ref[:, pl.ds(pl.multiple_of((1 - at_ref[3]) * HALF, HALF), HALF)]
+    dv_out[...] = dv_ref[:, pl.ds(pl.multiple_of((1 - at_ref[3]) * HALF, HALF), HALF)].astype(BF16)
     n = a0.shape[0]
     for j, part in enumerate((a0, a1)):
         first_ref[n * j : n * (j + 1), :] = part[...]
@@ -247,7 +247,7 @@
     cols = own_columns(at_ref)
     scale = scale_ref[:, cols]
     sums = jnp.zeros((1, HALF), F32)
-    terms = ((other_ref, dv_other[...], theirs_ref), (own_ref, dv_own[:, cols], mine_ref))
+    terms = ((other_ref, dv_other[...].astype(F32), theirs_ref), (own_ref, dv_own[:, cols], mine_ref))
     for hidden_ref, dv, values_ref in terms:
         raw = dot(hidden_ref[...], codes_ref[...], (1, 0))
         values_ref[...] = (raw * scale).astype(BF16)
@@ -367,7 +367,7 @@
     probs.append(p)
     n = first.shape[0]
     first, second, dv_half = call(
-        two_joins_kernel, "join", [shape(2 * n, HEAD), shape(4 * n, HEAD), shape(COUNT, HALF, dtype=F32)],
+        two_joins_kernel, "join", [shape(2 * n, HEAD), shape(4 * n, HEAD), shape(COUNT, HALF)],
         [(SMEM, at)] + [(VMEM, a) for a in [dv, first, first_x, second] + second_y],
     )
     pieces = [first] + [send(first, y_shift(k)) for k in (1, 2, 3)] + [second, send(second, X_SWAP)]
@@ -382,11 +382,12 @@
             values_far = send(theirs, C_SWAP)
             near = lax.ppermute(near, "seq", SEQ_SWAP)
             beside = lax.ppermute(beside, ("dp", "seq"), BESIDE)
-            after = (values_far,)
+            kept_far = send(kept, C_SWAP)
+            after = (values_far, kept_far)
         elif step < 5:
             g = step - 1
             if step == 4:
-                far = [send(a, C_SWAP) for a in (near, beside, kept)]
+                far = [send(a, C_SWAP) for a in (near, beside)] + [kept_far]
             *held, token = grads_part(g, at, queries, keys, upstream, mine, values_far, probs[g], held, (sums,))
             after = (token,)
         else:
@@ -397,9 +398,7 @@
             after = (token,)
         ins = [(VMEM, sums), (VMEM, got)]
         if step == 3:
-            sums, near, beside, kept = call(
-                add_kernel, "add", shape(1, HALF, dtype=F32), ins, after, (near, beside, kept)
-            )
+            sums, near, beside = call(add_kernel, "add", shape(1, HALF, dtype=F32), ins, after, (near, beside))
         else:
             sums = call(add_kernel, "add", shape(1, HALF, dtype=F32), ins, after)
     far = send(sums, C_SWAP)

time: 97.1 us -> 94.2 us (0.970)
  waiting for transfers between devices: 28.4 us -> 23.3 us
  starting transfers between devices: 37.9 us -> 40.1 us
    ppermute x25, waiting for transfers between devices: 27 us -> 21.3 us  [send(): return lax.ppermute(x, 'dp', perm)]
    ppermute x25, starting transfers between devices: 34.8 us -> 37.1 us  [send(): return lax.ppermute(x, 'dp', perm)]
  transfers between devices with their start and end apart: 27 -> 27, of which waited for: 12 -> 12; matrix products, arithmetic and copies ran while one was open for 1% -> 1% of each run, Pallas kernels for 25% -> 26%
where the time goes in v11:
time: 94.2 us; the launch traced here: 94.1 us
  starting transfers between devices  40.1 us (43%)
  Pallas kernels  28.5 us (30%)
  waiting for transfers between devices  23.3 us (25%)
    ppermute x25, starting transfers between devices, send(): return lax.ppermute(x, 'dp', perm)  37.1 us
    pallas_call x21, Pallas kernels, call(): pl.pallas_call(run, in_specs=list(specs) + [ANY] * (len(after) + len(thro...  28.5 us
    ppermute x25, waiting for transfers between devices, send(): return lax.ppermute(x, 'dp', perm)  21.3 us
    ppermute x1, waiting for transfers between devices, shards(): beside = lax.ppermute(beside, ('dp', 'seq'), BESIDE)  2.05 us
  transfers between devices with their start and end apart: 27, of which 12 were waited for; matrix products, arithmetic and copies ran while one was open for 1% of the time, Pallas kernels for 26%

profile of v11, /device:TPU:1, one launch (start us, length us, event | category | flops | bytes accessed | tf_op | source)
XLA Modules:
  0.0 94.1 jit_solution(12703694481468234858)
XLA Ops:
  0.6 3.3 %collective-permute-start = (bf16[32,512]{1,0:T(8,128)(2,1)}, bf16[32,512]{1,0:T(8,128)(2,1)S(1)}, u32[]{:S(2)}, u32[]{:S(2)}) collective-permute-start(bf16[32,512]{1,0:T(8,128)(2,1)} %refs_0_.1), channel_id=1, source_target_pairs={{0,2},{2,0},{4,6},{6,4},{8,10},{10,8},{12,14},{14,12},{16,18},{18,... | collective-permute-start | bytes 98312 | tf_op jit(solution)/shard_map/ppermute | solution.py:333
  4.0 0.7 slice_bitcast_fusion
  5.0 0.7 join.5.refs_5_.refs_0_
  5.8 5.3 %collective-permute-start.1 = (bf16[64,256]{1,0:T(8,128)(2,1)S(1)}, bf16[64,256]{1,0:T(8,128)(2,1)S(1)}, u32[]{:S(2)}, u32[]{:S(2)}) collective-permute-start(bf16[64,256]{1,0:T(8,128)(2,1)S(1)} %join.5.refs_5_.refs_0_), channel_id=1, source_target_pairs={{0,128},{2,130},{4,132},{6,134},{8,136},{10,138},{12,140},{14,142}... | collective-permute-start | bytes 98312 | tf_op jit(solution)/shard_map/ppermute | solution.py:333
  11.0 3.4 %probs_part.4 = (bf16[4,384,384]{2,1,0:T(8,128)(2,1)S(1)}, f32[384,512]{1,0:T(8,128)S(1)}, bf16[384,4096]{1,0:T(8,128)(2,1)S(1)}) custom-call(s32[8]{0:T(128)S(1)} %concatenate.11.refs_2_.refs_0_, bf16[384,2048]{1,0:T(8,128)(2,1)} %refs_1_.15, bf16[384,512]{1,0:T(8,128)(2,1)} %refs_2_.15, bf16[384,2048]{1,0:T(8,128)(2,1)} %refs_3_.15, ...), custom_call_target="tpu_custom_call" | custom-call | flops 1000 | bytes 1000 | tf_op jit(solution)/shard_map/probs_part/pallas_call | solution.py:53
  14.5 0.7 collective-permute-start.2
  15.2 1.2 %collective-permute-start.3 = (bf16[128,256]{1,0:T(8,128)(2,1)S(1)}, bf16[128,256]{1,0:T(8,128)(2,1)S(1)}, u32[]{:S(2)}, u32[]{:S(2)}) collective-permute-start(bf16[128,256]{1,0:T(8,128)(2,1)S(1)} %get-tuple-element.47.refs_5_.refs_0_), channel_id=1, source_target_pairs={{0,64},{2,66},{4,68},{6,70},{8,72},{10,74},{12,76},{14,78},{16,80}... | collective-permute-start | bytes 196616 | tf_op jit(solution)/shard_map/ppermute | solution.py:333
  16.4 2.2 %probs_part.5 = (bf16[4,384,384]{2,1,0:T(8,128)(2,1)S(1)}, f32[384,512]{1,0:T(8,128)S(1)}) custom-call(s32[8]{0:T(128)S(1)} %concatenate.11.refs_2_.refs_0_, bf16[384,2048]{1,0:T(8,128)(2,1)S(1)} %copy-done, bf16[384,512]{1,0:T(8,128)(2,1)S(1)} %copy-done.2, bf16[384,2048]{1,0:T(8,128)(2,1)S(1)} %copy-done.1, ...), custom_call_target="tpu_custom_call", output_to_operand_aliasing={{1}: (4, {})} | custom-call | flops 1000 | bytes 1000 | tf_op jit(solution)/shard_map/probs_part/pallas_call | solution.py:53
  18.6 2.6 %collective-permute-done.3.refs_1_ = bf16[128,256]{1,0:T(8,128)(2,1)S(1)} collective-permute-done((bf16[128,256]{1,0:T(8,128)(2,1)S(1)}, bf16[128,256]{1,0:T(8,128)(2,1)S(1)}, u32[]{:S(2)}, u32[]{:S(2)}) %collective-permute-start.3) | collective-permute-done | bytes 65568 | tf_op jit(solution)/shard_map/ppermute | solution.py:333
  21.3 2.2 %probs_part.6 = (bf16[4,384,384]{2,1,0:T(8,128)(2,1)S(1)}, f32[384,512]{1,0:T(8,128)S(1)}) custom-call(s32[8]{0:T(128)S(1)} %concatenate.11.refs_2_.refs_0_, bf16[384,2048]{1,0:T(8,128)(2,1)S(1)} %copy-done, bf16[384,512]{1,0:T(8,128)(2,1)S(1)} %copy-done.2, bf16[384,2048]{1,0:T(8,128)(2,1)S(1)} %copy-done.1, ...), custom_call_target="tpu_custom_call", output_to_operand_aliasing={{1}: (4, {})} | custom-call | flops 1000 | bytes 1000 | tf_op jit(solution)/shard_map/probs_part/pallas_call | solution.py:53
  23.5 1.9 %collective-permute-done.4.refs_1_ = bf16[256,256]{1,0:T(8,128)(2,1)S(1)} collective-permute-done((bf16[256,256]{1,0:T(8,128)(2,1)S(1)}, bf16[256,256]{1,0:T(8,128)(2,1)S(1)}, u32[]{:S(2)}, u32[]{:S(2)}) %collective-permute-start.4) | collective-permute-done | bytes 131104 | tf_op jit(solution)/shard_map/ppermute | solution.py:333
  25.5 2.8 %collective-permute-start.5 = (bf16[512,128]{1,0:T(8,128)(2,1)S(1)}, bf16[512,128]{1,0:T(8,128)(2,1)S(1)}, u32[]{:S(2)}, u32[]{:S(2)}) collective-permute-start(bf16[512,128]{1,0:T(8,128)(2,1)S(1)} %get-tuple-element.52.refs_5_.refs_2_), channel_id=1, source_target_pairs={{0,4},{2,6},{4,0},{6,2},{8,12},{10,14},{12,8},{14,10},{16,20},{18,... | collective-permute-start | bytes 393224 | tf_op jit(solution)/shard_map/ppermute | solution.py:333
  28.3 2.7 %collective-permute-start.8 = (bf16[512,128]{1,0:T(8,128)(2,1)S(1)}, bf16[512,128]{1,0:T(8,128)(2,1)S(1)}, u32[]{:S(2)}, u32[]{:S(2)}) collective-permute-start(bf16[512,128]{1,0:T(8,128)(2,1)S(1)} %get-tuple-element.54.refs_4_), channel_id=1, source_target_pairs={{0,24},{2,26},{4,28},{6,30},{8,0},{10,2},{12,4},{14,6},{16,8},{18,... | collective-permute-start | bytes 393224 | tf_op jit(solution)/shard_map/ppermute | solution.py:333
  31.1 0.4 collective-permute-start.7
  31.4 0.7 collective-permute-start.6
  32.1 2.2 %probs_part.7 = (bf16[4,384,384]{2,1,0:T(8,128)(2,1)S(1)}, f32[384,512]{1,0:T(8,128)S(1)}) custom-call(s32[8]{0:T(128)S(1)} %concatenate.11.refs_2_.refs_0_, bf16[384,2048]{1,0:T(8,128)(2,1)S(1)} %copy-done, bf16[384,512]{1,0:T(8,128)(2,1)S(1)} %copy-done.2, bf16[384,2048]{1,0:T(8,128)(2,1)S(1)} %copy-done.1, ...), custom_call_target="tpu_custom_call", output_to_operand_aliasing={{1}: (4, {})} | custom-call | flops 1000 | bytes 1000 | tf_op jit(solution)/shard_map/probs_part/pallas_call | solution.py:53
  34.3 2.2 %collective-permute-done.7.refs_6_ = bf16[512,128]{1,0:T(8,128)(2,1)S(1)} collective-permute-done((bf16[512,128]{1,0:T(8,128)(2,1)S(1)}, bf16[512,128]{1,0:T(8,128)(2,1)S(1)}, u32[]{:S(2)}, u32[]{:S(2)}) %collective-permute-start.7) | collective-permute-done | bytes 131104 | tf_op jit(solution)/shard_map/ppermute | solution.py:333
  36.5 1.3 %collective-permute-done.6.refs_5_ = bf16[512,128]{1,0:T(8,128)(2,1)S(1)} collective-permute-done((bf16[512,128]{1,0:T(8,128)(2,1)S(1)}, bf16[512,128]{1,0:T(8,128)(2,1)S(1)}, u32[]{:S(2)}, u32[]{:S(2)}) %collective-permute-start.6) | collective-permute-done | bytes 131104 | tf_op jit(solution)/shard_map/ppermute | solution.py:333
  37.8 0.6 join.9
  38.7 0.6 collective-permute-start.12
  39.4 0.4 collective-permute-start.11
  39.7 0.5 collective-permute-start.10
  40.2 4.3 %collective-permute-start.9 = (bf16[384,256]{1,0:T(8,128)(2,1)S(1)}, bf16[384,256]{1,0:T(8,128)(2,1)S(1)}, u32[]{:S(2)}, u32[]{:S(2)}) collective-permute-start(bf16[384,256]{1,0:T(8,128)(2,1)S(1)} %get-tuple-element.55), channel_id=1, source_target_pairs={{0,2},{2,0},{4,6},{6,4},{8,10},{10,8},{12,14},{14,12},{16,18},{18,... | collective-permute-start | bytes 589832 | tf_op jit(solution)/shard_map/ppermute | solution.py:333
  44.6 1.1 %collective-permute-done.9.refs_4_ = bf16[384,256]{1,0:T(8,128)(2,1)S(1)} collective-permute-done((bf16[384,256]{1,0:T(8,128)(2,1)S(1)}, bf16[384,256]{1,0:T(8,128)(2,1)S(1)}, u32[]{:S(2)}, u32[]{:S(2)}) %collective-permute-start.9) | collective-permute-done | bytes 196640 | tf_op jit(solution)/shard_map/ppermute | solution.py:333
  45.6 0.5 collective-permute-done.11.refs_8_
  46.2 6.8 %collective-permute-done.10.refs_7_ = bf16[1024,128]{1,0:T(8,128)(2,1)S(1)} collective-permute-done((bf16[1024,128]{1,0:T(8,128)(2,1)S(1)}, bf16[1024,128]{1,0:T(8,128)(2,1)S(1)}, u32[]{:S(2)}, u32[]{:S(2)}) %collective-permute-start.10) | collective-permute-done | bytes 262176 | tf_op jit(solution)/shard_map/ppermute | solution.py:333
  53.0 2.9 %raw_part.1 = (bf16[384,256]{1,0:T(8,128)(2,1)S(1)}, bf16[384,256]{1,0:T(8,128)(2,1)S(1)}, f32[1,256]{1,0:T(1,128)S(1)}, bf16[2048,256]{1,0:T(8,128)(2,1)S(1)}, ...) custom-call(s32[8]{0:T(128)S(1)} %concatenate.11.refs_2_.refs_0_, ...), custom_call_target="tpu_custom_call" | custom-call | flops 1000 | bytes 1000 | tf_op jit(solution)/shard_map/raw_part/pallas_call | solution.py:53
  55.9 2.3 %collective-permute-start.16 = (bf16[2048,256]{1,0:T(8,128)(2,1)S(1)}, bf16[2048,256]{1,0:T(8,128)(2,1)S(1)}, u32[]{:S(2)}, u32[]{:S(2)}) collective-permute-start(bf16[2048,256]{1,0:T(8,128)(2,1)S(1)} %get-tuple-element.62.refs_5_), channel_id=1, source_target_pairs={{0,2},{2,0},{4,6},{6,4},{8,10},{10,8},{12,14},{14,12},{16,18},{18,... | collective-permute-start | bytes 3145736 | tf_op jit(solution)/shard_map/ppermute | solution.py:333
  58.2 1.2 %collective-permute-start.20 = (bf16[1408,256]{1,0:T(8,128)(2,1)S(1)}, bf16[1408,256]{1,0:T(8,128)(2,1)S(1)}, u32[]{:S(2)}, u32[]{:S(2)}) collective-permute-start(bf16[1408,256]{1,0:T(8,128)(2,1)S(1)} %get-tuple-element.72), channel_id=1, source_target_pairs={{0,1},{1,0},{2,3},{3,2},{4,5},{5,4},{6,7},{7,6},{8,9},{9,8},{10,11... | collective-permute-start | bytes 2162696 | tf_op jit(solution)/shard_map/ppermute | solution.py:383
  59.4 1.8 %collective-permute-start.21 = (bf16[1408,256]{1,0:T(8,128)(2,1)S(1)}, bf16[1408,256]{1,0:T(8,128)(2,1)S(1)}, u32[]{:S(2)}, u32[]{:S(2)}) collective-permute-start(bf16[1408,256]{1,0:T(8,128)(2,1)S(1)} %get-tuple-element.73), channel_id=1, source_target_pairs={{0,5},{1,4},{2,7},{3,6},{4,1},{5,0},{6,3},{7,2},{8,13},{9,12},{10,... | collective-permute-start | bytes 2162696 | tf_op jit(solution)/shard_map/ppermute | solution.py:384
  61.2 0.6 collective-permute-start.14
  61.9 2.7 %collective-permute-done.15.refs_1_ = f32[1,256]{1,0:T(1,128)S(1)} collective-permute-done((f32[1,256]{1,0:T(1,128)S(1)}, f32[1,256]{1,0:T(1,128)S(1)}, u32[]{:S(2)}, u32[]{:S(2)}) %collective-permute-start.15) | collective-permute-done | bytes 1056 | tf_op jit(solution)/shard_map/ppermute | solution.py:333
  64.6 0.4 collective-permute-start.17
  65.0 2.6 %grads_part.4 = (bf16[384,2048]{1,0:T(8,128)(2,1)}, bf16[384,512]{1,0:T(8,128)(2,1)}, f32[8,128]{1,0:T(8,128)S(1)}) custom-call(s32[8]{0:T(128)S(1)} %concatenate.11.refs_2_.refs_0_, bf16[384,2048]{1,0:T(8,128)(2,1)S(1)} %copy-done, bf16[384,512]{1,0:T(8,128)(2,1)S(1)} %copy-done.2, bf16[384,2048]{1,0:T(8,128)(2,1)S(1)} %copy-done.1, ...), custom_call_target="tpu_custom_call" | custom-call | flops 1000 | bytes 1000 | tf_op jit(solution)/shard_map/grads_part/pallas_call | solution.py:53
  67.6 1.0 %collective-permute-done.17.refs_1_ = f32[1,256]{1,0:T(1,128)S(1)} collective-permute-done((f32[1,256]{1,0:T(1,128)S(1)}, f32[1,256]{1,0:T(1,128)S(1)}, u32[]{:S(2)}, u32[]{:S(2)}) %collective-permute-start.17) | collective-permute-done | bytes 1056 | tf_op jit(solution)/shard_map/ppermute | solution.py:333
  68.6 1.5 %collective-permute-start.18 = (f32[1,256]{1,0:T(1,128)S(1)}, f32[1,256]{1,0:T(1,128)S(1)}, u32[]{:S(2)}, u32[]{:S(2)}) collective-permute-start(f32[1,256]{1,0:T(1,128)S(1)} %add.25.refs_9_.refs_0_), channel_id=1, source_target_pairs={{0,32},{2,34},{4,36},{6,38},{8,40},{10,42},{12,44},{14,46},{16,48}... | collective-permute-start | bytes 3080 | tf_op jit(solution)/shard_map/ppermute | solution.py:333
  70.1 2.6 %grads_part.5 = (bf16[384,2048]{1,0:T(8,128)(2,1)}, bf16[384,512]{1,0:T(8,128)(2,1)}, f32[8,128]{1,0:T(8,128)S(1)}) custom-call(s32[8]{0:T(128)S(1)} %concatenate.11.refs_2_.refs_0_, bf16[384,2048]{1,0:T(8,128)(2,1)S(1)} %copy-done, bf16[384,512]{1,0:T(8,128)(2,1)S(1)} %copy-done.2, ...), custom_call_target="tpu_custom_call", output_to_operand_aliasing={{0}: (7, {}), {1}: (8, {})} | custom-call | flops 1000 | bytes 1000 | tf_op jit(solution)/shard_map/grads_part/pallas_call | solution.py:53
  72.7 0.6 collective-permute-start.19
  73.3 2.6 %grads_part.6 = (bf16[384,2048]{1,0:T(8,128)(2,1)}, bf16[384,512]{1,0:T(8,128)(2,1)}, f32[8,128]{1,0:T(8,128)S(1)}) custom-call(s32[8]{0:T(128)S(1)} %concatenate.11.refs_2_.refs_0_, bf16[384,2048]{1,0:T(8,128)(2,1)S(1)} %copy-done, bf16[384,512]{1,0:T(8,128)(2,1)S(1)} %copy-done.2, ...), custom_call_target="tpu_custom_call", output_to_operand_aliasing={{0}: (7, {}), {1}: (8, {})} | custom-call | flops 1000 | bytes 1000 | tf_op jit(solution)/shard_map/grads_part/pallas_call | solution.py:53
  75.9 2.1 %collective-permute-done.21.refs_4_ = bf16[1408,256]{1,0:T(8,128)(2,1)S(1)} collective-permute-done((bf16[1408,256]{1,0:T(8,128)(2,1)S(1)}, bf16[1408,256]{1,0:T(8,128)(2,1)S(1)}, u32[]{:S(2)}, u32[]{:S(2)}) %collective-permute-start.21) | collective-permute-done | bytes 720928 | tf_op jit(solution)/shard_map/ppermute | solution.py:384
  78.0 1.6 %collective-permute-start.22 = (bf16[1408,256]{1,0:T(8,128)(2,1)S(1)}, bf16[1408,256]{1,0:T(8,128)(2,1)S(1)}, u32[]{:S(2)}, u32[]{:S(2)}) collective-permute-start(bf16[1408,256]{1,0:T(8,128)(2,1)S(1)} %get-tuple-element.77.refs_3_), channel_id=1, source_target_pairs={{0,2},{2,0},{4,6},{6,4},{8,10},{10,8},{12,14},{14,12},{16,18},{18,... | collective-permute-start | bytes 2162696 | tf_op jit(solution)/shard_map/ppermute | solution.py:333
  79.7 3.7 %collective-permute-start.24 = (f32[1,256]{1,0:T(1,128)S(1)}, f32[1,256]{1,0:T(1,128)S(1)}, u32[]{:S(2)}, u32[]{:S(2)}) collective-permute-start(f32[1,256]{1,0:T(1,128)S(1)} %get-tuple-element.74.refs_9_.refs_0_), channel_id=1, source_target_pairs={{0,128},{2,130},{4,132},{6,134},{8,136},{10,138},{12,140},{14,142}... | collective-permute-start | bytes 3080 | tf_op jit(solution)/shard_map/ppermute | solution.py:333
  83.4 2.6 %grads_part.7 = (bf16[384,2048]{1,0:T(8,128)(2,1)}, bf16[384,512]{1,0:T(8,128)(2,1)}, f32[8,128]{1,0:T(8,128)S(1)}) custom-call(s32[8]{0:T(128)S(1)} %concatenate.11.refs_2_.refs_0_, bf16[384,2048]{1,0:T(8,128)(2,1)S(1)} %copy-done, bf16[384,512]{1,0:T(8,128)(2,1)S(1)} %copy-done.2, ...), custom_call_target="tpu_custom_call", output_to_operand_aliasing={{0}: (7, {}), {1}: (8, {})} | custom-call | flops 1000 | bytes 1000 | tf_op jit(solution)/shard_map/grads_part/pallas_call | solution.py:53
  86.0 1.3 %collective-permute-start.25 = (f32[1,256]{1,0:T(1,128)S(1)}, f32[1,256]{1,0:T(1,128)S(1)}, u32[]{:S(2)}, u32[]{:S(2)}) collective-permute-start(f32[1,256]{1,0:T(1,128)S(1)} %add.28.refs_9_.refs_0_), channel_id=1, source_target_pairs={{0,4},{2,6},{4,0},{6,2},{8,12},{10,14},{12,8},{14,10},{16,20},{18,... | collective-permute-start | bytes 3080 | tf_op jit(solution)/shard_map/ppermute | solution.py:333
  87.3 3.7 %hidden_part.1 = (bf16[384,2048]{1,0:T(8,128)(2,1)}, f32[8,128]{1,0:T(8,128)S(1)}) custom-call(s32[8]{0:T(128)S(1)} %concatenate.11.refs_2_.refs_0_, f32[384,512]{1,0:T(8,128)S(1)} %get-tuple-element.53.refs_1_.refs_3_, f32[1,512]{1,0:T(1,128)S(1)} %bitcast.11, bf16[1408,256]{1,0:T(8,128)(2,1)S(1)} %get-tuple-element.77.refs_3_, ...), custom_call_target="tpu_custom_call" | custom-call | flops 1000 | bytes 1000 | tf_op jit(solution)/shard_map/hidden_part/pallas_call | solution.py:53
  91.1 1.6 %collective-permute-start.26 = (f32[1,256]{1,0:T(1,128)S(1)}, f32[1,256]{1,0:T(1,128)S(1)}, u32[]{:S(2)}, u32[]{:S(2)}) collective-permute-start(f32[1,256]{1,0:T(1,128)S(1)} %add.29), channel_id=1, source_target_pairs={{0,2},{2,0},{4,6},{6,4},{8,10},{10,8},{12,14},{14,12},{16,18},{18,... | collective-permute-start | bytes 3080 | tf_op jit(solution)/shard_map/ppermute | solution.py:333
  92.6 0.8 collective-permute-done.26
  93.5 0.6 maximum_multiply_fusion
  (39 shorter events, 1.1 us)
Async XLA Ops:
  0.6 4.4 %collective-permute-start = (bf16[32,512]{1,0:T(8,128)(2,1)}, bf16[32,512]{1,0:T(8,128)(2,1)S(1)}, u32[]{:S(2)}, u32[]{:S(2)}) collective-permute-start(bf16[32,512]{1,0:T(8,128)(2,1)} %refs_0_.1), channel_id=1, source_target_pairs={{0,2},{2,0},{4,6},{6,4},{8,10},{10,8},{12,14},{14,12},{16,18},{18,... | collective-permute-start | bytes 98312 | tf_op jit(solution)/shard_map/ppermute | solution.py:333
  5.8 8.7 %collective-permute-start.1 = (bf16[64,256]{1,0:T(8,128)(2,1)S(1)}, bf16[64,256]{1,0:T(8,128)(2,1)S(1)}, u32[]{:S(2)}, u32[]{:S(2)}) collective-permute-start(bf16[64,256]{1,0:T(8,128)(2,1)S(1)} %join.5.refs_5_.refs_0_), channel_id=1, source_target_pairs={{0,128},{2,130},{4,132},{6,134},{8,136},{10,138},{12,140},{14,142}... | collective-permute-start | bytes 98312 | tf_op jit(solution)/shard_map/ppermute | solution.py:333
  14.5 2.0 %copy-start = (bf16[384,2048]{1,0:T(8,128)(2,1)S(1)}, bf16[384,2048]{1,0:T(8,128)(2,1)}, u32[]{:S(2)}) copy-start(bf16[384,2048]{1,0:T(8,128)(2,1)} %refs_1_.15) | copy-start | bytes 4718596
  14.5 2.0 %copy-start.1 = (bf16[384,2048]{1,0:T(8,128)(2,1)S(1)}, bf16[384,2048]{1,0:T(8,128)(2,1)}, u32[]{:S(2)}) copy-start(bf16[384,2048]{1,0:T(8,128)(2,1)} %refs_3_.15) | copy-start | bytes 4718596
  14.5 2.0 %copy-start.2 = (bf16[384,512]{1,0:T(8,128)(2,1)S(1)}, bf16[384,512]{1,0:T(8,128)(2,1)}, u32[]{:S(2)}) copy-start(bf16[384,512]{1,0:T(8,128)(2,1)} %refs_2_.15) | copy-start | bytes 1179652
  14.5 10.9 %collective-permute-start.2 = (bf16[384,4096]{1,0:T(8,128)(2,1)S(1)}, bf16[384,4096]{1,0:T(8,128)(2,1)S(1)}, u32[]{:S(2)}, u32[]{:S(2)}) collective-permute-start(bf16[384,4096]{1,0:T(8,128)(2,1)S(1)} %get-tuple-element.45.refs_1_), channel_id=1, source_target_pairs={{0,2},{2,0},{4,6},{6,4},{8,10},{10,8},{12,14},{14,12},{16,18},{18,... | collective-permute-start | bytes 9437192 | tf_op jit(solution)/shard_map/ppermute | solution.py:333
  15.2 6.0 %collective-permute-start.3 = (bf16[128,256]{1,0:T(8,128)(2,1)S(1)}, bf16[128,256]{1,0:T(8,128)(2,1)S(1)}, u32[]{:S(2)}, u32[]{:S(2)}) collective-permute-start(bf16[128,256]{1,0:T(8,128)(2,1)S(1)} %get-tuple-element.47.refs_5_.refs_0_), channel_id=1, source_target_pairs={{0,64},{2,66},{4,68},{6,70},{8,72},{10,74},{12,76},{14,78},{16,80}... | collective-permute-start | bytes 196616 | tf_op jit(solution)/shard_map/ppermute | solution.py:333
  21.2 4.2 %collective-permute-start.4 = (bf16[256,256]{1,0:T(8,128)(2,1)S(1)}, bf16[256,256]{1,0:T(8,128)(2,1)S(1)}, u32[]{:S(2)}, u32[]{:S(2)}) collective-permute-start(bf16[256,256]{1,0:T(8,128)(2,1)S(1)} %join.7.refs_5_.refs_0_), channel_id=1, source_target_pairs={{0,32},{2,34},{4,36},{6,38},{8,40},{10,42},{12,44},{14,46},{16,48}... | collective-permute-start | bytes 393224 | tf_op jit(solution)/shard_map/ppermute | solution.py:333
  25.5 8.8 %collective-permute-start.5 = (bf16[512,128]{1,0:T(8,128)(2,1)S(1)}, bf16[512,128]{1,0:T(8,128)(2,1)S(1)}, u32[]{:S(2)}, u32[]{:S(2)}) collective-permute-start(bf16[512,128]{1,0:T(8,128)(2,1)S(1)} %get-tuple-element.52.refs_5_.refs_2_), channel_id=1, source_target_pairs={{0,4},{2,6},{4,0},{6,2},{8,12},{10,14},{12,8},{14,10},{16,20},{18,... | collective-permute-start | bytes 393224 | tf_op jit(solution)/shard_map/ppermute | solution.py:333
  28.3 6.0 %collective-permute-start.8 = (bf16[512,128]{1,0:T(8,128)(2,1)S(1)}, bf16[512,128]{1,0:T(8,128)(2,1)S(1)}, u32[]{:S(2)}, u32[]{:S(2)}) collective-permute-start(bf16[512,128]{1,0:T(8,128)(2,1)S(1)} %get-tuple-element.54.refs_4_), channel_id=1, source_target_pairs={{0,24},{2,26},{4,28},{6,30},{8,0},{10,2},{12,4},{14,6},{16,8},{18,... | collective-permute-start | bytes 393224 | tf_op jit(solution)/shard_map/ppermute | solution.py:333
  31.1 5.4 %collective-permute-start.7 = (bf16[512,128]{1,0:T(8,128)(2,1)S(1)}, bf16[512,128]{1,0:T(8,128)(2,1)S(1)}, u32[]{:S(2)}, u32[]{:S(2)}) collective-permute-start(bf16[512,128]{1,0:T(8,128)(2,1)S(1)} %get-tuple-element.54.refs_4_), channel_id=1, source_target_pairs={{0,16},{2,18},{4,20},{6,22},{8,24},{10,26},{12,28},{14,30},{16,0},... | collective-permute-start | bytes 393224 | tf_op jit(solution)/shard_map/ppermute | solution.py:333
  31.4 6.4 %collective-permute-start.6 = (bf16[512,128]{1,0:T(8,128)(2,1)S(1)}, bf16[512,128]{1,0:T(8,128)(2,1)S(1)}, u32[]{:S(2)}, u32[]{:S(2)}) collective-permute-start(bf16[512,128]{1,0:T(8,128)(2,1)S(1)} %get-tuple-element.54.refs_4_), channel_id=1, source_target_pairs={{0,8},{2,10},{4,12},{6,14},{8,16},{10,18},{12,20},{14,22},{16,24},... | collective-permute-start | bytes 393224 | tf_op jit(solution)/shard_map/ppermute | solution.py:333
  34.3 18.7 %copy-start.3 = (f32[512]{0:T(512)S(1)}, f32[512]{0:T(512)}, u32[]{:S(2)}) copy-start(f32[512]{0:T(512)} %param.11) | copy-start | bytes 6148
  38.4 14.6 %collective-permute-start.13 = (bf16[2048,128]{1,0:T(8,128)(2,1)S(1)}, bf16[2048,128]{1,0:T(8,128)(2,1)S(1)}, u32[]{:S(2)}, u32[]{:S(2)}) collective-permute-start(bf16[2048,128]{1,0:T(8,128)(2,1)S(1)} %get-tuple-element.57.refs_10_), channel_id=1, source_target_pairs={{0,4},{2,6},{4,0},{6,2},{8,12},{10,14},{12,8},{14,10},{16,20},{18,... | collective-permute-start | bytes 1572872 | tf_op jit(solution)/shard_map/ppermute | solution.py:333
  38.7 6.9 %collective-permute-start.12 = (bf16[1024,128]{1,0:T(8,128)(2,1)S(1)}, bf16[1024,128]{1,0:T(8,128)(2,1)S(1)}, u32[]{:S(2)}, u32[]{:S(2)}) collective-permute-start(bf16[1024,128]{1,0:T(8,128)(2,1)S(1)} %get-tuple-element.56.refs_6_), channel_id=1, source_target_pairs={{0,24},{2,26},{4,28},{6,30},{8,0},{10,2},{12,4},{14,6},{16,8},{18,... | collective-permute-start | bytes 786440 | tf_op jit(solution)/shard_map/ppermute | solution.py:333
  39.4 6.8 %collective-permute-start.11 = (bf16[1024,128]{1,0:T(8,128)(2,1)S(1)}, bf16[1024,128]{1,0:T(8,128)(2,1)S(1)}, u32[]{:S(2)}, u32[]{:S(2)}) collective-permute-start(bf16[1024,128]{1,0:T(8,128)(2,1)S(1)} %get-tuple-element.56.refs_6_), channel_id=1, source_target_pairs={{0,16},{2,18},{4,20},{6,22},{8,24},{10,26},{12,28},{14,30},{16,0},... | collective-permute-start | bytes 786440 | tf_op jit(solution)/shard_map/ppermute | solution.py:333
  39.7 13.3 %collective-permute-start.10 = (bf16[1024,128]{1,0:T(8,128)(2,1)S(1)}, bf16[1024,128]{1,0:T(8,128)(2,1)S(1)}, u32[]{:S(2)}, u32[]{:S(2)}) collective-permute-start(bf16[1024,128]{1,0:T(8,128)(2,1)S(1)} %get-tuple-element.56.refs_6_), channel_id=1, source_target_pairs={{0,8},{2,10},{4,12},{6,14},{8,16},{10,18},{12,20},{14,22},{16,24},... | collective-permute-start | bytes 786440 | tf_op jit(solution)/shard_map/ppermute | solution.py:333
  40.2 5.4 %collective-permute-start.9 = (bf16[384,256]{1,0:T(8,128)(2,1)S(1)}, bf16[384,256]{1,0:T(8,128)(2,1)S(1)}, u32[]{:S(2)}, u32[]{:S(2)}) collective-permute-start(bf16[384,256]{1,0:T(8,128)(2,1)S(1)} %get-tuple-element.55), channel_id=1, source_target_pairs={{0,2},{2,0},{4,6},{6,4},{8,10},{10,8},{12,14},{14,12},{16,18},{18,... | collective-permute-start | bytes 589832 | tf_op jit(solution)/shard_map/ppermute | solution.py:333
  55.9 8.6 %collective-permute-start.16 = (bf16[2048,256]{1,0:T(8,128)(2,1)S(1)}, bf16[2048,256]{1,0:T(8,128)(2,1)S(1)}, u32[]{:S(2)}, u32[]{:S(2)}) collective-permute-start(bf16[2048,256]{1,0:T(8,128)(2,1)S(1)} %get-tuple-element.62.refs_5_), channel_id=1, source_target_pairs={{0,2},{2,0},{4,6},{6,4},{8,10},{10,8},{12,14},{14,12},{16,18},{18,... | collective-permute-start | bytes 3145736 | tf_op jit(solution)/shard_map/ppermute | solution.py:333
  58.2 17.7 %collective-permute-start.20 = (bf16[1408,256]{1,0:T(8,128)(2,1)S(1)}, bf16[1408,256]{1,0:T(8,128)(2,1)S(1)}, u32[]{:S(2)}, u32[]{:S(2)}) collective-permute-start(bf16[1408,256]{1,0:T(8,128)(2,1)S(1)} %get-tuple-element.72), channel_id=1, source_target_pairs={{0,1},{1,0},{2,3},{3,2},{4,5},{5,4},{6,7},{7,6},{8,9},{9,8},{10,11... | collective-permute-start | bytes 2162696 | tf_op jit(solution)/shard_map/ppermute | solution.py:383
  59.4 18.6 %collective-permute-start.21 = (bf16[1408,256]{1,0:T(8,128)(2,1)S(1)}, bf16[1408,256]{1,0:T(8,128)(2,1)S(1)}, u32[]{:S(2)}, u32[]{:S(2)}) collective-permute-start(bf16[1408,256]{1,0:T(8,128)(2,1)S(1)} %get-tuple-element.73), channel_id=1, source_target_pairs={{0,5},{1,4},{2,7},{3,6},{4,1},{5,0},{6,3},{7,2},{8,13},{9,12},{10,... | collective-permute-start | bytes 2162696 | tf_op jit(solution)/shard_map/ppermute | solution.py:384
  61.2 3.4 %collective-permute-start.14 = (bf16[384,256]{1,0:T(8,128)(2,1)S(1)}, bf16[384,256]{1,0:T(8,128)(2,1)S(1)}, u32[]{:S(2)}, u32[]{:S(2)}) collective-permute-start(bf16[384,256]{1,0:T(8,128)(2,1)S(1)} %get-tuple-element.59), channel_id=1, source_target_pairs={{0,2},{2,0},{4,6},{6,4},{8,10},{10,8},{12,14},{14,12},{16,18},{18,... | collective-permute-start | bytes 589832 | tf_op jit(solution)/shard_map/ppermute | solution.py:333
  61.9 2.7 %collective-permute-start.15 = (f32[1,256]{1,0:T(1,128)S(1)}, f32[1,256]{1,0:T(1,128)S(1)}, u32[]{:S(2)}, u32[]{:S(2)}) collective-permute-start(f32[1,256]{1,0:T(1,128)S(1)} %get-tuple-element.61.refs_0_), channel_id=1, source_target_pairs={{0,8},{2,10},{4,12},{6,14},{8,0},{10,2},{12,4},{14,6},{16,24},{18,... | collective-permute-start | bytes 3080 | tf_op jit(solution)/shard_map/ppermute | solution.py:333
  64.6 4.0 %collective-permute-start.17 = (f32[1,256]{1,0:T(1,128)S(1)}, f32[1,256]{1,0:T(1,128)S(1)}, u32[]{:S(2)}, u32[]{:S(2)}) collective-permute-start(f32[1,256]{1,0:T(1,128)S(1)} %add.24.refs_7_.refs_0_), channel_id=1, source_target_pairs={{0,16},{2,18},{4,20},{6,22},{8,24},{10,26},{12,28},{14,30},{16,0},... | collective-permute-start | bytes 3080 | tf_op jit(solution)/shard_map/ppermute | solution.py:333
  68.6 4.1 %collective-permute-start.18 = (f32[1,256]{1,0:T(1,128)S(1)}, f32[1,256]{1,0:T(1,128)S(1)}, u32[]{:S(2)}, u32[]{:S(2)}) collective-permute-start(f32[1,256]{1,0:T(1,128)S(1)} %add.25.refs_9_.refs_0_), channel_id=1, source_target_pairs={{0,32},{2,34},{4,36},{6,38},{8,40},{10,42},{12,44},{14,46},{16,48}... | collective-permute-start | bytes 3080 | tf_op jit(solution)/shard_map/ppermute | solution.py:333
  72.7 5.2 %collective-permute-start.19 = (f32[1,256]{1,0:T(1,128)S(1)}, f32[1,256]{1,0:T(1,128)S(1)}, u32[]{:S(2)}, u32[]{:S(2)}) collective-permute-start(f32[1,256]{1,0:T(1,128)S(1)} %add.26.refs_9_.refs_0_), channel_id=1, source_target_pairs={{0,64},{2,66},{4,68},{6,70},{8,72},{10,74},{12,76},{14,78},{16,80}... | collective-permute-start | bytes 3080 | tf_op jit(solution)/shard_map/ppermute | solution.py:333
  78.0 9.3 %collective-permute-start.22 = (bf16[1408,256]{1,0:T(8,128)(2,1)S(1)}, bf16[1408,256]{1,0:T(8,128)(2,1)S(1)}, u32[]{:S(2)}, u32[]{:S(2)}) collective-permute-start(bf16[1408,256]{1,0:T(8,128)(2,1)S(1)} %get-tuple-element.77.refs_3_), channel_id=1, source_target_pairs={{0,2},{2,0},{4,6},{6,4},{8,10},{10,8},{12,14},{14,12},{16,18},{18,... | collective-permute-start | bytes 2162696 | tf_op jit(solution)/shard_map/ppermute | solution.py:333
  79.6 7.7 %collective-permute-start.23 = (bf16[1408,256]{1,0:T(8,128)(2,1)S(1)}, bf16[1408,256]{1,0:T(8,128)(2,1)S(1)}, u32[]{:S(2)}, u32[]{:S(2)}) collective-permute-start(bf16[1408,256]{1,0:T(8,128)(2,1)S(1)} %get-tuple-element.78.refs_4_), channel_id=1, source_target_pairs={{0,2},{2,0},{4,6},{6,4},{8,10},{10,8},{12,14},{14,12},{16,18},{18,... | collective-permute-start | bytes 2162696 | tf_op jit(solution)/shard_map/ppermute | solution.py:333
  79.7 6.4 %collective-permute-start.24 = (f32[1,256]{1,0:T(1,128)S(1)}, f32[1,256]{1,0:T(1,128)S(1)}, u32[]{:S(2)}, u32[]{:S(2)}) collective-permute-start(f32[1,256]{1,0:T(1,128)S(1)} %get-tuple-element.74.refs_9_.refs_0_), channel_id=1, source_target_pairs={{0,128},{2,130},{4,132},{6,134},{8,136},{10,138},{12,140},{14,142}... | collective-permute-start | bytes 3080 | tf_op jit(solution)/shard_map/ppermute | solution.py:333
  86.0 5.0 %collective-permute-start.25 = (f32[1,256]{1,0:T(1,128)S(1)}, f32[1,256]{1,0:T(1,128)S(1)}, u32[]{:S(2)}, u32[]{:S(2)}) collective-permute-start(f32[1,256]{1,0:T(1,128)S(1)} %add.28.refs_9_.refs_0_), channel_id=1, source_target_pairs={{0,4},{2,6},{4,0},{6,2},{8,12},{10,14},{12,8},{14,10},{16,20},{18,... | collective-permute-start | bytes 3080 | tf_op jit(solution)/shard_map/ppermute | solution.py:333
  91.1 2.4 %collective-permute-start.26 = (f32[1,256]{1,0:T(1,128)S(1)}, f32[1,256]{1,0:T(1,128)S(1)}, u32[]{:S(2)}, u32[]{:S(2)}) collective-permute-start(f32[1,256]{1,0:T(1,128)S(1)} %add.29), channel_id=1, source_target_pairs={{0,2},{2,0},{4,6},{6,4},{8,10},{10,8},{12,14},{14,12},{16,18},{18,... | collective-permute-start | bytes 3080 | tf_op jit(solution)/shard_map/ppermute | solution.py:333

commit v12 on v11

--- a/solution.py
+++ b/solution.py
@@ -276,27 +276,40 @@
 BATCH = 512
 
 
-def hidden_kernel(
-    at_ref, dv_ref, scale_ref, near_ref, beside_ref, kept_ref, near_far, beside_far, kept_far, out_ref, token_ref
-):
+def hidden_kernel(first, at_ref, dv_ref, scale_ref, near_ref, codes_ref, codes_far, kept_ref, kept_far, *refs):
+    out_ref, token_ref, part_ref, sem = refs[-4:]
     token_ref[...] = jnp.zeros_like(token_ref)
+    base, size, skip = (0, NEAR, 2 * COUNT) if first else (NEAR, BESIDES, 0)
     sides = []
-    for other, near, beside, kept in ((0, near_ref, beside_ref, kept_ref), (1, near_far, beside_far, kept_far)):
+    for other, codes, kept in ((0, codes_ref, kept_ref), (1, codes_far, kept_far)):
         c = at_ref[3] ^ other
         cols = pl.ds(pl.multiple_of(c * HALF, HALF), HALF)
         own = (dv_ref[:, cols] * scale_ref[:, cols]).astype(BF16)
         seq = near_ref[pl.ds(pl.multiple_of(c * COUNT, COUNT), COUNT), :]
-        sides.append((own, seq, near, beside, kept))
-    at = 0
-    while at < DEPTH // 2:
-        end = min(at + BATCH, NEAR if at < NEAR else DEPTH // 2)
+        sides.append((own, seq, codes, kept))
+    for at in range(0, size, BATCH):
+        end = min(at + BATCH, size)
         total = 0.0
-        for own, seq, near, beside, kept in sides:
-            total += dot(own, kept[at:end, :], (1, 1))
-            codes = near[2 * COUNT + at : 2 * COUNT + end, :] if at < NEAR else beside[at - NEAR : end - NEAR, :]
-            total += dot(seq, codes, (1, 1))
-        out_ref[:, at:end] = total.astype(BF16)
-        at = end
+        for own, seq, codes, kept in sides:
+            total += dot(own, kept[base + at : base + end, :], (1, 1))
+            total += dot(seq, codes[skip + at : skip + end, :], (1, 1))
+        part_ref[:, at:end] = total.astype(BF16)
+    copy = pltpu.make_async_copy(part_ref, out_ref.at[:, pl.ds(base, size)], sem)
+    copy.start()
+    copy.wait()
+
+
+def hidden_part(first, arrays, held, after):
+    extra = {}
+    ins = [(SMEM, arrays[0])] + [(VMEM, a) for a in arrays[1:]]
+    if held is not None:
+        extra["input_output_aliases"] = {len(ins): 0}
+        ins.append((ANY, held))
+    return call(
+        functools.partial(hidden_kernel, first), "hidden_part", [shape(COUNT, DEPTH // 2), TOKEN], ins, after,
+        out_specs=[ANY, VMEM],
+        scratch_shapes=[pltpu.VMEM((COUNT, NEAR if first else BESIDES), BF16), pltpu.SemaphoreType.DMA], **extra,
+    )
 
 
 def add_kernel(a_ref, b_ref, out_ref):
@@ -374,7 +387,7 @@
     dv_other = send(dv_half, C_SWAP)
     mine, theirs, sums, kept, near, beside = raw_part(at, hidden, hidden_other, dv, dv_other, scale, pieces)
 
-    held, far = None, None
+    held = None
     for step, perm in enumerate((y_swap(1), y_swap(2), z_swap(1), z_swap(2), z_swap(4), X_SWAP)):
         got = send(sums, perm)
         after, through = (), ()
@@ -387,13 +400,16 @@
         elif step < 5:
             g = step - 1
             if step == 4:
-                far = [send(a, C_SWAP) for a in (near, beside)] + [kept_far]
+                near_far, beside_far = send(near, C_SWAP), send(beside, C_SWAP)
             *held, token = grads_part(g, at, queries, keys, upstream, mine, values_far, probs[g], held, (sums,))
+            if step == 4:
+                grad_hidden, token = hidden_part(
+                    True, (at, dv, scale, near, near, near_far, kept, kept_far), None, (token,)
+                )
             after = (token,)
         else:
-            grad_hidden, token = call(
-                hidden_kernel, "hidden_part", [shape(COUNT, DEPTH // 2), TOKEN],
-                [(SMEM, at)] + [(VMEM, a) for a in [dv, scale, near, beside, kept] + far], (sums,),
+            grad_hidden, token = hidden_part(
+                False, (at, dv, scale, near, beside, beside_far, kept, kept_far), grad_hidden, (sums,)
             )
             after = (token,)
         ins = [(VMEM, sums), (VMEM, got)]

time: 94.2 us -> 95.6 us (1.015)
  Pallas kernels: 28.5 us -> 29.9 us
    pallas_call x21 -> x22, Pallas kernels: 28.5 us -> 29.9 us  [call(): pl.pallas_call(run, in_specs=list(specs) + [ANY] * (len(after) + len(thro...]
  transfers between devices with their start and end apart: 27 -> 27, of which waited for: 12 -> 12; matrix products, arithmetic and copies ran while one was open for 1% -> 1% of each run, Pallas kernels for 26% -> 27%
where the time goes in v12:
time: 95.6 us; the launch traced here: 95.5 us
  starting transfers between devices  40.1 us (42%)
  Pallas kernels  29.9 us (31%)
  waiting for transfers between devices  23.3 us (24%)
    ppermute x25, starting transfers between devices, send(): return lax.ppermute(x, 'dp', perm)  37.1 us
    pallas_call x22, Pallas kernels, call(): pl.pallas_call(run, in_specs=list(specs) + [ANY] * (len(after) + len(thro...  29.9 us
    ppermute x25, waiting for transfers between devices, send(): return lax.ppermute(x, 'dp', perm)  21.3 us
    ppermute x1, waiting for transfers between devices, shards(): beside = lax.ppermute(beside, ('dp', 'seq'), BESIDE)  2.05 us
  transfers between devices with their start and end apart: 27, of which 12 were waited for; matrix products, arithmetic and copies ran while one was open for 1% of the time, Pallas kernels for 27%

profile of v12, /device:TPU:1, one launch (start us, length us, event | category | flops | bytes accessed | tf_op | source)
XLA Modules:
  0.0 95.5 jit_solution(5659232996628294902)
XLA Ops:
  0.6 3.3 %collective-permute-start = (bf16[32,512]{1,0:T(8,128)(2,1)}, bf16[32,512]{1,0:T(8,128)(2,1)S(1)}, u32[]{:S(2)}, u32[]{:S(2)}) collective-permute-start(bf16[32,512]{1,0:T(8,128)(2,1)} %refs_0_.1), channel_id=1, source_target_pairs={{0,2},{2,0},{4,6},{6,4},{8,10},{10,8},{12,14},{14,12},{16,18},{18,... | collective-permute-start | bytes 98312 | tf_op jit(solution)/shard_map/ppermute | solution.py:346
  4.0 0.7 slice_bitcast_fusion
  5.0 0.7 join.5.refs_5_.refs_0_
  5.8 5.3 %collective-permute-start.1 = (bf16[64,256]{1,0:T(8,128)(2,1)S(1)}, bf16[64,256]{1,0:T(8,128)(2,1)S(1)}, u32[]{:S(2)}, u32[]{:S(2)}) collective-permute-start(bf16[64,256]{1,0:T(8,128)(2,1)S(1)} %join.5.refs_5_.refs_0_), channel_id=1, source_target_pairs={{0,128},{2,130},{4,132},{6,134},{8,136},{10,138},{12,140},{14,142}... | collective-permute-start | bytes 98312 | tf_op jit(solution)/shard_map/ppermute | solution.py:346
  11.0 3.4 %probs_part.4 = (bf16[4,384,384]{2,1,0:T(8,128)(2,1)S(1)}, f32[384,512]{1,0:T(8,128)S(1)}, bf16[384,4096]{1,0:T(8,128)(2,1)S(1)}) custom-call(s32[8]{0:T(128)S(1)} %concatenate.11.refs_2_.refs_0_, bf16[384,2048]{1,0:T(8,128)(2,1)} %refs_1_.15, bf16[384,512]{1,0:T(8,128)(2,1)} %refs_2_.15, bf16[384,2048]{1,0:T(8,128)(2,1)} %refs_3_.15, ...), custom_call_target="tpu_custom_call" | custom-call | flops 1000 | bytes 1000 | tf_op jit(solution)/shard_map/probs_part/pallas_call | solution.py:53
  14.5 0.7 collective-permute-start.2
  15.2 1.2 %collective-permute-start.3 = (bf16[128,256]{1,0:T(8,128)(2,1)S(1)}, bf16[128,256]{1,0:T(8,128)(2,1)S(1)}, u32[]{:S(2)}, u32[]{:S(2)}) collective-permute-start(bf16[128,256]{1,0:T(8,128)(2,1)S(1)} %get-tuple-element.49.refs_5_.refs_0_), channel_id=1, source_target_pairs={{0,64},{2,66},{4,68},{6,70},{8,72},{10,74},{12,76},{14,78},{16,80}... | collective-permute-start | bytes 196616 | tf_op jit(solution)/shard_map/ppermute | solution.py:346
  16.4 2.2 %probs_part.5 = (bf16[4,384,384]{2,1,0:T(8,128)(2,1)S(1)}, f32[384,512]{1,0:T(8,128)S(1)}) custom-call(s32[8]{0:T(128)S(1)} %concatenate.11.refs_2_.refs_0_, bf16[384,2048]{1,0:T(8,128)(2,1)S(1)} %copy-done, bf16[384,512]{1,0:T(8,128)(2,1)S(1)} %copy-done.2, bf16[384,2048]{1,0:T(8,128)(2,1)S(1)} %copy-done.1, ...), custom_call_target="tpu_custom_call", output_to_operand_aliasing={{1}: (4, {})} | custom-call | flops 1000 | bytes 1000 | tf_op jit(solution)/shard_map/probs_part/pallas_call | solution.py:53
  18.6 2.6 %collective-permute-done.3.refs_1_ = bf16[128,256]{1,0:T(8,128)(2,1)S(1)} collective-permute-done((bf16[128,256]{1,0:T(8,128)(2,1)S(1)}, bf16[128,256]{1,0:T(8,128)(2,1)S(1)}, u32[]{:S(2)}, u32[]{:S(2)}) %collective-permute-start.3) | collective-permute-done | bytes 65568 | tf_op jit(solution)/shard_map/ppermute | solution.py:346
  21.3 2.2 %probs_part.6 = (bf16[4,384,384]{2,1,0:T(8,128)(2,1)S(1)}, f32[384,512]{1,0:T(8,128)S(1)}) custom-call(s32[8]{0:T(128)S(1)} %concatenate.11.refs_2_.refs_0_, bf16[384,2048]{1,0:T(8,128)(2,1)S(1)} %copy-done, bf16[384,512]{1,0:T(8,128)(2,1)S(1)} %copy-done.2, bf16[384,2048]{1,0:T(8,128)(2,1)S(1)} %copy-done.1, ...), custom_call_target="tpu_custom_call", output_to_operand_aliasing={{1}: (4, {})} | custom-call | flops 1000 | bytes 1000 | tf_op jit(solution)/shard_map/probs_part/pallas_call | solution.py:53
  23.5 1.9 %collective-permute-done.4.refs_1_ = bf16[256,256]{1,0:T(8,128)(2,1)S(1)} collective-permute-done((bf16[256,256]{1,0:T(8,128)(2,1)S(1)}, bf16[256,256]{1,0:T(8,128)(2,1)S(1)}, u32[]{:S(2)}, u32[]{:S(2)}) %collective-permute-start.4) | collective-permute-done | bytes 131104 | tf_op jit(solution)/shard_map/ppermute | solution.py:346
  25.5 2.8 %collective-permute-start.5 = (bf16[512,128]{1,0:T(8,128)(2,1)S(1)}, bf16[512,128]{1,0:T(8,128)(2,1)S(1)}, u32[]{:S(2)}, u32[]{:S(2)}) collective-permute-start(bf16[512,128]{1,0:T(8,128)(2,1)S(1)} %get-tuple-element.54.refs_5_.refs_2_), channel_id=1, source_target_pairs={{0,4},{2,6},{4,0},{6,2},{8,12},{10,14},{12,8},{14,10},{16,20},{18,... | collective-permute-start | bytes 393224 | tf_op jit(solution)/shard_map/ppermute | solution.py:346
  28.3 2.7 %collective-permute-start.8 = (bf16[512,128]{1,0:T(8,128)(2,1)S(1)}, bf16[512,128]{1,0:T(8,128)(2,1)S(1)}, u32[]{:S(2)}, u32[]{:S(2)}) collective-permute-start(bf16[512,128]{1,0:T(8,128)(2,1)S(1)} %get-tuple-element.56.refs_4_), channel_id=1, source_target_pairs={{0,24},{2,26},{4,28},{6,30},{8,0},{10,2},{12,4},{14,6},{16,8},{18,... | collective-permute-start | bytes 393224 | tf_op jit(solution)/shard_map/ppermute | solution.py:346
  31.1 0.3 collective-permute-start.7
  31.4 0.7 collective-permute-start.6
  32.1 2.2 %probs_part.7 = (bf16[4,384,384]{2,1,0:T(8,128)(2,1)S(1)}, f32[384,512]{1,0:T(8,128)S(1)}) custom-call(s32[8]{0:T(128)S(1)} %concatenate.11.refs_2_.refs_0_, bf16[384,2048]{1,0:T(8,128)(2,1)S(1)} %copy-done, bf16[384,512]{1,0:T(8,128)(2,1)S(1)} %copy-done.2, bf16[384,2048]{1,0:T(8,128)(2,1)S(1)} %copy-done.1, ...), custom_call_target="tpu_custom_call", output_to_operand_aliasing={{1}: (4, {})} | custom-call | flops 1000 | bytes 1000 | tf_op jit(solution)/shard_map/probs_part/pallas_call | solution.py:53
  34.3 2.2 %collective-permute-done.7.refs_6_ = bf16[512,128]{1,0:T(8,128)(2,1)S(1)} collective-permute-done((bf16[512,128]{1,0:T(8,128)(2,1)S(1)}, bf16[512,128]{1,0:T(8,128)(2,1)S(1)}, u32[]{:S(2)}, u32[]{:S(2)}) %collective-permute-start.7) | collective-permute-done | bytes 131104 | tf_op jit(solution)/shard_map/ppermute | solution.py:346
  36.5 1.3 %collective-permute-done.6.refs_5_ = bf16[512,128]{1,0:T(8,128)(2,1)S(1)} collective-permute-done((bf16[512,128]{1,0:T(8,128)(2,1)S(1)}, bf16[512,128]{1,0:T(8,128)(2,1)S(1)}, u32[]{:S(2)}, u32[]{:S(2)}) %collective-permute-start.6) | collective-permute-done | bytes 131104 | tf_op jit(solution)/shard_map/ppermute | solution.py:346
  37.8 0.6 join.9
  38.7 0.6 collective-permute-start.12
  39.7 0.5 collective-permute-start.10
  40.2 4.3 %collective-permute-start.9 = (bf16[384,256]{1,0:T(8,128)(2,1)S(1)}, bf16[384,256]{1,0:T(8,128)(2,1)S(1)}, u32[]{:S(2)}, u32[]{:S(2)}) collective-permute-start(bf16[384,256]{1,0:T(8,128)(2,1)S(1)} %get-tuple-element.57), channel_id=1, source_target_pairs={{0,2},{2,0},{4,6},{6,4},{8,10},{10,8},{12,14},{14,12},{16,18},{18,... | collective-permute-start | bytes 589832 | tf_op jit(solution)/shard_map/ppermute | solution.py:346
  44.6 1.1 %collective-permute-done.9.refs_4_ = bf16[384,256]{1,0:T(8,128)(2,1)S(1)} collective-permute-done((bf16[384,256]{1,0:T(8,128)(2,1)S(1)}, bf16[384,256]{1,0:T(8,128)(2,1)S(1)}, u32[]{:S(2)}, u32[]{:S(2)}) %collective-permute-start.9) | collective-permute-done | bytes 196640 | tf_op jit(solution)/shard_map/ppermute | solution.py:346
  45.6 0.5 collective-permute-done.11.refs_8_
  46.2 6.8 %collective-permute-done.10.refs_7_ = bf16[1024,128]{1,0:T(8,128)(2,1)S(1)} collective-permute-done((bf16[1024,128]{1,0:T(8,128)(2,1)S(1)}, bf16[1024,128]{1,0:T(8,128)(2,1)S(1)}, u32[]{:S(2)}, u32[]{:S(2)}) %collective-permute-start.10) | collective-permute-done | bytes 262176 | tf_op jit(solution)/shard_map/ppermute | solution.py:346
  53.0 2.9 %raw_part.1 = (bf16[384,256]{1,0:T(8,128)(2,1)S(1)}, bf16[384,256]{1,0:T(8,128)(2,1)S(1)}, f32[1,256]{1,0:T(1,128)S(1)}, bf16[2048,256]{1,0:T(8,128)(2,1)S(1)}, ...) custom-call(s32[8]{0:T(128)S(1)} %concatenate.11.refs_2_.refs_0_, ...), custom_call_target="tpu_custom_call" | custom-call | flops 1000 | bytes 1000 | tf_op jit(solution)/shard_map/raw_part/pallas_call | solution.py:53
  56.0 2.3 %collective-permute-start.16 = (bf16[2048,256]{1,0:T(8,128)(2,1)S(1)}, bf16[2048,256]{1,0:T(8,128)(2,1)S(1)}, u32[]{:S(2)}, u32[]{:S(2)}) collective-permute-start(bf16[2048,256]{1,0:T(8,128)(2,1)S(1)} %get-tuple-element.64.refs_6_), channel_id=1, source_target_pairs={{0,2},{2,0},{4,6},{6,4},{8,10},{10,8},{12,14},{14,12},{16,18},{18,... | collective-permute-start | bytes 3145736 | tf_op jit(solution)/shard_map/ppermute | solution.py:346
  58.2 1.2 %collective-permute-start.20 = (bf16[1408,256]{1,0:T(8,128)(2,1)S(1)}, bf16[1408,256]{1,0:T(8,128)(2,1)S(1)}, u32[]{:S(2)}, u32[]{:S(2)}) collective-permute-start(bf16[1408,256]{1,0:T(8,128)(2,1)S(1)} %get-tuple-element.74), channel_id=1, source_target_pairs={{0,1},{1,0},{2,3},{3,2},{4,5},{5,4},{6,7},{7,6},{8,9},{9,8},{10,11... | collective-permute-start | bytes 2162696 | tf_op jit(solution)/shard_map/ppermute | solution.py:396
  59.4 1.8 %collective-permute-start.21 = (bf16[1408,256]{1,0:T(8,128)(2,1)S(1)}, bf16[1408,256]{1,0:T(8,128)(2,1)S(1)}, u32[]{:S(2)}, u32[]{:S(2)}) collective-permute-start(bf16[1408,256]{1,0:T(8,128)(2,1)S(1)} %get-tuple-element.75), channel_id=1, source_target_pairs={{0,5},{1,4},{2,7},{3,6},{4,1},{5,0},{6,3},{7,2},{8,13},{9,12},{10,... | collective-permute-start | bytes 2162696 | tf_op jit(solution)/shard_map/ppermute | solution.py:397
  61.2 0.6 collective-permute-start.14
  61.9 2.7 %collective-permute-done.15.refs_1_ = f32[1,256]{1,0:T(1,128)S(1)} collective-permute-done((f32[1,256]{1,0:T(1,128)S(1)}, f32[1,256]{1,0:T(1,128)S(1)}, u32[]{:S(2)}, u32[]{:S(2)}) %collective-permute-start.15) | collective-permute-done | bytes 1056 | tf_op jit(solution)/shard_map/ppermute | solution.py:346
  64.6 0.4 collective-permute-start.17
  65.0 2.6 %grads_part.4 = (bf16[384,2048]{1,0:T(8,128)(2,1)}, bf16[384,512]{1,0:T(8,128)(2,1)}, f32[8,128]{1,0:T(8,128)S(1)}) custom-call(s32[8]{0:T(128)S(1)} %concatenate.11.refs_2_.refs_0_, bf16[384,2048]{1,0:T(8,128)(2,1)S(1)} %copy-done, bf16[384,512]{1,0:T(8,128)(2,1)S(1)} %copy-done.2, bf16[384,2048]{1,0:T(8,128)(2,1)S(1)} %copy-done.1, ...), custom_call_target="tpu_custom_call" | custom-call | flops 1000 | bytes 1000 | tf_op jit(solution)/shard_map/grads_part/pallas_call | solution.py:53
  67.6 1.0 %collective-permute-done.17.refs_1_ = f32[1,256]{1,0:T(1,128)S(1)} collective-permute-done((f32[1,256]{1,0:T(1,128)S(1)}, f32[1,256]{1,0:T(1,128)S(1)}, u32[]{:S(2)}, u32[]{:S(2)}) %collective-permute-start.17) | collective-permute-done | bytes 1056 | tf_op jit(solution)/shard_map/ppermute | solution.py:346
  68.6 1.5 %collective-permute-start.18 = (f32[1,256]{1,0:T(1,128)S(1)}, f32[1,256]{1,0:T(1,128)S(1)}, u32[]{:S(2)}, u32[]{:S(2)}) collective-permute-start(f32[1,256]{1,0:T(1,128)S(1)} %add.25.refs_9_.refs_0_), channel_id=1, source_target_pairs={{0,32},{2,34},{4,36},{6,38},{8,40},{10,42},{12,44},{14,46},{16,48}... | collective-permute-start | bytes 3080 | tf_op jit(solution)/shard_map/ppermute | solution.py:346
  70.1 2.6 %grads_part.5 = (bf16[384,2048]{1,0:T(8,128)(2,1)}, bf16[384,512]{1,0:T(8,128)(2,1)}, f32[8,128]{1,0:T(8,128)S(1)}) custom-call(s32[8]{0:T(128)S(1)} %concatenate.11.refs_2_.refs_0_, bf16[384,2048]{1,0:T(8,128)(2,1)S(1)} %copy-done, bf16[384,512]{1,0:T(8,128)(2,1)S(1)} %copy-done.2, ...), custom_call_target="tpu_custom_call", output_to_operand_aliasing={{0}: (7, {}), {1}: (8, {})} | custom-call | flops 1000 | bytes 1000 | tf_op jit(solution)/shard_map/grads_part/pallas_call | solution.py:53
  72.8 0.6 collective-permute-start.19
  73.3 2.6 %grads_part.6 = (bf16[384,2048]{1,0:T(8,128)(2,1)}, bf16[384,512]{1,0:T(8,128)(2,1)}, f32[8,128]{1,0:T(8,128)S(1)}) custom-call(s32[8]{0:T(128)S(1)} %concatenate.11.refs_2_.refs_0_, bf16[384,2048]{1,0:T(8,128)(2,1)S(1)} %copy-done, bf16[384,512]{1,0:T(8,128)(2,1)S(1)} %copy-done.2, ...), custom_call_target="tpu_custom_call", output_to_operand_aliasing={{0}: (7, {}), {1}: (8, {})} | custom-call | flops 1000 | bytes 1000 | tf_op jit(solution)/shard_map/grads_part/pallas_call | solution.py:53
  75.9 2.1 %collective-permute-done.21.refs_4_ = bf16[1408,256]{1,0:T(8,128)(2,1)S(1)} collective-permute-done((bf16[1408,256]{1,0:T(8,128)(2,1)S(1)}, bf16[1408,256]{1,0:T(8,128)(2,1)S(1)}, u32[]{:S(2)}, u32[]{:S(2)}) %collective-permute-start.21) | collective-permute-done | bytes 720928 | tf_op jit(solution)/shard_map/ppermute | solution.py:397
  78.0 1.6 %collective-permute-start.23 = (bf16[1408,256]{1,0:T(8,128)(2,1)S(1)}, bf16[1408,256]{1,0:T(8,128)(2,1)S(1)}, u32[]{:S(2)}, u32[]{:S(2)}) collective-permute-start(bf16[1408,256]{1,0:T(8,128)(2,1)S(1)} %get-tuple-element.79.refs_3_.refs_4_), channel_id=1, source_target_pairs={{0,2},{2,0},{4,6},{6,4},{8,10},{10,8},{12,14},{14,12},{16,18},{18,... | collective-permute-start | bytes 2162696 | tf_op jit(solution)/shard_map/ppermute | solution.py:346
  79.7 3.7 %collective-permute-start.24 = (f32[1,256]{1,0:T(1,128)S(1)}, f32[1,256]{1,0:T(1,128)S(1)}, u32[]{:S(2)}, u32[]{:S(2)}) collective-permute-start(f32[1,256]{1,0:T(1,128)S(1)} %get-tuple-element.76.refs_9_.refs_0_), channel_id=1, source_target_pairs={{0,128},{2,130},{4,132},{6,134},{8,136},{10,138},{12,140},{14,142}... | collective-permute-start | bytes 3080 | tf_op jit(solution)/shard_map/ppermute | solution.py:346
  83.4 2.6 %grads_part.7 = (bf16[384,2048]{1,0:T(8,128)(2,1)}, bf16[384,512]{1,0:T(8,128)(2,1)}, f32[8,128]{1,0:T(8,128)S(1)}) custom-call(s32[8]{0:T(128)S(1)} %concatenate.11.refs_2_.refs_0_, bf16[384,2048]{1,0:T(8,128)(2,1)S(1)} %copy-done, bf16[384,512]{1,0:T(8,128)(2,1)S(1)} %copy-done.2, ...), custom_call_target="tpu_custom_call", output_to_operand_aliasing={{0}: (7, {}), {1}: (8, {})} | custom-call | flops 1000 | bytes 1000 | tf_op jit(solution)/shard_map/grads_part/pallas_call | solution.py:53
  86.0 2.1 %hidden_part.2 = (bf16[384,2048]{1,0:T(8,128)(2,1)}, f32[8,128]{1,0:T(8,128)S(1)}) custom-call(s32[8]{0:T(128)S(1)} %concatenate.11.refs_2_.refs_0_, f32[384,512]{1,0:T(8,128)S(1)} %get-tuple-element.55.refs_1_.refs_3_, f32[1,512]{1,0:T(1,128)S(1)} %bitcast.11, bf16[1408,256]{1,0:T(8,128)(2,1)S(1)} %get-tuple-element.79.refs_3_.refs_4_, ...), custom_call_target="tpu_custom_call" | custom-call | flops 1000 | bytes 1000 | tf_op jit(solution)/shard_map/hidden_part/pallas_call | solution.py:53
  88.2 1.3 %collective-permute-start.25 = (f32[1,256]{1,0:T(1,128)S(1)}, f32[1,256]{1,0:T(1,128)S(1)}, u32[]{:S(2)}, u32[]{:S(2)}) collective-permute-start(f32[1,256]{1,0:T(1,128)S(1)} %add.28.refs_9_.refs_0_), channel_id=1, source_target_pairs={{0,4},{2,6},{4,0},{6,2},{8,12},{10,14},{12,8},{14,10},{16,20},{18,... | collective-permute-start | bytes 3080 | tf_op jit(solution)/shard_map/ppermute | solution.py:346
  89.5 2.9 %hidden_part.3 = (bf16[384,2048]{1,0:T(8,128)(2,1)}, f32[8,128]{1,0:T(8,128)S(1)}) custom-call(s32[8]{0:T(128)S(1)} %concatenate.11.refs_2_.refs_0_, f32[384,512]{1,0:T(8,128)S(1)} %get-tuple-element.55.refs_1_.refs_3_, f32[1,512]{1,0:T(1,128)S(1)} %bitcast.12, ...), custom_call_target="tpu_custom_call", output_to_operand_aliasing={{0}: (8, {})} | custom-call | flops 1000 | bytes 1000 | tf_op jit(solution)/shard_map/hidden_part/pallas_call | solution.py:53
  92.5 1.6 %collective-permute-start.26 = (f32[1,256]{1,0:T(1,128)S(1)}, f32[1,256]{1,0:T(1,128)S(1)}, u32[]{:S(2)}, u32[]{:S(2)}) collective-permute-start(f32[1,256]{1,0:T(1,128)S(1)} %add.29), channel_id=1, source_target_pairs={{0,2},{2,0},{4,6},{6,4},{8,10},{10,8},{12,14},{14,12},{16,18},{18,... | collective-permute-start | bytes 3080 | tf_op jit(solution)/shard_map/ppermute | solution.py:346
  94.1 0.8 collective-permute-done.26
  94.9 0.6 maximum_multiply_fusion
  (40 shorter events, 1.4 us)
Async XLA Ops:
  0.6 4.4 %collective-permute-start = (bf16[32,512]{1,0:T(8,128)(2,1)}, bf16[32,512]{1,0:T(8,128)(2,1)S(1)}, u32[]{:S(2)}, u32[]{:S(2)}) collective-permute-start(bf16[32,512]{1,0:T(8,128)(2,1)} %refs_0_.1), channel_id=1, source_target_pairs={{0,2},{2,0},{4,6},{6,4},{8,10},{10,8},{12,14},{14,12},{16,18},{18,... | collective-permute-start | bytes 98312 | tf_op jit(solution)/shard_map/ppermute | solution.py:346
  5.8 8.7 %collective-permute-start.1 = (bf16[64,256]{1,0:T(8,128)(2,1)S(1)}, bf16[64,256]{1,0:T(8,128)(2,1)S(1)}, u32[]{:S(2)}, u32[]{:S(2)}) collective-permute-start(bf16[64,256]{1,0:T(8,128)(2,1)S(1)} %join.5.refs_5_.refs_0_), channel_id=1, source_target_pairs={{0,128},{2,130},{4,132},{6,134},{8,136},{10,138},{12,140},{14,142}... | collective-permute-start | bytes 98312 | tf_op jit(solution)/shard_map/ppermute | solution.py:346
  14.5 2.0 %copy-start = (bf16[384,2048]{1,0:T(8,128)(2,1)S(1)}, bf16[384,2048]{1,0:T(8,128)(2,1)}, u32[]{:S(2)}) copy-start(bf16[384,2048]{1,0:T(8,128)(2,1)} %refs_1_.15) | copy-start | bytes 4718596
  14.5 2.0 %copy-start.1 = (bf16[384,2048]{1,0:T(8,128)(2,1)S(1)}, bf16[384,2048]{1,0:T(8,128)(2,1)}, u32[]{:S(2)}) copy-start(bf16[384,2048]{1,0:T(8,128)(2,1)} %refs_3_.15) | copy-start | bytes 4718596
  14.5 2.0 %copy-start.2 = (bf16[384,512]{1,0:T(8,128)(2,1)S(1)}, bf16[384,512]{1,0:T(8,128)(2,1)}, u32[]{:S(2)}) copy-start(bf16[384,512]{1,0:T(8,128)(2,1)} %refs_2_.15) | copy-start | bytes 1179652
  14.5 10.9 %collective-permute-start.2 = (bf16[384,4096]{1,0:T(8,128)(2,1)S(1)}, bf16[384,4096]{1,0:T(8,128)(2,1)S(1)}, u32[]{:S(2)}, u32[]{:S(2)}) collective-permute-start(bf16[384,4096]{1,0:T(8,128)(2,1)S(1)} %get-tuple-element.47.refs_1_), channel_id=1, source_target_pairs={{0,2},{2,0},{4,6},{6,4},{8,10},{10,8},{12,14},{14,12},{16,18},{18,... | collective-permute-start | bytes 9437192 | tf_op jit(solution)/shard_map/ppermute | solution.py:346
  15.2 6.0 %collective-permute-start.3 = (bf16[128,256]{1,0:T(8,128)(2,1)S(1)}, bf16[128,256]{1,0:T(8,128)(2,1)S(1)}, u32[]{:S(2)}, u32[]{:S(2)}) collective-permute-start(bf16[128,256]{1,0:T(8,128)(2,1)S(1)} %get-tuple-element.49.refs_5_.refs_0_), channel_id=1, source_target_pairs={{0,64},{2,66},{4,68},{6,70},{8,72},{10,74},{12,76},{14,78},{16,80}... | collective-permute-start | bytes 196616 | tf_op jit(solution)/shard_map/ppermute | solution.py:346
  21.2 4.2 %collective-permute-start.4 = (bf16[256,256]{1,0:T(8,128)(2,1)S(1)}, bf16[256,256]{1,0:T(8,128)(2,1)S(1)}, u32[]{:S(2)}, u32[]{:S(2)}) collective-permute-start(bf16[256,256]{1,0:T(8,128)(2,1)S(1)} %join.7.refs_5_.refs_0_), channel_id=1, source_target_pairs={{0,32},{2,34},{4,36},{6,38},{8,40},{10,42},{12,44},{14,46},{16,48}... | collective-permute-start | bytes 393224 | tf_op jit(solution)/shard_map/ppermute | solution.py:346
  25.5 8.8 %collective-permute-start.5 = (bf16[512,128]{1,0:T(8,128)(2,1)S(1)}, bf16[512,128]{1,0:T(8,128)(2,1)S(1)}, u32[]{:S(2)}, u32[]{:S(2)}) collective-permute-start(bf16[512,128]{1,0:T(8,128)(2,1)S(1)} %get-tuple-element.54.refs_5_.refs_2_), channel_id=1, source_target_pairs={{0,4},{2,6},{4,0},{6,2},{8,12},{10,14},{12,8},{14,10},{16,20},{18,... | collective-permute-start | bytes 393224 | tf_op jit(solution)/shard_map/ppermute | solution.py:346
  28.3 6.0 %collective-permute-start.8 = (bf16[512,128]{1,0:T(8,128)(2,1)S(1)}, bf16[512,128]{1,0:T(8,128)(2,1)S(1)}, u32[]{:S(2)}, u32[]{:S(2)}) collective-permute-start(bf16[512,128]{1,0:T(8,128)(2,1)S(1)} %get-tuple-element.56.refs_4_), channel_id=1, source_target_pairs={{0,24},{2,26},{4,28},{6,30},{8,0},{10,2},{12,4},{14,6},{16,8},{18,... | collective-permute-start | bytes 393224 | tf_op jit(solution)/shard_map/ppermute | solution.py:346
  31.1 5.4 %collective-permute-start.7 = (bf16[512,128]{1,0:T(8,128)(2,1)S(1)}, bf16[512,128]{1,0:T(8,128)(2,1)S(1)}, u32[]{:S(2)}, u32[]{:S(2)}) collective-permute-start(bf16[512,128]{1,0:T(8,128)(2,1)S(1)} %get-tuple-element.56.refs_4_), channel_id=1, source_target_pairs={{0,16},{2,18},{4,20},{6,22},{8,24},{10,26},{12,28},{14,30},{16,0},... | collective-permute-start | bytes 393224 | tf_op jit(solution)/shard_map/ppermute | solution.py:346
  31.4 6.4 %collective-permute-start.6 = (bf16[512,128]{1,0:T(8,128)(2,1)S(1)}, bf16[512,128]{1,0:T(8,128)(2,1)S(1)}, u32[]{:S(2)}, u32[]{:S(2)}) collective-permute-start(bf16[512,128]{1,0:T(8,128)(2,1)S(1)} %get-tuple-element.56.refs_4_), channel_id=1, source_target_pairs={{0,8},{2,10},{4,12},{6,14},{8,16},{10,18},{12,20},{14,22},{16,24},... | collective-permute-start | bytes 393224 | tf_op jit(solution)/shard_map/ppermute | solution.py:346
  34.3 18.7 %copy-start.3 = (f32[512]{0:T(512)S(1)}, f32[512]{0:T(512)}, u32[]{:S(2)}) copy-start(f32[512]{0:T(512)} %param.11) | copy-start | bytes 6148
  38.4 14.6 %collective-permute-start.13 = (bf16[2048,128]{1,0:T(8,128)(2,1)S(1)}, bf16[2048,128]{1,0:T(8,128)(2,1)S(1)}, u32[]{:S(2)}, u32[]{:S(2)}) collective-permute-start(bf16[2048,128]{1,0:T(8,128)(2,1)S(1)} %get-tuple-element.59.refs_10_), channel_id=1, source_target_pairs={{0,4},{2,6},{4,0},{6,2},{8,12},{10,14},{12,8},{14,10},{16,20},{18,... | collective-permute-start | bytes 1572872 | tf_op jit(solution)/shard_map/ppermute | solution.py:346
  38.7 6.9 %collective-permute-start.12 = (bf16[1024,128]{1,0:T(8,128)(2,1)S(1)}, bf16[1024,128]{1,0:T(8,128)(2,1)S(1)}, u32[]{:S(2)}, u32[]{:S(2)}) collective-permute-start(bf16[1024,128]{1,0:T(8,128)(2,1)S(1)} %get-tuple-element.58.refs_6_), channel_id=1, source_target_pairs={{0,24},{2,26},{4,28},{6,30},{8,0},{10,2},{12,4},{14,6},{16,8},{18,... | collective-permute-start | bytes 786440 | tf_op jit(solution)/shard_map/ppermute | solution.py:346
  39.4 6.8 %collective-permute-start.11 = (bf16[1024,128]{1,0:T(8,128)(2,1)S(1)}, bf16[1024,128]{1,0:T(8,128)(2,1)S(1)}, u32[]{:S(2)}, u32[]{:S(2)}) collective-permute-start(bf16[1024,128]{1,0:T(8,128)(2,1)S(1)} %get-tuple-element.58.refs_6_), channel_id=1, source_target_pairs={{0,16},{2,18},{4,20},{6,22},{8,24},{10,26},{12,28},{14,30},{16,0},... | collective-permute-start | bytes 786440 | tf_op jit(solution)/shard_map/ppermute | solution.py:346
  39.7 13.3 %collective-permute-start.10 = (bf16[1024,128]{1,0:T(8,128)(2,1)S(1)}, bf16[1024,128]{1,0:T(8,128)(2,1)S(1)}, u32[]{:S(2)}, u32[]{:S(2)}) collective-permute-start(bf16[1024,128]{1,0:T(8,128)(2,1)S(1)} %get-tuple-element.58.refs_6_), channel_id=1, source_target_pairs={{0,8},{2,10},{4,12},{6,14},{8,16},{10,18},{12,20},{14,22},{16,24},... | collective-permute-start | bytes 786440 | tf_op jit(solution)/shard_map/ppermute | solution.py:346
  40.2 5.4 %collective-permute-start.9 = (bf16[384,256]{1,0:T(8,128)(2,1)S(1)}, bf16[384,256]{1,0:T(8,128)(2,1)S(1)}, u32[]{:S(2)}, u32[]{:S(2)}) collective-permute-start(bf16[384,256]{1,0:T(8,128)(2,1)S(1)} %get-tuple-element.57), channel_id=1, source_target_pairs={{0,2},{2,0},{4,6},{6,4},{8,10},{10,8},{12,14},{14,12},{16,18},{18,... | collective-permute-start | bytes 589832 | tf_op jit(solution)/shard_map/ppermute | solution.py:346
  56.0 8.6 %collective-permute-start.16 = (bf16[2048,256]{1,0:T(8,128)(2,1)S(1)}, bf16[2048,256]{1,0:T(8,128)(2,1)S(1)}, u32[]{:S(2)}, u32[]{:S(2)}) collective-permute-start(bf16[2048,256]{1,0:T(8,128)(2,1)S(1)} %get-tuple-element.64.refs_6_), channel_id=1, source_target_pairs={{0,2},{2,0},{4,6},{6,4},{8,10},{10,8},{12,14},{14,12},{16,18},{18,... | collective-permute-start | bytes 3145736 | tf_op jit(solution)/shard_map/ppermute | solution.py:346
  58.2 17.7 %collective-permute-start.20 = (bf16[1408,256]{1,0:T(8,128)(2,1)S(1)}, bf16[1408,256]{1,0:T(8,128)(2,1)S(1)}, u32[]{:S(2)}, u32[]{:S(2)}) collective-permute-start(bf16[1408,256]{1,0:T(8,128)(2,1)S(1)} %get-tuple-element.74), channel_id=1, source_target_pairs={{0,1},{1,0},{2,3},{3,2},{4,5},{5,4},{6,7},{7,6},{8,9},{9,8},{10,11... | collective-permute-start | bytes 2162696 | tf_op jit(solution)/shard_map/ppermute | solution.py:396
  59.4 18.6 %collective-permute-start.21 = (bf16[1408,256]{1,0:T(8,128)(2,1)S(1)}, bf16[1408,256]{1,0:T(8,128)(2,1)S(1)}, u32[]{:S(2)}, u32[]{:S(2)}) collective-permute-start(bf16[1408,256]{1,0:T(8,128)(2,1)S(1)} %get-tuple-element.75), channel_id=1, source_target_pairs={{0,5},{1,4},{2,7},{3,6},{4,1},{5,0},{6,3},{7,2},{8,13},{9,12},{10,... | collective-permute-start | bytes 2162696 | tf_op jit(solution)/shard_map/ppermute | solution.py:397
  61.2 3.4 %collective-permute-start.14 = (bf16[384,256]{1,0:T(8,128)(2,1)S(1)}, bf16[384,256]{1,0:T(8,128)(2,1)S(1)}, u32[]{:S(2)}, u32[]{:S(2)}) collective-permute-start(bf16[384,256]{1,0:T(8,128)(2,1)S(1)} %get-tuple-element.61), channel_id=1, source_target_pairs={{0,2},{2,0},{4,6},{6,4},{8,10},{10,8},{12,14},{14,12},{16,18},{18,... | collective-permute-start | bytes 589832 | tf_op jit(solution)/shard_map/ppermute | solution.py:346
  61.9 2.7 %collective-permute-start.15 = (f32[1,256]{1,0:T(1,128)S(1)}, f32[1,256]{1,0:T(1,128)S(1)}, u32[]{:S(2)}, u32[]{:S(2)}) collective-permute-start(f32[1,256]{1,0:T(1,128)S(1)} %get-tuple-element.63.refs_0_), channel_id=1, source_target_pairs={{0,8},{2,10},{4,12},{6,14},{8,0},{10,2},{12,4},{14,6},{16,24},{18,... | collective-permute-start | bytes 3080 | tf_op jit(solution)/shard_map/ppermute | solution.py:346
  64.6 4.0 %collective-permute-start.17 = (f32[1,256]{1,0:T(1,128)S(1)}, f32[1,256]{1,0:T(1,128)S(1)}, u32[]{:S(2)}, u32[]{:S(2)}) collective-permute-start(f32[1,256]{1,0:T(1,128)S(1)} %add.24.refs_7_.refs_0_), channel_id=1, source_target_pairs={{0,16},{2,18},{4,20},{6,22},{8,24},{10,26},{12,28},{14,30},{16,0},... | collective-permute-start | bytes 3080 | tf_op jit(solution)/shard_map/ppermute | solution.py:346
  68.6 4.1 %collective-permute-start.18 = (f32[1,256]{1,0:T(1,128)S(1)}, f32[1,256]{1,0:T(1,128)S(1)}, u32[]{:S(2)}, u32[]{:S(2)}) collective-permute-start(f32[1,256]{1,0:T(1,128)S(1)} %add.25.refs_9_.refs_0_), channel_id=1, source_target_pairs={{0,32},{2,34},{4,36},{6,38},{8,40},{10,42},{12,44},{14,46},{16,48}... | collective-permute-start | bytes 3080 | tf_op jit(solution)/shard_map/ppermute | solution.py:346
  72.8 5.2 %collective-permute-start.19 = (f32[1,256]{1,0:T(1,128)S(1)}, f32[1,256]{1,0:T(1,128)S(1)}, u32[]{:S(2)}, u32[]{:S(2)}) collective-permute-start(f32[1,256]{1,0:T(1,128)S(1)} %add.26.refs_9_.refs_0_), channel_id=1, source_target_pairs={{0,64},{2,66},{4,68},{6,70},{8,72},{10,74},{12,76},{14,78},{16,80}... | collective-permute-start | bytes 3080 | tf_op jit(solution)/shard_map/ppermute | solution.py:346
  78.0 8.1 %collective-permute-start.23 = (bf16[1408,256]{1,0:T(8,128)(2,1)S(1)}, bf16[1408,256]{1,0:T(8,128)(2,1)S(1)}, u32[]{:S(2)}, u32[]{:S(2)}) collective-permute-start(bf16[1408,256]{1,0:T(8,128)(2,1)S(1)} %get-tuple-element.79.refs_3_.refs_4_), channel_id=1, source_target_pairs={{0,2},{2,0},{4,6},{6,4},{8,10},{10,8},{12,14},{14,12},{16,18},{18,... | collective-permute-start | bytes 2162696 | tf_op jit(solution)/shard_map/ppermute | solution.py:346
  79.6 9.9 %collective-permute-start.22 = (bf16[1408,256]{1,0:T(8,128)(2,1)S(1)}, bf16[1408,256]{1,0:T(8,128)(2,1)S(1)}, u32[]{:S(2)}, u32[]{:S(2)}) collective-permute-start(bf16[1408,256]{1,0:T(8,128)(2,1)S(1)} %get-tuple-element.80.refs_4_), channel_id=1, source_target_pairs={{0,2},{2,0},{4,6},{6,4},{8,10},{10,8},{12,14},{14,12},{16,18},{18,... | collective-permute-start | bytes 2162696 | tf_op jit(solution)/shard_map/ppermute | solution.py:346
  79.7 8.5 %collective-permute-start.24 = (f32[1,256]{1,0:T(1,128)S(1)}, f32[1,256]{1,0:T(1,128)S(1)}, u32[]{:S(2)}, u32[]{:S(2)}) collective-permute-start(f32[1,256]{1,0:T(1,128)S(1)} %get-tuple-element.76.refs_9_.refs_0_), channel_id=1, source_target_pairs={{0,128},{2,130},{4,132},{6,134},{8,136},{10,138},{12,140},{14,142}... | collective-permute-start | bytes 3080 | tf_op jit(solution)/shard_map/ppermute | solution.py:346
  88.2 4.2 %collective-permute-start.25 = (f32[1,256]{1,0:T(1,128)S(1)}, f32[1,256]{1,0:T(1,128)S(1)}, u32[]{:S(2)}, u32[]{:S(2)}) collective-permute-start(f32[1,256]{1,0:T(1,128)S(1)} %add.28.refs_9_.refs_0_), channel_id=1, source_target_pairs={{0,4},{2,6},{4,0},{6,2},{8,12},{10,14},{12,8},{14,10},{16,20},{18,... | collective-permute-start | bytes 3080 | tf_op jit(solution)/shard_map/ppermute | solution.py:346
  92.5 2.4 %collective-permute-start.26 = (f32[1,256]{1,0:T(1,128)S(1)}, f32[1,256]{1,0:T(1,128)S(1)}, u32[]{:S(2)}, u32[]{:S(2)}) collective-permute-start(f32[1,256]{1,0:T(1,128)S(1)} %add.29), channel_id=1, source_target_pairs={{0,2},{2,0},{4,6},{6,4},{8,10},{10,8},{12,14},{14,12},{16,18},{18,... | collective-permute-start | bytes 3080 | tf_op jit(solution)/shard_map/ppermute | solution.py:346

commit v13 on v12

--- a/solution.py
+++ b/solution.py
@@ -237,7 +237,7 @@
                 place(pieces[4 + xi], (k * 8 + i) * CHIP, i, k, xi, HEAD)
 
 
-NEAR = 640
+NEAR = 512
 BESIDES = DEPTH // 2 - NEAR
 
 
@@ -400,7 +400,7 @@
         elif step < 5:
             g = step - 1
             if step == 4:
-                near_far, beside_far = send(near, C_SWAP), send(beside, C_SWAP)
+                near_far = send(near, C_SWAP)
             *held, token = grads_part(g, at, queries, keys, upstream, mine, values_far, probs[g], held, (sums,))
             if step == 4:
                 grad_hidden, token = hidden_part(
@@ -408,13 +408,16 @@
                 )
             after = (token,)
         else:
+            beside_far = send(beside, C_SWAP)
             grad_hidden, token = hidden_part(
                 False, (at, dv, scale, near, beside, beside_far, kept, kept_far), grad_hidden, (sums,)
             )
             after = (token,)
         ins = [(VMEM, sums), (VMEM, got)]
         if step == 3:
-            sums, near, beside = call(add_kernel, "add", shape(1, HALF, dtype=F32), ins, after, (near, beside))
+            sums, near = call(add_kernel, "add", shape(1, HALF, dtype=F32), ins, after, (near,))
+        elif step == 4:
+            sums, beside = call(add_kernel, "add", shape(1, HALF, dtype=F32), ins, after, (beside,))
         else:
             sums = call(add_kernel, "add", shape(1, HALF, dtype=F32), ins, after)
     far = send(sums, C_SWAP)

time: 95.6 us -> 94.9 us (level)
    ppermute x25, waiting for transfers between devices: 21.3 us -> 23.4 us  [send(): return lax.ppermute(x, 'dp', perm)]
    ppermute x1, waiting for transfers between devices: 2.05 us -> 0.01 us  [shards(): beside = lax.ppermute(beside, ('dp', 'seq'), BESIDE)]
  transfers between devices with their start and end apart: 27 -> 27, of which waited for: 12 -> 13; matrix products, arithmetic and copies ran while one was open for 1% -> 1% of each run, Pallas kernels for 27% -> 27%
where the time goes in v13:
time: 94.9 us; the launch traced here: 94.8 us
  starting transfers between devices  39.5 us (42%)
  Pallas kernels  29.7 us (31%)
  waiting for transfers between devices  23.4 us (25%)
    ppermute x25, starting transfers between devices, send(): return lax.ppermute(x, 'dp', perm)  36.5 us
    pallas_call x22, Pallas kernels, call(): pl.pallas_call(run, in_specs=list(specs) + [ANY] * (len(after) + len(thro...  29.7 us
    ppermute x25, waiting for transfers between devices, send(): return lax.ppermute(x, 'dp', perm)  23.4 us
  transfers between devices with their start and end apart: 27, of which 13 were waited for; matrix products, arithmetic and copies ran while one was open for 1% of the time, Pallas kernels for 27%

profile of v13, /device:TPU:1, one launch (start us, length us, event | category | flops | bytes accessed | tf_op | source)
XLA Modules:
  0.0 94.8 jit_solution(1686796984221808969)
XLA Ops:
  0.6 3.3 %collective-permute-start = (bf16[32,512]{1,0:T(8,128)(2,1)}, bf16[32,512]{1,0:T(8,128)(2,1)S(1)}, u32[]{:S(2)}, u32[]{:S(2)}) collective-permute-start(bf16[32,512]{1,0:T(8,128)(2,1)} %refs_0_.1), channel_id=1, source_target_pairs={{0,2},{2,0},{4,6},{6,4},{8,10},{10,8},{12,14},{14,12},{16,18},{18,... | collective-permute-start | bytes 98312 | tf_op jit(solution)/shard_map/ppermute | solution.py:346
  4.0 0.7 slice_bitcast_fusion
  5.0 0.7 join.5.refs_5_.refs_0_
  5.8 5.3 %collective-permute-start.1 = (bf16[64,256]{1,0:T(8,128)(2,1)S(1)}, bf16[64,256]{1,0:T(8,128)(2,1)S(1)}, u32[]{:S(2)}, u32[]{:S(2)}) collective-permute-start(bf16[64,256]{1,0:T(8,128)(2,1)S(1)} %join.5.refs_5_.refs_0_), channel_id=1, source_target_pairs={{0,128},{2,130},{4,132},{6,134},{8,136},{10,138},{12,140},{14,142}... | collective-permute-start | bytes 98312 | tf_op jit(solution)/shard_map/ppermute | solution.py:346
  11.0 3.4 %probs_part.4 = (bf16[4,384,384]{2,1,0:T(8,128)(2,1)S(1)}, f32[384,512]{1,0:T(8,128)S(1)}, bf16[384,4096]{1,0:T(8,128)(2,1)S(1)}) custom-call(s32[8]{0:T(128)S(1)} %concatenate.11.refs_2_.refs_0_, bf16[384,2048]{1,0:T(8,128)(2,1)} %refs_1_.15, bf16[384,512]{1,0:T(8,128)(2,1)} %refs_2_.15, bf16[384,2048]{1,0:T(8,128)(2,1)} %refs_3_.15, ...), custom_call_target="tpu_custom_call" | custom-call | flops 1000 | bytes 1000 | tf_op jit(solution)/shard_map/probs_part/pallas_call | solution.py:53
  14.5 0.7 collective-permute-start.2
  15.2 1.2 %collective-permute-start.3 = (bf16[128,256]{1,0:T(8,128)(2,1)S(1)}, bf16[128,256]{1,0:T(8,128)(2,1)S(1)}, u32[]{:S(2)}, u32[]{:S(2)}) collective-permute-start(bf16[128,256]{1,0:T(8,128)(2,1)S(1)} %get-tuple-element.50.refs_5_.refs_0_), channel_id=1, source_target_pairs={{0,64},{2,66},{4,68},{6,70},{8,72},{10,74},{12,76},{14,78},{16,80}... | collective-permute-start | bytes 196616 | tf_op jit(solution)/shard_map/ppermute | solution.py:346
  16.4 2.2 %probs_part.5 = (bf16[4,384,384]{2,1,0:T(8,128)(2,1)S(1)}, f32[384,512]{1,0:T(8,128)S(1)}) custom-call(s32[8]{0:T(128)S(1)} %concatenate.11.refs_2_.refs_0_, bf16[384,2048]{1,0:T(8,128)(2,1)S(1)} %copy-done, bf16[384,512]{1,0:T(8,128)(2,1)S(1)} %copy-done.2, bf16[384,2048]{1,0:T(8,128)(2,1)S(1)} %copy-done.1, ...), custom_call_target="tpu_custom_call", output_to_operand_aliasing={{1}: (4, {})} | custom-call | flops 1000 | bytes 1000 | tf_op jit(solution)/shard_map/probs_part/pallas_call | solution.py:53
  18.6 2.6 %collective-permute-done.3.refs_1_ = bf16[128,256]{1,0:T(8,128)(2,1)S(1)} collective-permute-done((bf16[128,256]{1,0:T(8,128)(2,1)S(1)}, bf16[128,256]{1,0:T(8,128)(2,1)S(1)}, u32[]{:S(2)}, u32[]{:S(2)}) %collective-permute-start.3) | collective-permute-done | bytes 65568 | tf_op jit(solution)/shard_map/ppermute | solution.py:346
  21.3 2.2 %probs_part.6 = (bf16[4,384,384]{2,1,0:T(8,128)(2,1)S(1)}, f32[384,512]{1,0:T(8,128)S(1)}) custom-call(s32[8]{0:T(128)S(1)} %concatenate.11.refs_2_.refs_0_, bf16[384,2048]{1,0:T(8,128)(2,1)S(1)} %copy-done, bf16[384,512]{1,0:T(8,128)(2,1)S(1)} %copy-done.2, bf16[384,2048]{1,0:T(8,128)(2,1)S(1)} %copy-done.1, ...), custom_call_target="tpu_custom_call", output_to_operand_aliasing={{1}: (4, {})} | custom-call | flops 1000 | bytes 1000 | tf_op jit(solution)/shard_map/probs_part/pallas_call | solution.py:53
  23.5 1.9 %collective-permute-done.4.refs_1_ = bf16[256,256]{1,0:T(8,128)(2,1)S(1)} collective-permute-done((bf16[256,256]{1,0:T(8,128)(2,1)S(1)}, bf16[256,256]{1,0:T(8,128)(2,1)S(1)}, u32[]{:S(2)}, u32[]{:S(2)}) %collective-permute-start.4) | collective-permute-done | bytes 131104 | tf_op jit(solution)/shard_map/ppermute | solution.py:346
  25.5 2.8 %collective-permute-start.5 = (bf16[512,128]{1,0:T(8,128)(2,1)S(1)}, bf16[512,128]{1,0:T(8,128)(2,1)S(1)}, u32[]{:S(2)}, u32[]{:S(2)}) collective-permute-start(bf16[512,128]{1,0:T(8,128)(2,1)S(1)} %get-tuple-element.55.refs_5_.refs_2_), channel_id=1, source_target_pairs={{0,4},{2,6},{4,0},{6,2},{8,12},{10,14},{12,8},{14,10},{16,20},{18,... | collective-permute-start | bytes 393224 | tf_op jit(solution)/shard_map/ppermute | solution.py:346
  28.3 2.7 %collective-permute-start.8 = (bf16[512,128]{1,0:T(8,128)(2,1)S(1)}, bf16[512,128]{1,0:T(8,128)(2,1)S(1)}, u32[]{:S(2)}, u32[]{:S(2)}) collective-permute-start(bf16[512,128]{1,0:T(8,128)(2,1)S(1)} %get-tuple-element.57.refs_4_), channel_id=1, source_target_pairs={{0,24},{2,26},{4,28},{6,30},{8,0},{10,2},{12,4},{14,6},{16,8},{18,... | collective-permute-start | bytes 393224 | tf_op jit(solution)/shard_map/ppermute | solution.py:346
  31.4 0.7 collective-permute-start.6
  32.1 2.2 %probs_part.7 = (bf16[4,384,384]{2,1,0:T(8,128)(2,1)S(1)}, f32[384,512]{1,0:T(8,128)S(1)}) custom-call(s32[8]{0:T(128)S(1)} %concatenate.11.refs_2_.refs_0_, bf16[384,2048]{1,0:T(8,128)(2,1)S(1)} %copy-done, bf16[384,512]{1,0:T(8,128)(2,1)S(1)} %copy-done.2, bf16[384,2048]{1,0:T(8,128)(2,1)S(1)} %copy-done.1, ...), custom_call_target="tpu_custom_call", output_to_operand_aliasing={{1}: (4, {})} | custom-call | flops 1000 | bytes 1000 | tf_op jit(solution)/shard_map/probs_part/pallas_call | solution.py:53
  34.3 2.2 %collective-permute-done.7.refs_6_ = bf16[512,128]{1,0:T(8,128)(2,1)S(1)} collective-permute-done((bf16[512,128]{1,0:T(8,128)(2,1)S(1)}, bf16[512,128]{1,0:T(8,128)(2,1)S(1)}, u32[]{:S(2)}, u32[]{:S(2)}) %collective-permute-start.7) | collective-permute-done | bytes 131104 | tf_op jit(solution)/shard_map/ppermute | solution.py:346
  36.5 1.3 %collective-permute-done.6.refs_5_ = bf16[512,128]{1,0:T(8,128)(2,1)S(1)} collective-permute-done((bf16[512,128]{1,0:T(8,128)(2,1)S(1)}, bf16[512,128]{1,0:T(8,128)(2,1)S(1)}, u32[]{:S(2)}, u32[]{:S(2)}) %collective-permute-start.6) | collective-permute-done | bytes 131104 | tf_op jit(solution)/shard_map/ppermute | solution.py:346
  37.8 0.6 join.9
  38.7 0.6 collective-permute-start.12
  39.7 0.5 collective-permute-start.10
  40.2 4.3 %collective-permute-start.9 = (bf16[384,256]{1,0:T(8,128)(2,1)S(1)}, bf16[384,256]{1,0:T(8,128)(2,1)S(1)}, u32[]{:S(2)}, u32[]{:S(2)}) collective-permute-start(bf16[384,256]{1,0:T(8,128)(2,1)S(1)} %get-tuple-element.58), channel_id=1, source_target_pairs={{0,2},{2,0},{4,6},{6,4},{8,10},{10,8},{12,14},{14,12},{16,18},{18,... | collective-permute-start | bytes 589832 | tf_op jit(solution)/shard_map/ppermute | solution.py:346
  44.6 1.1 %collective-permute-done.9.refs_4_ = bf16[384,256]{1,0:T(8,128)(2,1)S(1)} collective-permute-done((bf16[384,256]{1,0:T(8,128)(2,1)S(1)}, bf16[384,256]{1,0:T(8,128)(2,1)S(1)}, u32[]{:S(2)}, u32[]{:S(2)}) %collective-permute-start.9) | collective-permute-done | bytes 196640 | tf_op jit(solution)/shard_map/ppermute | solution.py:346
  45.6 0.5 collective-permute-done.11.refs_8_
  46.2 6.8 %collective-permute-done.10.refs_7_ = bf16[1024,128]{1,0:T(8,128)(2,1)S(1)} collective-permute-done((bf16[1024,128]{1,0:T(8,128)(2,1)S(1)}, bf16[1024,128]{1,0:T(8,128)(2,1)S(1)}, u32[]{:S(2)}, u32[]{:S(2)}) %collective-permute-start.10) | collective-permute-done | bytes 262176 | tf_op jit(solution)/shard_map/ppermute | solution.py:346
  53.0 2.9 %raw_part.1 = (bf16[384,256]{1,0:T(8,128)(2,1)S(1)}, bf16[384,256]{1,0:T(8,128)(2,1)S(1)}, f32[1,256]{1,0:T(1,128)S(1)}, bf16[2048,256]{1,0:T(8,128)(2,1)S(1)}, ...) custom-call(s32[8]{0:T(128)S(1)} %concatenate.11.refs_2_.refs_0_, ...), custom_call_target="tpu_custom_call" | custom-call | flops 1000 | bytes 1000 | tf_op jit(solution)/shard_map/raw_part/pallas_call | solution.py:53
  56.0 2.3 %collective-permute-start.16 = (bf16[2048,256]{1,0:T(8,128)(2,1)S(1)}, bf16[2048,256]{1,0:T(8,128)(2,1)S(1)}, u32[]{:S(2)}, u32[]{:S(2)}) collective-permute-start(bf16[2048,256]{1,0:T(8,128)(2,1)S(1)} %get-tuple-element.65.refs_6_), channel_id=1, source_target_pairs={{0,2},{2,0},{4,6},{6,4},{8,10},{10,8},{12,14},{14,12},{16,18},{18,... | collective-permute-start | bytes 3145736 | tf_op jit(solution)/shard_map/ppermute | solution.py:346
  58.2 1.2 %collective-permute-start.20 = (bf16[1280,256]{1,0:T(8,128)(2,1)S(1)}, bf16[1280,256]{1,0:T(8,128)(2,1)S(1)}, u32[]{:S(2)}, u32[]{:S(2)}) collective-permute-start(bf16[1280,256]{1,0:T(8,128)(2,1)S(1)} %get-tuple-element.75), channel_id=1, source_target_pairs={{0,1},{1,0},{2,3},{3,2},{4,5},{5,4},{6,7},{7,6},{8,9},{9,8},{10,11... | collective-permute-start | bytes 1966088 | tf_op jit(solution)/shard_map/ppermute | solution.py:396
  59.4 0.4 collective-permute-start.14
  59.8 1.8 %collective-permute-start.23 = (bf16[1536,256]{1,0:T(8,128)(2,1)S(1)}, bf16[1536,256]{1,0:T(8,128)(2,1)S(1)}, u32[]{:S(2)}, u32[]{:S(2)}) collective-permute-start(bf16[1536,256]{1,0:T(8,128)(2,1)S(1)} %get-tuple-element.82), channel_id=1, source_target_pairs={{0,5},{1,4},{2,7},{3,6},{4,1},{5,0},{6,3},{7,2},{8,13},{9,12},{10,... | collective-permute-start | bytes 2359304 | tf_op jit(solution)/shard_map/ppermute | solution.py:397
  61.6 2.7 %collective-permute-done.15.refs_1_ = f32[1,256]{1,0:T(1,128)S(1)} collective-permute-done((f32[1,256]{1,0:T(1,128)S(1)}, f32[1,256]{1,0:T(1,128)S(1)}, u32[]{:S(2)}, u32[]{:S(2)}) %collective-permute-start.15) | collective-permute-done | bytes 1056 | tf_op jit(solution)/shard_map/ppermute | solution.py:346
  64.3 0.4 collective-permute-start.17
  64.7 2.6 %grads_part.4 = (bf16[384,2048]{1,0:T(8,128)(2,1)}, bf16[384,512]{1,0:T(8,128)(2,1)}, f32[8,128]{1,0:T(8,128)S(1)}) custom-call(s32[8]{0:T(128)S(1)} %concatenate.11.refs_2_.refs_0_, bf16[384,2048]{1,0:T(8,128)(2,1)S(1)} %copy-done, bf16[384,512]{1,0:T(8,128)(2,1)S(1)} %copy-done.2, bf16[384,2048]{1,0:T(8,128)(2,1)S(1)} %copy-done.1, ...), custom_call_target="tpu_custom_call" | custom-call | flops 1000 | bytes 1000 | tf_op jit(solution)/shard_map/grads_part/pallas_call | solution.py:53
  67.4 1.0 %collective-permute-done.17.refs_1_ = f32[1,256]{1,0:T(1,128)S(1)} collective-permute-done((f32[1,256]{1,0:T(1,128)S(1)}, f32[1,256]{1,0:T(1,128)S(1)}, u32[]{:S(2)}, u32[]{:S(2)}) %collective-permute-start.17) | collective-permute-done | bytes 1056 | tf_op jit(solution)/shard_map/ppermute | solution.py:346
  68.3 1.5 %collective-permute-start.18 = (f32[1,256]{1,0:T(1,128)S(1)}, f32[1,256]{1,0:T(1,128)S(1)}, u32[]{:S(2)}, u32[]{:S(2)}) collective-permute-start(f32[1,256]{1,0:T(1,128)S(1)} %add.25.refs_9_.refs_0_), channel_id=1, source_target_pairs={{0,32},{2,34},{4,36},{6,38},{8,40},{10,42},{12,44},{14,46},{16,48}... | collective-permute-start | bytes 3080 | tf_op jit(solution)/shard_map/ppermute | solution.py:346
  69.8 2.6 %grads_part.5 = (bf16[384,2048]{1,0:T(8,128)(2,1)}, bf16[384,512]{1,0:T(8,128)(2,1)}, f32[8,128]{1,0:T(8,128)S(1)}) custom-call(s32[8]{0:T(128)S(1)} %concatenate.11.refs_2_.refs_0_, bf16[384,2048]{1,0:T(8,128)(2,1)S(1)} %copy-done, bf16[384,512]{1,0:T(8,128)(2,1)S(1)} %copy-done.2, ...), custom_call_target="tpu_custom_call", output_to_operand_aliasing={{0}: (7, {}), {1}: (8, {})} | custom-call | flops 1000 | bytes 1000 | tf_op jit(solution)/shard_map/grads_part/pallas_call | solution.py:53
  72.5 0.6 collective-permute-start.19
  73.0 2.6 %grads_part.6 = (bf16[384,2048]{1,0:T(8,128)(2,1)}, bf16[384,512]{1,0:T(8,128)(2,1)}, f32[8,128]{1,0:T(8,128)S(1)}) custom-call(s32[8]{0:T(128)S(1)} %concatenate.11.refs_2_.refs_0_, bf16[384,2048]{1,0:T(8,128)(2,1)S(1)} %copy-done, bf16[384,512]{1,0:T(8,128)(2,1)S(1)} %copy-done.2, ...), custom_call_target="tpu_custom_call", output_to_operand_aliasing={{0}: (7, {}), {1}: (8, {})} | custom-call | flops 1000 | bytes 1000 | tf_op jit(solution)/shard_map/grads_part/pallas_call | solution.py:53
  75.6 0.5 collective-permute-done.19.refs_1_
  76.2 3.6 %collective-permute-start.22 = (bf16[1280,256]{1,0:T(8,128)(2,1)S(1)}, bf16[1280,256]{1,0:T(8,128)(2,1)S(1)}, u32[]{:S(2)}, u32[]{:S(2)}) collective-permute-start(bf16[1280,256]{1,0:T(8,128)(2,1)S(1)} %get-tuple-element.79.refs_3_.refs_4_), channel_id=1, source_target_pairs={{0,2},{2,0},{4,6},{6,4},{8,10},{10,8},{12,14},{14,12},{16,18},{18,... | collective-permute-start | bytes 1966088 | tf_op jit(solution)/shard_map/ppermute | solution.py:346
  79.8 3.2 %collective-permute-start.21 = (f32[1,256]{1,0:T(1,128)S(1)}, f32[1,256]{1,0:T(1,128)S(1)}, u32[]{:S(2)}, u32[]{:S(2)}) collective-permute-start(f32[1,256]{1,0:T(1,128)S(1)} %get-tuple-element.76.refs_9_.refs_0_), channel_id=1, source_target_pairs={{0,128},{2,130},{4,132},{6,134},{8,136},{10,138},{12,140},{14,142}... | collective-permute-start | bytes 3080 | tf_op jit(solution)/shard_map/ppermute | solution.py:346
  83.0 2.6 %grads_part.7 = (bf16[384,2048]{1,0:T(8,128)(2,1)}, bf16[384,512]{1,0:T(8,128)(2,1)}, f32[8,128]{1,0:T(8,128)S(1)}) custom-call(s32[8]{0:T(128)S(1)} %concatenate.11.refs_2_.refs_0_, bf16[384,2048]{1,0:T(8,128)(2,1)S(1)} %copy-done, bf16[384,512]{1,0:T(8,128)(2,1)S(1)} %copy-done.2, ...), custom_call_target="tpu_custom_call", output_to_operand_aliasing={{0}: (7, {}), {1}: (8, {})} | custom-call | flops 1000 | bytes 1000 | tf_op jit(solution)/shard_map/grads_part/pallas_call | solution.py:53
  85.6 1.9 %hidden_part.2 = (bf16[384,2048]{1,0:T(8,128)(2,1)}, f32[8,128]{1,0:T(8,128)S(1)}) custom-call(s32[8]{0:T(128)S(1)} %concatenate.11.refs_2_.refs_0_, f32[384,512]{1,0:T(8,128)S(1)} %get-tuple-element.56.refs_1_.refs_3_, f32[1,512]{1,0:T(1,128)S(1)} %bitcast.11, bf16[1280,256]{1,0:T(8,128)(2,1)S(1)} %get-tuple-element.79.refs_3_.refs_4_, ...), custom_call_target="tpu_custom_call" | custom-call | flops 1000 | bytes 1000 | tf_op jit(solution)/shard_map/hidden_part/pallas_call | solution.py:53
  87.5 0.5 collective-permute-start.24
  88.3 1.6 %collective-permute-done.24.refs_5_ = bf16[1536,256]{1,0:T(8,128)(2,1)S(1)} collective-permute-done((bf16[1536,256]{1,0:T(8,128)(2,1)S(1)}, bf16[1536,256]{1,0:T(8,128)(2,1)S(1)}, u32[]{:S(2)}, u32[]{:S(2)}) %collective-permute-start.24) | collective-permute-done | bytes 786464 | tf_op jit(solution)/shard_map/ppermute | solution.py:346
  89.9 3.0 %hidden_part.3 = (bf16[384,2048]{1,0:T(8,128)(2,1)}, f32[8,128]{1,0:T(8,128)S(1)}) custom-call(s32[8]{0:T(128)S(1)} %concatenate.11.refs_2_.refs_0_, f32[384,512]{1,0:T(8,128)S(1)} %get-tuple-element.56.refs_1_.refs_3_, f32[1,512]{1,0:T(1,128)S(1)} %bitcast.12, ...), custom_call_target="tpu_custom_call", output_to_operand_aliasing={{0}: (8, {})} | custom-call | flops 1000 | bytes 1000 | tf_op jit(solution)/shard_map/hidden_part/pallas_call | solution.py:53
  92.9 0.4 collective-permute-start.26
  93.4 0.8 collective-permute-done.26
  94.2 0.6 maximum_multiply_fusion
  (40 shorter events, 2.0 us)
Async XLA Ops:
  0.6 4.4 %collective-permute-start = (bf16[32,512]{1,0:T(8,128)(2,1)}, bf16[32,512]{1,0:T(8,128)(2,1)S(1)}, u32[]{:S(2)}, u32[]{:S(2)}) collective-permute-start(bf16[32,512]{1,0:T(8,128)(2,1)} %refs_0_.1), channel_id=1, source_target_pairs={{0,2},{2,0},{4,6},{6,4},{8,10},{10,8},{12,14},{14,12},{16,18},{18,... | collective-permute-start | bytes 98312 | tf_op jit(solution)/shard_map/ppermute | solution.py:346
  5.8 8.7 %collective-permute-start.1 = (bf16[64,256]{1,0:T(8,128)(2,1)S(1)}, bf16[64,256]{1,0:T(8,128)(2,1)S(1)}, u32[]{:S(2)}, u32[]{:S(2)}) collective-permute-start(bf16[64,256]{1,0:T(8,128)(2,1)S(1)} %join.5.refs_5_.refs_0_), channel_id=1, source_target_pairs={{0,128},{2,130},{4,132},{6,134},{8,136},{10,138},{12,140},{14,142}... | collective-permute-start | bytes 98312 | tf_op jit(solution)/shard_map/ppermute | solution.py:346
  14.5 2.0 %copy-start = (bf16[384,2048]{1,0:T(8,128)(2,1)S(1)}, bf16[384,2048]{1,0:T(8,128)(2,1)}, u32[]{:S(2)}) copy-start(bf16[384,2048]{1,0:T(8,128)(2,1)} %refs_1_.15) | copy-start | bytes 4718596
  14.5 2.0 %copy-start.1 = (bf16[384,2048]{1,0:T(8,128)(2,1)S(1)}, bf16[384,2048]{1,0:T(8,128)(2,1)}, u32[]{:S(2)}) copy-start(bf16[384,2048]{1,0:T(8,128)(2,1)} %refs_3_.15) | copy-start | bytes 4718596
  14.5 2.0 %copy-start.2 = (bf16[384,512]{1,0:T(8,128)(2,1)S(1)}, bf16[384,512]{1,0:T(8,128)(2,1)}, u32[]{:S(2)}) copy-start(bf16[384,512]{1,0:T(8,128)(2,1)} %refs_2_.15) | copy-start | bytes 1179652
  14.5 10.9 %collective-permute-start.2 = (bf16[384,4096]{1,0:T(8,128)(2,1)S(1)}, bf16[384,4096]{1,0:T(8,128)(2,1)S(1)}, u32[]{:S(2)}, u32[]{:S(2)}) collective-permute-start(bf16[384,4096]{1,0:T(8,128)(2,1)S(1)} %get-tuple-element.48.refs_1_), channel_id=1, source_target_pairs={{0,2},{2,0},{4,6},{6,4},{8,10},{10,8},{12,14},{14,12},{16,18},{18,... | collective-permute-start | bytes 9437192 | tf_op jit(solution)/shard_map/ppermute | solution.py:346
  15.2 6.0 %collective-permute-start.3 = (bf16[128,256]{1,0:T(8,128)(2,1)S(1)}, bf16[128,256]{1,0:T(8,128)(2,1)S(1)}, u32[]{:S(2)}, u32[]{:S(2)}) collective-permute-start(bf16[128,256]{1,0:T(8,128)(2,1)S(1)} %get-tuple-element.50.refs_5_.refs_0_), channel_id=1, source_target_pairs={{0,64},{2,66},{4,68},{6,70},{8,72},{10,74},{12,76},{14,78},{16,80}... | collective-permute-start | bytes 196616 | tf_op jit(solution)/shard_map/ppermute | solution.py:346
  21.2 4.2 %collective-permute-start.4 = (bf16[256,256]{1,0:T(8,128)(2,1)S(1)}, bf16[256,256]{1,0:T(8,128)(2,1)S(1)}, u32[]{:S(2)}, u32[]{:S(2)}) collective-permute-start(bf16[256,256]{1,0:T(8,128)(2,1)S(1)} %join.7.refs_5_.refs_0_), channel_id=1, source_target_pairs={{0,32},{2,34},{4,36},{6,38},{8,40},{10,42},{12,44},{14,46},{16,48}... | collective-permute-start | bytes 393224 | tf_op jit(solution)/shard_map/ppermute | solution.py:346
  25.5 8.8 %collective-permute-start.5 = (bf16[512,128]{1,0:T(8,128)(2,1)S(1)}, bf16[512,128]{1,0:T(8,128)(2,1)S(1)}, u32[]{:S(2)}, u32[]{:S(2)}) collective-permute-start(bf16[512,128]{1,0:T(8,128)(2,1)S(1)} %get-tuple-element.55.refs_5_.refs_2_), channel_id=1, source_target_pairs={{0,4},{2,6},{4,0},{6,2},{8,12},{10,14},{12,8},{14,10},{16,20},{18,... | collective-permute-start | bytes 393224 | tf_op jit(solution)/shard_map/ppermute | solution.py:346
  28.3 6.0 %collective-permute-start.8 = (bf16[512,128]{1,0:T(8,128)(2,1)S(1)}, bf16[512,128]{1,0:T(8,128)(2,1)S(1)}, u32[]{:S(2)}, u32[]{:S(2)}) collective-permute-start(bf16[512,128]{1,0:T(8,128)(2,1)S(1)} %get-tuple-element.57.refs_4_), channel_id=1, source_target_pairs={{0,24},{2,26},{4,28},{6,30},{8,0},{10,2},{12,4},{14,6},{16,8},{18,... | collective-permute-start | bytes 393224 | tf_op jit(solution)/shard_map/ppermute | solution.py:346
  31.1 5.4 %collective-permute-start.7 = (bf16[512,128]{1,0:T(8,128)(2,1)S(1)}, bf16[512,128]{1,0:T(8,128)(2,1)S(1)}, u32[]{:S(2)}, u32[]{:S(2)}) collective-permute-start(bf16[512,128]{1,0:T(8,128)(2,1)S(1)} %get-tuple-element.57.refs_4_), channel_id=1, source_target_pairs={{0,16},{2,18},{4,20},{6,22},{8,24},{10,26},{12,28},{14,30},{16,0},... | collective-permute-start | bytes 393224 | tf_op jit(solution)/shard_map/ppermute | solution.py:346
  31.4 6.4 %collective-permute-start.6 = (bf16[512,128]{1,0:T(8,128)(2,1)S(1)}, bf16[512,128]{1,0:T(8,128)(2,1)S(1)}, u32[]{:S(2)}, u32[]{:S(2)}) collective-permute-start(bf16[512,128]{1,0:T(8,128)(2,1)S(1)} %get-tuple-element.57.refs_4_), channel_id=1, source_target_pairs={{0,8},{2,10},{4,12},{6,14},{8,16},{10,18},{12,20},{14,22},{16,24},... | collective-permute-start | bytes 393224 | tf_op jit(solution)/shard_map/ppermute | solution.py:346
  34.3 18.7 %copy-start.3 = (f32[512]{0:T(512)S(1)}, f32[512]{0:T(512)}, u32[]{:S(2)}) copy-start(f32[512]{0:T(512)} %param.11) | copy-start | bytes 6148
  38.4 14.6 %collective-permute-start.13 = (bf16[2048,128]{1,0:T(8,128)(2,1)S(1)}, bf16[2048,128]{1,0:T(8,128)(2,1)S(1)}, u32[]{:S(2)}, u32[]{:S(2)}) collective-permute-start(bf16[2048,128]{1,0:T(8,128)(2,1)S(1)} %get-tuple-element.60.refs_10_), channel_id=1, source_target_pairs={{0,4},{2,6},{4,0},{6,2},{8,12},{10,14},{12,8},{14,10},{16,20},{18,... | collective-permute-start | bytes 1572872 | tf_op jit(solution)/shard_map/ppermute | solution.py:346
  38.7 6.9 %collective-permute-start.12 = (bf16[1024,128]{1,0:T(8,128)(2,1)S(1)}, bf16[1024,128]{1,0:T(8,128)(2,1)S(1)}, u32[]{:S(2)}, u32[]{:S(2)}) collective-permute-start(bf16[1024,128]{1,0:T(8,128)(2,1)S(1)} %get-tuple-element.59.refs_6_), channel_id=1, source_target_pairs={{0,24},{2,26},{4,28},{6,30},{8,0},{10,2},{12,4},{14,6},{16,8},{18,... | collective-permute-start | bytes 786440 | tf_op jit(solution)/shard_map/ppermute | solution.py:346
  39.4 6.8 %collective-permute-start.11 = (bf16[1024,128]{1,0:T(8,128)(2,1)S(1)}, bf16[1024,128]{1,0:T(8,128)(2,1)S(1)}, u32[]{:S(2)}, u32[]{:S(2)}) collective-permute-start(bf16[1024,128]{1,0:T(8,128)(2,1)S(1)} %get-tuple-element.59.refs_6_), channel_id=1, source_target_pairs={{0,16},{2,18},{4,20},{6,22},{8,24},{10,26},{12,28},{14,30},{16,0},... | collective-permute-start | bytes 786440 | tf_op jit(solution)/shard_map/ppermute | solution.py:346
  39.7 13.3 %collective-permute-start.10 = (bf16[1024,128]{1,0:T(8,128)(2,1)S(1)}, bf16[1024,128]{1,0:T(8,128)(2,1)S(1)}, u32[]{:S(2)}, u32[]{:S(2)}) collective-permute-start(bf16[1024,128]{1,0:T(8,128)(2,1)S(1)} %get-tuple-element.59.refs_6_), channel_id=1, source_target_pairs={{0,8},{2,10},{4,12},{6,14},{8,16},{10,18},{12,20},{14,22},{16,24},... | collective-permute-start | bytes 786440 | tf_op jit(solution)/shard_map/ppermute | solution.py:346
  40.2 5.4 %collective-permute-start.9 = (bf16[384,256]{1,0:T(8,128)(2,1)S(1)}, bf16[384,256]{1,0:T(8,128)(2,1)S(1)}, u32[]{:S(2)}, u32[]{:S(2)}) collective-permute-start(bf16[384,256]{1,0:T(8,128)(2,1)S(1)} %get-tuple-element.58), channel_id=1, source_target_pairs={{0,2},{2,0},{4,6},{6,4},{8,10},{10,8},{12,14},{14,12},{16,18},{18,... | collective-permute-start | bytes 589832 | tf_op jit(solution)/shard_map/ppermute | solution.py:346
  56.0 8.3 %collective-permute-start.16 = (bf16[2048,256]{1,0:T(8,128)(2,1)S(1)}, bf16[2048,256]{1,0:T(8,128)(2,1)S(1)}, u32[]{:S(2)}, u32[]{:S(2)}) collective-permute-start(bf16[2048,256]{1,0:T(8,128)(2,1)S(1)} %get-tuple-element.65.refs_6_), channel_id=1, source_target_pairs={{0,2},{2,0},{4,6},{6,4},{8,10},{10,8},{12,14},{14,12},{16,18},{18,... | collective-permute-start | bytes 3145736 | tf_op jit(solution)/shard_map/ppermute | solution.py:346
  58.2 17.4 %collective-permute-start.20 = (bf16[1280,256]{1,0:T(8,128)(2,1)S(1)}, bf16[1280,256]{1,0:T(8,128)(2,1)S(1)}, u32[]{:S(2)}, u32[]{:S(2)}) collective-permute-start(bf16[1280,256]{1,0:T(8,128)(2,1)S(1)} %get-tuple-element.75), channel_id=1, source_target_pairs={{0,1},{1,0},{2,3},{3,2},{4,5},{5,4},{6,7},{7,6},{8,9},{9,8},{10,11... | collective-permute-start | bytes 1966088 | tf_op jit(solution)/shard_map/ppermute | solution.py:396
  59.4 4.9 %collective-permute-start.14 = (bf16[384,256]{1,0:T(8,128)(2,1)S(1)}, bf16[384,256]{1,0:T(8,128)(2,1)S(1)}, u32[]{:S(2)}, u32[]{:S(2)}) collective-permute-start(bf16[384,256]{1,0:T(8,128)(2,1)S(1)} %get-tuple-element.62), channel_id=1, source_target_pairs={{0,2},{2,0},{4,6},{6,4},{8,10},{10,8},{12,14},{14,12},{16,18},{18,... | collective-permute-start | bytes 589832 | tf_op jit(solution)/shard_map/ppermute | solution.py:346
  59.8 27.7 %collective-permute-start.23 = (bf16[1536,256]{1,0:T(8,128)(2,1)S(1)}, bf16[1536,256]{1,0:T(8,128)(2,1)S(1)}, u32[]{:S(2)}, u32[]{:S(2)}) collective-permute-start(bf16[1536,256]{1,0:T(8,128)(2,1)S(1)} %get-tuple-element.82), channel_id=1, source_target_pairs={{0,5},{1,4},{2,7},{3,6},{4,1},{5,0},{6,3},{7,2},{8,13},{9,12},{10,... | collective-permute-start | bytes 2359304 | tf_op jit(solution)/shard_map/ppermute | solution.py:397
  61.6 2.7 %collective-permute-start.15 = (f32[1,256]{1,0:T(1,128)S(1)}, f32[1,256]{1,0:T(1,128)S(1)}, u32[]{:S(2)}, u32[]{:S(2)}) collective-permute-start(f32[1,256]{1,0:T(1,128)S(1)} %get-tuple-element.64.refs_0_), channel_id=1, source_target_pairs={{0,8},{2,10},{4,12},{6,14},{8,0},{10,2},{12,4},{14,6},{16,24},{18,... | collective-permute-start | bytes 3080 | tf_op jit(solution)/shard_map/ppermute | solution.py:346
  64.3 4.0 %collective-permute-start.17 = (f32[1,256]{1,0:T(1,128)S(1)}, f32[1,256]{1,0:T(1,128)S(1)}, u32[]{:S(2)}, u32[]{:S(2)}) collective-permute-start(f32[1,256]{1,0:T(1,128)S(1)} %add.24.refs_7_.refs_0_), channel_id=1, source_target_pairs={{0,16},{2,18},{4,20},{6,22},{8,24},{10,26},{12,28},{14,30},{16,0},... | collective-permute-start | bytes 3080 | tf_op jit(solution)/shard_map/ppermute | solution.py:346
  68.3 4.1 %collective-permute-start.18 = (f32[1,256]{1,0:T(1,128)S(1)}, f32[1,256]{1,0:T(1,128)S(1)}, u32[]{:S(2)}, u32[]{:S(2)}) collective-permute-start(f32[1,256]{1,0:T(1,128)S(1)} %add.25.refs_9_.refs_0_), channel_id=1, source_target_pairs={{0,32},{2,34},{4,36},{6,38},{8,40},{10,42},{12,44},{14,46},{16,48}... | collective-permute-start | bytes 3080 | tf_op jit(solution)/shard_map/ppermute | solution.py:346
  72.5 3.7 %collective-permute-start.19 = (f32[1,256]{1,0:T(1,128)S(1)}, f32[1,256]{1,0:T(1,128)S(1)}, u32[]{:S(2)}, u32[]{:S(2)}) collective-permute-start(f32[1,256]{1,0:T(1,128)S(1)} %add.26.refs_9_.refs_0_), channel_id=1, source_target_pairs={{0,64},{2,66},{4,68},{6,70},{8,72},{10,74},{12,76},{14,78},{16,80}... | collective-permute-start | bytes 3080 | tf_op jit(solution)/shard_map/ppermute | solution.py:346
  76.2 9.4 %collective-permute-start.22 = (bf16[1280,256]{1,0:T(8,128)(2,1)S(1)}, bf16[1280,256]{1,0:T(8,128)(2,1)S(1)}, u32[]{:S(2)}, u32[]{:S(2)}) collective-permute-start(bf16[1280,256]{1,0:T(8,128)(2,1)S(1)} %get-tuple-element.79.refs_3_.refs_4_), channel_id=1, source_target_pairs={{0,2},{2,0},{4,6},{6,4},{8,10},{10,8},{12,14},{14,12},{16,18},{18,... | collective-permute-start | bytes 1966088 | tf_op jit(solution)/shard_map/ppermute | solution.py:346
  79.8 7.8 %collective-permute-start.21 = (f32[1,256]{1,0:T(1,128)S(1)}, f32[1,256]{1,0:T(1,128)S(1)}, u32[]{:S(2)}, u32[]{:S(2)}) collective-permute-start(f32[1,256]{1,0:T(1,128)S(1)} %get-tuple-element.76.refs_9_.refs_0_), channel_id=1, source_target_pairs={{0,128},{2,130},{4,132},{6,134},{8,136},{10,138},{12,140},{14,142}... | collective-permute-start | bytes 3080 | tf_op jit(solution)/shard_map/ppermute | solution.py:346
  87.5 2.4 %collective-permute-start.24 = (bf16[1536,256]{1,0:T(8,128)(2,1)S(1)}, bf16[1536,256]{1,0:T(8,128)(2,1)S(1)}, u32[]{:S(2)}, u32[]{:S(2)}) collective-permute-start(bf16[1536,256]{1,0:T(8,128)(2,1)S(1)} %get-tuple-element.83.refs_4_), channel_id=1, source_target_pairs={{0,2},{2,0},{4,6},{6,4},{8,10},{10,8},{12,14},{14,12},{16,18},{18,... | collective-permute-start | bytes 2359304 | tf_op jit(solution)/shard_map/ppermute | solution.py:346
  88.0 4.9 %collective-permute-start.25 = (f32[1,256]{1,0:T(1,128)S(1)}, f32[1,256]{1,0:T(1,128)S(1)}, u32[]{:S(2)}, u32[]{:S(2)}) collective-permute-start(f32[1,256]{1,0:T(1,128)S(1)} %get-tuple-element.85.refs_9_.refs_0_), channel_id=1, source_target_pairs={{0,4},{2,6},{4,0},{6,2},{8,12},{10,14},{12,8},{14,10},{16,20},{18,... | collective-permute-start | bytes 3080 | tf_op jit(solution)/shard_map/ppermute | solution.py:346
  92.9 1.3 %collective-permute-start.26 = (f32[1,256]{1,0:T(1,128)S(1)}, f32[1,256]{1,0:T(1,128)S(1)}, u32[]{:S(2)}, u32[]{:S(2)}) collective-permute-start(f32[1,256]{1,0:T(1,128)S(1)} %add.29), channel_id=1, source_target_pairs={{0,2},{2,0},{4,6},{6,4},{8,10},{10,8},{12,14},{14,12},{16,18},{18,... | collective-permute-start | bytes 3080 | tf_op jit(solution)/shard_map/ppermute | solution.py:346

commit v14 on v13

--- a/solution.py
+++ b/solution.py
@@ -390,22 +390,23 @@
     held = None
     for step, perm in enumerate((y_swap(1), y_swap(2), z_swap(1), z_swap(2), z_swap(4), X_SWAP)):
         got = send(sums, perm)
-        after, through = (), ()
+        after = ()
         if step == 0:
             values_far = send(theirs, C_SWAP)
             near = lax.ppermute(near, "seq", SEQ_SWAP)
             beside = lax.ppermute(beside, ("dp", "seq"), BESIDE)
             kept_far = send(kept, C_SWAP)
-            after = (values_far, kept_far)
-        elif step < 5:
-            g = step - 1
-            if step == 4:
-                near_far = send(near, C_SWAP)
-            *held, token = grads_part(g, at, queries, keys, upstream, mine, values_far, probs[g], held, (sums,))
-            if step == 4:
-                grad_hidden, token = hidden_part(
-                    True, (at, dv, scale, near, near, near_far, kept, kept_far), None, (token,)
-                )
+            after = (kept_far,)
+        if step < 4:
+            *held, token = grads_part(
+                step, at, queries, keys, upstream, mine, values_far, probs[step], held, (sums,)
+            )
+            after += (token,)
+        elif step == 4:
+            near_far = send(near, C_SWAP)
+            grad_hidden, token = hidden_part(
+                True, (at, dv, scale, near, near, near_far, kept, kept_far), None, (sums,)
+            )
             after = (token,)
         else:
             beside_far = send(beside, C_SWAP)

time: 94.9 us -> 94.3 us (level)
  waiting for transfers between devices: 23.4 us -> 20.6 us
  starting transfers between devices: 39.5 us -> 41.8 us
    ppermute x25, waiting for transfers between devices: 23.4 us -> 20.6 us  [send(): return lax.ppermute(x, 'dp', perm)]
    ppermute x25, starting transfers between devices: 36.5 us -> 38.7 us  [send(): return lax.ppermute(x, 'dp', perm)]
where the time goes in v14:
time: 94.3 us; the launch traced here: 94.2 us
  starting transfers between devices  41.8 us (44%)
  Pallas kernels  29.6 us (31%)
  waiting for transfers between devices  20.6 us (22%)
    ppermute x25, starting transfers between devices, send(): return lax.ppermute(x, 'dp', perm)  38.7 us
    pallas_call x22, Pallas kernels, call(): pl.pallas_call(run, in_specs=list(specs) + [ANY] * (len(after) + len(thro...  29.6 us
    ppermute x25, waiting for transfers between devices, send(): return lax.ppermute(x, 'dp', perm)  20.6 us
  transfers between devices with their start and end apart: 27, of which 13 were waited for; matrix products, arithmetic and copies ran while one was open for 1% of the time, Pallas kernels for 27%

profile of v14, /device:TPU:1, one launch (start us, length us, event | category | flops | bytes accessed | tf_op | source)
XLA Modules:
  0.0 94.2 jit_solution(10383034040166184116)
XLA Ops:
  0.6 3.3 %collective-permute-start = (bf16[32,512]{1,0:T(8,128)(2,1)}, bf16[32,512]{1,0:T(8,128)(2,1)S(1)}, u32[]{:S(2)}, u32[]{:S(2)}) collective-permute-start(bf16[32,512]{1,0:T(8,128)(2,1)} %refs_0_.1), channel_id=1, source_target_pairs={{0,2},{2,0},{4,6},{6,4},{8,10},{10,8},{12,14},{14,12},{16,18},{18,... | collective-permute-start | bytes 98312 | tf_op jit(solution)/shard_map/ppermute | solution.py:346
  4.0 0.7 slice_bitcast_fusion
  5.0 0.7 join.5.refs_5_.refs_0_
  5.8 5.3 %collective-permute-start.1 = (bf16[64,256]{1,0:T(8,128)(2,1)S(1)}, bf16[64,256]{1,0:T(8,128)(2,1)S(1)}, u32[]{:S(2)}, u32[]{:S(2)}) collective-permute-start(bf16[64,256]{1,0:T(8,128)(2,1)S(1)} %join.5.refs_5_.refs_0_), channel_id=1, source_target_pairs={{0,128},{2,130},{4,132},{6,134},{8,136},{10,138},{12,140},{14,142}... | collective-permute-start | bytes 98312 | tf_op jit(solution)/shard_map/ppermute | solution.py:346
  11.0 3.4 %probs_part.4 = (bf16[4,384,384]{2,1,0:T(8,128)(2,1)S(1)}, f32[384,512]{1,0:T(8,128)S(1)}, bf16[384,4096]{1,0:T(8,128)(2,1)S(1)}) custom-call(s32[8]{0:T(128)S(1)} %concatenate.11.refs_2_.refs_0_, bf16[384,2048]{1,0:T(8,128)(2,1)} %refs_1_.15, bf16[384,512]{1,0:T(8,128)(2,1)} %refs_2_.15, bf16[384,2048]{1,0:T(8,128)(2,1)} %refs_3_.15, ...), custom_call_target="tpu_custom_call" | custom-call | flops 1000 | bytes 1000 | tf_op jit(solution)/shard_map/probs_part/pallas_call | solution.py:53
  14.5 0.7 collective-permute-start.2
  15.2 1.2 %collective-permute-start.3 = (bf16[128,256]{1,0:T(8,128)(2,1)S(1)}, bf16[128,256]{1,0:T(8,128)(2,1)S(1)}, u32[]{:S(2)}, u32[]{:S(2)}) collective-permute-start(bf16[128,256]{1,0:T(8,128)(2,1)S(1)} %get-tuple-element.50.refs_5_.refs_0_), channel_id=1, source_target_pairs={{0,64},{2,66},{4,68},{6,70},{8,72},{10,74},{12,76},{14,78},{16,80}... | collective-permute-start | bytes 196616 | tf_op jit(solution)/shard_map/ppermute | solution.py:346
  16.4 2.2 %probs_part.5 = (bf16[4,384,384]{2,1,0:T(8,128)(2,1)S(1)}, f32[384,512]{1,0:T(8,128)S(1)}) custom-call(s32[8]{0:T(128)S(1)} %concatenate.11.refs_2_.refs_0_, bf16[384,2048]{1,0:T(8,128)(2,1)S(1)} %copy-done, bf16[384,512]{1,0:T(8,128)(2,1)S(1)} %copy-done.2, bf16[384,2048]{1,0:T(8,128)(2,1)S(1)} %copy-done.1, ...), custom_call_target="tpu_custom_call", output_to_operand_aliasing={{1}: (4, {})} | custom-call | flops 1000 | bytes 1000 | tf_op jit(solution)/shard_map/probs_part/pallas_call | solution.py:53
  18.6 2.6 %collective-permute-done.3.refs_1_ = bf16[128,256]{1,0:T(8,128)(2,1)S(1)} collective-permute-done((bf16[128,256]{1,0:T(8,128)(2,1)S(1)}, bf16[128,256]{1,0:T(8,128)(2,1)S(1)}, u32[]{:S(2)}, u32[]{:S(2)}) %collective-permute-start.3) | collective-permute-done | bytes 65568 | tf_op jit(solution)/shard_map/ppermute | solution.py:346
  21.3 2.2 %probs_part.6 = (bf16[4,384,384]{2,1,0:T(8,128)(2,1)S(1)}, f32[384,512]{1,0:T(8,128)S(1)}) custom-call(s32[8]{0:T(128)S(1)} %concatenate.11.refs_2_.refs_0_, bf16[384,2048]{1,0:T(8,128)(2,1)S(1)} %copy-done, bf16[384,512]{1,0:T(8,128)(2,1)S(1)} %copy-done.2, bf16[384,2048]{1,0:T(8,128)(2,1)S(1)} %copy-done.1, ...), custom_call_target="tpu_custom_call", output_to_operand_aliasing={{1}: (4, {})} | custom-call | flops 1000 | bytes 1000 | tf_op jit(solution)/shard_map/probs_part/pallas_call | solution.py:53
  23.5 1.9 %collective-permute-done.4.refs_1_ = bf16[256,256]{1,0:T(8,128)(2,1)S(1)} collective-permute-done((bf16[256,256]{1,0:T(8,128)(2,1)S(1)}, bf16[256,256]{1,0:T(8,128)(2,1)S(1)}, u32[]{:S(2)}, u32[]{:S(2)}) %collective-permute-start.4) | collective-permute-done | bytes 131104 | tf_op jit(solution)/shard_map/ppermute | solution.py:346
  25.5 2.8 %collective-permute-start.5 = (bf16[512,128]{1,0:T(8,128)(2,1)S(1)}, bf16[512,128]{1,0:T(8,128)(2,1)S(1)}, u32[]{:S(2)}, u32[]{:S(2)}) collective-permute-start(bf16[512,128]{1,0:T(8,128)(2,1)S(1)} %get-tuple-element.55.refs_5_.refs_2_), channel_id=1, source_target_pairs={{0,4},{2,6},{4,0},{6,2},{8,12},{10,14},{12,8},{14,10},{16,20},{18,... | collective-permute-start | bytes 393224 | tf_op jit(solution)/shard_map/ppermute | solution.py:346
  28.3 2.7 %collective-permute-start.8 = (bf16[512,128]{1,0:T(8,128)(2,1)S(1)}, bf16[512,128]{1,0:T(8,128)(2,1)S(1)}, u32[]{:S(2)}, u32[]{:S(2)}) collective-permute-start(bf16[512,128]{1,0:T(8,128)(2,1)S(1)} %get-tuple-element.57.refs_4_), channel_id=1, source_target_pairs={{0,24},{2,26},{4,28},{6,30},{8,0},{10,2},{12,4},{14,6},{16,8},{18,... | collective-permute-start | bytes 393224 | tf_op jit(solution)/shard_map/ppermute | solution.py:346
  31.4 0.7 collective-permute-start.6
  32.1 2.2 %probs_part.7 = (bf16[4,384,384]{2,1,0:T(8,128)(2,1)S(1)}, f32[384,512]{1,0:T(8,128)S(1)}) custom-call(s32[8]{0:T(128)S(1)} %concatenate.11.refs_2_.refs_0_, bf16[384,2048]{1,0:T(8,128)(2,1)S(1)} %copy-done, bf16[384,512]{1,0:T(8,128)(2,1)S(1)} %copy-done.2, bf16[384,2048]{1,0:T(8,128)(2,1)S(1)} %copy-done.1, ...), custom_call_target="tpu_custom_call", output_to_operand_aliasing={{1}: (4, {})} | custom-call | flops 1000 | bytes 1000 | tf_op jit(solution)/shard_map/probs_part/pallas_call | solution.py:53
  34.3 2.2 %collective-permute-done.7.refs_6_ = bf16[512,128]{1,0:T(8,128)(2,1)S(1)} collective-permute-done((bf16[512,128]{1,0:T(8,128)(2,1)S(1)}, bf16[512,128]{1,0:T(8,128)(2,1)S(1)}, u32[]{:S(2)}, u32[]{:S(2)}) %collective-permute-start.7) | collective-permute-done | bytes 131104 | tf_op jit(solution)/shard_map/ppermute | solution.py:346
  36.5 1.3 %collective-permute-done.6.refs_5_ = bf16[512,128]{1,0:T(8,128)(2,1)S(1)} collective-permute-done((bf16[512,128]{1,0:T(8,128)(2,1)S(1)}, bf16[512,128]{1,0:T(8,128)(2,1)S(1)}, u32[]{:S(2)}, u32[]{:S(2)}) %collective-permute-start.6) | collective-permute-done | bytes 131104 | tf_op jit(solution)/shard_map/ppermute | solution.py:346
  37.8 0.6 join.9
  38.7 0.6 collective-permute-start.12
  39.7 0.5 collective-permute-start.10
  40.2 4.3 %collective-permute-start.9 = (bf16[384,256]{1,0:T(8,128)(2,1)S(1)}, bf16[384,256]{1,0:T(8,128)(2,1)S(1)}, u32[]{:S(2)}, u32[]{:S(2)}) collective-permute-start(bf16[384,256]{1,0:T(8,128)(2,1)S(1)} %get-tuple-element.58), channel_id=1, source_target_pairs={{0,2},{2,0},{4,6},{6,4},{8,10},{10,8},{12,14},{14,12},{16,18},{18,... | collective-permute-start | bytes 589832 | tf_op jit(solution)/shard_map/ppermute | solution.py:346
  44.6 1.1 %collective-permute-done.9.refs_4_ = bf16[384,256]{1,0:T(8,128)(2,1)S(1)} collective-permute-done((bf16[384,256]{1,0:T(8,128)(2,1)S(1)}, bf16[384,256]{1,0:T(8,128)(2,1)S(1)}, u32[]{:S(2)}, u32[]{:S(2)}) %collective-permute-start.9) | collective-permute-done | bytes 196640 | tf_op jit(solution)/shard_map/ppermute | solution.py:346
  45.6 0.5 collective-permute-done.11.refs_8_
  46.2 6.8 %collective-permute-done.10.refs_7_ = bf16[1024,128]{1,0:T(8,128)(2,1)S(1)} collective-permute-done((bf16[1024,128]{1,0:T(8,128)(2,1)S(1)}, bf16[1024,128]{1,0:T(8,128)(2,1)S(1)}, u32[]{:S(2)}, u32[]{:S(2)}) %collective-permute-start.10) | collective-permute-done | bytes 262176 | tf_op jit(solution)/shard_map/ppermute | solution.py:346
  53.0 2.9 %raw_part.1 = (bf16[384,256]{1,0:T(8,128)(2,1)S(1)}, bf16[384,256]{1,0:T(8,128)(2,1)S(1)}, f32[1,256]{1,0:T(1,128)S(1)}, bf16[2048,256]{1,0:T(8,128)(2,1)S(1)}, ...) custom-call(s32[8]{0:T(128)S(1)} %concatenate.11.refs_2_.refs_0_, ...), custom_call_target="tpu_custom_call" | custom-call | flops 1000 | bytes 1000 | tf_op jit(solution)/shard_map/raw_part/pallas_call | solution.py:53
  56.0 2.3 %collective-permute-start.16 = (bf16[2048,256]{1,0:T(8,128)(2,1)S(1)}, bf16[2048,256]{1,0:T(8,128)(2,1)S(1)}, u32[]{:S(2)}, u32[]{:S(2)}) collective-permute-start(bf16[2048,256]{1,0:T(8,128)(2,1)S(1)} %get-tuple-element.67.refs_6_), channel_id=1, source_target_pairs={{0,2},{2,0},{4,6},{6,4},{8,10},{10,8},{12,14},{14,12},{16,18},{18,... | collective-permute-start | bytes 3145736 | tf_op jit(solution)/shard_map/ppermute | solution.py:346
  58.2 1.2 %collective-permute-start.20 = (bf16[1280,256]{1,0:T(8,128)(2,1)S(1)}, bf16[1280,256]{1,0:T(8,128)(2,1)S(1)}, u32[]{:S(2)}, u32[]{:S(2)}) collective-permute-start(bf16[1280,256]{1,0:T(8,128)(2,1)S(1)} %get-tuple-element.78), channel_id=1, source_target_pairs={{0,1},{1,0},{2,3},{3,2},{4,5},{5,4},{6,7},{7,6},{8,9},{9,8},{10,11... | collective-permute-start | bytes 1966088 | tf_op jit(solution)/shard_map/ppermute | solution.py:396
  59.4 0.4 collective-permute-start.14
  59.8 1.8 %collective-permute-start.23 = (bf16[1536,256]{1,0:T(8,128)(2,1)S(1)}, bf16[1536,256]{1,0:T(8,128)(2,1)S(1)}, u32[]{:S(2)}, u32[]{:S(2)}) collective-permute-start(bf16[1536,256]{1,0:T(8,128)(2,1)S(1)} %get-tuple-element.82), channel_id=1, source_target_pairs={{0,5},{1,4},{2,7},{3,6},{4,1},{5,0},{6,3},{7,2},{8,13},{9,12},{10,... | collective-permute-start | bytes 2359304 | tf_op jit(solution)/shard_map/ppermute | solution.py:397
  61.6 2.6 %grads_part.4 = (bf16[384,2048]{1,0:T(8,128)(2,1)}, bf16[384,512]{1,0:T(8,128)(2,1)}, f32[8,128]{1,0:T(8,128)S(1)}) custom-call(s32[8]{0:T(128)S(1)} %concatenate.11.refs_2_.refs_0_, bf16[384,2048]{1,0:T(8,128)(2,1)S(1)} %copy-done, bf16[384,512]{1,0:T(8,128)(2,1)S(1)} %copy-done.2, bf16[384,2048]{1,0:T(8,128)(2,1)S(1)} %copy-done.1, ...), custom_call_target="tpu_custom_call" | custom-call | flops 1000 | bytes 1000 | tf_op jit(solution)/shard_map/grads_part/pallas_call | solution.py:53
  64.3 1.5 %collective-permute-start.17 = (f32[1,256]{1,0:T(1,128)S(1)}, f32[1,256]{1,0:T(1,128)S(1)}, u32[]{:S(2)}, u32[]{:S(2)}) collective-permute-start(f32[1,256]{1,0:T(1,128)S(1)} %add.24.refs_9_.refs_0_), channel_id=1, source_target_pairs={{0,16},{2,18},{4,20},{6,22},{8,24},{10,26},{12,28},{14,30},{16,0},... | collective-permute-start | bytes 3080 | tf_op jit(solution)/shard_map/ppermute | solution.py:346
  65.8 2.6 %grads_part.5 = (bf16[384,2048]{1,0:T(8,128)(2,1)}, bf16[384,512]{1,0:T(8,128)(2,1)}, f32[8,128]{1,0:T(8,128)S(1)}) custom-call(s32[8]{0:T(128)S(1)} %concatenate.11.refs_2_.refs_0_, bf16[384,2048]{1,0:T(8,128)(2,1)S(1)} %copy-done, bf16[384,512]{1,0:T(8,128)(2,1)S(1)} %copy-done.2, ...), custom_call_target="tpu_custom_call", output_to_operand_aliasing={{0}: (7, {}), {1}: (8, {})} | custom-call | flops 1000 | bytes 1000 | tf_op jit(solution)/shard_map/grads_part/pallas_call | solution.py:53
  68.5 2.1 %collective-permute-start.18 = (f32[1,256]{1,0:T(1,128)S(1)}, f32[1,256]{1,0:T(1,128)S(1)}, u32[]{:S(2)}, u32[]{:S(2)}) collective-permute-start(f32[1,256]{1,0:T(1,128)S(1)} %add.25.refs_9_.refs_0_), channel_id=1, source_target_pairs={{0,32},{2,34},{4,36},{6,38},{8,40},{10,42},{12,44},{14,46},{16,48}... | collective-permute-start | bytes 3080 | tf_op jit(solution)/shard_map/ppermute | solution.py:346
  70.6 2.6 %grads_part.6 = (bf16[384,2048]{1,0:T(8,128)(2,1)}, bf16[384,512]{1,0:T(8,128)(2,1)}, f32[8,128]{1,0:T(8,128)S(1)}) custom-call(s32[8]{0:T(128)S(1)} %concatenate.11.refs_2_.refs_0_, bf16[384,2048]{1,0:T(8,128)(2,1)S(1)} %copy-done, bf16[384,512]{1,0:T(8,128)(2,1)S(1)} %copy-done.2, ...), custom_call_target="tpu_custom_call", output_to_operand_aliasing={{0}: (7, {}), {1}: (8, {})} | custom-call | flops 1000 | bytes 1000 | tf_op jit(solution)/shard_map/grads_part/pallas_call | solution.py:53
  73.2 0.8 collective-permute-start.19
  74.0 2.6 %grads_part.7 = (bf16[384,2048]{1,0:T(8,128)(2,1)}, bf16[384,512]{1,0:T(8,128)(2,1)}, f32[8,128]{1,0:T(8,128)S(1)}) custom-call(s32[8]{0:T(128)S(1)} %concatenate.11.refs_2_.refs_0_, bf16[384,2048]{1,0:T(8,128)(2,1)S(1)} %copy-done, bf16[384,512]{1,0:T(8,128)(2,1)S(1)} %copy-done.2, ...), custom_call_target="tpu_custom_call", output_to_operand_aliasing={{0}: (7, {}), {1}: (8, {})} | custom-call | flops 1000 | bytes 1000 | tf_op jit(solution)/shard_map/grads_part/pallas_call | solution.py:53
  76.6 0.5 collective-permute-done.19.refs_1_
  77.1 2.7 %collective-permute-start.22 = (bf16[1280,256]{1,0:T(8,128)(2,1)S(1)}, bf16[1280,256]{1,0:T(8,128)(2,1)S(1)}, u32[]{:S(2)}, u32[]{:S(2)}) collective-permute-start(bf16[1280,256]{1,0:T(8,128)(2,1)S(1)} %get-tuple-element.79.refs_3_.refs_4_), channel_id=1, source_target_pairs={{0,2},{2,0},{4,6},{6,4},{8,10},{10,8},{12,14},{14,12},{16,18},{18,... | collective-permute-start | bytes 1966088 | tf_op jit(solution)/shard_map/ppermute | solution.py:346
  79.9 3.0 %collective-permute-start.21 = (f32[1,256]{1,0:T(1,128)S(1)}, f32[1,256]{1,0:T(1,128)S(1)}, u32[]{:S(2)}, u32[]{:S(2)}) collective-permute-start(f32[1,256]{1,0:T(1,128)S(1)} %get-tuple-element.80.refs_8_.refs_0_), channel_id=1, source_target_pairs={{0,128},{2,130},{4,132},{6,134},{8,136},{10,138},{12,140},{14,142}... | collective-permute-start | bytes 3080 | tf_op jit(solution)/shard_map/ppermute | solution.py:346
  82.9 1.9 %hidden_part.2 = (bf16[384,2048]{1,0:T(8,128)(2,1)}, f32[8,128]{1,0:T(8,128)S(1)}) custom-call(s32[8]{0:T(128)S(1)} %concatenate.11.refs_2_.refs_0_, f32[384,512]{1,0:T(8,128)S(1)} %get-tuple-element.56.refs_1_.refs_3_, f32[1,512]{1,0:T(1,128)S(1)} %bitcast.11, bf16[1280,256]{1,0:T(8,128)(2,1)S(1)} %get-tuple-element.79.refs_3_.refs_4_, ...), custom_call_target="tpu_custom_call" | custom-call | flops 1000 | bytes 1000 | tf_op jit(solution)/shard_map/hidden_part/pallas_call | solution.py:53
  84.8 1.4 %collective-permute-done.21.refs_1_ = f32[1,256]{1,0:T(1,128)S(1)} collective-permute-done((f32[1,256]{1,0:T(1,128)S(1)}, f32[1,256]{1,0:T(1,128)S(1)}, u32[]{:S(2)}, u32[]{:S(2)}) %collective-permute-start.21) | collective-permute-done | bytes 1056 | tf_op jit(solution)/shard_map/ppermute | solution.py:346
  86.2 1.2 %collective-permute-start.24 = (bf16[1536,256]{1,0:T(8,128)(2,1)S(1)}, bf16[1536,256]{1,0:T(8,128)(2,1)S(1)}, u32[]{:S(2)}, u32[]{:S(2)}) collective-permute-start(bf16[1536,256]{1,0:T(8,128)(2,1)S(1)} %get-tuple-element.83.refs_4_), channel_id=1, source_target_pairs={{0,2},{2,0},{4,6},{6,4},{8,10},{10,8},{12,14},{14,12},{16,18},{18,... | collective-permute-start | bytes 2359304 | tf_op jit(solution)/shard_map/ppermute | solution.py:346
  87.4 1.0 %collective-permute-start.25 = (f32[1,256]{1,0:T(1,128)S(1)}, f32[1,256]{1,0:T(1,128)S(1)}, u32[]{:S(2)}, u32[]{:S(2)}) collective-permute-start(f32[1,256]{1,0:T(1,128)S(1)} %get-tuple-element.85.refs_9_.refs_0_), channel_id=1, source_target_pairs={{0,4},{2,6},{4,0},{6,2},{8,12},{10,14},{12,8},{14,10},{16,20},{18,... | collective-permute-start | bytes 3080 | tf_op jit(solution)/shard_map/ppermute | solution.py:346
  88.3 0.9 %collective-permute-done.24.refs_5_ = bf16[1536,256]{1,0:T(8,128)(2,1)S(1)} collective-permute-done((bf16[1536,256]{1,0:T(8,128)(2,1)S(1)}, bf16[1536,256]{1,0:T(8,128)(2,1)S(1)}, u32[]{:S(2)}, u32[]{:S(2)}) %collective-permute-start.24) | collective-permute-done | bytes 786464 | tf_op jit(solution)/shard_map/ppermute | solution.py:346
  89.3 3.0 %hidden_part.3 = (bf16[384,2048]{1,0:T(8,128)(2,1)}, f32[8,128]{1,0:T(8,128)S(1)}) custom-call(s32[8]{0:T(128)S(1)} %concatenate.11.refs_2_.refs_0_, f32[384,512]{1,0:T(8,128)S(1)} %get-tuple-element.56.refs_1_.refs_3_, f32[1,512]{1,0:T(1,128)S(1)} %bitcast.12, ...), custom_call_target="tpu_custom_call", output_to_operand_aliasing={{0}: (8, {})} | custom-call | flops 1000 | bytes 1000 | tf_op jit(solution)/shard_map/hidden_part/pallas_call | solution.py:53
  92.3 0.5 collective-permute-start.26
  92.7 0.8 collective-permute-done.26
  93.6 0.6 maximum_multiply_fusion
  (40 shorter events, 1.8 us)
Async XLA Ops:
  0.6 4.4 %collective-permute-start = (bf16[32,512]{1,0:T(8,128)(2,1)}, bf16[32,512]{1,0:T(8,128)(2,1)S(1)}, u32[]{:S(2)}, u32[]{:S(2)}) collective-permute-start(bf16[32,512]{1,0:T(8,128)(2,1)} %refs_0_.1), channel_id=1, source_target_pairs={{0,2},{2,0},{4,6},{6,4},{8,10},{10,8},{12,14},{14,12},{16,18},{18,... | collective-permute-start | bytes 98312 | tf_op jit(solution)/shard_map/ppermute | solution.py:346
  5.8 8.7 %collective-permute-start.1 = (bf16[64,256]{1,0:T(8,128)(2,1)S(1)}, bf16[64,256]{1,0:T(8,128)(2,1)S(1)}, u32[]{:S(2)}, u32[]{:S(2)}) collective-permute-start(bf16[64,256]{1,0:T(8,128)(2,1)S(1)} %join.5.refs_5_.refs_0_), channel_id=1, source_target_pairs={{0,128},{2,130},{4,132},{6,134},{8,136},{10,138},{12,140},{14,142}... | collective-permute-start | bytes 98312 | tf_op jit(solution)/shard_map/ppermute | solution.py:346
  14.5 2.0 %copy-start = (bf16[384,2048]{1,0:T(8,128)(2,1)S(1)}, bf16[384,2048]{1,0:T(8,128)(2,1)}, u32[]{:S(2)}) copy-start(bf16[384,2048]{1,0:T(8,128)(2,1)} %refs_1_.15) | copy-start | bytes 4718596
  14.5 2.0 %copy-start.1 = (bf16[384,2048]{1,0:T(8,128)(2,1)S(1)}, bf16[384,2048]{1,0:T(8,128)(2,1)}, u32[]{:S(2)}) copy-start(bf16[384,2048]{1,0:T(8,128)(2,1)} %refs_3_.15) | copy-start | bytes 4718596
  14.5 2.0 %copy-start.2 = (bf16[384,512]{1,0:T(8,128)(2,1)S(1)}, bf16[384,512]{1,0:T(8,128)(2,1)}, u32[]{:S(2)}) copy-start(bf16[384,512]{1,0:T(8,128)(2,1)} %refs_2_.15) | copy-start | bytes 1179652
  14.5 10.9 %collective-permute-start.2 = (bf16[384,4096]{1,0:T(8,128)(2,1)S(1)}, bf16[384,4096]{1,0:T(8,128)(2,1)S(1)}, u32[]{:S(2)}, u32[]{:S(2)}) collective-permute-start(bf16[384,4096]{1,0:T(8,128)(2,1)S(1)} %get-tuple-element.48.refs_1_), channel_id=1, source_target_pairs={{0,2},{2,0},{4,6},{6,4},{8,10},{10,8},{12,14},{14,12},{16,18},{18,... | collective-permute-start | bytes 9437192 | tf_op jit(solution)/shard_map/ppermute | solution.py:346
  15.2 6.0 %collective-permute-start.3 = (bf16[128,256]{1,0:T(8,128)(2,1)S(1)}, bf16[128,256]{1,0:T(8,128)(2,1)S(1)}, u32[]{:S(2)}, u32[]{:S(2)}) collective-permute-start(bf16[128,256]{1,0:T(8,128)(2,1)S(1)} %get-tuple-element.50.refs_5_.refs_0_), channel_id=1, source_target_pairs={{0,64},{2,66},{4,68},{6,70},{8,72},{10,74},{12,76},{14,78},{16,80}... | collective-permute-start | bytes 196616 | tf_op jit(solution)/shard_map/ppermute | solution.py:346
  21.2 4.2 %collective-permute-start.4 = (bf16[256,256]{1,0:T(8,128)(2,1)S(1)}, bf16[256,256]{1,0:T(8,128)(2,1)S(1)}, u32[]{:S(2)}, u32[]{:S(2)}) collective-permute-start(bf16[256,256]{1,0:T(8,128)(2,1)S(1)} %join.7.refs_5_.refs_0_), channel_id=1, source_target_pairs={{0,32},{2,34},{4,36},{6,38},{8,40},{10,42},{12,44},{14,46},{16,48}... | collective-permute-start | bytes 393224 | tf_op jit(solution)/shard_map/ppermute | solution.py:346
  25.5 8.8 %collective-permute-start.5 = (bf16[512,128]{1,0:T(8,128)(2,1)S(1)}, bf16[512,128]{1,0:T(8,128)(2,1)S(1)}, u32[]{:S(2)}, u32[]{:S(2)}) collective-permute-start(bf16[512,128]{1,0:T(8,128)(2,1)S(1)} %get-tuple-element.55.refs_5_.refs_2_), channel_id=1, source_target_pairs={{0,4},{2,6},{4,0},{6,2},{8,12},{10,14},{12,8},{14,10},{16,20},{18,... | collective-permute-start | bytes 393224 | tf_op jit(solution)/shard_map/ppermute | solution.py:346
  28.3 6.0 %collective-permute-start.8 = (bf16[512,128]{1,0:T(8,128)(2,1)S(1)}, bf16[512,128]{1,0:T(8,128)(2,1)S(1)}, u32[]{:S(2)}, u32[]{:S(2)}) collective-permute-start(bf16[512,128]{1,0:T(8,128)(2,1)S(1)} %get-tuple-element.57.refs_4_), channel_id=1, source_target_pairs={{0,24},{2,26},{4,28},{6,30},{8,0},{10,2},{12,4},{14,6},{16,8},{18,... | collective-permute-start | bytes 393224 | tf_op jit(solution)/shard_map/ppermute | solution.py:346
  31.1 5.4 %collective-permute-start.7 = (bf16[512,128]{1,0:T(8,128)(2,1)S(1)}, bf16[512,128]{1,0:T(8,128)(2,1)S(1)}, u32[]{:S(2)}, u32[]{:S(2)}) collective-permute-start(bf16[512,128]{1,0:T(8,128)(2,1)S(1)} %get-tuple-element.57.refs_4_), channel_id=1, source_target_pairs={{0,16},{2,18},{4,20},{6,22},{8,24},{10,26},{12,28},{14,30},{16,0},... | collective-permute-start | bytes 393224 | tf_op jit(solution)/shard_map/ppermute | solution.py:346
  31.4 6.4 %collective-permute-start.6 = (bf16[512,128]{1,0:T(8,128)(2,1)S(1)}, bf16[512,128]{1,0:T(8,128)(2,1)S(1)}, u32[]{:S(2)}, u32[]{:S(2)}) collective-permute-start(bf16[512,128]{1,0:T(8,128)(2,1)S(1)} %get-tuple-element.57.refs_4_), channel_id=1, source_target_pairs={{0,8},{2,10},{4,12},{6,14},{8,16},{10,18},{12,20},{14,22},{16,24},... | collective-permute-start | bytes 393224 | tf_op jit(solution)/shard_map/ppermute | solution.py:346
  34.3 18.7 %copy-start.3 = (f32[512]{0:T(512)S(1)}, f32[512]{0:T(512)}, u32[]{:S(2)}) copy-start(f32[512]{0:T(512)} %param.11) | copy-start | bytes 6148
  38.4 14.6 %collective-permute-start.13 = (bf16[2048,128]{1,0:T(8,128)(2,1)S(1)}, bf16[2048,128]{1,0:T(8,128)(2,1)S(1)}, u32[]{:S(2)}, u32[]{:S(2)}) collective-permute-start(bf16[2048,128]{1,0:T(8,128)(2,1)S(1)} %get-tuple-element.60.refs_10_), channel_id=1, source_target_pairs={{0,4},{2,6},{4,0},{6,2},{8,12},{10,14},{12,8},{14,10},{16,20},{18,... | collective-permute-start | bytes 1572872 | tf_op jit(solution)/shard_map/ppermute | solution.py:346
  38.7 6.9 %collective-permute-start.12 = (bf16[1024,128]{1,0:T(8,128)(2,1)S(1)}, bf16[1024,128]{1,0:T(8,128)(2,1)S(1)}, u32[]{:S(2)}, u32[]{:S(2)}) collective-permute-start(bf16[1024,128]{1,0:T(8,128)(2,1)S(1)} %get-tuple-element.59.refs_6_), channel_id=1, source_target_pairs={{0,24},{2,26},{4,28},{6,30},{8,0},{10,2},{12,4},{14,6},{16,8},{18,... | collective-permute-start | bytes 786440 | tf_op jit(solution)/shard_map/ppermute | solution.py:346
  39.4 6.8 %collective-permute-start.11 = (bf16[1024,128]{1,0:T(8,128)(2,1)S(1)}, bf16[1024,128]{1,0:T(8,128)(2,1)S(1)}, u32[]{:S(2)}, u32[]{:S(2)}) collective-permute-start(bf16[1024,128]{1,0:T(8,128)(2,1)S(1)} %get-tuple-element.59.refs_6_), channel_id=1, source_target_pairs={{0,16},{2,18},{4,20},{6,22},{8,24},{10,26},{12,28},{14,30},{16,0},... | collective-permute-start | bytes 786440 | tf_op jit(solution)/shard_map/ppermute | solution.py:346
  39.7 13.3 %collective-permute-start.10 = (bf16[1024,128]{1,0:T(8,128)(2,1)S(1)}, bf16[1024,128]{1,0:T(8,128)(2,1)S(1)}, u32[]{:S(2)}, u32[]{:S(2)}) collective-permute-start(bf16[1024,128]{1,0:T(8,128)(2,1)S(1)} %get-tuple-element.59.refs_6_), channel_id=1, source_target_pairs={{0,8},{2,10},{4,12},{6,14},{8,16},{10,18},{12,20},{14,22},{16,24},... | collective-permute-start | bytes 786440 | tf_op jit(solution)/shard_map/ppermute | solution.py:346
  40.2 5.4 %collective-permute-start.9 = (bf16[384,256]{1,0:T(8,128)(2,1)S(1)}, bf16[384,256]{1,0:T(8,128)(2,1)S(1)}, u32[]{:S(2)}, u32[]{:S(2)}) collective-permute-start(bf16[384,256]{1,0:T(8,128)(2,1)S(1)} %get-tuple-element.58), channel_id=1, source_target_pairs={{0,2},{2,0},{4,6},{6,4},{8,10},{10,8},{12,14},{14,12},{16,18},{18,... | collective-permute-start | bytes 589832 | tf_op jit(solution)/shard_map/ppermute | solution.py:346
  56.0 8.3 %collective-permute-start.16 = (bf16[2048,256]{1,0:T(8,128)(2,1)S(1)}, bf16[2048,256]{1,0:T(8,128)(2,1)S(1)}, u32[]{:S(2)}, u32[]{:S(2)}) collective-permute-start(bf16[2048,256]{1,0:T(8,128)(2,1)S(1)} %get-tuple-element.67.refs_6_), channel_id=1, source_target_pairs={{0,2},{2,0},{4,6},{6,4},{8,10},{10,8},{12,14},{14,12},{16,18},{18,... | collective-permute-start | bytes 3145736 | tf_op jit(solution)/shard_map/ppermute | solution.py:346
  58.2 18.4 %collective-permute-start.20 = (bf16[1280,256]{1,0:T(8,128)(2,1)S(1)}, bf16[1280,256]{1,0:T(8,128)(2,1)S(1)}, u32[]{:S(2)}, u32[]{:S(2)}) collective-permute-start(bf16[1280,256]{1,0:T(8,128)(2,1)S(1)} %get-tuple-element.78), channel_id=1, source_target_pairs={{0,1},{1,0},{2,3},{3,2},{4,5},{5,4},{6,7},{7,6},{8,9},{9,8},{10,11... | collective-permute-start | bytes 1966088 | tf_op jit(solution)/shard_map/ppermute | solution.py:396
  59.4 2.2 %collective-permute-start.14 = (bf16[384,256]{1,0:T(8,128)(2,1)S(1)}, bf16[384,256]{1,0:T(8,128)(2,1)S(1)}, u32[]{:S(2)}, u32[]{:S(2)}) collective-permute-start(bf16[384,256]{1,0:T(8,128)(2,1)S(1)} %get-tuple-element.62), channel_id=1, source_target_pairs={{0,2},{2,0},{4,6},{6,4},{8,10},{10,8},{12,14},{14,12},{16,18},{18,... | collective-permute-start | bytes 589832 | tf_op jit(solution)/shard_map/ppermute | solution.py:346
  59.8 25.0 %collective-permute-start.23 = (bf16[1536,256]{1,0:T(8,128)(2,1)S(1)}, bf16[1536,256]{1,0:T(8,128)(2,1)S(1)}, u32[]{:S(2)}, u32[]{:S(2)}) collective-permute-start(bf16[1536,256]{1,0:T(8,128)(2,1)S(1)} %get-tuple-element.82), channel_id=1, source_target_pairs={{0,5},{1,4},{2,7},{3,6},{4,1},{5,0},{6,3},{7,2},{8,13},{9,12},{10,... | collective-permute-start | bytes 2359304 | tf_op jit(solution)/shard_map/ppermute | solution.py:397
  61.6 2.7 %collective-permute-start.15 = (f32[1,256]{1,0:T(1,128)S(1)}, f32[1,256]{1,0:T(1,128)S(1)}, u32[]{:S(2)}, u32[]{:S(2)}) collective-permute-start(f32[1,256]{1,0:T(1,128)S(1)} %get-tuple-element.64.refs_7_.refs_0_), channel_id=1, source_target_pairs={{0,8},{2,10},{4,12},{6,14},{8,0},{10,2},{12,4},{14,6},{16,24},{18,... | collective-permute-start | bytes 3080 | tf_op jit(solution)/shard_map/ppermute | solution.py:346
  64.3 4.2 %collective-permute-start.17 = (f32[1,256]{1,0:T(1,128)S(1)}, f32[1,256]{1,0:T(1,128)S(1)}, u32[]{:S(2)}, u32[]{:S(2)}) collective-permute-start(f32[1,256]{1,0:T(1,128)S(1)} %add.24.refs_9_.refs_0_), channel_id=1, source_target_pairs={{0,16},{2,18},{4,20},{6,22},{8,24},{10,26},{12,28},{14,30},{16,0},... | collective-permute-start | bytes 3080 | tf_op jit(solution)/shard_map/ppermute | solution.py:346
  68.5 4.7 %collective-permute-start.18 = (f32[1,256]{1,0:T(1,128)S(1)}, f32[1,256]{1,0:T(1,128)S(1)}, u32[]{:S(2)}, u32[]{:S(2)}) collective-permute-start(f32[1,256]{1,0:T(1,128)S(1)} %add.25.refs_9_.refs_0_), channel_id=1, source_target_pairs={{0,32},{2,34},{4,36},{6,38},{8,40},{10,42},{12,44},{14,46},{16,48}... | collective-permute-start | bytes 3080 | tf_op jit(solution)/shard_map/ppermute | solution.py:346
  73.2 3.9 %collective-permute-start.19 = (f32[1,256]{1,0:T(1,128)S(1)}, f32[1,256]{1,0:T(1,128)S(1)}, u32[]{:S(2)}, u32[]{:S(2)}) collective-permute-start(f32[1,256]{1,0:T(1,128)S(1)} %add.26.refs_9_.refs_0_), channel_id=1, source_target_pairs={{0,64},{2,66},{4,68},{6,70},{8,72},{10,74},{12,76},{14,78},{16,80}... | collective-permute-start | bytes 3080 | tf_op jit(solution)/shard_map/ppermute | solution.py:346
  77.1 5.7 %collective-permute-start.22 = (bf16[1280,256]{1,0:T(8,128)(2,1)S(1)}, bf16[1280,256]{1,0:T(8,128)(2,1)S(1)}, u32[]{:S(2)}, u32[]{:S(2)}) collective-permute-start(bf16[1280,256]{1,0:T(8,128)(2,1)S(1)} %get-tuple-element.79.refs_3_.refs_4_), channel_id=1, source_target_pairs={{0,2},{2,0},{4,6},{6,4},{8,10},{10,8},{12,14},{14,12},{16,18},{18,... | collective-permute-start | bytes 1966088 | tf_op jit(solution)/shard_map/ppermute | solution.py:346
  79.9 6.3 %collective-permute-start.21 = (f32[1,256]{1,0:T(1,128)S(1)}, f32[1,256]{1,0:T(1,128)S(1)}, u32[]{:S(2)}, u32[]{:S(2)}) collective-permute-start(f32[1,256]{1,0:T(1,128)S(1)} %get-tuple-element.80.refs_8_.refs_0_), channel_id=1, source_target_pairs={{0,128},{2,130},{4,132},{6,134},{8,136},{10,138},{12,140},{14,142}... | collective-permute-start | bytes 3080 | tf_op jit(solution)/shard_map/ppermute | solution.py:346
  86.2 3.1 %collective-permute-start.24 = (bf16[1536,256]{1,0:T(8,128)(2,1)S(1)}, bf16[1536,256]{1,0:T(8,128)(2,1)S(1)}, u32[]{:S(2)}, u32[]{:S(2)}) collective-permute-start(bf16[1536,256]{1,0:T(8,128)(2,1)S(1)} %get-tuple-element.83.refs_4_), channel_id=1, source_target_pairs={{0,2},{2,0},{4,6},{6,4},{8,10},{10,8},{12,14},{14,12},{16,18},{18,... | collective-permute-start | bytes 2359304 | tf_op jit(solution)/shard_map/ppermute | solution.py:346
  87.4 4.9 %collective-permute-start.25 = (f32[1,256]{1,0:T(1,128)S(1)}, f32[1,256]{1,0:T(1,128)S(1)}, u32[]{:S(2)}, u32[]{:S(2)}) collective-permute-start(f32[1,256]{1,0:T(1,128)S(1)} %get-tuple-element.85.refs_9_.refs_0_), channel_id=1, source_target_pairs={{0,4},{2,6},{4,0},{6,2},{8,12},{10,14},{12,8},{14,10},{16,20},{18,... | collective-permute-start | bytes 3080 | tf_op jit(solution)/shard_map/ppermute | solution.py:346
  92.3 1.3 %collective-permute-start.26 = (f32[1,256]{1,0:T(1,128)S(1)}, f32[1,256]{1,0:T(1,128)S(1)}, u32[]{:S(2)}, u32[]{:S(2)}) collective-permute-start(f32[1,256]{1,0:T(1,128)S(1)} %add.29), channel_id=1, source_target_pairs={{0,2},{2,0},{4,6},{6,4},{8,10},{10,8},{12,14},{14,12},{16,18},{18,... | collective-permute-start | bytes 3080 | tf_op jit(solution)/shard_map/ppermute | solution.py:346
